TPU v7x, 512 devices: a whole 4x8x8 slice. The times are simulated.
512 devices in a mesh: seq: 128 (over x_hi, z, y), dp: 4 (over x_lo, core).
Axes of the slice: x: 4 (x_hi: 2, x_lo: 2; x = x_hi * 2 + x_lo), y: 8, z: 8, core: 2. Of those that a mesh axis runs over, the one named last changes fastest.
Arguments:
- teacher_query: bfloat16 [4, 32768, 512], P('dp', 'seq'), may hold values from -24 to 24
- teacher_key: bfloat16 [4, 32768, 512], P('dp', 'seq'), may hold values from -24 to 24
- student_query: bfloat16 [4, 32768, 512], P('dp', 'seq'), may hold values from -24 to 24
- student_key: bfloat16 [4, 32768, 512], P('dp', 'seq'), may hold values from -24 to 24
- segment_ids: int32 [4, 32768], P('dp'), may hold values from 0 to 36, never falling along the last dimension, each value on 1 to 1792 neighbouring positions
- head_weight: float32 [4], replicated, may hold values from 100 to 400
Outputs:
- query_grad: float32 [4, 32768, 512], P('dp', 'seq')
- key_grad: float32 [4, 32768, 512], P('dp', 'seq')
Inputs may be any that keep to these rules, and one draw needn't show every extreme that they name: `segment_ids`: every document of a window spans at most 1792 positions, and one spans exactly 1792.
All inputs are finite; a program needn't handle non-finite values.
Results may differ from a plain program's by a relative error of at most 0.0025.
Values may be sent and summed in bfloat16 or wider, within the bound.
No kernel may reach another device: no remote copies, remote signals or barrier semaphores. Data moves between devices by JAX's collectives and lax.ppermute only.
A program may use at most 64 MiB of HBM per device.

v0:
```python
import math

import jax
import jax.numpy as jnp
from jax import lax
from jax.sharding import PartitionSpec as P


def from_behind(block, axis, distance):
    devices = range(lax.axis_size(axis))
    route = [(i - distance, i) for i in devices if i - distance in devices]
    return lax.ppermute(block, axis, route)


def shortened(shard):

    def short(part):
        return part.astype(jnp.bfloat16) if part.dtype == jnp.float32 else part

    return jax.tree.map(short, shard)


def row_log_totals(scores, visible):
    masked = jnp.where(visible, scores, jnp.float32(-1e30))
    row_top = jnp.max(masked, axis=-1)
    summed = jnp.sum(
        jnp.where(visible, jnp.exp(masked - row_top[..., None]), jnp.float32(0.0)), axis=-1
    )
    return row_top + jnp.log(summed)


def softmax_rows(scores, log_total, visible):
    return jnp.where(visible, jnp.exp(scores - log_total[..., None]), jnp.float32(0.0))


def per_device(teacher_query, teacher_key, student_query, student_key, segment_ids, head_weight):
    tok_rows = teacher_query.shape[1]
    rel_width = teacher_query.shape[2]
    head_count = head_weight.shape[0]
    head_dim = rel_width // head_count
    score_scale = 1.0 / math.sqrt(head_dim)
    seq_index = lax.axis_index("seq")
    band = 8
    span = band * tok_rows

    def head_first(states):
        return states.reshape(states.shape[0], head_count, head_dim).transpose(1, 0, 2)

    def head_last(states):
        return states.transpose(1, 0, 2).reshape(states.shape[1], rel_width)

    teacher_band = teacher_key[0]
    student_band = student_key[0]
    shift_by = 1
    while shift_by < band:
        moved = from_behind((teacher_band, student_band), "seq", shift_by)
        teacher_band = jnp.concatenate([moved[0], teacher_band], axis=0)
        student_band = jnp.concatenate([moved[1], student_band], axis=0)
        shift_by = shift_by * 2
    own_start = seq_index * tok_rows
    seg_all = segment_ids[0]
    filler = jnp.full((span - tok_rows,), -1, jnp.int32)
    seg_own = lax.dynamic_slice_in_dim(seg_all, own_start, tok_rows)
    positions = own_start + jnp.arange(tok_rows, dtype=jnp.int32)
    seg_before = lax.dynamic_slice_in_dim(
        jnp.concatenate([filler, seg_all], axis=0), own_start, span
    )
    band_pos = own_start - (span - tok_rows) + jnp.arange(span, dtype=jnp.int32)
    visible = (band_pos[None, :] <= positions[:, None]) & (seg_before[None, :] == seg_own[:, None])

    def forward_head(inputs):
        teacher_rows, student_rows, teacher_cols, student_cols, weight = inputs
        teacher_scores = (
            jnp.einsum("qd,kd->qk", teacher_rows, teacher_cols, preferred_element_type=jnp.float32)
            * score_scale
        )
        student_scores = (
            jnp.einsum("qd,kd->qk", student_rows, student_cols, preferred_element_type=jnp.float32)
            * score_scale
        )
        teacher_total = row_log_totals(teacher_scores, visible)
        student_total = row_log_totals(student_scores, visible)
        teacher_probs = softmax_rows(teacher_scores, teacher_total, visible)
        student_probs = softmax_rows(student_scores, student_total, visible)
        grad_weights = (weight * (student_probs - teacher_probs)).astype(jnp.bfloat16)
        query_part = (
            jnp.einsum("qk,kd->qd", grad_weights, student_cols, preferred_element_type=jnp.float32)
            * score_scale
        )
        return (query_part, teacher_total, student_total)

    results = lax.map(
        forward_head,
        (
            head_first(teacher_query[0]),
            head_first(student_query[0]),
            head_first(teacher_band),
            head_first(student_band),
            head_weight,
        ),
    )
    query_grad = head_last(results[0]).reshape(1, tok_rows, rel_width)
    teacher_totals = results[1]
    student_totals = results[2]
    query_rows = (teacher_query[0], student_query[0])
    total_rows = (teacher_totals.T, student_totals.T)
    shift_by = 1
    while shift_by < band:
        moved = jax.tree.map(
            lambda part, own: part.astype(own.dtype),
            from_behind(shortened(query_rows), "seq", -shift_by),
            query_rows,
        )
        moved_totals = from_behind(total_rows, "seq", -shift_by)
        query_rows = tuple(
            (jnp.concatenate([mine, theirs], axis=0) for mine, theirs in zip(query_rows, moved))
        )
        total_rows = tuple(
            (
                jnp.concatenate([mine, theirs], axis=0)
                for mine, theirs in zip(total_rows, moved_totals)
            )
        )
        shift_by = shift_by * 2
    seg_after = lax.dynamic_slice_in_dim(
        jnp.concatenate([seg_all, filler], axis=0), own_start, span
    )
    after_pos = own_start + jnp.arange(span, dtype=jnp.int32)
    seen = (positions[None, :] <= after_pos[:, None]) & (seg_own[None, :] == seg_after[:, None])

    def key_head(inputs):
        (
            teacher_rows,
            student_rows,
            teacher_logs,
            student_logs,
            teacher_cols,
            student_cols,
            weight,
        ) = inputs
        teacher_scores = (
            jnp.einsum("qd,kd->qk", teacher_rows, teacher_cols, preferred_element_type=jnp.float32)
            * score_scale
        )
        student_scores = (
            jnp.einsum("qd,kd->qk", student_rows, student_cols, preferred_element_type=jnp.float32)
            * score_scale
        )
        teacher_probs = softmax_rows(teacher_scores, teacher_logs, seen)
        student_probs = softmax_rows(student_scores, student_logs, seen)
        grad_weights = (weight * (student_probs - teacher_probs)).astype(jnp.bfloat16)
        return jnp.einsum(
            "qk,qd->kd", grad_weights, student_rows, preferred_element_type=jnp.float32
        )

    key_parts = lax.map(
        key_head,
        (
            head_first(query_rows[0]),
            head_first(query_rows[1]),
            total_rows[0].T,
            total_rows[1].T,
            head_first(teacher_key[0]),
            head_first(student_key[0]),
            head_weight,
        ),
    )
    summed_keys = head_last(key_parts)
    key_grad = (summed_keys * score_scale).reshape(1, tok_rows, rel_width)
    return (query_grad, key_grad)


def solution(mesh):
    in_specs = (
        P("dp", "seq", None),
        P("dp", "seq", None),
        P("dp", "seq", None),
        P("dp", "seq", None),
        P("dp", None),
        P(),
    )
    out_specs = (P("dp", "seq", None), P("dp", "seq", None))
    return jax.shard_map(
        per_device, mesh=mesh, in_specs=in_specs, out_specs=out_specs, check_vma=False
    )
```

profile of v0, /device:TPU:460, one launch (start us, length us, event | category | flops | bytes accessed | tf_op | source)
XLA Modules:
  0.0 462.8 jit_solution(7465999766035041865)
XLA Ops:
  0.6 1.1 copy.14
  1.8 3.5 collective-permute-start.3
  5.3 1.1 copy.11
  6.4 3.5 collective-permute-start
  9.9 3.0 collective-permute-done.3
  12.9 0.8 pad_maximum_fusion.5
  13.7 4.8 %collective-permute-start.4 = (bf16[512,512]{0,1:T(8,128)(2,1)}, bf16[512,512]{0,1:T(8,128)(2,1)S(1)}, u32[]{:S(2)}, u32[]{:S(2)}) collective-permute-start(bf16[512,512]{0,1:T(8,128)(2,1)} %pad_maximum_fusion.5), channel_id=1, source_target_pairs={{0,8},{4,12},{8,16},{12,20},{16,24},{20,28},{24,32},{28,36},{32,40... | collective-permute-start | bytes 1572872 | tf_op jit(solution)/shard_map/ppermute | solution.py:12
  18.5 0.8 pad_maximum_fusion.4
  19.4 4.6 collective-permute-start.1
  24.1 18.0 %collective-permute-start.6 = (bf16[256,512]{0,1:T(8,128)(2,1)S(1)}, bf16[256,512]{0,1:T(8,128)(2,1)S(1)}, u32[]{:S(2)}, u32[]{:S(2)}) collective-permute-start(bf16[256,512]{0,1:T(8,128)(2,1)S(1)} %bitcast.160), channel_id=1, source_target_pairs={{4,0},{8,4},{12,8},{16,12},{20,16},{24,20},{28,24},{32,28},{36,32}... | collective-permute-start | bytes 786440 | tf_op jit(solution)/shard_map/ppermute | solution.py:12
  42.2 1.9 collective-permute-start.12
  44.1 141.1 %collective-permute-done.4 = bf16[512,512]{0,1:T(8,128)(2,1)S(1)} collective-permute-done((bf16[512,512]{0,1:T(8,128)(2,1)}, bf16[512,512]{0,1:T(8,128)(2,1)S(1)}, u32[]{:S(2)}, u32[]{:S(2)}) %collective-permute-start.4) | collective-permute-done | bytes 524320 | tf_op jit(solution)/shard_map/ppermute | solution.py:12
  185.3 1.2 pad_maximum_fusion.1
  186.4 8.5 %collective-permute-start.5 = (bf16[1024,512]{0,1:T(8,128)(2,1)}, bf16[1024,512]{0,1:T(8,128)(2,1)}, u32[]{:S(2)}, u32[]{:S(2)}) collective-permute-start(bf16[1024,512]{0,1:T(8,128)(2,1)} %pad_maximum_fusion.1), channel_id=1, source_target_pairs={{0,16},{4,20},{8,24},{12,28},{16,32},{20,36},{24,40},{28,44},{32,4... | collective-permute-start | bytes 3145736 | tf_op jit(solution)/shard_map/ppermute | solution.py:12
  195.0 0.8 pad_maximum_fusion.6
  195.8 3.2 collective-permute-start.7
  199.0 1.1 pad_maximum_fusion
  200.2 4.7 %collective-permute-start.2 = (bf16[1024,512]{0,1:T(8,128)(2,1)}, bf16[1024,512]{0,1:T(8,128)(2,1)}, u32[]{:S(2)}, u32[]{:S(2)}) collective-permute-start(bf16[1024,512]{0,1:T(8,128)(2,1)} %pad_maximum_fusion), channel_id=1, source_target_pairs={{0,16},{4,20},{8,24},{12,28},{16,32},{20,36},{24,40},{28,44},{32,4... | collective-permute-start | bytes 3145736 | tf_op jit(solution)/shard_map/ppermute | solution.py:12
  204.9 0.8 pad_maximum_fusion.7
  205.8 5.2 %collective-permute-start.13 = (bf16[512,512]{0,1:T(8,128)(2,1)}, bf16[512,512]{0,1:T(8,128)(2,1)S(1)}, u32[]{:S(2)}, u32[]{:S(2)}) collective-permute-start(bf16[512,512]{0,1:T(8,128)(2,1)} %pad_maximum_fusion.7), channel_id=1, source_target_pairs={{8,0},{12,4},{16,8},{20,12},{24,16},{28,20},{32,24},{36,28},{40,32... | collective-permute-start | bytes 1572872 | tf_op jit(solution)/shard_map/ppermute | solution.py:12
  211.1 59.7 %collective-permute-done.7 = bf16[512,512]{0,1:T(8,128)(2,1)S(1)} collective-permute-done((bf16[512,512]{0,1:T(8,128)(2,1)}, bf16[512,512]{0,1:T(8,128)(2,1)S(1)}, u32[]{:S(2)}, u32[]{:S(2)}) %collective-permute-start.7) | collective-permute-done | bytes 524320 | tf_op jit(solution)/shard_map/ppermute | solution.py:12
  270.9 1.1 pad_maximum_fusion.2
  272.0 1.9 collective-permute-start.8
  273.9 53.2 %collective-permute-done.13 = bf16[512,512]{0,1:T(8,128)(2,1)S(1)} collective-permute-done((bf16[512,512]{0,1:T(8,128)(2,1)}, bf16[512,512]{0,1:T(8,128)(2,1)S(1)}, u32[]{:S(2)}, u32[]{:S(2)}) %collective-permute-start.13) | collective-permute-done | bytes 524320 | tf_op jit(solution)/shard_map/ppermute | solution.py:12
  327.1 1.2 pad_maximum_fusion.3
  328.3 10.5 %collective-permute-start.14 = (bf16[1024,512]{0,1:T(8,128)(2,1)}, bf16[1024,512]{0,1:T(8,128)(2,1)}, u32[]{:S(2)}, u32[]{:S(2)}) collective-permute-start(bf16[1024,512]{0,1:T(8,128)(2,1)} %pad_maximum_fusion.3), channel_id=1, source_target_pairs={{16,0},{20,4},{24,8},{28,12},{32,16},{36,20},{40,24},{44,28},{48,3... | collective-permute-start | bytes 3145736 | tf_op jit(solution)/shard_map/ppermute | solution.py:12
  338.9 2.9 maximum_bitcast_fusion.1
  341.8 2.8 maximum_bitcast_fusion
  344.6 32.9 %while.26 = (s32[]{:T(128)}, f32[4,256,128]{2,1,0:T(8,128)S(1)}, f32[4,256]{1,0:T(4,128)S(1)}, f32[4,256]{1,0:T(4,128)S(1)}, f32[4]{0:T(128)S(1)}, /*index=5*/bf...) while((s32[]{:T(128)}, f32[4,256,128]{2,1,0:T(8,128)S(1)}, ...), condition=%wide.region_5.6_spmd.clone, body=%wide.region_0.5_spmd.clone.sunk | while | flops 419986944 | bytes 14513825 | solution.py:92
  344.6 1.8 fusion.72
  346.4 2.2 select_reduce_fusion.4
  350.0 2.8 fusion.73
  352.8 1.8 fusion.72
  354.6 2.2 select_reduce_fusion.4
  358.2 2.8 fusion.73
  361.0 1.8 fusion.72
  362.8 2.2 select_reduce_fusion.4
  365.1 0.7 select_reduce_fusion.5
  366.4 2.8 fusion.73
  369.3 1.8 fusion.72
  371.1 2.2 select_reduce_fusion.4
  374.6 2.8 fusion.73
  377.5 1.9 collective-permute-start.15
  379.4 1.9 collective-permute-start.9
  381.4 2.9 maximum_bitcast_fusion.2
  384.2 10.4 %collective-permute-done.14 = bf16[1024,512]{0,1:T(8,128)(2,1)} collective-permute-done((bf16[1024,512]{0,1:T(8,128)(2,1)}, bf16[1024,512]{0,1:T(8,128)(2,1)}, u32[]{:S(2)}, u32[]{:S(2)}) %collective-permute-start.14) | collective-permute-done | bytes 1048608 | tf_op jit(solution)/shard_map/ppermute | solution.py:12
  394.6 2.8 maximum_bitcast_fusion.3
  397.4 1.1 copy.20
  398.6 2.0 reshape_reshape.3
  400.6 1.9 collective-permute-start.16
  402.6 9.9 %collective-permute-start.10 = (f32[512,4]{0,1:T(4,128)S(1)}, f32[512,4]{0,1:T(4,128)S(1)}, u32[]{:S(2)}, u32[]{:S(2)}) collective-permute-start(f32[512,4]{0,1:T(4,128)S(1)} %pad_maximum_fusion.10), channel_id=1, source_target_pairs={{8,0},{12,4},{16,8},{20,12},{24,16},{28,20},{32,24},{36,28},{40,32... | collective-permute-start | bytes 24584 | tf_op jit(solution)/shard_map/ppermute | solution.py:12
  412.5 7.9 %collective-permute-start.17 = (f32[1024,4]{0,1:T(4,128)S(1)}, f32[1024,4]{0,1:T(4,128)S(1)}, u32[]{:S(2)}, u32[]{:S(2)}) collective-permute-start(f32[1024,4]{0,1:T(4,128)S(1)} %pad_maximum_fusion.9), channel_id=1, source_target_pairs={{16,0},{20,4},{24,8},{28,12},{32,16},{36,20},{40,24},{44,28},{48,3... | collective-permute-start | bytes 49160 | tf_op jit(solution)/shard_map/ppermute | solution.py:12
  420.5 3.9 collective-permute-start.11
  424.4 5.6 %collective-permute-done.11 = f32[1024,4]{0,1:T(4,128)S(1)} collective-permute-done((f32[1024,4]{0,1:T(4,128)S(1)}, f32[1024,4]{0,1:T(4,128)S(1)}, u32[]{:S(2)}, u32[]{:S(2)}) %collective-permute-start.11) | collective-permute-done | bytes 16416 | tf_op jit(solution)/shard_map/ppermute | solution.py:12
  430.1 31.3 %while.27 = (s32[]{:T(128)}, f32[4,256,128]{2,1,0:T(8,128)S(1)}, f32[4]{0:T(128)S(1)}, bf16[4,2048,128]{1,2,0:T(8,128)(2,1)S(1)}, bf16[4,256,128]{1,2,0:T(8,128)...) while((s32[]{:T(128)}, f32[4,256,128]{2,1,0:T(8,128)S(1)}, ...), condition=%wide.region_7.8_spmd.clone, body=%wide.region_6.7_spmd.clone.sunk | while | flops 410517504 | bytes 6119061 | solution.py:156
  430.1 2.9 fusion.79
  433.6 4.3 fusion.80
  437.9 2.9 fusion.79
  441.4 4.3 fusion.80
  445.7 2.9 fusion.79
  449.2 4.3 fusion.80
  453.6 2.9 fusion.79
  457.1 4.3 fusion.80
  461.8 1.0 mul.53
  (80 shorter events, 8.3 us)
Async XLA Ops:
  0.6 23.3 %copy-start.7 = (bf16[1,256,512]{2,1,0:T(8,128)(2,1)S(1)}, bf16[1,256,512]{2,1,0:T(8,128)(2,1)}, u32[]{:S(2)}) copy-start(bf16[1,256,512]{2,1,0:T(8,128)(2,1)} %param.12) | copy-start | bytes 786436
  0.6 41.4 %copy-start.8 = (bf16[1,256,512]{2,1,0:T(8,128)(2,1)S(1)}, bf16[1,256,512]{2,1,0:T(8,128)(2,1)}, u32[]{:S(2)}) copy-start(bf16[1,256,512]{2,1,0:T(8,128)(2,1)} %param.10) | copy-start | bytes 786436
  1.8 11.1 %collective-permute-start.3 = (bf16[256,512]{0,1:T(8,128)(2,1)S(1)}, bf16[256,512]{0,1:T(8,128)(2,1)S(1)}, u32[]{:S(2)}, u32[]{:S(2)}) collective-permute-start(bf16[256,512]{0,1:T(8,128)(2,1)S(1)} %bitcast.145), channel_id=1, source_target_pairs={{0,4},{4,8},{8,12},{12,16},{16,20},{20,24},{24,28},{28,32},{32,36}... | collective-permute-start | bytes 786440 | tf_op jit(solution)/shard_map/ppermute | solution.py:12
  6.4 12.1 %collective-permute-start = (bf16[256,512]{0,1:T(8,128)(2,1)S(1)}, bf16[256,512]{0,1:T(8,128)(2,1)S(1)}, u32[]{:S(2)}, u32[]{:S(2)}) collective-permute-start(bf16[256,512]{0,1:T(8,128)(2,1)S(1)} %bitcast.150), channel_id=1, source_target_pairs={{0,4},{4,8},{8,12},{12,16},{16,20},{20,24},{24,28},{28,32},{32,36}... | collective-permute-start | bytes 786440 | tf_op jit(solution)/shard_map/ppermute | solution.py:12
  13.7 171.5 %collective-permute-start.4 = (bf16[512,512]{0,1:T(8,128)(2,1)}, bf16[512,512]{0,1:T(8,128)(2,1)S(1)}, u32[]{:S(2)}, u32[]{:S(2)}) collective-permute-start(bf16[512,512]{0,1:T(8,128)(2,1)} %pad_maximum_fusion.5), channel_id=1, source_target_pairs={{0,8},{4,12},{8,16},{12,20},{16,24},{20,28},{24,32},{28,36},{32,40... | collective-permute-start | bytes 1572872 | tf_op jit(solution)/shard_map/ppermute | solution.py:12
  19.4 179.7 %collective-permute-start.1 = (bf16[512,512]{0,1:T(8,128)(2,1)}, bf16[512,512]{0,1:T(8,128)(2,1)S(1)}, u32[]{:S(2)}, u32[]{:S(2)}) collective-permute-start(bf16[512,512]{0,1:T(8,128)(2,1)} %pad_maximum_fusion.4), channel_id=1, source_target_pairs={{0,8},{4,12},{8,16},{12,20},{16,24},{20,28},{24,32},{28,36},{32,40... | collective-permute-start | bytes 1572872 | tf_op jit(solution)/shard_map/ppermute | solution.py:12
  24.1 170.9 %collective-permute-start.6 = (bf16[256,512]{0,1:T(8,128)(2,1)S(1)}, bf16[256,512]{0,1:T(8,128)(2,1)S(1)}, u32[]{:S(2)}, u32[]{:S(2)}) collective-permute-start(bf16[256,512]{0,1:T(8,128)(2,1)S(1)} %bitcast.160), channel_id=1, source_target_pairs={{4,0},{8,4},{12,8},{16,12},{20,16},{24,20},{28,24},{32,28},{36,32}... | collective-permute-start | bytes 786440 | tf_op jit(solution)/shard_map/ppermute | solution.py:12
  42.2 162.7 %collective-permute-start.12 = (bf16[256,512]{0,1:T(8,128)(2,1)S(1)}, bf16[256,512]{0,1:T(8,128)(2,1)S(1)}, u32[]{:S(2)}, u32[]{:S(2)}) collective-permute-start(bf16[256,512]{0,1:T(8,128)(2,1)S(1)} %bitcast.155), channel_id=1, source_target_pairs={{4,0},{8,4},{12,8},{16,12},{20,16},{24,20},{28,24},{32,28},{36,32}... | collective-permute-start | bytes 786440 | tf_op jit(solution)/shard_map/ppermute | solution.py:12
  185.3 9.7 %copy-start.3 = (bf16[512,512]{0,1:T(8,128)(2,1)}, bf16[512,512]{0,1:T(8,128)(2,1)S(1)}, u32[]{:S(2)}) copy-start(bf16[512,512]{0,1:T(8,128)(2,1)S(1)} %collective-permute-done.4) | copy-start | bytes 1572868
  186.4 24.5 %copy-start.9 = (s32[1,32768]{1,0:T(1,128)S(1)}, s32[1,32768]{1,0:T(1,128)}, u32[]{:S(2)}) copy-start(s32[1,32768]{1,0:T(1,128)} %param.14) | copy-start | bytes 393220
  186.4 152.4 %collective-permute-start.5 = (bf16[1024,512]{0,1:T(8,128)(2,1)}, bf16[1024,512]{0,1:T(8,128)(2,1)}, u32[]{:S(2)}, u32[]{:S(2)}) collective-permute-start(bf16[1024,512]{0,1:T(8,128)(2,1)} %pad_maximum_fusion.1), channel_id=1, source_target_pairs={{0,16},{4,20},{8,24},{12,28},{16,32},{20,36},{24,40},{28,44},{32,4... | collective-permute-start | bytes 3145736 | tf_op jit(solution)/shard_map/ppermute | solution.py:12
  195.8 75.0 %collective-permute-start.7 = (bf16[512,512]{0,1:T(8,128)(2,1)}, bf16[512,512]{0,1:T(8,128)(2,1)S(1)}, u32[]{:S(2)}, u32[]{:S(2)}) collective-permute-start(bf16[512,512]{0,1:T(8,128)(2,1)} %pad_maximum_fusion.6), channel_id=1, source_target_pairs={{8,0},{12,4},{16,8},{20,12},{24,16},{28,20},{32,24},{36,28},{40,32... | collective-permute-start | bytes 1572872 | tf_op jit(solution)/shard_map/ppermute | solution.py:12
  199.0 5.9 %copy-start.5 = (bf16[512,512]{0,1:T(8,128)(2,1)}, bf16[512,512]{0,1:T(8,128)(2,1)S(1)}, u32[]{:S(2)}) copy-start(bf16[512,512]{0,1:T(8,128)(2,1)S(1)} %collective-permute-done.1) | copy-start | bytes 1572868
  200.2 141.6 %collective-permute-start.2 = (bf16[1024,512]{0,1:T(8,128)(2,1)}, bf16[1024,512]{0,1:T(8,128)(2,1)}, u32[]{:S(2)}, u32[]{:S(2)}) collective-permute-start(bf16[1024,512]{0,1:T(8,128)(2,1)} %pad_maximum_fusion), channel_id=1, source_target_pairs={{0,16},{4,20},{8,24},{12,28},{16,32},{20,36},{24,40},{28,44},{32,4... | collective-permute-start | bytes 3145736 | tf_op jit(solution)/shard_map/ppermute | solution.py:12
  205.8 121.3 %collective-permute-start.13 = (bf16[512,512]{0,1:T(8,128)(2,1)}, bf16[512,512]{0,1:T(8,128)(2,1)S(1)}, u32[]{:S(2)}, u32[]{:S(2)}) collective-permute-start(bf16[512,512]{0,1:T(8,128)(2,1)} %pad_maximum_fusion.7), channel_id=1, source_target_pairs={{8,0},{12,4},{16,8},{20,12},{24,16},{28,20},{32,24},{36,28},{40,32... | collective-permute-start | bytes 1572872 | tf_op jit(solution)/shard_map/ppermute | solution.py:12
  211.1 127.8 %copy-start.4 = (bf16[512,512]{0,1:T(8,128)(2,1)S(1)}, bf16[512,512]{0,1:T(8,128)(2,1)}, u32[]{:S(2)}) copy-start(bf16[512,512]{0,1:T(8,128)(2,1)} %copy-done.3) | copy-start | bytes 1572868
  272.0 109.4 %collective-permute-start.8 = (bf16[1024,512]{0,1:T(8,128)(2,1)}, bf16[1024,512]{0,1:T(8,128)(2,1)}, u32[]{:S(2)}, u32[]{:S(2)}) collective-permute-start(bf16[1024,512]{0,1:T(8,128)(2,1)} %pad_maximum_fusion.2), channel_id=1, source_target_pairs={{16,0},{20,4},{24,8},{28,12},{32,16},{36,20},{40,24},{44,28},{48,3... | collective-permute-start | bytes 3145736 | tf_op jit(solution)/shard_map/ppermute | solution.py:12
  327.1 14.7 %copy-start.1 = (bf16[512,512]{0,1:T(8,128)(2,1)}, bf16[512,512]{0,1:T(8,128)(2,1)S(1)}, u32[]{:S(2)}) copy-start(bf16[512,512]{0,1:T(8,128)(2,1)S(1)} %collective-permute-done.13) | copy-start | bytes 1572868
  328.3 66.3 %collective-permute-start.14 = (bf16[1024,512]{0,1:T(8,128)(2,1)}, bf16[1024,512]{0,1:T(8,128)(2,1)}, u32[]{:S(2)}, u32[]{:S(2)}) collective-permute-start(bf16[1024,512]{0,1:T(8,128)(2,1)} %pad_maximum_fusion.3), channel_id=1, source_target_pairs={{16,0},{20,4},{24,8},{28,12},{32,16},{36,20},{40,24},{44,28},{48,3... | collective-permute-start | bytes 3145736 | tf_op jit(solution)/shard_map/ppermute | solution.py:12
  338.9 2.9 copy-start.6
  341.8 2.8 copy-start.10
  377.5 23.1 %collective-permute-start.15 = (f32[256,4]{0,1:T(4,128)S(1)}, f32[256,4]{0,1:T(4,128)S(1)}, u32[]{:S(2)}, u32[]{:S(2)}) collective-permute-start(f32[256,4]{0,1:T(4,128)S(1)} %bitcast.180), channel_id=1, source_target_pairs={{4,0},{8,4},{12,8},{16,12},{20,16},{24,20},{28,24},{32,28},{36,32}... | collective-permute-start | bytes 12296 | tf_op jit(solution)/shard_map/ppermute | solution.py:12
  379.4 23.1 %collective-permute-start.9 = (f32[256,4]{0,1:T(4,128)S(1)}, f32[256,4]{0,1:T(4,128)S(1)}, u32[]{:S(2)}, u32[]{:S(2)}) collective-permute-start(f32[256,4]{0,1:T(4,128)S(1)} %bitcast.184), channel_id=1, source_target_pairs={{4,0},{8,4},{12,8},{16,12},{20,16},{24,20},{28,24},{32,28},{36,32}... | collective-permute-start | bytes 12296 | tf_op jit(solution)/shard_map/ppermute | solution.py:12
  381.3 13.2 %copy-start.2 = (bf16[512,512]{0,1:T(8,128)(2,1)S(1)}, bf16[512,512]{0,1:T(8,128)(2,1)}, u32[]{:S(2)}) copy-start(bf16[512,512]{0,1:T(8,128)(2,1)} %copy-done.1) | copy-start | bytes 1572868
  397.4 32.6 %copy-start = (bf16[4,2048,128]{1,2,0:T(8,128)(2,1)S(1)}, bf16[4,2048,128]{1,2,0:T(8,128)(2,1)}, u32[]{:S(2)}) copy-start(bf16[4,2048,128]{1,2,0:T(8,128)(2,1)} %maximum_bitcast_fusion.2) | copy-start | bytes 6291460
  400.6 11.9 %collective-permute-start.16 = (f32[512,4]{0,1:T(4,128)S(1)}, f32[512,4]{0,1:T(4,128)S(1)}, u32[]{:S(2)}, u32[]{:S(2)}) collective-permute-start(f32[512,4]{0,1:T(4,128)S(1)} %pad_maximum_fusion.11), channel_id=1, source_target_pairs={{8,0},{12,4},{16,8},{20,12},{24,16},{28,20},{32,24},{36,28},{40,32... | collective-permute-start | bytes 24584 | tf_op jit(solution)/shard_map/ppermute | solution.py:12
  402.6 17.9 %collective-permute-start.10 = (f32[512,4]{0,1:T(4,128)S(1)}, f32[512,4]{0,1:T(4,128)S(1)}, u32[]{:S(2)}, u32[]{:S(2)}) collective-permute-start(f32[512,4]{0,1:T(4,128)S(1)} %pad_maximum_fusion.10), channel_id=1, source_target_pairs={{8,0},{12,4},{16,8},{20,12},{24,16},{28,20},{32,24},{36,28},{40,32... | collective-permute-start | bytes 24584 | tf_op jit(solution)/shard_map/ppermute | solution.py:12
  412.5 11.9 %collective-permute-start.17 = (f32[1024,4]{0,1:T(4,128)S(1)}, f32[1024,4]{0,1:T(4,128)S(1)}, u32[]{:S(2)}, u32[]{:S(2)}) collective-permute-start(f32[1024,4]{0,1:T(4,128)S(1)} %pad_maximum_fusion.9), channel_id=1, source_target_pairs={{16,0},{20,4},{24,8},{28,12},{32,16},{36,20},{40,24},{44,28},{48,3... | collective-permute-start | bytes 49160 | tf_op jit(solution)/shard_map/ppermute | solution.py:12
  420.5 9.5 %collective-permute-start.11 = (f32[1024,4]{0,1:T(4,128)S(1)}, f32[1024,4]{0,1:T(4,128)S(1)}, u32[]{:S(2)}, u32[]{:S(2)}) collective-permute-start(f32[1024,4]{0,1:T(4,128)S(1)} %pad_maximum_fusion.8), channel_id=1, source_target_pairs={{16,0},{20,4},{24,8},{28,12},{32,16},{36,20},{40,24},{44,28},{48,3... | collective-permute-start | bytes 49160 | tf_op jit(solution)/shard_map/ppermute | solution.py:12
where the time goes:
time: 464 us; the launch traced here: 463 us
  waiting for transfers between devices  273 us (59%)
  starting transfers between devices  97.7 us (21%)
  matrix products  55.9 us (12%)
  other arithmetic  22.4 us (5%)
  local copies, waits for them, and re-layouts  12.3 us (3%)
    ppermute x18, waiting for transfers between devices, from_behind(): return lax.ppermute(block, axis, route)  273 us
    ppermute x18, starting transfers between devices, from_behind(): return lax.ppermute(block, axis, route)  97.7 us
    dot_general x4, matrix products, key_head(): jnp.einsum('qk,qd->kd', grad_weights, student_rows, preferred_element_typ...  17.2 us
    dot_general x4, matrix products, key_head(): jnp.einsum('qd,kd->qk', student_rows, student_cols, preferred_element_typ...  11.6 us
    transpose x4, other arithmetic, head_first(): states.reshape(states.shape[0], head_count, head_dim).transpose(1, 0, 2)  11.3 us
    dot_general x4, matrix products, forward_head(): jnp.einsum('qk,kd->qd', grad_weights, student_cols, preferred_element_typ...  11.1 us
  transfers between devices with their start and end apart: 18, of which 6 were waited for; matrix products, arithmetic and copies ran while one was open for 12% of the time, Pallas kernels for 0%

commit v1 on v0

v1 whole, which is shorter than its diff:
```python
import functools
import math

import jax
import jax.numpy as jnp
from jax import lax
from jax.experimental import pallas as pl
from jax.experimental.pallas import tpu as pltpu
from jax.sharding import PartitionSpec as P

HEADS = 4
DIM = 128
TOK = 256
ROW = 8
QUART = 4
MASKED = -1e30
F32 = jnp.float32
BF16 = jnp.bfloat16
VMEM = pl.BlockSpec(memory_space=pltpu.VMEM)
SMEM = pl.BlockSpec(memory_space=pltpu.SMEM)
AXES = ("seq", "dp")


def routes(seq, dp):
    def index(y, rest, x_lo, core):
        return ((rest * ROW + y) * (dp // 2) + x_lo) * 2 + core

    rounds = [[] for _ in range(HEADS)]
    swap, down = [], []
    for rest in range(seq // ROW):
        for y in range(ROW):
            for x_lo in range(dp // 2):
                for core in range(2):
                    me = index(y, rest, x_lo, core)
                    swap.append((me, index(y, rest, x_lo, 1 - core)))
                    if rest + 1 < seq // ROW:
                        down.append((me, index(y, rest + 1, x_lo, core)))
                    for k in range(HEADS):
                        head = (y // 2 + k) % HEADS
                        rounds[k].append((me, index(2 * head + core, rest, x_lo, y % 2)))
    return rounds, swap, down


def reverse(route):
    return [(b, a) for a, b in route]


def pack_kernel(half_ref, a_ref, b_ref, *outs):
    for k, out in enumerate(outs):
        head = lax.rem(half_ref[0] + k, HEADS)
        columns = pl.ds(pl.multiple_of(head * DIM, DIM), DIM)
        out[0] = a_ref[:, columns]
        out[1] = b_ref[:, columns]


def pack(half, a, b):
    return pl.pallas_call(
        pack_kernel,
        out_shape=[jax.ShapeDtypeStruct((2, TOK, DIM), BF16)] * HEADS,
        in_specs=[SMEM, VMEM, VMEM],
        out_specs=[VMEM] * HEADS,
        cost_estimate=pl.CostEstimate(flops=0, bytes_accessed=4 * TOK * 512 * 2, transcendentals=0),
    )(half, a, b)


def unpack_kernel(half_ref, *refs):
    out = refs[-1]
    for k in range(HEADS):
        head = lax.rem(half_ref[0] + k, HEADS)
        columns = pl.ds(pl.multiple_of(head * DIM, DIM), DIM)
        out[:, columns] = refs[k][...].astype(F32)


def unpack(half, pieces):
    return pl.pallas_call(
        unpack_kernel,
        out_shape=jax.ShapeDtypeStruct((TOK, HEADS * DIM), F32),
        in_specs=[SMEM] + [VMEM] * HEADS,
        out_specs=VMEM,
        cost_estimate=pl.CostEstimate(flops=0, bytes_accessed=6 * TOK * 512, transcendentals=0),
    )(half, *pieces)


def main_kernel(
    info_ref, low_ref, weight_ref, segq_ref, segk_ref, q0, q1, q2, q3, own_ref, oth_ref, own_prev_ref, oth_prev_ref,
    dq_ref, keep_ref, send_ref,
    kt, ks, dk, pt, ps, top_t, top_s, sum_t, sum_s, dq_acc,
):
    head, side = info_ref[0], info_ref[1]
    weight = weight_ref[0]
    scale = 1.0 / math.sqrt(DIM)
    pace = scale * math.log2(math.e)
    queries = (q0, q1, q2, q3)

    def rows(block):
        return pl.ds(pl.multiple_of(block * TOK, TOK), TOK)

    def place(k, parity):
        return 2 * lax.rem(head - k + HEADS, HEADS) + parity

    for k in range(HEADS):
        for row, (mine, theirs) in enumerate(((own_prev_ref, oth_prev_ref), (own_ref, oth_ref))):
            here, there = rows(row * ROW + place(k, side)), rows(row * ROW + place(k, 1 - side))
            kt[here, :] = mine[k, 0]
            ks[here, :] = mine[k, 1]
            kt[there, :] = theirs[k, 0]
            ks[there, :] = theirs[k, 1]

    def clear(block, _):
        dk[rows(block), :] = jnp.zeros((TOK, DIM), F32)
        return 0

    lax.fori_loop(0, 2 * ROW, clear, 0)

    def halves(op, wide):
        return op(wide[:, :DIM], wide[:, DIM:])

    for k in range(HEADS):
        here = place(k, side)
        block = ROW + here
        low = low_ref[block]
        q_t, q_s = queries[k][0], queries[k][1]
        seg_q = segq_ref[rows(here), :]

        top_t[...] = jnp.full((TOK, DIM), MASKED, F32)
        top_s[...] = jnp.full((TOK, DIM), MASKED, F32)

        def scores(kb, visible):
            dims = (((1,), (1,)), ((), ()))
            s_t = lax.dot_general(q_t, kt[rows(kb), :], dims, preferred_element_type=F32)
            s_s = lax.dot_general(q_s, ks[rows(kb), :], dims, preferred_element_type=F32)
            s_t = jnp.where(visible, s_t, MASKED)
            s_s = jnp.where(visible, s_s, MASKED)
            pt[kb - low] = s_t
            ps[kb - low] = s_s
            top_t[...] = jnp.maximum(top_t[...], halves(jnp.maximum, s_t))
            top_s[...] = jnp.maximum(top_s[...], halves(jnp.maximum, s_s))

        def first(kb, _):
            scores(kb, segk_ref[pl.ds(kb, 1), :] == seg_q)
            return 0

        lax.fori_loop(low, block, first, 0)
        causal = lax.broadcasted_iota(jnp.int32, (TOK, TOK), 1) <= lax.broadcasted_iota(jnp.int32, (TOK, TOK), 0)
        scores(block, causal & (segk_ref[pl.ds(block, 1), :] == seg_q))

        m_t = jnp.max(top_t[...], axis=1, keepdims=True)
        m_s = jnp.max(top_s[...], axis=1, keepdims=True)
        sum_t[...] = jnp.zeros((TOK, DIM), F32)
        sum_s[...] = jnp.zeros((TOK, DIM), F32)

        def second(slot, _):
            e_t = jnp.exp2((pt[slot] - m_t) * pace)
            e_s = jnp.exp2((ps[slot] - m_s) * pace)
            pt[slot] = e_t
            ps[slot] = e_s
            sum_t[...] += halves(jnp.add, e_t)
            sum_s[...] += halves(jnp.add, e_s)
            return 0

        lax.fori_loop(0, block + 1 - low, second, 0)
        r_t = weight / jnp.sum(sum_t[...], axis=1, keepdims=True)
        r_s = weight / jnp.sum(sum_s[...], axis=1, keepdims=True)
        dq_acc[...] = jnp.zeros((TOK, DIM), F32)

        def third(kb, _):
            grad = (ps[kb - low] * r_s - pt[kb - low] * r_t).astype(BF16)
            dq_acc[...] += jnp.dot(grad, ks[rows(kb), :], preferred_element_type=F32)
            dk[rows(kb), :] += lax.dot_general(grad, q_s, (((0,), (0,)), ((), ())), preferred_element_type=F32)
            return 0

        lax.fori_loop(low, block + 1, third, 0)
        dq_ref[k] = (dq_acc[...] * scale).astype(BF16)

    for k in range(HEADS):
        for row in range(2):
            keep_ref[row, k] = dk[rows(row * ROW + place(k, side)), :] * scale
            send_ref[row, k] = dk[rows(row * ROW + place(k, 1 - side)), :] * scale


def attend(info, low, weight, seg_q, seg_k, queries, own, oth, own_prev, oth_prev):
    return pl.pallas_call(
        main_kernel,
        out_shape=[
            jax.ShapeDtypeStruct((QUART, TOK, DIM), BF16),
            jax.ShapeDtypeStruct((2, QUART, TOK, DIM), F32),
            jax.ShapeDtypeStruct((2, QUART, TOK, DIM), F32),
        ],
        in_specs=[SMEM] * 3 + [VMEM] * 10,
        out_specs=[VMEM] * 3,
        scratch_shapes=[
            pltpu.VMEM((2 * ROW * TOK, DIM), BF16),
            pltpu.VMEM((2 * ROW * TOK, DIM), BF16),
            pltpu.VMEM((2 * ROW * TOK, DIM), F32),
            pltpu.VMEM((ROW, TOK, TOK), F32),
            pltpu.VMEM((ROW, TOK, TOK), F32),
            pltpu.VMEM((TOK, DIM), F32),
            pltpu.VMEM((TOK, DIM), F32),
            pltpu.VMEM((TOK, DIM), F32),
            pltpu.VMEM((TOK, DIM), F32),
            pltpu.VMEM((TOK, DIM), F32),
        ],
        compiler_params=pltpu.CompilerParams(vmem_limit_bytes=36 * 1024 * 1024),
        cost_estimate=pl.CostEstimate(flops=10**9, bytes_accessed=8 * 2**20, transcendentals=4 * 10**6),
    )(info, low, weight, seg_q, seg_k, *queries, own, oth, own_prev, oth_prev)


def per_device(seq, dp, teacher_query, teacher_key, student_query, student_key, segment_ids, head_weight):
    rounds, swap, down = routes(seq, dp)
    seq_index = lax.axis_index("seq")
    core = lax.rem(lax.axis_index("dp"), 2)
    y = lax.rem(seq_index, ROW)
    row_index = seq_index // ROW
    head, window = y // 2, lax.rem(y, 2)
    half = head.reshape(1)

    def move(x, route):
        return lax.ppermute(x, AXES, route)

    keys = [move(x, r) for x, r in zip(pack(half, teacher_key[0], student_key[0]), rounds)]
    queries = [move(x, r) for x, r in zip(pack(half, teacher_query[0], student_query[0]), rounds)]

    row_tokens = ROW * TOK
    filler = jnp.full((row_tokens,), -1, jnp.int32)
    seg_mine = lax.dynamic_slice_in_dim(
        jnp.concatenate([filler, segment_ids[0]]), row_index * row_tokens, 2 * row_tokens
    ).reshape(2 * ROW, TOK)
    seg = jnp.where(core == window, seg_mine, move(seg_mine, swap))
    reach = (seg[None, :, TOK - 1] == seg[:, None, 0]) & (
        jnp.arange(2 * ROW)[None, :] < jnp.arange(2 * ROW)[:, None]
    )
    low = jnp.arange(2 * ROW, dtype=jnp.int32) - jnp.sum(reach, axis=1, dtype=jnp.int32)
    seg_q = seg[ROW:].reshape(row_tokens, 1)

    own = jnp.stack(keys)
    own_prev = move(own, down)
    oth = move(own, swap)
    oth_prev = move(own_prev, swap)

    info = jnp.stack([head, core]).astype(jnp.int32)
    weight = lax.dynamic_slice_in_dim(head_weight, head, 1)
    dq, keep, send = attend(info, low, weight, seg_q, seg, queries, own, oth, own_prev, oth_prev)

    query_grad = unpack(half, [move(dq[k], reverse(rounds[k])) for k in range(HEADS)])

    both = keep + move(send, swap)
    back = move(both[0].astype(BF16), reverse(down))
    total = (both[1] + back.astype(F32)).astype(BF16)
    key_grad = unpack(half, [move(total[k], reverse(rounds[k])) for k in range(HEADS)])
    return query_grad[None], key_grad[None]


def solution(mesh):
    seq, dp = mesh.shape["seq"], mesh.shape["dp"]
    spec = P("dp", "seq", None)
    return jax.shard_map(
        functools.partial(per_device, seq, dp),
        mesh=mesh,
        in_specs=(spec, spec, spec, spec, P("dp", None), P()),
        out_specs=(spec, spec),
        check_vma=False,
    )
```

time: 464 us -> 132 us (0.28)
  the two profiles are of different devices: /device:TPU:460 before, /device:TPU:5 now
where the time goes in v1:
time: 132 us; the launch traced here: 131 us
  starting transfers between devices  89.7 us (68%)
  Pallas kernels  19.6 us (15%)
  waiting for transfers between devices  13.1 us (10%)
  local copies, waits for them, and re-layouts  6.27 us (5%)
    ppermute x22, starting transfers between devices, move(): return lax.ppermute(x, AXES, route)  89.7 us
    ppermute x22, waiting for transfers between devices, move(): return lax.ppermute(x, AXES, route)  13.1 us
    pallas_call x1, Pallas kernels, attend(): pl.pallas_call(main_kernel, out_shape=[jax.ShapeDtypeStruct((QUART, TOK,...  12.2 us
    unnamed x29, local copies, waits for them, and re-layouts  4.88 us
    pallas_call x2, Pallas kernels, pack(): pl.pallas_call(pack_kernel, out_shape=[jax.ShapeDtypeStruct((2, TOK, DIM)...  3.81 us
    pallas_call x2, Pallas kernels, unpack(): pl.pallas_call(unpack_kernel, out_shape=jax.ShapeDtypeStruct((TOK, HEADS...  3.59 us
  transfers between devices with their start and end apart: 22, of which 4 were waited for; matrix products, arithmetic and copies ran while one was open for 3% of the time, Pallas kernels for 3%

profile of v1, /device:TPU:5, one launch (start us, length us, event | category | flops | bytes accessed | tf_op | source)
XLA Modules:
  0.0 130.9 jit_solution(4434463752661633502)
XLA Ops:
  0.7 1.9 %shard_map.78 = (bf16[2,256,128]{2,1,0:T(8,128)(2,1)}, bf16[2,256,128]{2,1,0:T(8,128)(2,1)}, bf16[2,256,128]{2,1,0:T(8,128)(2,1)}, bf16[2,256,128]{2,1,0:T(8,128)(2,1)}) custom-call(s32[1]{0:T(128)} %bitcast.half_ref, bf16[256,512]{1,0:T(8,128)(2,1)} %bitcast.45, bf16[256,512]{1,0:T(8,128)(2,1)} %bitcast.46), custom_call_target="tpu_custom_call" | custom-call | bytes 1048576 | tf_op jit(solution)/shard_map/pallas_call | solution.py:57
  2.6 3.8 %collective-permute-start.5 = (bf16[2,256,128]{2,1,0:T(8,128)(2,1)}, bf16[2,256,128]{2,1,0:T(8,128)(2,1)S(1)}, u32[]{:S(2)}, u32[]{:S(2)}) collective-permute-start(bf16[2,256,128]{2,1,0:T(8,128)(2,1)} %get-tuple-element.17), channel_id=1, source_target_pairs={{0,0},{1,4},{2,2},{3,6},{4,1},{5,5},{6,3},{7,7},{8,8},{9,12},{10,1... | collective-permute-start | bytes 393224 | tf_op jit(solution)/shard_map/ppermute | solution.py:218
  6.3 3.9 %collective-permute-start.6 = (bf16[2,256,128]{2,1,0:T(8,128)(2,1)}, bf16[2,256,128]{2,1,0:T(8,128)(2,1)S(1)}, u32[]{:S(2)}, u32[]{:S(2)}) collective-permute-start(bf16[2,256,128]{2,1,0:T(8,128)(2,1)} %get-tuple-element.18), channel_id=1, source_target_pairs={{0,8},{1,12},{2,10},{3,14},{4,9},{5,13},{6,11},{7,15},{8,16},{9,20... | collective-permute-start | bytes 393224 | tf_op jit(solution)/shard_map/ppermute | solution.py:218
  10.3 4.4 %collective-permute-start.7 = (bf16[2,256,128]{2,1,0:T(8,128)(2,1)}, bf16[2,256,128]{2,1,0:T(8,128)(2,1)S(1)}, u32[]{:S(2)}, u32[]{:S(2)}) collective-permute-start(bf16[2,256,128]{2,1,0:T(8,128)(2,1)} %get-tuple-element.19), channel_id=1, source_target_pairs={{0,16},{1,20},{2,18},{3,22},{4,17},{5,21},{6,19},{7,23},{8,24},{9,... | collective-permute-start | bytes 393224 | tf_op jit(solution)/shard_map/ppermute | solution.py:218
  14.7 5.5 %collective-permute-start.8 = (bf16[2,256,128]{2,1,0:T(8,128)(2,1)}, bf16[2,256,128]{2,1,0:T(8,128)(2,1)S(1)}, u32[]{:S(2)}, u32[]{:S(2)}) collective-permute-start(bf16[2,256,128]{2,1,0:T(8,128)(2,1)} %get-tuple-element.20), channel_id=1, source_target_pairs={{0,24},{1,28},{2,26},{3,30},{4,25},{5,29},{6,27},{7,31},{8,0},{9,4... | collective-permute-start | bytes 393224 | tf_op jit(solution)/shard_map/ppermute | solution.py:218
  20.2 0.0 collective-permute-done.5
  20.2 0.0 collective-permute-done.6
  20.2 2.0 %collective-permute-done.7 = bf16[2,256,128]{2,1,0:T(8,128)(2,1)S(1)} collective-permute-done((bf16[2,256,128]{2,1,0:T(8,128)(2,1)}, bf16[2,256,128]{2,1,0:T(8,128)(2,1)S(1)}, u32[]{:S(2)}, u32[]{:S(2)}) %collective-permute-start.7) | collective-permute-done | bytes 131104 | tf_op jit(solution)/shard_map/ppermute | solution.py:218
  22.2 2.6 %collective-permute-done.8 = bf16[2,256,128]{2,1,0:T(8,128)(2,1)S(1)} collective-permute-done((bf16[2,256,128]{2,1,0:T(8,128)(2,1)}, bf16[2,256,128]{2,1,0:T(8,128)(2,1)S(1)}, u32[]{:S(2)}, u32[]{:S(2)}) %collective-permute-start.8) | collective-permute-done | bytes 131104 | tf_op jit(solution)/shard_map/ppermute | solution.py:218
  24.8 0.1 pad_maximum_fusion.own_ref
  24.9 4.0 %collective-permute-start.10 = (bf16[4,2,256,128]{3,2,1,0:T(8,128)(2,1)S(1)}, bf16[4,2,256,128]{3,2,1,0:T(8,128)(2,1)S(1)}, u32[]{:S(2)}, u32[]{:S(2)}) collective-permute-start(bf16[4,2,256,128]{3,2,1,0:T(8,128)(2,1)S(1)} %pad_maximum_fusion.own_ref), channel_id=1, source_target_pairs={{0,32},{1,33},{2,34},{3,35},{4,36},{5,37},{6,38},{7,39},{8,40},{9,... | collective-permute-start | bytes 1572872 | tf_op jit(solution)/shard_map/ppermute | solution.py:218
  29.0 4.4 %collective-permute-start = (s32[16,256]{1,0:T(8,128)S(1)}, s32[16,256]{1,0:T(8,128)S(1)}, u32[]{:S(2)}, u32[]{:S(2)}) collective-permute-start(s32[16,256]{1,0:T(8,128)S(1)} %reshape.16), channel_id=1, source_target_pairs={{0,1},{1,0},{2,3},{3,2},{4,5},{5,4},{6,7},{7,6},{8,9},{9,8},{10,11... | collective-permute-start | bytes 49160 | tf_op jit(solution)/shard_map/ppermute | solution.py:218
  33.4 1.9 %shard_map.77 = (bf16[2,256,128]{2,1,0:T(8,128)(2,1)}, bf16[2,256,128]{2,1,0:T(8,128)(2,1)}, bf16[2,256,128]{2,1,0:T(8,128)(2,1)}, bf16[2,256,128]{2,1,0:T(8,128)(2,1)}) custom-call(s32[1]{0:T(128)} %bitcast.half_ref, bf16[256,512]{1,0:T(8,128)(2,1)} %bitcast.47, bf16[256,512]{1,0:T(8,128)(2,1)} %bitcast.48), custom_call_target="tpu_custom_call" | custom-call | bytes 1048576 | tf_op jit(solution)/shard_map/pallas_call | solution.py:57
  35.3 2.7 %collective-permute-start.1 = (bf16[2,256,128]{2,1,0:T(8,128)(2,1)}, bf16[2,256,128]{2,1,0:T(8,128)(2,1)S(1)}, u32[]{:S(2)}, u32[]{:S(2)}) collective-permute-start(bf16[2,256,128]{2,1,0:T(8,128)(2,1)} %get-tuple-element.13), channel_id=1, source_target_pairs={{0,0},{1,4},{2,2},{3,6},{4,1},{5,5},{6,3},{7,7},{8,8},{9,12},{10,1... | collective-permute-start | bytes 393224 | tf_op jit(solution)/shard_map/ppermute | solution.py:218
  38.0 4.7 %collective-permute-start.2 = (bf16[2,256,128]{2,1,0:T(8,128)(2,1)}, bf16[2,256,128]{2,1,0:T(8,128)(2,1)S(1)}, u32[]{:S(2)}, u32[]{:S(2)}) collective-permute-start(bf16[2,256,128]{2,1,0:T(8,128)(2,1)} %get-tuple-element.14), channel_id=1, source_target_pairs={{0,8},{1,12},{2,10},{3,14},{4,9},{5,13},{6,11},{7,15},{8,16},{9,20... | collective-permute-start | bytes 393224 | tf_op jit(solution)/shard_map/ppermute | solution.py:218
  42.8 3.0 %collective-permute-start.3 = (bf16[2,256,128]{2,1,0:T(8,128)(2,1)}, bf16[2,256,128]{2,1,0:T(8,128)(2,1)S(1)}, u32[]{:S(2)}, u32[]{:S(2)}) collective-permute-start(bf16[2,256,128]{2,1,0:T(8,128)(2,1)} %get-tuple-element.15), channel_id=1, source_target_pairs={{0,16},{1,20},{2,18},{3,22},{4,17},{5,21},{6,19},{7,23},{8,24},{9,... | collective-permute-start | bytes 393224 | tf_op jit(solution)/shard_map/ppermute | solution.py:218
  45.8 0.7 pad_add_fusion.info_ref
  46.4 0.7 copy-done.12
  47.1 0.6 dynamic_slice.7.weight_ref
  47.7 0.0 collective-permute-done
  47.7 2.8 %collective-permute-start.9 = (bf16[4,2,256,128]{3,2,1,0:T(8,128)(2,1)S(1)}, bf16[4,2,256,128]{3,2,1,0:T(8,128)(2,1)S(1)}, u32[]{:S(2)}, u32[]{:S(2)}) collective-permute-start(bf16[4,2,256,128]{3,2,1,0:T(8,128)(2,1)S(1)} %pad_maximum_fusion.own_ref), channel_id=1, source_target_pairs={{0,1},{1,0},{2,3},{3,2},{4,5},{5,4},{6,7},{7,6},{8,9},{9,8},{10,11... | collective-permute-start | bytes 1572872 | tf_op jit(solution)/shard_map/ppermute | solution.py:218
  50.5 0.0 collective-permute-done.10.own_prev_ref
  50.5 1.9 %collective-permute-start.11 = (bf16[4,2,256,128]{3,2,1,0:T(8,128)(2,1)S(1)}, bf16[4,2,256,128]{3,2,1,0:T(8,128)(2,1)S(1)}, u32[]{:S(2)}, u32[]{:S(2)}) collective-permute-start(bf16[4,2,256,128]{3,2,1,0:T(8,128)(2,1)S(1)} %collective-permute-done.10.own_prev_ref), channel_id=1, source_target_pairs={{0,1},{1,0},{2,3},{3,2},{4,5},{5,4},{6,7},{7,6},{8,9},{9,8},{10,11... | collective-permute-start | bytes 1572872 | tf_op jit(solution)/shard_map/ppermute | solution.py:218
  52.4 0.7 slice_reduce_fusion
  53.1 0.6 copy.11
  53.7 1.1 copy.12
  54.8 0.6 copy-done.10
  55.5 0.2 convert_reduce_fusion
  55.6 0.0 collective-permute-done.1.q0
  55.6 5.2 %collective-permute-start.4 = (bf16[2,256,128]{2,1,0:T(8,128)(2,1)}, bf16[2,256,128]{2,1,0:T(8,128)(2,1)S(1)}, u32[]{:S(2)}, u32[]{:S(2)}) collective-permute-start(bf16[2,256,128]{2,1,0:T(8,128)(2,1)} %get-tuple-element.16), channel_id=1, source_target_pairs={{0,24},{1,28},{2,26},{3,30},{4,25},{5,29},{6,27},{7,31},{8,0},{9,4... | collective-permute-start | bytes 393224 | tf_op jit(solution)/shard_map/ppermute | solution.py:218
  60.8 0.0 collective-permute-done.2.q1
  60.9 0.0 collective-permute-done.3.q2
  60.9 6.2 %collective-permute-done.4.q3 = bf16[2,256,128]{2,1,0:T(8,128)(2,1)S(1)} collective-permute-done((bf16[2,256,128]{2,1,0:T(8,128)(2,1)}, bf16[2,256,128]{2,1,0:T(8,128)(2,1)S(1)}, u32[]{:S(2)}, u32[]{:S(2)}) %collective-permute-start.4) | collective-permute-done | bytes 131104 | tf_op jit(solution)/shard_map/ppermute | solution.py:218
  67.0 0.0 collective-permute-done.9.oth_ref
  67.0 0.0 collective-permute-done.11.oth_prev_ref
  67.0 12.2 %shard_map.79 = (bf16[4,256,128]{2,1,0:T(8,128)(2,1)S(1)}, f32[2,4,256,128]{3,2,1,0:T(8,128)S(1)}, f32[2,4,256,128]{3,2,1,0:T(8,128)S(1)}) custom-call(s32[2]{0:T(128)S(1)} %copy-done, s32[16]{0:T(128)S(1)} %iota_subtract_fusion.low_ref, f32[1]{0:T(128)} %dynamic_slice.7.weight_ref, s32[2048,1]{1,0:T(8,128)S(1)} %bitcast.42, ...), custom_call_target="tpu_custom_call" | custom-call | flops 1000000000 | bytes 8388608 | tf_op jit(solution)/shard_map/pallas_call | solution.py:182
  79.2 2.5 %collective-permute-start.16 = (f32[2,4,256,128]{3,2,1,0:T(8,128)S(1)}, f32[2,4,256,128]{3,2,1,0:T(8,128)S(1)}, u32[]{:S(2)}, u32[]{:S(2)}) collective-permute-start(f32[2,4,256,128]{3,2,1,0:T(8,128)S(1)} %get-tuple-element.23), channel_id=1, source_target_pairs={{0,1},{1,0},{2,3},{3,2},{4,5},{5,4},{6,7},{7,6},{8,9},{9,8},{10,11... | collective-permute-start | bytes 3145736 | tf_op jit(solution)/shard_map/ppermute | solution.py:218
  81.8 2.3 %collective-permute-done.16 = f32[2,4,256,128]{3,2,1,0:T(8,128)S(1)} collective-permute-done((f32[2,4,256,128]{3,2,1,0:T(8,128)S(1)}, f32[2,4,256,128]{3,2,1,0:T(8,128)S(1)}, u32[]{:S(2)}, u32[]{:S(2)}) %collective-permute-start.16) | collective-permute-done | bytes 1048608 | tf_op jit(solution)/shard_map/ppermute | solution.py:218
  84.0 0.1 add.18
  84.2 11.4 %collective-permute-start.17 = (bf16[4,256,128]{2,1,0:T(8,128)(2,1)S(1)}, bf16[4,256,128]{2,1,0:T(8,128)(2,1)S(1)}, u32[]{:S(2)}, u32[]{:S(2)}) collective-permute-start(bf16[4,256,128]{2,1,0:T(8,128)(2,1)S(1)} %fusion.2), channel_id=1, source_target_pairs={{32,0},{33,1},{34,2},{35,3},{36,4},{37,5},{38,6},{39,7},{40,8},{41... | collective-permute-start | bytes 786440 | tf_op jit(solution)/shard_map/ppermute | solution.py:218
  95.6 1.9 %collective-permute-start.15 = (bf16[256,128]{1,0:T(8,128)(2,1)S(1)}, bf16[256,128]{1,0:T(8,128)(2,1)S(1)}, u32[]{:S(2)}, u32[]{:S(2)}) collective-permute-start(bf16[256,128]{1,0:T(8,128)(2,1)S(1)} %get-tuple-element.30), channel_id=1, source_target_pairs={{24,0},{28,1},{26,2},{30,3},{25,4},{29,5},{27,6},{31,7},{0,8},{4,9... | collective-permute-start | bytes 196616 | tf_op jit(solution)/shard_map/ppermute | solution.py:218
  97.6 6.3 %collective-permute-start.14 = (bf16[256,128]{1,0:T(8,128)(2,1)S(1)}, bf16[256,128]{1,0:T(8,128)(2,1)S(1)}, u32[]{:S(2)}, u32[]{:S(2)}) collective-permute-start(bf16[256,128]{1,0:T(8,128)(2,1)S(1)} %get-tuple-element.31), channel_id=1, source_target_pairs={{16,0},{20,1},{18,2},{22,3},{17,4},{21,5},{19,6},{23,7},{24,8},{28... | collective-permute-start | bytes 196616 | tf_op jit(solution)/shard_map/ppermute | solution.py:218
  103.8 1.9 %collective-permute-start.13 = (bf16[256,128]{1,0:T(8,128)(2,1)S(1)}, bf16[256,128]{1,0:T(8,128)(2,1)S(1)}, u32[]{:S(2)}, u32[]{:S(2)}) collective-permute-start(bf16[256,128]{1,0:T(8,128)(2,1)S(1)} %get-tuple-element.32), channel_id=1, source_target_pairs={{8,0},{12,1},{10,2},{14,3},{9,4},{13,5},{11,6},{15,7},{16,8},{20,9... | collective-permute-start | bytes 196616 | tf_op jit(solution)/shard_map/ppermute | solution.py:218
  105.8 4.2 %collective-permute-start.12 = (bf16[256,128]{1,0:T(8,128)(2,1)S(1)}, bf16[256,128]{1,0:T(8,128)(2,1)S(1)}, u32[]{:S(2)}, u32[]{:S(2)}) collective-permute-start(bf16[256,128]{1,0:T(8,128)(2,1)S(1)} %get-tuple-element.33), channel_id=1, source_target_pairs={{0,0},{4,1},{2,2},{6,3},{1,4},{5,5},{3,6},{7,7},{8,8},{12,9},{10,1... | collective-permute-start | bytes 196616 | tf_op jit(solution)/shard_map/ppermute | solution.py:218
  110.0 0.0 collective-permute-done.17
  110.0 0.1 fusion.1
  110.1 3.1 %collective-permute-start.21 = (bf16[256,128]{1,0:T(8,128)(2,1)S(1)}, bf16[256,128]{1,0:T(8,128)(2,1)S(1)}, u32[]{:S(2)}, u32[]{:S(2)}) collective-permute-start(bf16[256,128]{1,0:T(8,128)(2,1)S(1)} %get-tuple-element.26), channel_id=1, source_target_pairs={{24,0},{28,1},{26,2},{30,3},{25,4},{29,5},{27,6},{31,7},{0,8},{4,9... | collective-permute-start | bytes 196616 | tf_op jit(solution)/shard_map/ppermute | solution.py:218
  113.3 0.0 collective-permute-done.15.refs_3_
  113.3 3.2 %collective-permute-start.20 = (bf16[256,128]{1,0:T(8,128)(2,1)S(1)}, bf16[256,128]{1,0:T(8,128)(2,1)S(1)}, u32[]{:S(2)}, u32[]{:S(2)}) collective-permute-start(bf16[256,128]{1,0:T(8,128)(2,1)S(1)} %get-tuple-element.27), channel_id=1, source_target_pairs={{16,0},{20,1},{18,2},{22,3},{17,4},{21,5},{19,6},{23,7},{24,8},{28... | collective-permute-start | bytes 196616 | tf_op jit(solution)/shard_map/ppermute | solution.py:218
  116.5 0.0 collective-permute-done.14.refs_2_
  116.5 5.2 %collective-permute-start.19 = (bf16[256,128]{1,0:T(8,128)(2,1)S(1)}, bf16[256,128]{1,0:T(8,128)(2,1)S(1)}, u32[]{:S(2)}, u32[]{:S(2)}) collective-permute-start(bf16[256,128]{1,0:T(8,128)(2,1)S(1)} %get-tuple-element.28), channel_id=1, source_target_pairs={{8,0},{12,1},{10,2},{14,3},{9,4},{13,5},{11,6},{15,7},{16,8},{20,9... | collective-permute-start | bytes 196616 | tf_op jit(solution)/shard_map/ppermute | solution.py:218
  121.7 0.0 collective-permute-done.13.refs_1_
  121.7 3.6 %collective-permute-start.18 = (bf16[256,128]{1,0:T(8,128)(2,1)S(1)}, bf16[256,128]{1,0:T(8,128)(2,1)S(1)}, u32[]{:S(2)}, u32[]{:S(2)}) collective-permute-start(bf16[256,128]{1,0:T(8,128)(2,1)S(1)} %get-tuple-element.29), channel_id=1, source_target_pairs={{0,0},{4,1},{2,2},{6,3},{1,4},{5,5},{3,6},{7,7},{8,8},{12,9},{10,1... | collective-permute-start | bytes 196616 | tf_op jit(solution)/shard_map/ppermute | solution.py:218
  125.3 0.0 collective-permute-done.12.refs_0_
  125.4 0.0 copy-start.6
  125.4 0.6 copy-done.6
  126.0 1.8 %shard_map.80 = f32[256,512]{1,0:T(8,128)} custom-call(s32[1]{0:T(128)} %bitcast.half_ref, bf16[256,128]{1,0:T(8,128)(2,1)} %copy-done.6, bf16[256,128]{1,0:T(8,128)(2,1)} %copy-done.4, bf16[256,128]{1,0:T(8,128)(2,1)} %copy-done.3, bf16[256,128]{1,0:T(8,128)(2,1)} %copy-done.2), custom_call_target="tpu_custom_call" | custom-call | bytes 786432 | tf_op jit(solution)/shard_map/pallas_call | solution.py:75
  127.8 0.0 collective-permute-done.21.refs_3_
  127.8 0.0 collective-permute-done.19.refs_1_
  127.9 0.6 copy-done.5
  128.4 0.0 copy-done.7
  128.5 0.0 copy-done.8
  128.5 0.6 copy-done.9
  129.1 1.8 %shard_map.81 = f32[256,512]{1,0:T(8,128)} custom-call(s32[1]{0:T(128)} %bitcast.half_ref, bf16[256,128]{1,0:T(8,128)(2,1)} %copy-done.9, bf16[256,128]{1,0:T(8,128)(2,1)} %copy-done.8, bf16[256,128]{1,0:T(8,128)(2,1)} %copy-done.7, bf16[256,128]{1,0:T(8,128)(2,1)} %copy-done.5), custom_call_target="tpu_custom_call" | custom-call | bytes 786432 | tf_op jit(solution)/shard_map/pallas_call | solution.py:75
  (28 shorter events, 0.1 us)
Async XLA Ops:
  2.6 17.6 %collective-permute-start.5 = (bf16[2,256,128]{2,1,0:T(8,128)(2,1)}, bf16[2,256,128]{2,1,0:T(8,128)(2,1)S(1)}, u32[]{:S(2)}, u32[]{:S(2)}) collective-permute-start(bf16[2,256,128]{2,1,0:T(8,128)(2,1)} %get-tuple-element.17), channel_id=1, source_target_pairs={{0,0},{1,4},{2,2},{3,6},{4,1},{5,5},{6,3},{7,7},{8,8},{9,12},{10,1... | collective-permute-start | bytes 393224 | tf_op jit(solution)/shard_map/ppermute | solution.py:218
  6.3 13.9 %collective-permute-start.6 = (bf16[2,256,128]{2,1,0:T(8,128)(2,1)}, bf16[2,256,128]{2,1,0:T(8,128)(2,1)S(1)}, u32[]{:S(2)}, u32[]{:S(2)}) collective-permute-start(bf16[2,256,128]{2,1,0:T(8,128)(2,1)} %get-tuple-element.18), channel_id=1, source_target_pairs={{0,8},{1,12},{2,10},{3,14},{4,9},{5,13},{6,11},{7,15},{8,16},{9,20... | collective-permute-start | bytes 393224 | tf_op jit(solution)/shard_map/ppermute | solution.py:218
  10.3 11.9 %collective-permute-start.7 = (bf16[2,256,128]{2,1,0:T(8,128)(2,1)}, bf16[2,256,128]{2,1,0:T(8,128)(2,1)S(1)}, u32[]{:S(2)}, u32[]{:S(2)}) collective-permute-start(bf16[2,256,128]{2,1,0:T(8,128)(2,1)} %get-tuple-element.19), channel_id=1, source_target_pairs={{0,16},{1,20},{2,18},{3,22},{4,17},{5,21},{6,19},{7,23},{8,24},{9,... | collective-permute-start | bytes 393224 | tf_op jit(solution)/shard_map/ppermute | solution.py:218
  14.7 10.1 %collective-permute-start.8 = (bf16[2,256,128]{2,1,0:T(8,128)(2,1)}, bf16[2,256,128]{2,1,0:T(8,128)(2,1)S(1)}, u32[]{:S(2)}, u32[]{:S(2)}) collective-permute-start(bf16[2,256,128]{2,1,0:T(8,128)(2,1)} %get-tuple-element.20), channel_id=1, source_target_pairs={{0,24},{1,28},{2,26},{3,30},{4,25},{5,29},{6,27},{7,31},{8,0},{9,4... | collective-permute-start | bytes 393224 | tf_op jit(solution)/shard_map/ppermute | solution.py:218
  24.8 4.1 %copy-start.1 = (s32[1,32768]{1,0:T(1,128)S(1)}, s32[1,32768]{1,0:T(1,128)}, u32[]{:S(2)}) copy-start(s32[1,32768]{1,0:T(1,128)} %param.10) | copy-start | bytes 393220
  24.9 25.6 %collective-permute-start.10 = (bf16[4,2,256,128]{3,2,1,0:T(8,128)(2,1)S(1)}, bf16[4,2,256,128]{3,2,1,0:T(8,128)(2,1)S(1)}, u32[]{:S(2)}, u32[]{:S(2)}) collective-permute-start(bf16[4,2,256,128]{3,2,1,0:T(8,128)(2,1)S(1)} %pad_maximum_fusion.own_ref), channel_id=1, source_target_pairs={{0,32},{1,33},{2,34},{3,35},{4,36},{5,37},{6,38},{7,39},{8,40},{9,... | collective-permute-start | bytes 1572872 | tf_op jit(solution)/shard_map/ppermute | solution.py:218
  29.0 18.7 %collective-permute-start = (s32[16,256]{1,0:T(8,128)S(1)}, s32[16,256]{1,0:T(8,128)S(1)}, u32[]{:S(2)}, u32[]{:S(2)}) collective-permute-start(s32[16,256]{1,0:T(8,128)S(1)} %reshape.16), channel_id=1, source_target_pairs={{0,1},{1,0},{2,3},{3,2},{4,5},{5,4},{6,7},{7,6},{8,9},{9,8},{10,11... | collective-permute-start | bytes 49160 | tf_op jit(solution)/shard_map/ppermute | solution.py:218
  35.3 20.4 %collective-permute-start.1 = (bf16[2,256,128]{2,1,0:T(8,128)(2,1)}, bf16[2,256,128]{2,1,0:T(8,128)(2,1)S(1)}, u32[]{:S(2)}, u32[]{:S(2)}) collective-permute-start(bf16[2,256,128]{2,1,0:T(8,128)(2,1)} %get-tuple-element.13), channel_id=1, source_target_pairs={{0,0},{1,4},{2,2},{3,6},{4,1},{5,5},{6,3},{7,7},{8,8},{9,12},{10,1... | collective-permute-start | bytes 393224 | tf_op jit(solution)/shard_map/ppermute | solution.py:218
  38.0 22.8 %collective-permute-start.2 = (bf16[2,256,128]{2,1,0:T(8,128)(2,1)}, bf16[2,256,128]{2,1,0:T(8,128)(2,1)S(1)}, u32[]{:S(2)}, u32[]{:S(2)}) collective-permute-start(bf16[2,256,128]{2,1,0:T(8,128)(2,1)} %get-tuple-element.14), channel_id=1, source_target_pairs={{0,8},{1,12},{2,10},{3,14},{4,9},{5,13},{6,11},{7,15},{8,16},{9,20... | collective-permute-start | bytes 393224 | tf_op jit(solution)/shard_map/ppermute | solution.py:218
  42.8 18.1 %collective-permute-start.3 = (bf16[2,256,128]{2,1,0:T(8,128)(2,1)}, bf16[2,256,128]{2,1,0:T(8,128)(2,1)S(1)}, u32[]{:S(2)}, u32[]{:S(2)}) collective-permute-start(bf16[2,256,128]{2,1,0:T(8,128)(2,1)} %get-tuple-element.15), channel_id=1, source_target_pairs={{0,16},{1,20},{2,18},{3,22},{4,17},{5,21},{6,19},{7,23},{8,24},{9,... | collective-permute-start | bytes 393224 | tf_op jit(solution)/shard_map/ppermute | solution.py:218
  46.4 0.7 copy-start.12
  47.7 19.3 %collective-permute-start.9 = (bf16[4,2,256,128]{3,2,1,0:T(8,128)(2,1)S(1)}, bf16[4,2,256,128]{3,2,1,0:T(8,128)(2,1)S(1)}, u32[]{:S(2)}, u32[]{:S(2)}) collective-permute-start(bf16[4,2,256,128]{3,2,1,0:T(8,128)(2,1)S(1)} %pad_maximum_fusion.own_ref), channel_id=1, source_target_pairs={{0,1},{1,0},{2,3},{3,2},{4,5},{5,4},{6,7},{7,6},{8,9},{9,8},{10,11... | collective-permute-start | bytes 1572872 | tf_op jit(solution)/shard_map/ppermute | solution.py:218
  50.5 16.5 %collective-permute-start.11 = (bf16[4,2,256,128]{3,2,1,0:T(8,128)(2,1)S(1)}, bf16[4,2,256,128]{3,2,1,0:T(8,128)(2,1)S(1)}, u32[]{:S(2)}, u32[]{:S(2)}) collective-permute-start(bf16[4,2,256,128]{3,2,1,0:T(8,128)(2,1)S(1)} %collective-permute-done.10.own_prev_ref), channel_id=1, source_target_pairs={{0,1},{1,0},{2,3},{3,2},{4,5},{5,4},{6,7},{7,6},{8,9},{9,8},{10,11... | collective-permute-start | bytes 1572872 | tf_op jit(solution)/shard_map/ppermute | solution.py:218
  54.8 0.7 copy-start.10
  54.8 0.7 copy-start.11
  55.6 11.4 %collective-permute-start.4 = (bf16[2,256,128]{2,1,0:T(8,128)(2,1)}, bf16[2,256,128]{2,1,0:T(8,128)(2,1)S(1)}, u32[]{:S(2)}, u32[]{:S(2)}) collective-permute-start(bf16[2,256,128]{2,1,0:T(8,128)(2,1)} %get-tuple-element.16), channel_id=1, source_target_pairs={{0,24},{1,28},{2,26},{3,30},{4,25},{5,29},{6,27},{7,31},{8,0},{9,4... | collective-permute-start | bytes 393224 | tf_op jit(solution)/shard_map/ppermute | solution.py:218
  60.8 6.2 %copy-start = (s32[2]{0:T(128)S(1)}, s32[2]{0:T(128)}, u32[]{:S(2)}) copy-start(s32[2]{0:T(128)} %pad_add_fusion.info_ref) | copy-start | bytes 28
  79.2 4.8 %collective-permute-start.16 = (f32[2,4,256,128]{3,2,1,0:T(8,128)S(1)}, f32[2,4,256,128]{3,2,1,0:T(8,128)S(1)}, u32[]{:S(2)}, u32[]{:S(2)}) collective-permute-start(f32[2,4,256,128]{3,2,1,0:T(8,128)S(1)} %get-tuple-element.23), channel_id=1, source_target_pairs={{0,1},{1,0},{2,3},{3,2},{4,5},{5,4},{6,7},{7,6},{8,9},{9,8},{10,11... | collective-permute-start | bytes 3145736 | tf_op jit(solution)/shard_map/ppermute | solution.py:218
  84.2 25.8 %collective-permute-start.17 = (bf16[4,256,128]{2,1,0:T(8,128)(2,1)S(1)}, bf16[4,256,128]{2,1,0:T(8,128)(2,1)S(1)}, u32[]{:S(2)}, u32[]{:S(2)}) collective-permute-start(bf16[4,256,128]{2,1,0:T(8,128)(2,1)S(1)} %fusion.2), channel_id=1, source_target_pairs={{32,0},{33,1},{34,2},{35,3},{36,4},{37,5},{38,6},{39,7},{40,8},{41... | collective-permute-start | bytes 786440 | tf_op jit(solution)/shard_map/ppermute | solution.py:218
  95.6 17.6 %collective-permute-start.15 = (bf16[256,128]{1,0:T(8,128)(2,1)S(1)}, bf16[256,128]{1,0:T(8,128)(2,1)S(1)}, u32[]{:S(2)}, u32[]{:S(2)}) collective-permute-start(bf16[256,128]{1,0:T(8,128)(2,1)S(1)} %get-tuple-element.30), channel_id=1, source_target_pairs={{24,0},{28,1},{26,2},{30,3},{25,4},{29,5},{27,6},{31,7},{0,8},{4,9... | collective-permute-start | bytes 196616 | tf_op jit(solution)/shard_map/ppermute | solution.py:218
  97.6 18.9 %collective-permute-start.14 = (bf16[256,128]{1,0:T(8,128)(2,1)S(1)}, bf16[256,128]{1,0:T(8,128)(2,1)S(1)}, u32[]{:S(2)}, u32[]{:S(2)}) collective-permute-start(bf16[256,128]{1,0:T(8,128)(2,1)S(1)} %get-tuple-element.31), channel_id=1, source_target_pairs={{16,0},{20,1},{18,2},{22,3},{17,4},{21,5},{19,6},{23,7},{24,8},{28... | collective-permute-start | bytes 196616 | tf_op jit(solution)/shard_map/ppermute | solution.py:218
  103.8 17.8 %collective-permute-start.13 = (bf16[256,128]{1,0:T(8,128)(2,1)S(1)}, bf16[256,128]{1,0:T(8,128)(2,1)S(1)}, u32[]{:S(2)}, u32[]{:S(2)}) collective-permute-start(bf16[256,128]{1,0:T(8,128)(2,1)S(1)} %get-tuple-element.32), channel_id=1, source_target_pairs={{8,0},{12,1},{10,2},{14,3},{9,4},{13,5},{11,6},{15,7},{16,8},{20,9... | collective-permute-start | bytes 196616 | tf_op jit(solution)/shard_map/ppermute | solution.py:218
  105.8 19.6 %collective-permute-start.12 = (bf16[256,128]{1,0:T(8,128)(2,1)S(1)}, bf16[256,128]{1,0:T(8,128)(2,1)S(1)}, u32[]{:S(2)}, u32[]{:S(2)}) collective-permute-start(bf16[256,128]{1,0:T(8,128)(2,1)S(1)} %get-tuple-element.33), channel_id=1, source_target_pairs={{0,0},{4,1},{2,2},{6,3},{1,4},{5,5},{3,6},{7,7},{8,8},{12,9},{10,1... | collective-permute-start | bytes 196616 | tf_op jit(solution)/shard_map/ppermute | solution.py:218
  110.1 17.7 %collective-permute-start.21 = (bf16[256,128]{1,0:T(8,128)(2,1)S(1)}, bf16[256,128]{1,0:T(8,128)(2,1)S(1)}, u32[]{:S(2)}, u32[]{:S(2)}) collective-permute-start(bf16[256,128]{1,0:T(8,128)(2,1)S(1)} %get-tuple-element.26), channel_id=1, source_target_pairs={{24,0},{28,1},{26,2},{30,3},{25,4},{29,5},{27,6},{31,7},{0,8},{4,9... | collective-permute-start | bytes 196616 | tf_op jit(solution)/shard_map/ppermute | solution.py:218
  113.3 12.1 %copy-start.2 = (bf16[256,128]{1,0:T(8,128)(2,1)}, bf16[256,128]{1,0:T(8,128)(2,1)S(1)}, u32[]{:S(2)}) copy-start(bf16[256,128]{1,0:T(8,128)(2,1)S(1)} %collective-permute-done.15.refs_3_) | copy-start | bytes 196612
  113.3 14.5 %collective-permute-start.20 = (bf16[256,128]{1,0:T(8,128)(2,1)S(1)}, bf16[256,128]{1,0:T(8,128)(2,1)S(1)}, u32[]{:S(2)}, u32[]{:S(2)}) collective-permute-start(bf16[256,128]{1,0:T(8,128)(2,1)S(1)} %get-tuple-element.27), channel_id=1, source_target_pairs={{16,0},{20,1},{18,2},{22,3},{17,4},{21,5},{19,6},{23,7},{24,8},{28... | collective-permute-start | bytes 196616 | tf_op jit(solution)/shard_map/ppermute | solution.py:218
  116.5 8.9 %copy-start.3 = (bf16[256,128]{1,0:T(8,128)(2,1)}, bf16[256,128]{1,0:T(8,128)(2,1)S(1)}, u32[]{:S(2)}) copy-start(bf16[256,128]{1,0:T(8,128)(2,1)S(1)} %collective-permute-done.14.refs_2_) | copy-start | bytes 196612
  116.5 11.3 %collective-permute-start.19 = (bf16[256,128]{1,0:T(8,128)(2,1)S(1)}, bf16[256,128]{1,0:T(8,128)(2,1)S(1)}, u32[]{:S(2)}, u32[]{:S(2)}) collective-permute-start(bf16[256,128]{1,0:T(8,128)(2,1)S(1)} %get-tuple-element.28), channel_id=1, source_target_pairs={{8,0},{12,1},{10,2},{14,3},{9,4},{13,5},{11,6},{15,7},{16,8},{20,9... | collective-permute-start | bytes 196616 | tf_op jit(solution)/shard_map/ppermute | solution.py:218
  121.7 3.7 %copy-start.4 = (bf16[256,128]{1,0:T(8,128)(2,1)}, bf16[256,128]{1,0:T(8,128)(2,1)S(1)}, u32[]{:S(2)}) copy-start(bf16[256,128]{1,0:T(8,128)(2,1)S(1)} %collective-permute-done.13.refs_1_) | copy-start | bytes 196612
  121.7 6.2 %collective-permute-start.18 = (bf16[256,128]{1,0:T(8,128)(2,1)S(1)}, bf16[256,128]{1,0:T(8,128)(2,1)S(1)}, u32[]{:S(2)}, u32[]{:S(2)}) collective-permute-start(bf16[256,128]{1,0:T(8,128)(2,1)S(1)} %get-tuple-element.29), channel_id=1, source_target_pairs={{0,0},{4,1},{2,2},{6,3},{1,4},{5,5},{3,6},{7,7},{8,8},{12,9},{10,1... | collective-permute-start | bytes 196616 | tf_op jit(solution)/shard_map/ppermute | solution.py:218
  125.4 0.6 copy-start.6
  127.8 0.6 copy-start.5
  127.8 0.6 copy-start.7
  127.8 0.7 copy-start.8
  128.5 0.6 copy-start.9

commit v2 on v1

v2 whole, which is shorter than its diff:
```python
import functools
import math

import jax
import jax.numpy as jnp
from jax import lax
from jax.experimental import pallas as pl
from jax.experimental.pallas import tpu as pltpu
from jax.sharding import PartitionSpec as P

HEADS = 4
DIM = 128
TOK = 256
ROW = 8
QUART = 4
MASKED = -1e30
F32 = jnp.float32
BF16 = jnp.bfloat16
VMEM = pl.BlockSpec(memory_space=pltpu.VMEM)
SMEM = pl.BlockSpec(memory_space=pltpu.SMEM)
AXES = ("seq", "dp")


def routes(seq, dp):
    def index(y, rest, x_lo, core):
        return ((rest * ROW + y) * (dp // 2) + x_lo) * 2 + core

    rounds = [[] for _ in range(HEADS)]
    swap, down = [], []
    for rest in range(seq // ROW):
        for y in range(ROW):
            for x_lo in range(dp // 2):
                for core in range(2):
                    me = index(y, rest, x_lo, core)
                    swap.append((me, index(y, rest, x_lo, 1 - core)))
                    if rest + 1 < seq // ROW:
                        down.append((me, index(y, rest + 1, x_lo, core)))
                    for k in range(HEADS):
                        head = (y // 2 + k) % HEADS
                        rounds[k].append((me, index(2 * head + core, rest, x_lo, y % 2)))
    return rounds, swap, down


def reverse(route):
    return [(b, a) for a, b in route]


def pack_kernel(half_ref, a_ref, b_ref, c_ref, d_ref, *outs):
    for k, out in enumerate(outs):
        head = lax.rem(half_ref[0] + k, HEADS)
        columns = pl.ds(pl.multiple_of(head * DIM, DIM), DIM)
        for i, ref in enumerate((a_ref, b_ref, c_ref, d_ref)):
            out[i] = ref[:, columns]


def pack(half, *states):
    return pl.pallas_call(
        pack_kernel,
        out_shape=[jax.ShapeDtypeStruct((4, TOK, DIM), BF16)] * HEADS,
        in_specs=[SMEM] + [VMEM] * 4,
        out_specs=[VMEM] * HEADS,
        cost_estimate=pl.CostEstimate(flops=0, bytes_accessed=8 * TOK * 512 * 2, transcendentals=0),
    )(half, *states)


def unpack_kernel(half_ref, p0, p1, p2, p3, query_ref, key_ref):
    for k, piece in enumerate((p0, p1, p2, p3)):
        head = lax.rem(half_ref[0] + k, HEADS)
        columns = pl.ds(pl.multiple_of(head * DIM, DIM), DIM)
        query_ref[:, columns] = piece[0].astype(F32)
        key_ref[:, columns] = piece[1].astype(F32)


def unpack(half, pieces):
    return pl.pallas_call(
        unpack_kernel,
        out_shape=[jax.ShapeDtypeStruct((TOK, HEADS * DIM), F32)] * 2,
        in_specs=[SMEM] + [VMEM] * HEADS,
        out_specs=[VMEM] * 2,
        cost_estimate=pl.CostEstimate(flops=0, bytes_accessed=12 * TOK * 512, transcendentals=0),
    )(half, *pieces)


def finish_kernel(dq_ref, keep_ref, recv_ref, back_ref, *outs):
    for k, out in enumerate(outs):
        out[0] = dq_ref[k]
        out[1] = (keep_ref[1, k] + recv_ref[1, k] + back_ref[k].astype(F32)).astype(BF16)


def finish(dq, keep, recv, back):
    return pl.pallas_call(
        finish_kernel,
        out_shape=[jax.ShapeDtypeStruct((2, TOK, DIM), BF16)] * HEADS,
        in_specs=[VMEM] * 4,
        out_specs=[VMEM] * HEADS,
        cost_estimate=pl.CostEstimate(flops=0, bytes_accessed=4 * 2**20, transcendentals=0),
    )(dq, keep, recv, back)


def main_kernel(
    info_ref, low_ref, weight_ref, start_ref, p0, p1, p2, p3, oth_ref, own_prev_ref, oth_prev_ref,
    dq_ref, keep_ref, send_ref,
    kt, ks, ks_turned, dk, et, es, top_t, top_s, dq_acc,
):
    head, side = info_ref[0], info_ref[1]
    weight = weight_ref[0]
    scale = 1.0 / math.sqrt(DIM)
    pace = scale * math.log2(math.e)
    pieces = (p0, p1, p2, p3)
    along_depth = (((1,), (1,)), ((), ()))

    def rows(block):
        return pl.ds(pl.multiple_of(block * TOK, TOK), TOK)

    def place(k, parity):
        return 2 * lax.rem(head - k + HEADS, HEADS) + parity

    for k in range(HEADS):
        blocks = (
            (place(k, side), own_prev_ref.at[k]),
            (place(k, 1 - side), oth_prev_ref.at[k]),
            (ROW + place(k, side), pieces[k]),
            (ROW + place(k, 1 - side), oth_ref.at[k]),
        )
        for block, ref in blocks:
            kt[rows(block), :] = ref[0]
            ks[rows(block), :] = ref[1]

    def prepare(block, _):
        ks_turned[block] = ks[rows(block), :].T
        dk[rows(block), :] = jnp.zeros((TOK, DIM), F32)
        return 0

    lax.fori_loop(0, 2 * ROW, prepare, 0)

    key_row = lax.broadcasted_iota(jnp.int32, (TOK, TOK), 0)
    query_column = lax.broadcasted_iota(jnp.int32, (TOK, TOK), 1)

    for k in range(HEADS):
        here = place(k, side)
        block = ROW + here
        low = low_ref[here] // TOK
        q_t, q_s = pieces[k][2], pieces[k][3]
        start = start_ref[pl.ds(here, 1), :]

        def one(keys, queries, visible, slot, top, total, top_out, out):
            s = lax.dot_general(keys, queries, along_depth, preferred_element_type=F32)
            s = jnp.where(visible, s, MASKED)
            new_top = jnp.maximum(top, jnp.max(s, axis=0, keepdims=True))
            e = jnp.exp2((s - new_top) * pace)
            out[slot] = e
            top_out[slot] = new_top
            return new_top, total * jnp.exp2((top - new_top) * pace) + jnp.sum(e, axis=0, keepdims=True)

        def score(kb, visible, carry):
            m_t, l_t, m_s, l_s = carry
            m_t, l_t = one(kt[rows(kb), :], q_t, visible, kb - low, m_t, l_t, top_t, et)
            m_s, l_s = one(ks[rows(kb), :], q_s, visible, kb - low, m_s, l_s, top_s, es)
            return m_t, l_t, m_s, l_s

        def score_before(kb, carry):
            return score(kb, key_row >= start - kb * TOK, carry)

        none, zero = jnp.full((1, TOK), MASKED, F32), jnp.zeros((1, TOK), F32)
        own_visible = (key_row <= query_column) & (key_row >= start - block * TOK)
        carry = score(block, own_visible, (none, zero, none, zero))
        m_t, l_t, m_s, l_s = lax.fori_loop(low, block, score_before, carry)
        r_t, r_s = weight / l_t, weight / l_s
        dq_acc[...] = jnp.zeros((DIM, TOK), F32)

        def grads(kb, _):
            slot = kb - low
            f_t = jnp.exp2((top_t[slot] - m_t) * pace) * r_t
            f_s = jnp.exp2((top_s[slot] - m_s) * pace) * r_s
            grad = (es[slot] * f_s - et[slot] * f_t).astype(BF16)
            dk[rows(kb), :] += jnp.dot(grad, q_s, preferred_element_type=F32)
            dq_acc[...] += jnp.dot(ks_turned[kb], grad, preferred_element_type=F32)
            return 0

        lax.fori_loop(low, block + 1, grads, 0)
        dq_ref[k] = (dq_acc[...] * scale).T.astype(BF16)

    for k in range(HEADS):
        for row in range(2):
            keep_ref[row, k] = dk[rows(row * ROW + place(k, side)), :] * scale
            send_ref[row, k] = dk[rows(row * ROW + place(k, 1 - side)), :] * scale


def attend(info, low, weight, start, pieces, oth, own_prev, oth_prev):
    return pl.pallas_call(
        main_kernel,
        out_shape=[
            jax.ShapeDtypeStruct((QUART, TOK, DIM), BF16),
            jax.ShapeDtypeStruct((2, QUART, TOK, DIM), F32),
            jax.ShapeDtypeStruct((2, QUART, TOK, DIM), F32),
        ],
        in_specs=[SMEM] * 3 + [VMEM] * 8,
        out_specs=[VMEM] * 3,
        scratch_shapes=[
            pltpu.VMEM((2 * ROW * TOK, DIM), BF16),
            pltpu.VMEM((2 * ROW * TOK, DIM), BF16),
            pltpu.VMEM((2 * ROW, DIM, TOK), BF16),
            pltpu.VMEM((2 * ROW * TOK, DIM), F32),
            pltpu.VMEM((ROW, TOK, TOK), F32),
            pltpu.VMEM((ROW, TOK, TOK), F32),
            pltpu.VMEM((ROW, 1, TOK), F32),
            pltpu.VMEM((ROW, 1, TOK), F32),
            pltpu.VMEM((DIM, TOK), F32),
        ],
        compiler_params=pltpu.CompilerParams(vmem_limit_bytes=36 * 1024 * 1024),
        cost_estimate=pl.CostEstimate(flops=10**9, bytes_accessed=8 * 2**20, transcendentals=4 * 10**6),
    )(info, low, weight, start, *pieces, oth, own_prev, oth_prev)


def per_device(seq, dp, teacher_query, teacher_key, student_query, student_key, segment_ids, head_weight):
    rounds, swap, down = routes(seq, dp)
    seq_index = lax.axis_index("seq")
    core = lax.rem(lax.axis_index("dp"), 2)
    y = lax.rem(seq_index, ROW)
    row_index = seq_index // ROW
    head, window = y // 2, lax.rem(y, 2)
    half = head.reshape(1)

    def move(x, route):
        return lax.ppermute(x, AXES, route)

    packed = pack(half, teacher_key[0], student_key[0], teacher_query[0], student_query[0])
    pieces = [move(x, r) for x, r in zip(packed, rounds)]

    row_tokens = ROW * TOK
    filler = jnp.full((row_tokens,), -1, jnp.int32)
    seg_mine = lax.dynamic_slice_in_dim(
        jnp.concatenate([filler, segment_ids[0]]), row_index * row_tokens, 2 * row_tokens
    ).reshape(2 * ROW, TOK)
    seg = jnp.where(core == window, seg_mine, move(seg_mine, swap))
    start = jnp.sum(
        seg.reshape(2 * row_tokens, 1, 1) < seg[None, ROW:], axis=0, dtype=jnp.int32
    )

    own = jnp.stack([piece[:2] for piece in pieces])
    own_prev = move(own, down)
    oth = move(own, swap)
    oth_prev = move(own_prev, swap)

    info = jnp.stack([head, core]).astype(jnp.int32)
    weight = lax.dynamic_slice_in_dim(head_weight, head, 1)
    dq, keep, send = attend(info, start[:, 0], weight, start, pieces, oth, own_prev, oth_prev)

    recv = move(send, swap)
    back = move((keep[0] + recv[0]).astype(BF16), reverse(down))
    results = finish(dq, keep, recv, back)
    query_grad, key_grad = unpack(half, [move(x, reverse(r)) for x, r in zip(results, rounds)])
    return query_grad[None], key_grad[None]


def solution(mesh):
    seq, dp = mesh.shape["seq"], mesh.shape["dp"]
    spec = P("dp", "seq", None)
    return jax.shard_map(
        functools.partial(per_device, seq, dp),
        mesh=mesh,
        in_specs=(spec, spec, spec, spec, P("dp", None), P()),
        out_specs=(spec, spec),
        check_vma=False,
    )
```

time: 132 us -> 132 us (level)
  the two profiles are of different devices: /device:TPU:5 before, /device:TPU:6 now
where the time goes in v2:
time: 132 us; the launch traced here: 130 us
  starting transfers between devices  52.5 us (40%)
  waiting for transfers between devices  43.9 us (33%)
  Pallas kernels  17.9 us (14%)
  other arithmetic  12.3 us (9%)
  local copies, waits for them, and re-layouts  2.84 us (2%)
    ppermute x14, starting transfers between devices, move(): return lax.ppermute(x, AXES, route)  52.5 us
    ppermute x14, waiting for transfers between devices, move(): return lax.ppermute(x, AXES, route)  43.9 us
    reduce_sum x1, other arithmetic, per_device(): jnp.sum(seg.reshape(2 * row_tokens, 1, 1) < seg[None, ROW:], axis=0, dtyp...  12.1 us
    pallas_call x1, Pallas kernels, attend(): pl.pallas_call(main_kernel, out_shape=[jax.ShapeDtypeStruct((QUART, TOK,...  10.9 us
  transfers between devices with their start and end apart: 14, of which 10 were waited for; matrix products, arithmetic and copies ran while one was open for 10% of the time, Pallas kernels for 0%

profile of v2, /device:TPU:6, one launch (start us, length us, event | category | flops | bytes accessed | tf_op | source)
XLA Modules:
  0.0 130.3 jit_solution(10165755803531845676)
XLA Ops:
  0.7 2.3 %shard_map.77 = (bf16[4,256,128]{2,1,0:T(8,128)(2,1)}, bf16[4,256,128]{2,1,0:T(8,128)(2,1)}, bf16[4,256,128]{2,1,0:T(8,128)(2,1)}, bf16[4,256,128]{2,1,0:T(8,128)(2,1)}) custom-call(s32[1]{0:T(128)} %bitcast.half_ref, bf16[256,512]{1,0:T(8,128)(2,1)} %bitcast.21, bf16[256,512]{1,0:T(8,128)(2,1)} %bitcast.22, bf16[256,512]{1,0:T(8,128)(2,1)} %bitcast.23, ...), custom_call_target="tpu_custom_call" | custom-call | bytes 2097152 | tf_op jit(solution)/shard_map/pallas_call | solution.py:57
  3.0 1.6 %collective-permute-start.1 = (bf16[4,256,128]{2,1,0:T(8,128)(2,1)}, bf16[4,256,128]{2,1,0:T(8,128)(2,1)S(1)}, u32[]{:S(2)}, u32[]{:S(2)}) collective-permute-start(bf16[4,256,128]{2,1,0:T(8,128)(2,1)} %get-tuple-element.15), channel_id=1, source_target_pairs={{0,0},{1,4},{2,2},{3,6},{4,1},{5,5},{6,3},{7,7},{8,8},{9,12},{10,1... | collective-permute-start | bytes 786440 | tf_op jit(solution)/shard_map/ppermute | solution.py:225
  4.6 4.5 %collective-permute-start.2 = (bf16[4,256,128]{2,1,0:T(8,128)(2,1)}, bf16[4,256,128]{2,1,0:T(8,128)(2,1)S(1)}, u32[]{:S(2)}, u32[]{:S(2)}) collective-permute-start(bf16[4,256,128]{2,1,0:T(8,128)(2,1)} %get-tuple-element.16), channel_id=1, source_target_pairs={{0,8},{1,12},{2,10},{3,14},{4,9},{5,13},{6,11},{7,15},{8,16},{9,20... | collective-permute-start | bytes 786440 | tf_op jit(solution)/shard_map/ppermute | solution.py:225
  9.1 5.9 %collective-permute-start.3 = (bf16[4,256,128]{2,1,0:T(8,128)(2,1)}, bf16[4,256,128]{2,1,0:T(8,128)(2,1)S(1)}, u32[]{:S(2)}, u32[]{:S(2)}) collective-permute-start(bf16[4,256,128]{2,1,0:T(8,128)(2,1)} %get-tuple-element.17), channel_id=1, source_target_pairs={{0,16},{1,20},{2,18},{3,22},{4,17},{5,21},{6,19},{7,23},{8,24},{9,... | collective-permute-start | bytes 786440 | tf_op jit(solution)/shard_map/ppermute | solution.py:225
  15.0 0.0 copy-start.8
  15.0 5.4 %collective-permute-start.4 = (bf16[4,256,128]{2,1,0:T(8,128)(2,1)}, bf16[4,256,128]{2,1,0:T(8,128)(2,1)S(1)}, u32[]{:S(2)}, u32[]{:S(2)}) collective-permute-start(bf16[4,256,128]{2,1,0:T(8,128)(2,1)} %get-tuple-element.18), channel_id=1, source_target_pairs={{0,24},{1,28},{2,26},{3,30},{4,25},{5,29},{6,27},{7,31},{8,0},{9,4... | collective-permute-start | bytes 786440 | tf_op jit(solution)/shard_map/ppermute | solution.py:225
  20.4 0.0 collective-permute-done.1.p0
  20.5 0.0 copy-start.9
  20.5 3.2 %collective-permute-done.2.p1 = bf16[4,256,128]{2,1,0:T(8,128)(2,1)S(1)} collective-permute-done((bf16[4,256,128]{2,1,0:T(8,128)(2,1)}, bf16[4,256,128]{2,1,0:T(8,128)(2,1)S(1)}, u32[]{:S(2)}, u32[]{:S(2)}) %collective-permute-start.2) | collective-permute-done | bytes 262176 | tf_op jit(solution)/shard_map/ppermute | solution.py:225
  23.7 7.6 %collective-permute-done.3.p2 = bf16[4,256,128]{2,1,0:T(8,128)(2,1)S(1)} collective-permute-done((bf16[4,256,128]{2,1,0:T(8,128)(2,1)}, bf16[4,256,128]{2,1,0:T(8,128)(2,1)S(1)}, u32[]{:S(2)}, u32[]{:S(2)}) %collective-permute-start.3) | collective-permute-done | bytes 262176 | tf_op jit(solution)/shard_map/ppermute | solution.py:225
  31.3 4.1 %collective-permute-done.4.p3 = bf16[4,256,128]{2,1,0:T(8,128)(2,1)S(1)} collective-permute-done((bf16[4,256,128]{2,1,0:T(8,128)(2,1)}, bf16[4,256,128]{2,1,0:T(8,128)(2,1)S(1)}, u32[]{:S(2)}, u32[]{:S(2)}) %collective-permute-start.4) | collective-permute-done | bytes 262176 | tf_op jit(solution)/shard_map/ppermute | solution.py:225
  35.4 0.1 pad_maximum_fusion
  35.5 4.3 %collective-permute-start.6 = (bf16[4,2,256,128]{3,2,1,0:T(8,128)(2,1)S(1)}, bf16[4,2,256,128]{3,2,1,0:T(8,128)(2,1)S(1)}, u32[]{:S(2)}, u32[]{:S(2)}) collective-permute-start(bf16[4,2,256,128]{3,2,1,0:T(8,128)(2,1)S(1)} %pad_maximum_fusion), channel_id=1, source_target_pairs={{0,32},{1,33},{2,34},{3,35},{4,36},{5,37},{6,38},{7,39},{8,40},{9,... | collective-permute-start | bytes 1572872 | tf_op jit(solution)/shard_map/ppermute | solution.py:225
  39.8 0.0 copy-done.8
  39.9 3.9 %collective-permute-start = (s32[16,256]{1,0:T(8,128)S(1)}, s32[16,256]{1,0:T(8,128)S(1)}, u32[]{:S(2)}, u32[]{:S(2)}) collective-permute-start(s32[16,256]{1,0:T(8,128)S(1)} %reshape.16), channel_id=1, source_target_pairs={{0,1},{1,0},{2,3},{3,2},{4,5},{5,4},{6,7},{7,6},{8,9},{9,8},{10,11... | collective-permute-start | bytes 49160 | tf_op jit(solution)/shard_map/ppermute | solution.py:225
  43.8 0.1 pad_add_fusion.info_ref
  43.8 0.0 copy-done.9
  43.9 0.6 dynamic_slice.7.weight_ref
  44.4 0.1 collective-permute-done
  44.6 2.3 %collective-permute-start.5 = (bf16[4,2,256,128]{3,2,1,0:T(8,128)(2,1)S(1)}, bf16[4,2,256,128]{3,2,1,0:T(8,128)(2,1)S(1)}, u32[]{:S(2)}, u32[]{:S(2)}) collective-permute-start(bf16[4,2,256,128]{3,2,1,0:T(8,128)(2,1)S(1)} %pad_maximum_fusion), channel_id=1, source_target_pairs={{0,1},{1,0},{2,3},{3,2},{4,5},{5,4},{6,7},{7,6},{8,9},{9,8},{10,11... | collective-permute-start | bytes 1572872 | tf_op jit(solution)/shard_map/ppermute | solution.py:225
  46.9 11.6 %collective-permute-done.6.own_prev_ref = bf16[4,2,256,128]{3,2,1,0:T(8,128)(2,1)S(1)} collective-permute-done((bf16[4,2,256,128]{3,2,1,0:T(8,128)(2,1)S(1)}, bf16[4,2,256,128]{3,2,1,0:T(8,128)(2,1)S(1)}, u32[]{:S(2)}, u32[]{:S(2)}) %collective-permute-start.6) | collective-permute-done | bytes 524320 | tf_op jit(solution)/shard_map/ppermute | solution.py:225
  58.4 3.4 %collective-permute-start.7 = (bf16[4,2,256,128]{3,2,1,0:T(8,128)(2,1)S(1)}, bf16[4,2,256,128]{3,2,1,0:T(8,128)(2,1)S(1)}, u32[]{:S(2)}, u32[]{:S(2)}) collective-permute-start(bf16[4,2,256,128]{3,2,1,0:T(8,128)(2,1)S(1)} %collective-permute-done.6.own_prev_ref), channel_id=1, source_target_pairs={{0,1},{1,0},{2,3},{3,2},{4,5},{5,4},{6,7},{7,6},{8,9},{9,8},{10,11... | collective-permute-start | bytes 1572872 | tf_op jit(solution)/shard_map/ppermute | solution.py:225
  61.8 12.1 %convert_reduce_fusion.start_ref = s32[8,256]{1,0:T(8,128)S(1)} fusion(s32[8,256]{1,0:T(8,128)S(1)} %slice.32, s32[4096]{0:T(1024)S(1)} %bitcast.27), kind=kLoop, calls=%fused_computation | loop fusion | flops 25163776 | bytes 32768 | tf_op jit(solution)/shard_map/reduce_sum | solution.py:236
  73.9 0.1 slice_reduce_fusion.low_ref
  74.0 0.0 collective-permute-done.5.oth_ref
  74.0 0.0 collective-permute-done.7.oth_prev_ref
  74.0 10.9 %shard_map.78 = (bf16[4,256,128]{2,1,0:T(8,128)(2,1)S(1)}, f32[2,4,256,128]{3,2,1,0:T(8,128)S(1)}, f32[2,4,256,128]{3,2,1,0:T(8,128)S(1)}) custom-call(s32[2]{0:T(128)S(1)} %pad_add_fusion.info_ref, s32[8]{0:T(128)S(1)} %slice_reduce_fusion.low_ref, f32[1]{0:T(128)} %dynamic_slice.7.weight_ref, s32[8,256]{1,0:T(8,128)S(1)} %convert_reduce_fusion.start_ref, ...), custom_call_target="tpu_custom_call" | custom-call | flops 1000000000 | bytes 8388608 | tf_op jit(solution)/shard_map/pallas_call | solution.py:190
  85.0 0.0 copy-start.1
  85.0 0.7 copy-done.1
  85.7 0.0 copy-start
  85.7 1.9 %collective-permute-start.8 = (f32[2,4,256,128]{3,2,1,0:T(8,128)S(1)}, f32[2,4,256,128]{3,2,1,0:T(8,128)S(1)}, u32[]{:S(2)}, u32[]{:S(2)}) collective-permute-start(f32[2,4,256,128]{3,2,1,0:T(8,128)S(1)} %get-tuple-element.21), channel_id=1, source_target_pairs={{0,1},{1,0},{2,3},{3,2},{4,5},{5,4},{6,7},{7,6},{8,9},{9,8},{10,11... | collective-permute-start | bytes 3145736 | tf_op jit(solution)/shard_map/ppermute | solution.py:225
  87.6 2.6 %collective-permute-done.8.recv_ref = f32[2,4,256,128]{3,2,1,0:T(8,128)S(1)} collective-permute-done((f32[2,4,256,128]{3,2,1,0:T(8,128)S(1)}, f32[2,4,256,128]{3,2,1,0:T(8,128)S(1)}, u32[]{:S(2)}, u32[]{:S(2)}) %collective-permute-start.8) | collective-permute-done | bytes 1048608 | tf_op jit(solution)/shard_map/ppermute | solution.py:225
  90.2 0.0 copy-start.2
  90.2 0.1 fusion.1
  90.3 4.5 %collective-permute-start.9 = (bf16[4,256,128]{2,1,0:T(8,128)(2,1)S(1)}, bf16[4,256,128]{2,1,0:T(8,128)(2,1)S(1)}, u32[]{:S(2)}, u32[]{:S(2)}) collective-permute-start(bf16[4,256,128]{2,1,0:T(8,128)(2,1)S(1)} %fusion.1), channel_id=1, source_target_pairs={{32,0},{33,1},{34,2},{35,3},{36,4},{37,5},{38,6},{39,7},{40,8},{41... | collective-permute-start | bytes 786440 | tf_op jit(solution)/shard_map/ppermute | solution.py:225
  94.8 5.8 %collective-permute-done.9.back_ref = bf16[4,256,128]{2,1,0:T(8,128)(2,1)S(1)} collective-permute-done((bf16[4,256,128]{2,1,0:T(8,128)(2,1)S(1)}, bf16[4,256,128]{2,1,0:T(8,128)(2,1)S(1)}, u32[]{:S(2)}, u32[]{:S(2)}) %collective-permute-start.9) | collective-permute-done | bytes 262176 | tf_op jit(solution)/shard_map/ppermute | solution.py:225
  100.6 0.0 copy-start.3
  100.6 0.0 copy-done
  100.6 0.0 copy-done.2
  100.6 0.7 copy-done.3
  101.3 2.5 %shard_map.79 = (bf16[2,256,128]{2,1,0:T(8,128)(2,1)}, bf16[2,256,128]{2,1,0:T(8,128)(2,1)}, bf16[2,256,128]{2,1,0:T(8,128)(2,1)}, bf16[2,256,128]{2,1,0:T(8,128)(2,1)}) custom-call(bf16[4,256,128]{2,1,0:T(8,128)(2,1)} %copy-done.1, f32[2,4,256,128]{3,2,1,0:T(8,128)} %copy-done, f32[2,4,256,128]{3,2,1,0:T(8,128)} %copy-done.2, bf16[4,256,128]{2,1,0:T(8,128)(2,1)} %copy-done.3), custom_call_target="tpu_custom_call" | custom-call | bytes 4194304 | tf_op jit(solution)/shard_map/pallas_call | solution.py:91
  103.8 1.6 %collective-permute-start.10 = (bf16[2,256,128]{2,1,0:T(8,128)(2,1)}, bf16[2,256,128]{2,1,0:T(8,128)(2,1)S(1)}, u32[]{:S(2)}, u32[]{:S(2)}) collective-permute-start(bf16[2,256,128]{2,1,0:T(8,128)(2,1)} %get-tuple-element.22), channel_id=1, source_target_pairs={{0,0},{4,1},{2,2},{6,3},{1,4},{5,5},{3,6},{7,7},{8,8},{12,9},{10,1... | collective-permute-start | bytes 393224 | tf_op jit(solution)/shard_map/ppermute | solution.py:225
  105.4 5.9 %collective-permute-start.11 = (bf16[2,256,128]{2,1,0:T(8,128)(2,1)}, bf16[2,256,128]{2,1,0:T(8,128)(2,1)S(1)}, u32[]{:S(2)}, u32[]{:S(2)}) collective-permute-start(bf16[2,256,128]{2,1,0:T(8,128)(2,1)} %get-tuple-element.23), channel_id=1, source_target_pairs={{8,0},{12,1},{10,2},{14,3},{9,4},{13,5},{11,6},{15,7},{16,8},{20,9... | collective-permute-start | bytes 393224 | tf_op jit(solution)/shard_map/ppermute | solution.py:225
  111.3 4.1 %collective-permute-start.12 = (bf16[2,256,128]{2,1,0:T(8,128)(2,1)}, bf16[2,256,128]{2,1,0:T(8,128)(2,1)S(1)}, u32[]{:S(2)}, u32[]{:S(2)}) collective-permute-start(bf16[2,256,128]{2,1,0:T(8,128)(2,1)} %get-tuple-element.24), channel_id=1, source_target_pairs={{16,0},{20,1},{18,2},{22,3},{17,4},{21,5},{19,6},{23,7},{24,8},{28... | collective-permute-start | bytes 393224 | tf_op jit(solution)/shard_map/ppermute | solution.py:225
  115.4 3.3 %collective-permute-start.13 = (bf16[2,256,128]{2,1,0:T(8,128)(2,1)}, bf16[2,256,128]{2,1,0:T(8,128)(2,1)S(1)}, u32[]{:S(2)}, u32[]{:S(2)}) collective-permute-start(bf16[2,256,128]{2,1,0:T(8,128)(2,1)} %get-tuple-element.25), channel_id=1, source_target_pairs={{24,0},{28,1},{26,2},{30,3},{25,4},{29,5},{27,6},{31,7},{0,8},{4,9... | collective-permute-start | bytes 393224 | tf_op jit(solution)/shard_map/ppermute | solution.py:225
  118.7 0.0 collective-permute-done.10.p0
  118.7 0.0 copy-start.4
  118.8 0.5 collective-permute-done.11.p1
  119.3 0.0 copy-start.5
  119.3 5.9 %collective-permute-done.12.p2 = bf16[2,256,128]{2,1,0:T(8,128)(2,1)S(1)} collective-permute-done((bf16[2,256,128]{2,1,0:T(8,128)(2,1)}, bf16[2,256,128]{2,1,0:T(8,128)(2,1)S(1)}, u32[]{:S(2)}, u32[]{:S(2)}) %collective-permute-start.12) | collective-permute-done | bytes 131104 | tf_op jit(solution)/shard_map/ppermute | solution.py:225
  125.2 0.0 copy-start.6
  125.2 2.3 %collective-permute-done.13.p3 = bf16[2,256,128]{2,1,0:T(8,128)(2,1)S(1)} collective-permute-done((bf16[2,256,128]{2,1,0:T(8,128)(2,1)}, bf16[2,256,128]{2,1,0:T(8,128)(2,1)S(1)}, u32[]{:S(2)}, u32[]{:S(2)}) %collective-permute-start.13) | collective-permute-done | bytes 131104 | tf_op jit(solution)/shard_map/ppermute | solution.py:225
  127.5 0.0 copy-done.4
  127.5 0.0 copy-done.5
  127.5 0.0 copy-done.6
  127.5 0.0 copy-start.7
  127.6 0.6 copy-done.7
  128.2 2.1 %shard_map.80 = (f32[256,512]{1,0:T(8,128)}, f32[256,512]{1,0:T(8,128)}) custom-call(s32[1]{0:T(128)} %bitcast.half_ref, bf16[2,256,128]{2,1,0:T(8,128)(2,1)} %copy-done.4, bf16[2,256,128]{2,1,0:T(8,128)(2,1)} %copy-done.5, bf16[2,256,128]{2,1,0:T(8,128)(2,1)} %copy-done.6, bf16[2,256,128]{2,1,0:T(8,128)(2,1)} %copy-done.7), custom_call_target="tpu_custom_call" | custom-call | bytes 1572864 | tf_op jit(solution)/shard_map/pallas_call | solution.py:75
  (9 shorter events, 0.1 us)
Async XLA Ops:
  3.0 17.4 %collective-permute-start.1 = (bf16[4,256,128]{2,1,0:T(8,128)(2,1)}, bf16[4,256,128]{2,1,0:T(8,128)(2,1)S(1)}, u32[]{:S(2)}, u32[]{:S(2)}) collective-permute-start(bf16[4,256,128]{2,1,0:T(8,128)(2,1)} %get-tuple-element.15), channel_id=1, source_target_pairs={{0,0},{1,4},{2,2},{3,6},{4,1},{5,5},{6,3},{7,7},{8,8},{9,12},{10,1... | collective-permute-start | bytes 786440 | tf_op jit(solution)/shard_map/ppermute | solution.py:225
  4.6 19.1 %collective-permute-start.2 = (bf16[4,256,128]{2,1,0:T(8,128)(2,1)}, bf16[4,256,128]{2,1,0:T(8,128)(2,1)S(1)}, u32[]{:S(2)}, u32[]{:S(2)}) collective-permute-start(bf16[4,256,128]{2,1,0:T(8,128)(2,1)} %get-tuple-element.16), channel_id=1, source_target_pairs={{0,8},{1,12},{2,10},{3,14},{4,9},{5,13},{6,11},{7,15},{8,16},{9,20... | collective-permute-start | bytes 786440 | tf_op jit(solution)/shard_map/ppermute | solution.py:225
  9.1 22.2 %collective-permute-start.3 = (bf16[4,256,128]{2,1,0:T(8,128)(2,1)}, bf16[4,256,128]{2,1,0:T(8,128)(2,1)S(1)}, u32[]{:S(2)}, u32[]{:S(2)}) collective-permute-start(bf16[4,256,128]{2,1,0:T(8,128)(2,1)} %get-tuple-element.17), channel_id=1, source_target_pairs={{0,16},{1,20},{2,18},{3,22},{4,17},{5,21},{6,19},{7,23},{8,24},{9,... | collective-permute-start | bytes 786440 | tf_op jit(solution)/shard_map/ppermute | solution.py:225
  15.0 24.8 %copy-start.8 = (s32[1,32768]{1,0:T(1,128)S(1)}, s32[1,32768]{1,0:T(1,128)}, u32[]{:S(2)}) copy-start(s32[1,32768]{1,0:T(1,128)} %param.10) | copy-start | bytes 393220
  15.0 20.4 %collective-permute-start.4 = (bf16[4,256,128]{2,1,0:T(8,128)(2,1)}, bf16[4,256,128]{2,1,0:T(8,128)(2,1)S(1)}, u32[]{:S(2)}, u32[]{:S(2)}) collective-permute-start(bf16[4,256,128]{2,1,0:T(8,128)(2,1)} %get-tuple-element.18), channel_id=1, source_target_pairs={{0,24},{1,28},{2,26},{3,30},{4,25},{5,29},{6,27},{7,31},{8,0},{9,4... | collective-permute-start | bytes 786440 | tf_op jit(solution)/shard_map/ppermute | solution.py:225
  20.5 23.4 %copy-start.9 = (f32[4]{0:T(128)S(1)}, f32[4]{0:T(128)}, u32[]{:S(2)}) copy-start(f32[4]{0:T(128)} %param.11) | copy-start | bytes 52
  35.5 22.9 %collective-permute-start.6 = (bf16[4,2,256,128]{3,2,1,0:T(8,128)(2,1)S(1)}, bf16[4,2,256,128]{3,2,1,0:T(8,128)(2,1)S(1)}, u32[]{:S(2)}, u32[]{:S(2)}) collective-permute-start(bf16[4,2,256,128]{3,2,1,0:T(8,128)(2,1)S(1)} %pad_maximum_fusion), channel_id=1, source_target_pairs={{0,32},{1,33},{2,34},{3,35},{4,36},{5,37},{6,38},{7,39},{8,40},{9,... | collective-permute-start | bytes 1572872 | tf_op jit(solution)/shard_map/ppermute | solution.py:225
  39.9 4.7 %collective-permute-start = (s32[16,256]{1,0:T(8,128)S(1)}, s32[16,256]{1,0:T(8,128)S(1)}, u32[]{:S(2)}, u32[]{:S(2)}) collective-permute-start(s32[16,256]{1,0:T(8,128)S(1)} %reshape.16), channel_id=1, source_target_pairs={{0,1},{1,0},{2,3},{3,2},{4,5},{5,4},{6,7},{7,6},{8,9},{9,8},{10,11... | collective-permute-start | bytes 49160 | tf_op jit(solution)/shard_map/ppermute | solution.py:225
  44.6 29.4 %collective-permute-start.5 = (bf16[4,2,256,128]{3,2,1,0:T(8,128)(2,1)S(1)}, bf16[4,2,256,128]{3,2,1,0:T(8,128)(2,1)S(1)}, u32[]{:S(2)}, u32[]{:S(2)}) collective-permute-start(bf16[4,2,256,128]{3,2,1,0:T(8,128)(2,1)S(1)} %pad_maximum_fusion), channel_id=1, source_target_pairs={{0,1},{1,0},{2,3},{3,2},{4,5},{5,4},{6,7},{7,6},{8,9},{9,8},{10,11... | collective-permute-start | bytes 1572872 | tf_op jit(solution)/shard_map/ppermute | solution.py:225
  58.4 15.6 %collective-permute-start.7 = (bf16[4,2,256,128]{3,2,1,0:T(8,128)(2,1)S(1)}, bf16[4,2,256,128]{3,2,1,0:T(8,128)(2,1)S(1)}, u32[]{:S(2)}, u32[]{:S(2)}) collective-permute-start(bf16[4,2,256,128]{3,2,1,0:T(8,128)(2,1)S(1)} %collective-permute-done.6.own_prev_ref), channel_id=1, source_target_pairs={{0,1},{1,0},{2,3},{3,2},{4,5},{5,4},{6,7},{7,6},{8,9},{9,8},{10,11... | collective-permute-start | bytes 1572872 | tf_op jit(solution)/shard_map/ppermute | solution.py:225
  85.0 0.7 copy-start.1
  85.7 14.9 %copy-start = (f32[2,4,256,128]{3,2,1,0:T(8,128)}, f32[2,4,256,128]{3,2,1,0:T(8,128)S(1)}, u32[]{:S(2)}) copy-start(f32[2,4,256,128]{3,2,1,0:T(8,128)S(1)} %get-tuple-element.20.keep_ref) | copy-start | bytes 3145732
  85.7 4.5 %collective-permute-start.8 = (f32[2,4,256,128]{3,2,1,0:T(8,128)S(1)}, f32[2,4,256,128]{3,2,1,0:T(8,128)S(1)}, u32[]{:S(2)}, u32[]{:S(2)}) collective-permute-start(f32[2,4,256,128]{3,2,1,0:T(8,128)S(1)} %get-tuple-element.21), channel_id=1, source_target_pairs={{0,1},{1,0},{2,3},{3,2},{4,5},{5,4},{6,7},{7,6},{8,9},{9,8},{10,11... | collective-permute-start | bytes 3145736 | tf_op jit(solution)/shard_map/ppermute | solution.py:225
  90.2 10.4 %copy-start.2 = (f32[2,4,256,128]{3,2,1,0:T(8,128)}, f32[2,4,256,128]{3,2,1,0:T(8,128)S(1)}, u32[]{:S(2)}) copy-start(f32[2,4,256,128]{3,2,1,0:T(8,128)S(1)} %collective-permute-done.8.recv_ref) | copy-start | bytes 3145732
  90.3 10.3 %collective-permute-start.9 = (bf16[4,256,128]{2,1,0:T(8,128)(2,1)S(1)}, bf16[4,256,128]{2,1,0:T(8,128)(2,1)S(1)}, u32[]{:S(2)}, u32[]{:S(2)}) collective-permute-start(bf16[4,256,128]{2,1,0:T(8,128)(2,1)S(1)} %fusion.1), channel_id=1, source_target_pairs={{32,0},{33,1},{34,2},{35,3},{36,4},{37,5},{38,6},{39,7},{40,8},{41... | collective-permute-start | bytes 786440 | tf_op jit(solution)/shard_map/ppermute | solution.py:225
  100.6 0.7 copy-start.3
  103.8 14.9 %collective-permute-start.10 = (bf16[2,256,128]{2,1,0:T(8,128)(2,1)}, bf16[2,256,128]{2,1,0:T(8,128)(2,1)S(1)}, u32[]{:S(2)}, u32[]{:S(2)}) collective-permute-start(bf16[2,256,128]{2,1,0:T(8,128)(2,1)} %get-tuple-element.22), channel_id=1, source_target_pairs={{0,0},{4,1},{2,2},{6,3},{1,4},{5,5},{3,6},{7,7},{8,8},{12,9},{10,1... | collective-permute-start | bytes 393224 | tf_op jit(solution)/shard_map/ppermute | solution.py:225
  105.4 13.9 %collective-permute-start.11 = (bf16[2,256,128]{2,1,0:T(8,128)(2,1)}, bf16[2,256,128]{2,1,0:T(8,128)(2,1)S(1)}, u32[]{:S(2)}, u32[]{:S(2)}) collective-permute-start(bf16[2,256,128]{2,1,0:T(8,128)(2,1)} %get-tuple-element.23), channel_id=1, source_target_pairs={{8,0},{12,1},{10,2},{14,3},{9,4},{13,5},{11,6},{15,7},{16,8},{20,9... | collective-permute-start | bytes 393224 | tf_op jit(solution)/shard_map/ppermute | solution.py:225
  111.3 13.9 %collective-permute-start.12 = (bf16[2,256,128]{2,1,0:T(8,128)(2,1)}, bf16[2,256,128]{2,1,0:T(8,128)(2,1)S(1)}, u32[]{:S(2)}, u32[]{:S(2)}) collective-permute-start(bf16[2,256,128]{2,1,0:T(8,128)(2,1)} %get-tuple-element.24), channel_id=1, source_target_pairs={{16,0},{20,1},{18,2},{22,3},{17,4},{21,5},{19,6},{23,7},{24,8},{28... | collective-permute-start | bytes 393224 | tf_op jit(solution)/shard_map/ppermute | solution.py:225
  115.4 12.1 %collective-permute-start.13 = (bf16[2,256,128]{2,1,0:T(8,128)(2,1)}, bf16[2,256,128]{2,1,0:T(8,128)(2,1)S(1)}, u32[]{:S(2)}, u32[]{:S(2)}) collective-permute-start(bf16[2,256,128]{2,1,0:T(8,128)(2,1)} %get-tuple-element.25), channel_id=1, source_target_pairs={{24,0},{28,1},{26,2},{30,3},{25,4},{29,5},{27,6},{31,7},{0,8},{4,9... | collective-permute-start | bytes 393224 | tf_op jit(solution)/shard_map/ppermute | solution.py:225
  118.7 8.8 %copy-start.4 = (bf16[2,256,128]{2,1,0:T(8,128)(2,1)}, bf16[2,256,128]{2,1,0:T(8,128)(2,1)S(1)}, u32[]{:S(2)}) copy-start(bf16[2,256,128]{2,1,0:T(8,128)(2,1)S(1)} %collective-permute-done.10.p0) | copy-start | bytes 393220
  119.3 8.2 %copy-start.5 = (bf16[2,256,128]{2,1,0:T(8,128)(2,1)}, bf16[2,256,128]{2,1,0:T(8,128)(2,1)S(1)}, u32[]{:S(2)}) copy-start(bf16[2,256,128]{2,1,0:T(8,128)(2,1)S(1)} %collective-permute-done.11.p1) | copy-start | bytes 393220
  125.2 2.3 %copy-start.6 = (bf16[2,256,128]{2,1,0:T(8,128)(2,1)}, bf16[2,256,128]{2,1,0:T(8,128)(2,1)S(1)}, u32[]{:S(2)}) copy-start(bf16[2,256,128]{2,1,0:T(8,128)(2,1)S(1)} %collective-permute-done.12.p2) | copy-start | bytes 393220
  127.5 0.7 copy-start.7

commit v3 on v2

v3 whole, which is shorter than its diff:
```python
import functools
import math

import jax
import jax.numpy as jnp
from jax import lax
from jax.experimental import pallas as pl
from jax.experimental.pallas import tpu as pltpu
from jax.sharding import PartitionSpec as P

HEADS = 4
DIM = 128
TOK = 256
LINE = 4
RING = 8
BEHIND = 7
BAND = 12
OWN = 8
PAIR = 2 * TOK
MASKED = -1e30
F32 = jnp.float32
BF16 = jnp.bfloat16
VMEM = pl.BlockSpec(memory_space=pltpu.VMEM)
SMEM = pl.BlockSpec(memory_space=pltpu.SMEM)
AXES = ("seq", "dp")


def routes(seq, dp):
    last, before_last = [], []
    for ring in range(seq // RING):
        for y in range(RING):
            for part in range(dp):
                me = (ring * RING + y) * dp + part
                ahead = ring + (y >= LINE)
                if ahead < seq // RING:
                    last.append((me, (ahead * RING + RING - 1 - y) * dp + part))
                if ring + 1 < seq // RING:
                    before_last.append((me, ((ring + 1) * RING + y) * dp + part))
    return last, before_last


def reverse(route):
    return [(b, a) for a, b in route]


def head_columns(flip, place):
    head = jnp.where(flip == 1, HEADS - 1 - place, place)
    return pl.ds(pl.multiple_of(head * DIM, DIM), DIM)


def pack_keys_kernel(flip_ref, a_ref, b_ref, out_ref):
    for place in range(HEADS):
        columns = head_columns(flip_ref[0], place)
        out_ref[place, 0] = a_ref[:, columns]
        out_ref[place, 1] = b_ref[:, columns]


def pack_queries_kernel(flip_ref, range_ref, a_ref, b_ref, seg_ref, out_ref, start_ref, low_ref):
    pack_keys_kernel(flip_ref, a_ref, b_ref, out_ref)
    first_block = range_ref[0] * LINE

    def ids(block):
        return seg_ref[0:1, pl.ds(pl.multiple_of(block * TOK, TOK), TOK)]

    own = [ids(first_block + j) for j in range(LINE)]
    ahead = [(first_block - b, ids(jnp.maximum(first_block - b, 0))) for b in range(1, BEHIND + 1)]
    counts = []
    for j in range(LINE):
        first = own[j][:, :1]
        same = jnp.zeros((1, TOK), jnp.int32)
        for i in range(j):
            same += (own[i] == first).astype(jnp.int32)
        for block, row in ahead[: BEHIND - j]:
            same += ((row == first) & (block >= 0)).astype(jnp.int32)
        counts.append(same)
    count = jnp.sum(jnp.concatenate(counts, axis=0), axis=1, keepdims=True)
    seg = jnp.concatenate(own, axis=0)
    column = lax.broadcasted_iota(jnp.int32, (LINE, TOK), 1)
    begin = jnp.where(seg != pltpu.roll(seg, 1, 1), column, 0)
    begin = jnp.where(column == 0, 0, begin)
    step = 1
    while step < TOK:
        begin = jnp.maximum(begin, jnp.where(column >= step, pltpu.roll(begin, step, 1), 0))
        step *= 2
    block_at = (OWN + lax.broadcasted_iota(jnp.int32, (LINE, TOK), 0)) * TOK
    start = block_at + jnp.where(begin > 0, begin, -count)
    start_ref[...] = start
    for j in range(LINE):
        low_ref[j] = jnp.min(start[j : j + 1, :])


def pack_keys(flip, a, b):
    return pl.pallas_call(
        pack_keys_kernel,
        out_shape=jax.ShapeDtypeStruct((HEADS, 2, TOK, DIM), BF16),
        in_specs=[SMEM, VMEM, VMEM],
        out_specs=VMEM,
        cost_estimate=pl.CostEstimate(flops=0, bytes_accessed=2**20, transcendentals=0),
    )(flip, a, b)


def pack_queries(flip, range_index, a, b, seg):
    return pl.pallas_call(
        pack_queries_kernel,
        out_shape=[
            jax.ShapeDtypeStruct((HEADS, 2, TOK, DIM), BF16),
            jax.ShapeDtypeStruct((LINE, TOK), jnp.int32),
            jax.ShapeDtypeStruct((LINE,), jnp.int32),
        ],
        in_specs=[SMEM, SMEM, VMEM, VMEM, VMEM],
        out_specs=[VMEM, VMEM, SMEM],
        cost_estimate=pl.CostEstimate(flops=0, bytes_accessed=2**20, transcendentals=0),
    )(flip, range_index, a, b, seg)


def unpack_kernel(flip_ref, dq_ref, dk_ref, query_ref, key_ref):
    for place in range(HEADS):
        columns = head_columns(flip_ref[0], place)
        query_ref[:, columns] = dq_ref[place].astype(F32)
        key_ref[:, columns] = dk_ref[place].astype(F32)


def unpack(flip, dq, dk):
    return pl.pallas_call(
        unpack_kernel,
        out_shape=[jax.ShapeDtypeStruct((TOK, HEADS * DIM), F32)] * 2,
        in_specs=[SMEM, VMEM, VMEM],
        out_specs=[VMEM] * 2,
        cost_estimate=pl.CostEstimate(flops=0, bytes_accessed=12 * TOK * 512, transcendentals=0),
    )(flip, dq, dk)


def main_kernel(
    head_ref, low_ref, weight_ref, start_ref, query_ref, own_ref, last_ref, before_ref,
    dq_ref, dk_own_ref, dk_last_ref, dk_before_ref,
    kt, ks, ks_turned, dk, et, es, top_t, top_s, dq_acc,
):
    weight = weight_ref[head_ref[0]]
    scale = 1.0 / math.sqrt(DIM)
    pace = scale * math.log2(math.e)
    along_depth = (((1,), (1,)), ((), ()))
    lowest = low_ref[0] // TOK

    def rows(block):
        return pl.ds(block * TOK, TOK)

    def load(block, ref, index):
        kt[rows(block), :] = ref[index, 0]
        ks[rows(block), :] = ref[index, 1]
        ks_turned[:, rows(block)] = ref[index, 1].T
        dk[rows(block), :] = jnp.zeros((TOK, DIM), F32)

    def clear(block):
        kt[rows(block), :] = jnp.zeros((TOK, DIM), BF16)
        ks[rows(block), :] = jnp.zeros((TOK, DIM), BF16)
        ks_turned[:, rows(block)] = jnp.zeros((DIM, TOK), BF16)
        dk[rows(block), :] = jnp.zeros((TOK, DIM), F32)

    for i in range(LINE):
        load(OWN + i, own_ref, i)

    @pl.when(lowest <= OWN)
    def _():
        for i in range(LINE):
            load(LINE + i, last_ref, i)

    @pl.when(lowest > OWN)
    def _():
        for i in range(LINE):
            clear(LINE + i)

    @pl.when(lowest <= LINE)
    def _():
        for i in range(LINE - 1):
            load(1 + i, before_ref, i)

    @pl.when(lowest > LINE)
    def _():
        for i in range(LINE - 1):
            clear(1 + i)

    key_row = lax.broadcasted_iota(jnp.int32, (PAIR, TOK), 0)
    query_column = lax.broadcasted_iota(jnp.int32, (PAIR, TOK), 1)

    for j in range(LINE):
        block = OWN + j
        pairs = (block + 2 - low_ref[j] // TOK) // 2
        q_t, q_s = query_ref[j, 0], query_ref[j, 1]
        start = start_ref[j : j + 1, :]

        def at(t):
            return pl.multiple_of((block - 1 - 2 * t) * TOK, TOK)

        def one(keys, queries, visible, t, top, total, top_out, out):
            s = lax.dot_general(keys, queries, along_depth, preferred_element_type=F32)
            s = jnp.where(visible, s, MASKED)
            new_top = jnp.maximum(top, jnp.max(s, axis=0, keepdims=True))
            e = jnp.exp2((s - new_top) * pace)
            out[t] = e
            top_out[t] = new_top
            return new_top, total * jnp.exp2((top - new_top) * pace) + jnp.sum(e, axis=0, keepdims=True)

        def score(t, visible, carry):
            m_t, l_t, m_s, l_s = carry
            here = pl.ds(at(t), PAIR)
            m_t, l_t = one(kt[here, :], q_t, visible, t, m_t, l_t, top_t, et)
            m_s, l_s = one(ks[here, :], q_s, visible, t, m_s, l_s, top_s, es)
            return m_t, l_t, m_s, l_s

        def score_before(t, carry):
            return score(t, key_row >= start - at(t), carry)

        none, zero = jnp.full((1, TOK), MASKED, F32), jnp.zeros((1, TOK), F32)
        own_visible = (key_row <= query_column + TOK) & (key_row >= start - at(0))
        carry = score(0, own_visible, (none, zero, none, zero))
        m_t, l_t, m_s, l_s = lax.fori_loop(1, pairs, score_before, carry)
        r_t, r_s = weight / l_t, weight / l_s
        dq_acc[...] = jnp.zeros((DIM, TOK), F32)

        def grads(t, _):
            here = pl.ds(at(t), PAIR)
            f_t = jnp.exp2((top_t[t] - m_t) * pace) * r_t
            f_s = jnp.exp2((top_s[t] - m_s) * pace) * r_s
            grad = (es[t] * f_s - et[t] * f_t).astype(BF16)
            dk[here, :] += jnp.dot(grad, q_s, preferred_element_type=F32)
            dq_acc[...] += jnp.dot(ks_turned[:, here], grad, preferred_element_type=F32)
            return 0

        lax.fori_loop(0, pairs, grads, 0)
        dq_ref[j] = (dq_acc[...] * scale).T.astype(BF16)

    for i in range(LINE):
        dk_own_ref[i] = dk[rows(OWN + i), :] * scale
        dk_last_ref[i] = (dk[rows(LINE + i), :] * scale).astype(BF16)
    for i in range(LINE - 1):
        dk_before_ref[i] = (dk[rows(1 + i), :] * scale).astype(BF16)


def attend(head, low, weight, start, queries, own, last, before):
    return pl.pallas_call(
        main_kernel,
        out_shape=[
            jax.ShapeDtypeStruct((LINE, TOK, DIM), BF16),
            jax.ShapeDtypeStruct((LINE, TOK, DIM), F32),
            jax.ShapeDtypeStruct((LINE, TOK, DIM), BF16),
            jax.ShapeDtypeStruct((LINE - 1, TOK, DIM), BF16),
        ],
        in_specs=[SMEM] * 3 + [VMEM] * 5,
        out_specs=[VMEM] * 4,
        scratch_shapes=[
            pltpu.VMEM((BAND * TOK, DIM), BF16),
            pltpu.VMEM((BAND * TOK, DIM), BF16),
            pltpu.VMEM((DIM, BAND * TOK), BF16),
            pltpu.VMEM((BAND * TOK, DIM), F32),
            pltpu.VMEM((LINE, PAIR, TOK), F32),
            pltpu.VMEM((LINE, PAIR, TOK), F32),
            pltpu.VMEM((LINE, 1, TOK), F32),
            pltpu.VMEM((LINE, 1, TOK), F32),
            pltpu.VMEM((DIM, TOK), F32),
        ],
        compiler_params=pltpu.CompilerParams(vmem_limit_bytes=32 * 1024 * 1024),
        cost_estimate=pl.CostEstimate(flops=10**9, bytes_accessed=6 * 2**20, transcendentals=4 * 10**6),
    )(head, low, weight, start, queries, own, last, before)


def per_device(seq, dp, teacher_query, teacher_key, student_query, student_key, segment_ids, head_weight):
    to_next, to_second = routes(seq, dp)
    lines = [list(range(i, i + LINE)) for i in range(0, seq, LINE)]
    seq_index = lax.axis_index("seq")
    range_index = seq_index // LINE
    flip = lax.rem(range_index, 2)
    place = lax.rem(seq_index, LINE)
    head = jnp.where(flip == 1, HEADS - 1 - place, place)

    def move(x, route):
        return lax.ppermute(x, AXES, route)

    def exchange(x):
        return lax.all_to_all(x, "seq", 0, 0, axis_index_groups=lines)

    flip, range_index, head = flip.reshape(1), range_index.reshape(1), head.reshape(1)
    own = exchange(pack_keys(flip, teacher_key[0], student_key[0]))
    last = move(own, to_next)
    before = move(own[1:], to_second)
    packed, start, low = pack_queries(flip, range_index, teacher_query[0], student_query[0], segment_ids)
    queries = exchange(packed)
    dq, dk_own, dk_last, dk_before = attend(head, low, head_weight, start, queries, own, last, before)

    back_last = move(dk_last, reverse(to_next)).astype(F32)
    back_before = move(dk_before, reverse(to_second)).astype(F32)
    dq_home = exchange(dq)
    total = dk_own + back_last + jnp.pad(back_before, ((1, 0), (0, 0), (0, 0)))
    query_grad, key_grad = unpack(flip, dq_home, exchange(total.astype(BF16)))
    return query_grad[None], key_grad[None]


def solution(mesh):
    seq, dp = mesh.shape["seq"], mesh.shape["dp"]
    spec = P("dp", "seq", None)
    return jax.shard_map(
        functools.partial(per_device, seq, dp),
        mesh=mesh,
        in_specs=(spec, spec, spec, spec, P("dp", None), P()),
        out_specs=(spec, spec),
        check_vma=False,
    )
```

time: 132 us -> 106 us (0.80)
  starting transfers between devices: 52.5 us -> 32 us
  other arithmetic: 12.3 us -> 0.08 us
  blocking collectives: 0 us -> 10.9 us
  Pallas kernels: 17.9 us -> 13.1 us
  waiting for transfers between devices: 43.9 us -> 47.8 us
  local copies, waits for them, and re-layouts: 2.84 us -> 0.72 us
    ppermute x14 -> x4, starting transfers between devices: 52.5 us -> 20.3 us  [move(): return lax.ppermute(x, AXES, route)]
    all_to_all x0 -> x3, waiting for transfers between devices: none -> 18.9 us  [exchange(): return lax.all_to_all(x, 'seq', 0, 0, axis_index_groups=lines)]
    ppermute x14 -> x4, waiting for transfers between devices: 43.9 us -> 29 us  [move(): return lax.ppermute(x, AXES, route)]
    reduce_sum x1 -> x0, other arithmetic: 12.1 us -> none  [per_device(): jnp.sum(seg.reshape(2 * row_tokens, 1, 1) < seg[None, ROW:], axis=0, dtyp...]
    all_to_all x0 -> x3, starting transfers between devices: none -> 11.8 us  [exchange(): return lax.all_to_all(x, 'seq', 0, 0, axis_index_groups=lines)]
    all_to_all x0 -> x1, blocking collectives: none -> 10.9 us  [exchange(): return lax.all_to_all(x, 'seq', 0, 0, axis_index_groups=lines)]
    pallas_call x3, Pallas kernels: 15.8 us -> 11 us  [the longest x1 6.44 us: attend(): pl.pallas_call(main_kernel, out_shape=[jax.ShapeDtypeStruct((LINE, TOK, D...]
    unnamed x21 -> x8, local copies, waits for them, and re-layouts: 2.08 us -> 0.7 us
  transfers between devices with their start and end apart: 14 -> 7, of which waited for: 10 -> 7; matrix products, arithmetic and copies ran while one was open for 10% -> 0% of each run, Pallas kernels for 0% -> 2%
where the time goes in v3:
time: 106 us; the launch traced here: 105 us
  waiting for transfers between devices  47.8 us (45%)
  starting transfers between devices  32 us (30%)
  Pallas kernels  13.1 us (12%)
  blocking collectives  10.9 us (10%)
    ppermute x4, waiting for transfers between devices, move(): return lax.ppermute(x, AXES, route)  29 us
    ppermute x4, starting transfers between devices, move(): return lax.ppermute(x, AXES, route)  20.3 us
    all_to_all x3, waiting for transfers between devices, exchange(): return lax.all_to_all(x, 'seq', 0, 0, axis_index_groups=lines)  18.9 us
    all_to_all x3, starting transfers between devices, exchange(): return lax.all_to_all(x, 'seq', 0, 0, axis_index_groups=lines)  11.8 us
    all_to_all x1, blocking collectives, exchange(): return lax.all_to_all(x, 'seq', 0, 0, axis_index_groups=lines)  10.9 us
    pallas_call x1, Pallas kernels, attend(): pl.pallas_call(main_kernel, out_shape=[jax.ShapeDtypeStruct((LINE, TOK, D...  6.44 us
    pallas_call x1, Pallas kernels, pack_queries(): pl.pallas_call(pack_queries_kernel, out_shape=[jax.ShapeDtypeStruct((HEAD...  2.61 us
  transfers between devices with their start and end apart: 7, of which 7 were waited for; matrix products, arithmetic and copies ran while one was open for 0% of the time, Pallas kernels for 2%

profile of v3, /device:TPU:6, one launch (start us, length us, event | category | flops | bytes accessed | tf_op | source)
XLA Modules:
  0.0 105.4 jit_solution(304703354710066712)
XLA Ops:
  0.7 1.9 %shard_map.78 = bf16[4,2,256,128]{3,2,1,0:T(8,128)(2,1)} custom-call(s32[1]{0:T(128)} %bitcast.flip_ref, bf16[256,512]{1,0:T(8,128)(2,1)} %bitcast.11, bf16[256,512]{1,0:T(8,128)(2,1)} %bitcast.12), custom_call_target="tpu_custom_call" | custom-call | bytes 1048576 | tf_op jit(solution)/shard_map/pallas_call | solution.py:93
  2.6 4.9 %all-to-all-start.1 = ((bf16[4,2,256,128]{3,2,1,0:T(8,128)(2,1)}), bf16[4,2,256,128]{3,2,1,0:T(8,128)(2,1)S(1)}, u32[]{:S(2)}, u32[]{:S(2)}) async-start(bf16[4,2,256,128]{3,2,1,0:T(8,128)(2,1)} %shard_map.78), calls=%async_computation.1 | async-start | bytes 1048576 | tf_op jit(solution)/shard_map/all_to_all | solution.py:279
  7.4 2.6 %shard_map.77 = (bf16[4,2,256,128]{3,2,1,0:T(8,128)(2,1)}, s32[4,256]{1,0:T(4,128)}, s32[4]{0:T(128)}) custom-call(s32[1]{0:T(128)} %bitcast.flip_ref, s32[1]{0:T(128)} %bitcast.2.range_ref, bf16[256,512]{1,0:T(8,128)(2,1)} %bitcast.9, bf16[256,512]{1,0:T(8,128)(2,1)} %bitcast.10, s32[1,32768]{1,0:T(1,128)} %seg_ref.1), custom_call_target="tpu_custom_call" | custom-call | bytes 1048576 | tf_op jit(solution)/shard_map/pallas_call | solution.py:103
  10.1 11.9 %all-to-all-done.1.own_ref = bf16[4,2,256,128]{3,2,1,0:T(8,128)(2,1)S(1)} async-done(((bf16[4,2,256,128]{3,2,1,0:T(8,128)(2,1)}), bf16[4,2,256,128]{3,2,1,0:T(8,128)(2,1)S(1)}, u32[]{:S(2)}, u32[]{:S(2)}) %all-to-all-start.1) | async-done | bytes 524320 | tf_op jit(solution)/shard_map/all_to_all | solution.py:279
  21.9 3.5 %all-to-all-start = ((bf16[4,2,256,128]{3,2,1,0:T(8,128)(2,1)}), bf16[4,2,256,128]{3,2,1,0:T(8,128)(2,1)S(1)}, u32[]{:S(2)}, u32[]{:S(2)}) async-start(bf16[4,2,256,128]{3,2,1,0:T(8,128)(2,1)} %get-tuple-element.13), calls=%async_computation | async-start | bytes 1048576 | tf_op jit(solution)/shard_map/all_to_all | solution.py:279
  25.4 7.1 %collective-permute-start = (bf16[4,2,256,128]{3,2,1,0:T(8,128)(2,1)S(1)}, bf16[4,2,256,128]{3,2,1,0:T(8,128)(2,1)S(1)}, u32[]{:S(2)}, u32[]{:S(2)}) collective-permute-start(bf16[4,2,256,128]{3,2,1,0:T(8,128)(2,1)S(1)} %all-to-all-done.1.own_ref), channel_id=1, source_target_pairs={{0,28},{1,29},{2,30},{3,31},{4,24},{5,25},{6,26},{7,27},{8,20},{9,... | collective-permute-start | bytes 1572872 | tf_op jit(solution)/shard_map/ppermute | solution.py:276
  32.6 4.3 %collective-permute-start.1 = (bf16[3,2,256,128]{3,2,1,0:T(8,128)(2,1)S(1)}, bf16[3,2,256,128]{3,2,1,0:T(8,128)(2,1)S(1)}, u32[]{:S(2)}, u32[]{:S(2)}) collective-permute-start(bf16[3,2,256,128]{3,2,1,0:T(8,128)(2,1)S(1)} %slice.4), channel_id=1, source_target_pairs={{0,32},{1,33},{2,34},{3,35},{4,36},{5,37},{6,38},{7,39},{8,40},{9,... | collective-permute-start | bytes 1179656 | tf_op jit(solution)/shard_map/ppermute | solution.py:276
  36.9 0.0 copy-start
  36.9 2.6 %all-to-all-done.query_ref = bf16[4,2,256,128]{3,2,1,0:T(8,128)(2,1)S(1)} async-done(((bf16[4,2,256,128]{3,2,1,0:T(8,128)(2,1)}), bf16[4,2,256,128]{3,2,1,0:T(8,128)(2,1)S(1)}, u32[]{:S(2)}, u32[]{:S(2)}) %all-to-all-start) | async-done | bytes 524320 | tf_op jit(solution)/shard_map/all_to_all | solution.py:279
  39.5 17.5 %collective-permute-done.1.before_ref = bf16[3,2,256,128]{3,2,1,0:T(8,128)(2,1)S(1)} collective-permute-done((bf16[3,2,256,128]{3,2,1,0:T(8,128)(2,1)S(1)}, bf16[3,2,256,128]{3,2,1,0:T(8,128)(2,1)S(1)}, u32[]{:S(2)}, u32[]{:S(2)}) %collective-permute-start.1) | collective-permute-done | bytes 393248 | tf_op jit(solution)/shard_map/ppermute | solution.py:276
  57.0 7.0 %collective-permute-done.last_ref = bf16[4,2,256,128]{3,2,1,0:T(8,128)(2,1)S(1)} collective-permute-done((bf16[4,2,256,128]{3,2,1,0:T(8,128)(2,1)S(1)}, bf16[4,2,256,128]{3,2,1,0:T(8,128)(2,1)S(1)}, u32[]{:S(2)}, u32[]{:S(2)}) %collective-permute-start) | collective-permute-done | bytes 524320 | tf_op jit(solution)/shard_map/ppermute | solution.py:276
  64.0 0.0 copy-start.1
  64.0 0.0 copy-start.2
  64.0 0.0 copy-done
  64.0 0.6 copy-done.1
  64.6 0.0 copy-done.2
  64.7 6.4 %shard_map.79 = (bf16[4,256,128]{2,1,0:T(8,128)(2,1)}, f32[4,256,128]{2,1,0:T(8,128)S(1)}, bf16[4,256,128]{2,1,0:T(8,128)(2,1)S(1)}, bf16[3,256,128]{2,1,0:T(8,128)(2,1)S(1)}) custom-call(s32[1]{0:T(128)} %bitcast.1.head_ref, s32[4]{0:T(128)S(1)} %copy-done.2, f32[4]{0:T(128)S(1)} %copy-done.1, s32[4,256]{1,0:T(4,128)S(1)} %copy-done, ...), custom_call_target="tpu_custom_call" | custom-call | flops 1000000000 | bytes 6291456 | tf_op jit(solution)/shard_map/pallas_call | solution.py:240
  71.1 4.8 %collective-permute-start.2 = (bf16[4,256,128]{2,1,0:T(8,128)(2,1)S(1)}, bf16[4,256,128]{2,1,0:T(8,128)(2,1)S(1)}, u32[]{:S(2)}, u32[]{:S(2)}) collective-permute-start(bf16[4,256,128]{2,1,0:T(8,128)(2,1)S(1)} %get-tuple-element.16), channel_id=1, source_target_pairs={{28,0},{29,1},{30,2},{31,3},{24,4},{25,5},{26,6},{27,7},{20,8},{21... | collective-permute-start | bytes 786440 | tf_op jit(solution)/shard_map/ppermute | solution.py:276
  75.9 4.1 %collective-permute-start.3 = (bf16[3,256,128]{2,1,0:T(8,128)(2,1)S(1)}, bf16[3,256,128]{2,1,0:T(8,128)(2,1)S(1)}, u32[]{:S(2)}, u32[]{:S(2)}) collective-permute-start(bf16[3,256,128]{2,1,0:T(8,128)(2,1)S(1)} %get-tuple-element.17), channel_id=1, source_target_pairs={{32,0},{33,1},{34,2},{35,3},{36,4},{37,5},{38,6},{39,7},{40,8},{41... | collective-permute-start | bytes 589832 | tf_op jit(solution)/shard_map/ppermute | solution.py:276
  80.0 3.4 %all-to-all-start.2 = ((bf16[4,256,128]{2,1,0:T(8,128)(2,1)}), bf16[4,256,128]{2,1,0:T(8,128)(2,1)S(1)}, u32[]{:S(2)}, u32[]{:S(2)}) async-start(bf16[4,256,128]{2,1,0:T(8,128)(2,1)} %get-tuple-element.14), calls=%async_computation.2 | async-start | bytes 524288 | tf_op jit(solution)/shard_map/all_to_all | solution.py:279
  83.4 1.3 %collective-permute-done.3 = bf16[3,256,128]{2,1,0:T(8,128)(2,1)S(1)} collective-permute-done((bf16[3,256,128]{2,1,0:T(8,128)(2,1)S(1)}, bf16[3,256,128]{2,1,0:T(8,128)(2,1)S(1)}, u32[]{:S(2)}, u32[]{:S(2)}) %collective-permute-start.3) | collective-permute-done | bytes 196640 | tf_op jit(solution)/shard_map/ppermute | solution.py:276
  84.8 3.2 %collective-permute-done.2 = bf16[4,256,128]{2,1,0:T(8,128)(2,1)S(1)} collective-permute-done((bf16[4,256,128]{2,1,0:T(8,128)(2,1)S(1)}, bf16[4,256,128]{2,1,0:T(8,128)(2,1)S(1)}, u32[]{:S(2)}, u32[]{:S(2)}) %collective-permute-start.2) | collective-permute-done | bytes 262176 | tf_op jit(solution)/shard_map/ppermute | solution.py:276
  87.9 0.1 add_convert_fusion
  88.0 4.4 %all-to-all-done.2.dq_ref = bf16[4,256,128]{2,1,0:T(8,128)(2,1)S(1)} async-done(((bf16[4,256,128]{2,1,0:T(8,128)(2,1)}), bf16[4,256,128]{2,1,0:T(8,128)(2,1)S(1)}, u32[]{:S(2)}, u32[]{:S(2)}) %all-to-all-start.2) | async-done | bytes 262176 | tf_op jit(solution)/shard_map/all_to_all | solution.py:279
  92.4 0.0 copy-start.3
  92.4 10.9 %all_to_all.20.dk_ref = bf16[4,256,128]{2,1,0:T(8,128)(2,1)} all-to-all(bf16[4,256,128]{2,1,0:T(8,128)(2,1)S(1)} %add_convert_fusion), channel_id=1, replica_groups={{0,4,8,12},{16,20,24,28},{32,36,40,44},{48,52,56,60},{64,68,72,76},{80,..., dimensions={0} | all-to-all | bytes 524288 | tf_op jit(solution)/shard_map/all_to_all | solution.py:279
  103.2 0.0 copy-done.3
  103.2 2.1 %shard_map.80 = (f32[256,512]{1,0:T(8,128)}, f32[256,512]{1,0:T(8,128)}) custom-call(s32[1]{0:T(128)} %bitcast.flip_ref, bf16[4,256,128]{2,1,0:T(8,128)(2,1)} %copy-done.3, bf16[4,256,128]{2,1,0:T(8,128)(2,1)} %all_to_all.20.dk_ref), custom_call_target="tpu_custom_call" | custom-call | bytes 1572864 | tf_op jit(solution)/shard_map/pallas_call | solution.py:124
  (1 shorter events, 0.0 us)
Async XLA Ops:
  2.6 19.4 %all-to-all-start.1 = ((bf16[4,2,256,128]{3,2,1,0:T(8,128)(2,1)}), bf16[4,2,256,128]{3,2,1,0:T(8,128)(2,1)S(1)}, u32[]{:S(2)}, u32[]{:S(2)}) async-start(bf16[4,2,256,128]{3,2,1,0:T(8,128)(2,1)} %shard_map.78), calls=%async_computation.1 | async-start | bytes 1048576 | tf_op jit(solution)/shard_map/all_to_all | solution.py:279
  21.9 17.5 %all-to-all-start = ((bf16[4,2,256,128]{3,2,1,0:T(8,128)(2,1)}), bf16[4,2,256,128]{3,2,1,0:T(8,128)(2,1)S(1)}, u32[]{:S(2)}, u32[]{:S(2)}) async-start(bf16[4,2,256,128]{3,2,1,0:T(8,128)(2,1)} %get-tuple-element.13), calls=%async_computation | async-start | bytes 1048576 | tf_op jit(solution)/shard_map/all_to_all | solution.py:279
  25.4 38.5 %collective-permute-start = (bf16[4,2,256,128]{3,2,1,0:T(8,128)(2,1)S(1)}, bf16[4,2,256,128]{3,2,1,0:T(8,128)(2,1)S(1)}, u32[]{:S(2)}, u32[]{:S(2)}) collective-permute-start(bf16[4,2,256,128]{3,2,1,0:T(8,128)(2,1)S(1)} %all-to-all-done.1.own_ref), channel_id=1, source_target_pairs={{0,28},{1,29},{2,30},{3,31},{4,24},{5,25},{6,26},{7,27},{8,20},{9,... | collective-permute-start | bytes 1572872 | tf_op jit(solution)/shard_map/ppermute | solution.py:276
  32.6 24.4 %collective-permute-start.1 = (bf16[3,2,256,128]{3,2,1,0:T(8,128)(2,1)S(1)}, bf16[3,2,256,128]{3,2,1,0:T(8,128)(2,1)S(1)}, u32[]{:S(2)}, u32[]{:S(2)}) collective-permute-start(bf16[3,2,256,128]{3,2,1,0:T(8,128)(2,1)S(1)} %slice.4), channel_id=1, source_target_pairs={{0,32},{1,33},{2,34},{3,35},{4,36},{5,37},{6,38},{7,39},{8,40},{9,... | collective-permute-start | bytes 1179656 | tf_op jit(solution)/shard_map/ppermute | solution.py:276
  36.9 27.1 %copy-start = (s32[4,256]{1,0:T(4,128)S(1)}, s32[4,256]{1,0:T(4,128)}, u32[]{:S(2)}) copy-start(s32[4,256]{1,0:T(4,128)} %get-tuple-element.12.start_ref) | copy-start | bytes 12292
  64.0 0.7 copy-start.1
  64.0 0.7 copy-start.2
  71.1 16.8 %collective-permute-start.2 = (bf16[4,256,128]{2,1,0:T(8,128)(2,1)S(1)}, bf16[4,256,128]{2,1,0:T(8,128)(2,1)S(1)}, u32[]{:S(2)}, u32[]{:S(2)}) collective-permute-start(bf16[4,256,128]{2,1,0:T(8,128)(2,1)S(1)} %get-tuple-element.16), channel_id=1, source_target_pairs={{28,0},{29,1},{30,2},{31,3},{24,4},{25,5},{26,6},{27,7},{20,8},{21... | collective-permute-start | bytes 786440 | tf_op jit(solution)/shard_map/ppermute | solution.py:276
  75.9 8.8 %collective-permute-start.3 = (bf16[3,256,128]{2,1,0:T(8,128)(2,1)S(1)}, bf16[3,256,128]{2,1,0:T(8,128)(2,1)S(1)}, u32[]{:S(2)}, u32[]{:S(2)}) collective-permute-start(bf16[3,256,128]{2,1,0:T(8,128)(2,1)S(1)} %get-tuple-element.17), channel_id=1, source_target_pairs={{32,0},{33,1},{34,2},{35,3},{36,4},{37,5},{38,6},{39,7},{40,8},{41... | collective-permute-start | bytes 589832 | tf_op jit(solution)/shard_map/ppermute | solution.py:276
  80.0 12.4 %all-to-all-start.2 = ((bf16[4,256,128]{2,1,0:T(8,128)(2,1)}), bf16[4,256,128]{2,1,0:T(8,128)(2,1)S(1)}, u32[]{:S(2)}, u32[]{:S(2)}) async-start(bf16[4,256,128]{2,1,0:T(8,128)(2,1)} %get-tuple-element.14), calls=%async_computation.2 | async-start | bytes 524288 | tf_op jit(solution)/shard_map/all_to_all | solution.py:279
  92.4 10.9 %copy-start.3 = (bf16[4,256,128]{2,1,0:T(8,128)(2,1)}, bf16[4,256,128]{2,1,0:T(8,128)(2,1)S(1)}, u32[]{:S(2)}) copy-start(bf16[4,256,128]{2,1,0:T(8,128)(2,1)S(1)} %all-to-all-done.2.dq_ref) | copy-start | bytes 786436

commit v4 on v3

--- a/solution.py
+++ b/solution.py
@@ -48,15 +48,18 @@
     return pl.ds(pl.multiple_of(head * DIM, DIM), DIM)
 
 
-def pack_keys_kernel(flip_ref, a_ref, b_ref, out_ref):
+def pack_keys_kernel(flip_ref, a_ref, b_ref, a_out_ref, b_out_ref):
+    for place in range(HEADS):
+        columns = head_columns(flip_ref[0], place)
+        a_out_ref[place] = a_ref[:, columns]
+        b_out_ref[place] = b_ref[:, columns]
+
+
+def pack_queries_kernel(flip_ref, range_ref, a_ref, b_ref, seg_ref, out_ref, start_ref, low_ref):
     for place in range(HEADS):
         columns = head_columns(flip_ref[0], place)
         out_ref[place, 0] = a_ref[:, columns]
         out_ref[place, 1] = b_ref[:, columns]
-
-
-def pack_queries_kernel(flip_ref, range_ref, a_ref, b_ref, seg_ref, out_ref, start_ref, low_ref):
-    pack_keys_kernel(flip_ref, a_ref, b_ref, out_ref)
     first_block = range_ref[0] * LINE
 
     def ids(block):
@@ -92,9 +95,9 @@
 def pack_keys(flip, a, b):
     return pl.pallas_call(
         pack_keys_kernel,
-        out_shape=jax.ShapeDtypeStruct((HEADS, 2, TOK, DIM), BF16),
+        out_shape=[jax.ShapeDtypeStruct((HEADS, TOK, DIM), BF16)] * 2,
         in_specs=[SMEM, VMEM, VMEM],
-        out_specs=VMEM,
+        out_specs=[VMEM] * 2,
         cost_estimate=pl.CostEstimate(flops=0, bytes_accessed=2**20, transcendentals=0),
     )(flip, a, b)
 
@@ -131,7 +134,7 @@
 
 
 def main_kernel(
-    head_ref, low_ref, weight_ref, start_ref, query_ref, own_ref, last_ref, before_ref,
+    head_ref, low_ref, weight_ref, start_ref, query_ref, own_t_ref, own_s_ref, last_t_ref, last_s_ref, before_ref,
     dq_ref, dk_own_ref, dk_last_ref, dk_before_ref,
     kt, ks, ks_turned, dk, et, es, top_t, top_s, dq_acc,
 ):
@@ -144,10 +147,10 @@
     def rows(block):
         return pl.ds(block * TOK, TOK)
 
-    def load(block, ref, index):
-        kt[rows(block), :] = ref[index, 0]
-        ks[rows(block), :] = ref[index, 1]
-        ks_turned[:, rows(block)] = ref[index, 1].T
+    def load(block, teacher, student):
+        kt[rows(block), :] = teacher
+        ks[rows(block), :] = student
+        ks_turned[:, rows(block)] = student.T
         dk[rows(block), :] = jnp.zeros((TOK, DIM), F32)
 
     def clear(block):
@@ -157,12 +160,12 @@
         dk[rows(block), :] = jnp.zeros((TOK, DIM), F32)
 
     for i in range(LINE):
-        load(OWN + i, own_ref, i)
+        load(OWN + i, own_t_ref[i], own_s_ref[i])
 
     @pl.when(lowest <= OWN)
     def _():
         for i in range(LINE):
-            load(LINE + i, last_ref, i)
+            load(LINE + i, last_t_ref[i], last_s_ref[i])
 
     @pl.when(lowest > OWN)
     def _():
@@ -172,7 +175,7 @@
     @pl.when(lowest <= LINE)
     def _():
         for i in range(LINE - 1):
-            load(1 + i, before_ref, i)
+            load(1 + i, before_ref[0, i], before_ref[1, i])
 
     @pl.when(lowest > LINE)
     def _():
@@ -236,7 +239,7 @@
         dk_before_ref[i] = (dk[rows(1 + i), :] * scale).astype(BF16)
 
 
-def attend(head, low, weight, start, queries, own, last, before):
+def attend(head, low, weight, start, queries, *keys):
     return pl.pallas_call(
         main_kernel,
         out_shape=[
@@ -245,7 +248,7 @@
             jax.ShapeDtypeStruct((LINE, TOK, DIM), BF16),
             jax.ShapeDtypeStruct((LINE - 1, TOK, DIM), BF16),
         ],
-        in_specs=[SMEM] * 3 + [VMEM] * 5,
+        in_specs=[SMEM] * 3 + [VMEM] * 7,
         out_specs=[VMEM] * 4,
         scratch_shapes=[
             pltpu.VMEM((BAND * TOK, DIM), BF16),
@@ -260,7 +263,7 @@
         ],
         compiler_params=pltpu.CompilerParams(vmem_limit_bytes=32 * 1024 * 1024),
         cost_estimate=pl.CostEstimate(flops=10**9, bytes_accessed=6 * 2**20, transcendentals=4 * 10**6),
-    )(head, low, weight, start, queries, own, last, before)
+    )(head, low, weight, start, queries, *keys)
 
 
 def per_device(seq, dp, teacher_query, teacher_key, student_query, student_key, segment_ids, head_weight):
@@ -279,12 +282,15 @@
         return lax.all_to_all(x, "seq", 0, 0, axis_index_groups=lines)
 
     flip, range_index, head = flip.reshape(1), range_index.reshape(1), head.reshape(1)
-    own = exchange(pack_keys(flip, teacher_key[0], student_key[0]))
-    last = move(own, to_next)
-    before = move(own[1:], to_second)
+    own_t, own_s = [exchange(x) for x in pack_keys(flip, teacher_key[0], student_key[0])]
+    last_t, last_s = move(own_t, to_next), move(own_s, to_next)
+    before = move(jnp.stack([own_t[1:], own_s[1:]]), to_second)
+    teacher_query, own_s = lax.optimization_barrier((teacher_query, own_s))
     packed, start, low = pack_queries(flip, range_index, teacher_query[0], student_query[0], segment_ids)
     queries = exchange(packed)
-    dq, dk_own, dk_last, dk_before = attend(head, low, head_weight, start, queries, own, last, before)
+    dq, dk_own, dk_last, dk_before = attend(
+        head, low, head_weight, start, queries, own_t, own_s, last_t, last_s, before
+    )
 
     back_last = move(dk_last, reverse(to_next)).astype(F32)
     back_before = move(dk_before, reverse(to_second)).astype(F32)

time: 106 us -> 114 us (1.075)
  the two profiles are of different devices: /device:TPU:6 before, /device:TPU:4 now
where the time goes in v4:
time: 114 us
  waiting for transfers between devices  40 us (35%)
  starting transfers between devices  29.7 us (26%)
  blocking collectives  26.2 us (23%)
  Pallas kernels  16.3 us (14%)
    ppermute x5, waiting for transfers between devices, move(): return lax.ppermute(x, AXES, route)  26.2 us
    all_to_all x2, blocking collectives, exchange(): return lax.all_to_all(x, 'seq', 0, 0, axis_index_groups=lines)  26.2 us
    ppermute x5, starting transfers between devices, move(): return lax.ppermute(x, AXES, route)  19.4 us
    all_to_all x3, waiting for transfers between devices, exchange(): return lax.all_to_all(x, 'seq', 0, 0, axis_index_groups=lines)  13.8 us
    all_to_all x3, starting transfers between devices, exchange(): return lax.all_to_all(x, 'seq', 0, 0, axis_index_groups=lines)  10.3 us
    pallas_call x1, Pallas kernels, attend(): pl.pallas_call(main_kernel, out_shape=[jax.ShapeDtypeStruct((LINE, TOK, D...  9.61 us
    pallas_call x1, Pallas kernels, pack_queries(): pl.pallas_call(pack_queries_kernel, out_shape=[jax.ShapeDtypeStruct((HEAD...  2.61 us
  transfers between devices with their start and end apart: 8, of which 5 were waited for; matrix products, arithmetic and copies ran while one was open for 0% of the time, Pallas kernels for 2%

profile of v4, /device:TPU:4, one launch (start us, length us, event | category | flops | bytes accessed | tf_op | source)
XLA Modules:
  0.0 113.7 jit_solution(14640676100937625484)
XLA Ops:
  0.7 1.9 %shard_map.77 = (bf16[4,256,128]{2,1,0:T(8,128)(2,1)}, bf16[4,256,128]{2,1,0:T(8,128)(2,1)}) custom-call(s32[1]{0:T(128)} %bitcast.flip_ref, bf16[256,512]{1,0:T(8,128)(2,1)} %bitcast.15, bf16[256,512]{1,0:T(8,128)(2,1)} %bitcast.16), custom_call_target="tpu_custom_call" | custom-call | bytes 1048576 | tf_op jit(solution)/shard_map/pallas_call | solution.py:96
  2.6 13.7 %all_to_all.25.own_s_ref = bf16[4,256,128]{2,1,0:T(8,128)(2,1)S(1)} all-to-all(bf16[4,256,128]{2,1,0:T(8,128)(2,1)} %get-tuple-element.15), channel_id=1, replica_groups={{0,4,8,12},{16,20,24,28},{32,36,40,44},{48,52,56,60},{64,68,72,76},{80,..., dimensions={0} | all-to-all | bytes 524288 | tf_op jit(solution)/shard_map/all_to_all | solution.py:282
  16.3 3.4 %all-to-all-start.2 = ((bf16[4,256,128]{2,1,0:T(8,128)(2,1)}), bf16[4,256,128]{2,1,0:T(8,128)(2,1)S(1)}, u32[]{:S(2)}, u32[]{:S(2)}) async-start(bf16[4,256,128]{2,1,0:T(8,128)(2,1)} %get-tuple-element.20), calls=%async_computation.2 | async-start | bytes 524288 | tf_op jit(solution)/shard_map/all_to_all | solution.py:282
  19.7 2.6 %shard_map.78 = (bf16[4,2,256,128]{3,2,1,0:T(8,128)(2,1)}, s32[4,256]{1,0:T(4,128)}, s32[4]{0:T(128)}) custom-call(s32[1]{0:T(128)} %bitcast.flip_ref, s32[1]{0:T(128)} %bitcast.2.range_ref, bf16[256,512]{1,0:T(8,128)(2,1)} %bitcast.13, bf16[256,512]{1,0:T(8,128)(2,1)} %bitcast.14, s32[1,32768]{1,0:T(1,128)} %seg_ref.1), custom_call_target="tpu_custom_call" | custom-call | bytes 1048576 | tf_op jit(solution)/shard_map/pallas_call | solution.py:106
  22.3 5.3 %all-to-all-done.2.own_t_ref = bf16[4,256,128]{2,1,0:T(8,128)(2,1)S(1)} async-done(((bf16[4,256,128]{2,1,0:T(8,128)(2,1)}), bf16[4,256,128]{2,1,0:T(8,128)(2,1)S(1)}, u32[]{:S(2)}, u32[]{:S(2)}) %all-to-all-start.2) | async-done | bytes 262176 | tf_op jit(solution)/shard_map/all_to_all | solution.py:282
  27.6 3.5 %all-to-all-start.1 = ((bf16[4,2,256,128]{3,2,1,0:T(8,128)(2,1)}), bf16[4,2,256,128]{3,2,1,0:T(8,128)(2,1)S(1)}, u32[]{:S(2)}, u32[]{:S(2)}) async-start(bf16[4,2,256,128]{3,2,1,0:T(8,128)(2,1)} %get-tuple-element.19), calls=%async_computation.1 | async-start | bytes 1048576 | tf_op jit(solution)/shard_map/all_to_all | solution.py:282
  31.2 4.3 %collective-permute-start.2 = (bf16[2,3,256,128]{3,2,1,0:T(8,128)(2,1)S(1)}, bf16[2,3,256,128]{3,2,1,0:T(8,128)(2,1)S(1)}, u32[]{:S(2)}, u32[]{:S(2)}) collective-permute-start(bf16[2,3,256,128]{3,2,1,0:T(8,128)(2,1)S(1)} %pad_maximum_fusion), channel_id=1, source_target_pairs={{0,32},{1,33},{2,34},{3,35},{4,36},{5,37},{6,38},{7,39},{8,40},{9,... | collective-permute-start | bytes 1179656 | tf_op jit(solution)/shard_map/ppermute | solution.py:279
  35.5 7.0 %collective-permute-start = (bf16[4,256,128]{2,1,0:T(8,128)(2,1)S(1)}, bf16[4,256,128]{2,1,0:T(8,128)(2,1)S(1)}, u32[]{:S(2)}, u32[]{:S(2)}) collective-permute-start(bf16[4,256,128]{2,1,0:T(8,128)(2,1)S(1)} %all-to-all-done.2.own_t_ref), channel_id=1, source_target_pairs={{0,28},{1,29},{2,30},{3,31},{4,24},{5,25},{6,26},{7,27},{8,20},{9,... | collective-permute-start | bytes 786440 | tf_op jit(solution)/shard_map/ppermute | solution.py:279
  42.5 1.9 %collective-permute-start.1 = (bf16[4,256,128]{2,1,0:T(8,128)(2,1)S(1)}, bf16[4,256,128]{2,1,0:T(8,128)(2,1)S(1)}, u32[]{:S(2)}, u32[]{:S(2)}) collective-permute-start(bf16[4,256,128]{2,1,0:T(8,128)(2,1)S(1)} %all_to_all.25.own_s_ref), channel_id=1, source_target_pairs={{0,28},{1,29},{2,30},{3,31},{4,24},{5,25},{6,26},{7,27},{8,20},{9,... | collective-permute-start | bytes 786440 | tf_op jit(solution)/shard_map/ppermute | solution.py:279
  44.5 0.0 copy-start
  44.5 21.8 %collective-permute-done.last_t_ref = bf16[4,256,128]{2,1,0:T(8,128)(2,1)S(1)} collective-permute-done((bf16[4,256,128]{2,1,0:T(8,128)(2,1)S(1)}, bf16[4,256,128]{2,1,0:T(8,128)(2,1)S(1)}, u32[]{:S(2)}, u32[]{:S(2)}) %collective-permute-start) | collective-permute-done | bytes 262176 | tf_op jit(solution)/shard_map/ppermute | solution.py:279
  66.3 2.8 %collective-permute-done.1.last_s_ref = bf16[4,256,128]{2,1,0:T(8,128)(2,1)S(1)} collective-permute-done((bf16[4,256,128]{2,1,0:T(8,128)(2,1)S(1)}, bf16[4,256,128]{2,1,0:T(8,128)(2,1)S(1)}, u32[]{:S(2)}, u32[]{:S(2)}) %collective-permute-start.1) | collective-permute-done | bytes 262176 | tf_op jit(solution)/shard_map/ppermute | solution.py:279
  69.1 0.0 collective-permute-done.2.before_ref
  69.1 0.0 all-to-all-done.1.query_ref
  69.1 0.0 copy-start.1
  69.1 0.0 copy-start.2
  69.1 0.0 copy-done
  69.1 0.6 copy-done.1
  69.7 0.0 copy-done.2
  69.7 9.6 %shard_map.79 = (bf16[4,256,128]{2,1,0:T(8,128)(2,1)}, f32[4,256,128]{2,1,0:T(8,128)S(1)}, bf16[4,256,128]{2,1,0:T(8,128)(2,1)S(1)}, bf16[3,256,128]{2,1,0:T(8,128)(2,1)S(1)}) custom-call(s32[1]{0:T(128)} %bitcast.1.head_ref, s32[4]{0:T(128)S(1)} %copy-done.2, f32[4]{0:T(128)S(1)} %copy-done.1, s32[4,256]{1,0:T(4,128)S(1)} %copy-done, ...), custom_call_target="tpu_custom_call" | custom-call | flops 1000000000 | bytes 6291456 | tf_op jit(solution)/shard_map/pallas_call | solution.py:243
  79.4 1.9 %collective-permute-start.3 = (bf16[4,256,128]{2,1,0:T(8,128)(2,1)S(1)}, bf16[4,256,128]{2,1,0:T(8,128)(2,1)S(1)}, u32[]{:S(2)}, u32[]{:S(2)}) collective-permute-start(bf16[4,256,128]{2,1,0:T(8,128)(2,1)S(1)} %get-tuple-element.24), channel_id=1, source_target_pairs={{28,0},{29,1},{30,2},{31,3},{24,4},{25,5},{26,6},{27,7},{20,8},{21... | collective-permute-start | bytes 786440 | tf_op jit(solution)/shard_map/ppermute | solution.py:279
  81.3 4.3 %collective-permute-start.4 = (bf16[3,256,128]{2,1,0:T(8,128)(2,1)S(1)}, bf16[3,256,128]{2,1,0:T(8,128)(2,1)S(1)}, u32[]{:S(2)}, u32[]{:S(2)}) collective-permute-start(bf16[3,256,128]{2,1,0:T(8,128)(2,1)S(1)} %get-tuple-element.25), channel_id=1, source_target_pairs={{32,0},{33,1},{34,2},{35,3},{36,4},{37,5},{38,6},{39,7},{40,8},{41... | collective-permute-start | bytes 589832 | tf_op jit(solution)/shard_map/ppermute | solution.py:279
  85.5 3.4 %all-to-all-start.3 = ((bf16[4,256,128]{2,1,0:T(8,128)(2,1)}), bf16[4,256,128]{2,1,0:T(8,128)(2,1)S(1)}, u32[]{:S(2)}, u32[]{:S(2)}) async-start(bf16[4,256,128]{2,1,0:T(8,128)(2,1)} %get-tuple-element.22), calls=%async_computation.3 | async-start | bytes 524288 | tf_op jit(solution)/shard_map/all_to_all | solution.py:282
  89.0 1.6 %collective-permute-done.4 = bf16[3,256,128]{2,1,0:T(8,128)(2,1)S(1)} collective-permute-done((bf16[3,256,128]{2,1,0:T(8,128)(2,1)S(1)}, bf16[3,256,128]{2,1,0:T(8,128)(2,1)S(1)}, u32[]{:S(2)}, u32[]{:S(2)}) %collective-permute-start.4) | collective-permute-done | bytes 196640 | tf_op jit(solution)/shard_map/ppermute | solution.py:279
  90.6 0.0 collective-permute-done.3
  90.6 0.1 add_convert_fusion
  90.7 8.5 %all-to-all-done.3.dq_ref = bf16[4,256,128]{2,1,0:T(8,128)(2,1)S(1)} async-done(((bf16[4,256,128]{2,1,0:T(8,128)(2,1)}), bf16[4,256,128]{2,1,0:T(8,128)(2,1)S(1)}, u32[]{:S(2)}, u32[]{:S(2)}) %all-to-all-start.3) | async-done | bytes 262176 | tf_op jit(solution)/shard_map/all_to_all | solution.py:282
  99.2 0.0 copy-start.3
  99.2 12.4 %all_to_all.26.dk_ref = bf16[4,256,128]{2,1,0:T(8,128)(2,1)} all-to-all(bf16[4,256,128]{2,1,0:T(8,128)(2,1)S(1)} %add_convert_fusion), channel_id=1, replica_groups={{0,4,8,12},{16,20,24,28},{32,36,40,44},{48,52,56,60},{64,68,72,76},{80,..., dimensions={0} | all-to-all | bytes 524288 | tf_op jit(solution)/shard_map/all_to_all | solution.py:282
  111.6 0.0 copy-done.3
  111.6 2.1 %shard_map.80 = (f32[256,512]{1,0:T(8,128)}, f32[256,512]{1,0:T(8,128)}) custom-call(s32[1]{0:T(128)} %bitcast.flip_ref, bf16[4,256,128]{2,1,0:T(8,128)(2,1)} %copy-done.3, bf16[4,256,128]{2,1,0:T(8,128)(2,1)} %all_to_all.26.dk_ref), custom_call_target="tpu_custom_call" | custom-call | bytes 1572864 | tf_op jit(solution)/shard_map/pallas_call | solution.py:127
  (3 shorter events, 0.1 us)
Async XLA Ops:
  16.3 11.3 %all-to-all-start.2 = ((bf16[4,256,128]{2,1,0:T(8,128)(2,1)}), bf16[4,256,128]{2,1,0:T(8,128)(2,1)S(1)}, u32[]{:S(2)}, u32[]{:S(2)}) async-start(bf16[4,256,128]{2,1,0:T(8,128)(2,1)} %get-tuple-element.20), calls=%async_computation.2 | async-start | bytes 524288 | tf_op jit(solution)/shard_map/all_to_all | solution.py:282
  27.6 41.4 %all-to-all-start.1 = ((bf16[4,2,256,128]{3,2,1,0:T(8,128)(2,1)}), bf16[4,2,256,128]{3,2,1,0:T(8,128)(2,1)S(1)}, u32[]{:S(2)}, u32[]{:S(2)}) async-start(bf16[4,2,256,128]{3,2,1,0:T(8,128)(2,1)} %get-tuple-element.19), calls=%async_computation.1 | async-start | bytes 1048576 | tf_op jit(solution)/shard_map/all_to_all | solution.py:282
  31.2 37.9 %collective-permute-start.2 = (bf16[2,3,256,128]{3,2,1,0:T(8,128)(2,1)S(1)}, bf16[2,3,256,128]{3,2,1,0:T(8,128)(2,1)S(1)}, u32[]{:S(2)}, u32[]{:S(2)}) collective-permute-start(bf16[2,3,256,128]{3,2,1,0:T(8,128)(2,1)S(1)} %pad_maximum_fusion), channel_id=1, source_target_pairs={{0,32},{1,33},{2,34},{3,35},{4,36},{5,37},{6,38},{7,39},{8,40},{9,... | collective-permute-start | bytes 1179656 | tf_op jit(solution)/shard_map/ppermute | solution.py:279
  35.5 30.8 %collective-permute-start = (bf16[4,256,128]{2,1,0:T(8,128)(2,1)S(1)}, bf16[4,256,128]{2,1,0:T(8,128)(2,1)S(1)}, u32[]{:S(2)}, u32[]{:S(2)}) collective-permute-start(bf16[4,256,128]{2,1,0:T(8,128)(2,1)S(1)} %all-to-all-done.2.own_t_ref), channel_id=1, source_target_pairs={{0,28},{1,29},{2,30},{3,31},{4,24},{5,25},{6,26},{7,27},{8,20},{9,... | collective-permute-start | bytes 786440 | tf_op jit(solution)/shard_map/ppermute | solution.py:279
  42.5 26.5 %collective-permute-start.1 = (bf16[4,256,128]{2,1,0:T(8,128)(2,1)S(1)}, bf16[4,256,128]{2,1,0:T(8,128)(2,1)S(1)}, u32[]{:S(2)}, u32[]{:S(2)}) collective-permute-start(bf16[4,256,128]{2,1,0:T(8,128)(2,1)S(1)} %all_to_all.25.own_s_ref), channel_id=1, source_target_pairs={{0,28},{1,29},{2,30},{3,31},{4,24},{5,25},{6,26},{7,27},{8,20},{9,... | collective-permute-start | bytes 786440 | tf_op jit(solution)/shard_map/ppermute | solution.py:279
  44.5 24.6 %copy-start = (s32[4,256]{1,0:T(4,128)S(1)}, s32[4,256]{1,0:T(4,128)}, u32[]{:S(2)}) copy-start(s32[4,256]{1,0:T(4,128)} %get-tuple-element.18.start_ref) | copy-start | bytes 12292
  69.1 0.7 copy-start.1
  69.1 0.7 copy-start.2
  79.4 11.2 %collective-permute-start.3 = (bf16[4,256,128]{2,1,0:T(8,128)(2,1)S(1)}, bf16[4,256,128]{2,1,0:T(8,128)(2,1)S(1)}, u32[]{:S(2)}, u32[]{:S(2)}) collective-permute-start(bf16[4,256,128]{2,1,0:T(8,128)(2,1)S(1)} %get-tuple-element.24), channel_id=1, source_target_pairs={{28,0},{29,1},{30,2},{31,3},{24,4},{25,5},{26,6},{27,7},{20,8},{21... | collective-permute-start | bytes 786440 | tf_op jit(solution)/shard_map/ppermute | solution.py:279
  81.3 9.3 %collective-permute-start.4 = (bf16[3,256,128]{2,1,0:T(8,128)(2,1)S(1)}, bf16[3,256,128]{2,1,0:T(8,128)(2,1)S(1)}, u32[]{:S(2)}, u32[]{:S(2)}) collective-permute-start(bf16[3,256,128]{2,1,0:T(8,128)(2,1)S(1)} %get-tuple-element.25), channel_id=1, source_target_pairs={{32,0},{33,1},{34,2},{35,3},{36,4},{37,5},{38,6},{39,7},{40,8},{41... | collective-permute-start | bytes 589832 | tf_op jit(solution)/shard_map/ppermute | solution.py:279
  85.5 13.6 %all-to-all-start.3 = ((bf16[4,256,128]{2,1,0:T(8,128)(2,1)}), bf16[4,256,128]{2,1,0:T(8,128)(2,1)S(1)}, u32[]{:S(2)}, u32[]{:S(2)}) async-start(bf16[4,256,128]{2,1,0:T(8,128)(2,1)} %get-tuple-element.22), calls=%async_computation.3 | async-start | bytes 524288 | tf_op jit(solution)/shard_map/all_to_all | solution.py:282
  99.2 12.4 %copy-start.3 = (bf16[4,256,128]{2,1,0:T(8,128)(2,1)}, bf16[4,256,128]{2,1,0:T(8,128)(2,1)S(1)}, u32[]{:S(2)}) copy-start(bf16[4,256,128]{2,1,0:T(8,128)(2,1)S(1)} %all-to-all-done.3.dq_ref) | copy-start | bytes 786436

commit v5 on v3

--- a/solution.py
+++ b/solution.py
@@ -130,55 +130,50 @@
     )(flip, dq, dk)
 
 
+def layout_kernel(own_ref, last_ref, before_ref, kt, ks, ks_turned):
+    def load(block, teacher, student):
+        here = pl.ds(block * TOK, TOK)
+        kt[here, :] = teacher
+        ks[here, :] = student
+        ks_turned[:, here] = student.T
+
+    load(0, jnp.zeros((TOK, DIM), BF16), jnp.zeros((TOK, DIM), BF16))
+    for i in range(LINE - 1):
+        load(1 + i, before_ref[i, 0], before_ref[i, 1])
+    for i in range(LINE):
+        load(LINE + i, last_ref[i, 0], last_ref[i, 1])
+        load(OWN + i, own_ref[i, 0], own_ref[i, 1])
+
+
+def layout(own, last, before):
+    return pl.pallas_call(
+        layout_kernel,
+        out_shape=[
+            jax.ShapeDtypeStruct((BAND * TOK, DIM), BF16),
+            jax.ShapeDtypeStruct((BAND * TOK, DIM), BF16),
+            jax.ShapeDtypeStruct((DIM, BAND * TOK), BF16),
+        ],
+        in_specs=[VMEM] * 3,
+        out_specs=[VMEM] * 3,
+        compiler_params=pltpu.CompilerParams(vmem_limit_bytes=6 * 1024 * 1024),
+        cost_estimate=pl.CostEstimate(flops=10**10, bytes_accessed=16 * 2**20, transcendentals=0),
+    )(own, last, before)
+
+
 def main_kernel(
-    head_ref, low_ref, weight_ref, start_ref, query_ref, own_ref, last_ref, before_ref,
+    head_ref, low_ref, weight_ref, start_ref, query_ref, kt, ks, ks_turned,
     dq_ref, dk_own_ref, dk_last_ref, dk_before_ref,
-    kt, ks, ks_turned, dk, et, es, top_t, top_s, dq_acc,
+    dk, et, es, top_t, top_s, dq_acc,
 ):
     weight = weight_ref[head_ref[0]]
     scale = 1.0 / math.sqrt(DIM)
     pace = scale * math.log2(math.e)
     along_depth = (((1,), (1,)), ((), ()))
-    lowest = low_ref[0] // TOK
 
     def rows(block):
         return pl.ds(block * TOK, TOK)
 
-    def load(block, ref, index):
-        kt[rows(block), :] = ref[index, 0]
-        ks[rows(block), :] = ref[index, 1]
-        ks_turned[:, rows(block)] = ref[index, 1].T
-        dk[rows(block), :] = jnp.zeros((TOK, DIM), F32)
-
-    def clear(block):
-        kt[rows(block), :] = jnp.zeros((TOK, DIM), BF16)
-        ks[rows(block), :] = jnp.zeros((TOK, DIM), BF16)
-        ks_turned[:, rows(block)] = jnp.zeros((DIM, TOK), BF16)
-        dk[rows(block), :] = jnp.zeros((TOK, DIM), F32)
-
-    for i in range(LINE):
-        load(OWN + i, own_ref, i)
-
-    @pl.when(lowest <= OWN)
-    def _():
-        for i in range(LINE):
-            load(LINE + i, last_ref, i)
-
-    @pl.when(lowest > OWN)
-    def _():
-        for i in range(LINE):
-            clear(LINE + i)
-
-    @pl.when(lowest <= LINE)
-    def _():
-        for i in range(LINE - 1):
-            load(1 + i, before_ref, i)
-
-    @pl.when(lowest > LINE)
-    def _():
-        for i in range(LINE - 1):
-            clear(1 + i)
-
+    dk[...] = jnp.zeros((BAND * TOK, DIM), F32)
     key_row = lax.broadcasted_iota(jnp.int32, (PAIR, TOK), 0)
     query_column = lax.broadcasted_iota(jnp.int32, (PAIR, TOK), 1)
 
@@ -236,7 +231,7 @@
         dk_before_ref[i] = (dk[rows(1 + i), :] * scale).astype(BF16)
 
 
-def attend(head, low, weight, start, queries, own, last, before):
+def attend(head, low, weight, start, queries, *keys):
     return pl.pallas_call(
         main_kernel,
         out_shape=[
@@ -248,9 +243,6 @@
         in_specs=[SMEM] * 3 + [VMEM] * 5,
         out_specs=[VMEM] * 4,
         scratch_shapes=[
-            pltpu.VMEM((BAND * TOK, DIM), BF16),
-            pltpu.VMEM((BAND * TOK, DIM), BF16),
-            pltpu.VMEM((DIM, BAND * TOK), BF16),
             pltpu.VMEM((BAND * TOK, DIM), F32),
             pltpu.VMEM((LINE, PAIR, TOK), F32),
             pltpu.VMEM((LINE, PAIR, TOK), F32),
@@ -258,9 +250,9 @@
             pltpu.VMEM((LINE, 1, TOK), F32),
             pltpu.VMEM((DIM, TOK), F32),
         ],
-        compiler_params=pltpu.CompilerParams(vmem_limit_bytes=32 * 1024 * 1024),
+        compiler_params=pltpu.CompilerParams(vmem_limit_bytes=12 * 1024 * 1024),
         cost_estimate=pl.CostEstimate(flops=10**9, bytes_accessed=6 * 2**20, transcendentals=4 * 10**6),
-    )(head, low, weight, start, queries, own, last, before)
+    )(head, low, weight, start, queries, *keys)
 
 
 def per_device(seq, dp, teacher_query, teacher_key, student_query, student_key, segment_ids, head_weight):
@@ -284,7 +276,7 @@
     before = move(own[1:], to_second)
     packed, start, low = pack_queries(flip, range_index, teacher_query[0], student_query[0], segment_ids)
     queries = exchange(packed)
-    dq, dk_own, dk_last, dk_before = attend(head, low, head_weight, start, queries, own, last, before)
+    dq, dk_own, dk_last, dk_before = attend(head, low, head_weight, start, queries, *layout(own, last, before))
 
     back_last = move(dk_last, reverse(to_next)).astype(F32)
     back_before = move(dk_before, reverse(to_second)).astype(F32)

time: 106 us -> 103 us (0.972)
  blocking collectives: 10.9 us -> 30.2 us
  waiting for transfers between devices: 47.8 us -> 28.9 us
  starting transfers between devices: 32 us -> 24.9 us
  local copies, waits for them, and re-layouts: 0.72 us -> 2.74 us
    all_to_all x1 -> x2, blocking collectives: 10.9 us -> 30.2 us  [exchange(): return lax.all_to_all(x, 'seq', 0, 0, axis_index_groups=lines)]
    all_to_all x3 -> x2, waiting for transfers between devices: 18.9 us -> 3.57 us  [exchange(): return lax.all_to_all(x, 'seq', 0, 0, axis_index_groups=lines)]
    all_to_all x3 -> x2, starting transfers between devices: 11.8 us -> 7.07 us  [exchange(): return lax.all_to_all(x, 'seq', 0, 0, axis_index_groups=lines)]
    ppermute x4, waiting for transfers between devices: 29 us -> 25.4 us  [move(): return lax.ppermute(x, AXES, route)]
    ppermute x4, starting transfers between devices: 20.3 us -> 17.8 us  [move(): return lax.ppermute(x, AXES, route)]
    unnamed x8 -> x12, local copies, waits for them, and re-layouts: 0.7 us -> 2.71 us
  transfers between devices with their start and end apart: 7 -> 6, of which waited for: 7 -> 5; matrix products, arithmetic and copies ran while one was open for 0% -> 0% of each run, Pallas kernels for 2% -> 3%
where the time goes in v5:
time: 103 us; the launch traced here: 101 us
  blocking collectives  30.2 us (29%)
  waiting for transfers between devices  28.9 us (28%)
  starting transfers between devices  24.9 us (24%)
  Pallas kernels  13.8 us (13%)
  local copies, waits for them, and re-layouts  2.74 us (3%)
    all_to_all x2, blocking collectives, exchange(): return lax.all_to_all(x, 'seq', 0, 0, axis_index_groups=lines)  30.2 us
    ppermute x4, waiting for transfers between devices, move(): return lax.ppermute(x, AXES, route)  25.4 us
    ppermute x4, starting transfers between devices, move(): return lax.ppermute(x, AXES, route)  17.8 us
    all_to_all x2, starting transfers between devices, exchange(): return lax.all_to_all(x, 'seq', 0, 0, axis_index_groups=lines)  7.07 us
    pallas_call x1, Pallas kernels, attend(): pl.pallas_call(main_kernel, out_shape=[jax.ShapeDtypeStruct((LINE, TOK, D...  6.87 us
    all_to_all x2, waiting for transfers between devices, exchange(): return lax.all_to_all(x, 'seq', 0, 0, axis_index_groups=lines)  3.57 us
    unnamed x12, local copies, waits for them, and re-layouts  2.71 us
    pallas_call x1, Pallas kernels, pack_queries(): pl.pallas_call(pack_queries_kernel, out_shape=[jax.ShapeDtypeStruct((HEAD...  2.61 us
  transfers between devices with their start and end apart: 6, of which 5 were waited for; matrix products, arithmetic and copies ran while one was open for 0% of the time, Pallas kernels for 3%

profile of v5, /device:TPU:6, one launch (start us, length us, event | category | flops | bytes accessed | tf_op | source)
XLA Modules:
  0.0 101.4 jit_solution(17374488891104508688)
XLA Ops:
  0.7 1.9 %shard_map.78 = bf16[4,2,256,128]{3,2,1,0:T(8,128)(2,1)} custom-call(s32[1]{0:T(128)} %bitcast.flip_ref, bf16[256,512]{1,0:T(8,128)(2,1)} %bitcast.11, bf16[256,512]{1,0:T(8,128)(2,1)} %bitcast.12), custom_call_target="tpu_custom_call" | custom-call | bytes 1048576 | tf_op jit(solution)/shard_map/pallas_call | solution.py:93
  2.6 19.4 %all_to_all.20.own_ref = bf16[4,2,256,128]{3,2,1,0:T(8,128)(2,1)S(1)} all-to-all(bf16[4,2,256,128]{3,2,1,0:T(8,128)(2,1)} %shard_map.78), channel_id=1, replica_groups={{0,4,8,12},{16,20,24,28},{32,36,40,44},{48,52,56,60},{64,68,72,76},{80,..., dimensions={0} | all-to-all | bytes 1048576 | tf_op jit(solution)/shard_map/all_to_all | solution.py:271
  21.9 4.8 %collective-permute-start = (bf16[4,2,256,128]{3,2,1,0:T(8,128)(2,1)S(1)}, bf16[4,2,256,128]{3,2,1,0:T(8,128)(2,1)S(1)}, u32[]{:S(2)}, u32[]{:S(2)}) collective-permute-start(bf16[4,2,256,128]{3,2,1,0:T(8,128)(2,1)S(1)} %all_to_all.20.own_ref), channel_id=1, source_target_pairs={{0,28},{1,29},{2,30},{3,31},{4,24},{5,25},{6,26},{7,27},{8,20},{9,... | collective-permute-start | bytes 1572872 | tf_op jit(solution)/shard_map/ppermute | solution.py:268
  26.7 4.3 %collective-permute-start.1 = (bf16[3,2,256,128]{3,2,1,0:T(8,128)(2,1)S(1)}, bf16[3,2,256,128]{3,2,1,0:T(8,128)(2,1)S(1)}, u32[]{:S(2)}, u32[]{:S(2)}) collective-permute-start(bf16[3,2,256,128]{3,2,1,0:T(8,128)(2,1)S(1)} %slice.4), channel_id=1, source_target_pairs={{0,32},{1,33},{2,34},{3,35},{4,36},{5,37},{6,38},{7,39},{8,40},{9,... | collective-permute-start | bytes 1179656 | tf_op jit(solution)/shard_map/ppermute | solution.py:268
  31.0 2.6 %shard_map.77 = (bf16[4,2,256,128]{3,2,1,0:T(8,128)(2,1)}, s32[4,256]{1,0:T(4,128)}, s32[4]{0:T(128)}) custom-call(s32[1]{0:T(128)} %bitcast.flip_ref, s32[1]{0:T(128)} %bitcast.2.range_ref, bf16[256,512]{1,0:T(8,128)(2,1)} %bitcast.9, bf16[256,512]{1,0:T(8,128)(2,1)} %bitcast.10, s32[1,32768]{1,0:T(1,128)} %seg_ref.1), custom_call_target="tpu_custom_call" | custom-call | bytes 1048576 | tf_op jit(solution)/shard_map/pallas_call | solution.py:103
  33.6 3.6 %all-to-all-start = ((bf16[4,2,256,128]{3,2,1,0:T(8,128)(2,1)}), bf16[4,2,256,128]{3,2,1,0:T(8,128)(2,1)S(1)}, u32[]{:S(2)}, u32[]{:S(2)}) async-start(bf16[4,2,256,128]{3,2,1,0:T(8,128)(2,1)} %get-tuple-element.16), calls=%async_computation | async-start | bytes 1048576 | tf_op jit(solution)/shard_map/all_to_all | solution.py:271
  37.3 10.0 %collective-permute-done.1.before_ref = bf16[3,2,256,128]{3,2,1,0:T(8,128)(2,1)S(1)} collective-permute-done((bf16[3,2,256,128]{3,2,1,0:T(8,128)(2,1)S(1)}, bf16[3,2,256,128]{3,2,1,0:T(8,128)(2,1)S(1)}, u32[]{:S(2)}, u32[]{:S(2)}) %collective-permute-start.1) | collective-permute-done | bytes 393248 | tf_op jit(solution)/shard_map/ppermute | solution.py:268
  47.3 10.7 %collective-permute-done.last_ref = bf16[4,2,256,128]{3,2,1,0:T(8,128)(2,1)S(1)} collective-permute-done((bf16[4,2,256,128]{3,2,1,0:T(8,128)(2,1)S(1)}, bf16[4,2,256,128]{3,2,1,0:T(8,128)(2,1)S(1)}, u32[]{:S(2)}, u32[]{:S(2)}) %collective-permute-start) | collective-permute-done | bytes 524320 | tf_op jit(solution)/shard_map/ppermute | solution.py:268
  58.0 0.3 shard_map.79
  58.3 0.0 copy-start.3
  58.4 0.9 copy-done.3
  59.2 0.0 all-to-all-done.query_ref
  59.2 0.0 copy-start
  59.2 0.0 copy-start.1
  59.2 0.0 copy-start.2
  59.3 0.7 copy-done
  59.9 0.0 copy-done.1
  59.9 0.0 copy-done.2
  59.9 0.0 copy-start.4
  59.9 1.1 %copy-done.4 = bf16[128,3072]{1,0:T(8,128)(2,1)S(1)} copy-done((bf16[128,3072]{1,0:T(8,128)(2,1)S(1)}, bf16[128,3072]{1,0:T(8,128)(2,1)}, u32[]{:S(2)}) %copy-start.4) | copy-done | bytes 786456
  61.1 6.9 %shard_map.80 = (bf16[4,256,128]{2,1,0:T(8,128)(2,1)}, f32[4,256,128]{2,1,0:T(8,128)S(1)}, bf16[4,256,128]{2,1,0:T(8,128)(2,1)S(1)}, bf16[3,256,128]{2,1,0:T(8,128)(2,1)S(1)}) custom-call(s32[1]{0:T(128)} %bitcast.1.head_ref, s32[4]{0:T(128)S(1)} %copy-done.2, f32[4]{0:T(128)S(1)} %copy-done.1, s32[4,256]{1,0:T(4,128)S(1)} %copy-done, ...), custom_call_target="tpu_custom_call" | custom-call | flops 1000000000 | bytes 6291456 | tf_op jit(solution)/shard_map/pallas_call | solution.py:235
  67.9 5.5 %collective-permute-start.2 = (bf16[4,256,128]{2,1,0:T(8,128)(2,1)S(1)}, bf16[4,256,128]{2,1,0:T(8,128)(2,1)S(1)}, u32[]{:S(2)}, u32[]{:S(2)}) collective-permute-start(bf16[4,256,128]{2,1,0:T(8,128)(2,1)S(1)} %get-tuple-element.22), channel_id=1, source_target_pairs={{28,0},{29,1},{30,2},{31,3},{24,4},{25,5},{26,6},{27,7},{20,8},{21... | collective-permute-start | bytes 786440 | tf_op jit(solution)/shard_map/ppermute | solution.py:268
  73.5 3.2 %collective-permute-start.3 = (bf16[3,256,128]{2,1,0:T(8,128)(2,1)S(1)}, bf16[3,256,128]{2,1,0:T(8,128)(2,1)S(1)}, u32[]{:S(2)}, u32[]{:S(2)}) collective-permute-start(bf16[3,256,128]{2,1,0:T(8,128)(2,1)S(1)} %get-tuple-element.23), channel_id=1, source_target_pairs={{32,0},{33,1},{34,2},{35,3},{36,4},{37,5},{38,6},{39,7},{40,8},{41... | collective-permute-start | bytes 589832 | tf_op jit(solution)/shard_map/ppermute | solution.py:268
  76.7 3.4 %all-to-all-start.2 = ((bf16[4,256,128]{2,1,0:T(8,128)(2,1)}), bf16[4,256,128]{2,1,0:T(8,128)(2,1)S(1)}, u32[]{:S(2)}, u32[]{:S(2)}) async-start(bf16[4,256,128]{2,1,0:T(8,128)(2,1)} %get-tuple-element.20), calls=%async_computation.2 | async-start | bytes 524288 | tf_op jit(solution)/shard_map/all_to_all | solution.py:271
  80.1 2.3 %collective-permute-done.3 = bf16[3,256,128]{2,1,0:T(8,128)(2,1)S(1)} collective-permute-done((bf16[3,256,128]{2,1,0:T(8,128)(2,1)S(1)}, bf16[3,256,128]{2,1,0:T(8,128)(2,1)S(1)}, u32[]{:S(2)}, u32[]{:S(2)}) %collective-permute-start.3) | collective-permute-done | bytes 196640 | tf_op jit(solution)/shard_map/ppermute | solution.py:268
  82.5 2.3 %collective-permute-done.2 = bf16[4,256,128]{2,1,0:T(8,128)(2,1)S(1)} collective-permute-done((bf16[4,256,128]{2,1,0:T(8,128)(2,1)S(1)}, bf16[4,256,128]{2,1,0:T(8,128)(2,1)S(1)}, u32[]{:S(2)}, u32[]{:S(2)}) %collective-permute-start.2) | collective-permute-done | bytes 262176 | tf_op jit(solution)/shard_map/ppermute | solution.py:268
  84.8 0.1 add_convert_fusion
  84.8 3.6 %all-to-all-done.2.dq_ref = bf16[4,256,128]{2,1,0:T(8,128)(2,1)S(1)} async-done(((bf16[4,256,128]{2,1,0:T(8,128)(2,1)}), bf16[4,256,128]{2,1,0:T(8,128)(2,1)S(1)}, u32[]{:S(2)}, u32[]{:S(2)}) %all-to-all-start.2) | async-done | bytes 262176 | tf_op jit(solution)/shard_map/all_to_all | solution.py:271
  88.4 0.0 copy-start.5
  88.4 10.9 %all_to_all.21.dk_ref = bf16[4,256,128]{2,1,0:T(8,128)(2,1)} all-to-all(bf16[4,256,128]{2,1,0:T(8,128)(2,1)S(1)} %add_convert_fusion), channel_id=1, replica_groups={{0,4,8,12},{16,20,24,28},{32,36,40,44},{48,52,56,60},{64,68,72,76},{80,..., dimensions={0} | all-to-all | bytes 524288 | tf_op jit(solution)/shard_map/all_to_all | solution.py:271
  99.3 0.0 copy-done.5
  99.3 2.1 %shard_map.81 = (f32[256,512]{1,0:T(8,128)}, f32[256,512]{1,0:T(8,128)}) custom-call(s32[1]{0:T(128)} %bitcast.flip_ref, bf16[4,256,128]{2,1,0:T(8,128)(2,1)} %copy-done.5, bf16[4,256,128]{2,1,0:T(8,128)(2,1)} %all_to_all.21.dk_ref), custom_call_target="tpu_custom_call" | custom-call | bytes 1572864 | tf_op jit(solution)/shard_map/pallas_call | solution.py:124
  (1 shorter events, 0.0 us)
Async XLA Ops:
  21.9 36.1 %collective-permute-start = (bf16[4,2,256,128]{3,2,1,0:T(8,128)(2,1)S(1)}, bf16[4,2,256,128]{3,2,1,0:T(8,128)(2,1)S(1)}, u32[]{:S(2)}, u32[]{:S(2)}) collective-permute-start(bf16[4,2,256,128]{3,2,1,0:T(8,128)(2,1)S(1)} %all_to_all.20.own_ref), channel_id=1, source_target_pairs={{0,28},{1,29},{2,30},{3,31},{4,24},{5,25},{6,26},{7,27},{8,20},{9,... | collective-permute-start | bytes 1572872 | tf_op jit(solution)/shard_map/ppermute | solution.py:268
  26.7 20.5 %collective-permute-start.1 = (bf16[3,2,256,128]{3,2,1,0:T(8,128)(2,1)S(1)}, bf16[3,2,256,128]{3,2,1,0:T(8,128)(2,1)S(1)}, u32[]{:S(2)}, u32[]{:S(2)}) collective-permute-start(bf16[3,2,256,128]{3,2,1,0:T(8,128)(2,1)S(1)} %slice.4), channel_id=1, source_target_pairs={{0,32},{1,33},{2,34},{3,35},{4,36},{5,37},{6,38},{7,39},{8,40},{9,... | collective-permute-start | bytes 1179656 | tf_op jit(solution)/shard_map/ppermute | solution.py:268
  33.6 25.6 %all-to-all-start = ((bf16[4,2,256,128]{3,2,1,0:T(8,128)(2,1)}), bf16[4,2,256,128]{3,2,1,0:T(8,128)(2,1)S(1)}, u32[]{:S(2)}, u32[]{:S(2)}) async-start(bf16[4,2,256,128]{3,2,1,0:T(8,128)(2,1)} %get-tuple-element.16), calls=%async_computation | async-start | bytes 1048576 | tf_op jit(solution)/shard_map/all_to_all | solution.py:271
  58.3 0.9 copy-start.3
  59.2 0.7 copy-start
  59.2 0.7 copy-start.1
  59.2 0.7 copy-start.2
  59.9 1.1 %copy-start.4 = (bf16[128,3072]{1,0:T(8,128)(2,1)S(1)}, bf16[128,3072]{1,0:T(8,128)(2,1)}, u32[]{:S(2)}) copy-start(bf16[128,3072]{1,0:T(8,128)(2,1)} %copy-done.3) | copy-start | bytes 2359300
  67.9 16.8 %collective-permute-start.2 = (bf16[4,256,128]{2,1,0:T(8,128)(2,1)S(1)}, bf16[4,256,128]{2,1,0:T(8,128)(2,1)S(1)}, u32[]{:S(2)}, u32[]{:S(2)}) collective-permute-start(bf16[4,256,128]{2,1,0:T(8,128)(2,1)S(1)} %get-tuple-element.22), channel_id=1, source_target_pairs={{28,0},{29,1},{30,2},{31,3},{24,4},{25,5},{26,6},{27,7},{20,8},{21... | collective-permute-start | bytes 786440 | tf_op jit(solution)/shard_map/ppermute | solution.py:268
  73.5 9.0 %collective-permute-start.3 = (bf16[3,256,128]{2,1,0:T(8,128)(2,1)S(1)}, bf16[3,256,128]{2,1,0:T(8,128)(2,1)S(1)}, u32[]{:S(2)}, u32[]{:S(2)}) collective-permute-start(bf16[3,256,128]{2,1,0:T(8,128)(2,1)S(1)} %get-tuple-element.23), channel_id=1, source_target_pairs={{32,0},{33,1},{34,2},{35,3},{36,4},{37,5},{38,6},{39,7},{40,8},{41... | collective-permute-start | bytes 589832 | tf_op jit(solution)/shard_map/ppermute | solution.py:268
  76.7 11.7 %all-to-all-start.2 = ((bf16[4,256,128]{2,1,0:T(8,128)(2,1)}), bf16[4,256,128]{2,1,0:T(8,128)(2,1)S(1)}, u32[]{:S(2)}, u32[]{:S(2)}) async-start(bf16[4,256,128]{2,1,0:T(8,128)(2,1)} %get-tuple-element.20), calls=%async_computation.2 | async-start | bytes 524288 | tf_op jit(solution)/shard_map/all_to_all | solution.py:271
  88.4 10.9 %copy-start.5 = (bf16[4,256,128]{2,1,0:T(8,128)(2,1)}, bf16[4,256,128]{2,1,0:T(8,128)(2,1)S(1)}, u32[]{:S(2)}) copy-start(bf16[4,256,128]{2,1,0:T(8,128)(2,1)S(1)} %all-to-all-done.2.dq_ref) | copy-start | bytes 786436

commit v6 on v5

--- a/solution.py
+++ b/solution.py
@@ -26,17 +26,25 @@
 
 
 def routes(seq, dp):
-    last, before_last = [], []
-    for ring in range(seq // RING):
+    rings = seq // RING
+    seam = rings // 2 - 1 if dp == 4 else None
+    last, before_last, relay = [], [], []
+    for ring in range(rings):
         for y in range(RING):
             for part in range(dp):
                 me = (ring * RING + y) * dp + part
                 ahead = ring + (y >= LINE)
-                if ahead < seq // RING:
+                if ahead < rings:
                     last.append((me, (ahead * RING + RING - 1 - y) * dp + part))
-                if ring + 1 < seq // RING:
-                    before_last.append((me, ((ring + 1) * RING + y) * dp + part))
-    return last, before_last
+                if ring + 1 < rings:
+                    target = ((ring + 1) * RING + y) * dp + part
+                    if ring == seam:
+                        over = ((rings - 1 if part < 2 else seam) * RING + y) * dp + (part + 2) % 4
+                        relay.append((me, over))
+                        before_last.append((over, target))
+                    else:
+                        before_last.append((me, target))
+    return last, before_last, relay
 
 
 def reverse(route):
@@ -130,12 +138,11 @@
     )(flip, dq, dk)
 
 
-def layout_kernel(own_ref, last_ref, before_ref, kt, ks, ks_turned):
+def layout_kernel(own_ref, last_ref, before_ref, kt, ks):
     def load(block, teacher, student):
         here = pl.ds(block * TOK, TOK)
         kt[here, :] = teacher
         ks[here, :] = student
-        ks_turned[:, here] = student.T
 
     load(0, jnp.zeros((TOK, DIM), BF16), jnp.zeros((TOK, DIM), BF16))
     for i in range(LINE - 1):
@@ -151,19 +158,18 @@
         out_shape=[
             jax.ShapeDtypeStruct((BAND * TOK, DIM), BF16),
             jax.ShapeDtypeStruct((BAND * TOK, DIM), BF16),
-            jax.ShapeDtypeStruct((DIM, BAND * TOK), BF16),
         ],
         in_specs=[VMEM] * 3,
-        out_specs=[VMEM] * 3,
+        out_specs=[VMEM] * 2,
         compiler_params=pltpu.CompilerParams(vmem_limit_bytes=6 * 1024 * 1024),
         cost_estimate=pl.CostEstimate(flops=10**10, bytes_accessed=16 * 2**20, transcendentals=0),
     )(own, last, before)
 
 
 def main_kernel(
-    head_ref, low_ref, weight_ref, start_ref, query_ref, kt, ks, ks_turned,
+    head_ref, low_ref, weight_ref, start_ref, query_ref, kt, ks,
     dq_ref, dk_own_ref, dk_last_ref, dk_before_ref,
-    dk, et, es, top_t, top_s, dq_acc,
+    ks_turned, dk, et, es, top_t, top_s, dq_acc,
 ):
     weight = weight_ref[head_ref[0]]
     scale = 1.0 / math.sqrt(DIM)
@@ -174,6 +180,8 @@
         return pl.ds(block * TOK, TOK)
 
     dk[...] = jnp.zeros((BAND * TOK, DIM), F32)
+    for block in range(BAND):
+        ks_turned[:, rows(block)] = ks[rows(block), :].T
     key_row = lax.broadcasted_iota(jnp.int32, (PAIR, TOK), 0)
     query_column = lax.broadcasted_iota(jnp.int32, (PAIR, TOK), 1)
 
@@ -240,9 +248,10 @@
             jax.ShapeDtypeStruct((LINE, TOK, DIM), BF16),
             jax.ShapeDtypeStruct((LINE - 1, TOK, DIM), BF16),
         ],
-        in_specs=[SMEM] * 3 + [VMEM] * 5,
+        in_specs=[SMEM] * 3 + [VMEM] * 4,
         out_specs=[VMEM] * 4,
         scratch_shapes=[
+            pltpu.VMEM((DIM, BAND * TOK), BF16),
             pltpu.VMEM((BAND * TOK, DIM), F32),
             pltpu.VMEM((LINE, PAIR, TOK), F32),
             pltpu.VMEM((LINE, PAIR, TOK), F32),
@@ -256,7 +265,8 @@
 
 
 def per_device(seq, dp, teacher_query, teacher_key, student_query, student_key, segment_ids, head_weight):
-    to_next, to_second = routes(seq, dp)
+    to_next, to_second, relay = routes(seq, dp)
+    to_second_straight = [(i, i + RING * dp) for i in range((seq - RING) * dp)]
     lines = [list(range(i, i + LINE)) for i in range(0, seq, LINE)]
     seq_index = lax.axis_index("seq")
     range_index = seq_index // LINE
@@ -273,13 +283,18 @@
     flip, range_index, head = flip.reshape(1), range_index.reshape(1), head.reshape(1)
     own = exchange(pack_keys(flip, teacher_key[0], student_key[0]))
     last = move(own, to_next)
-    before = move(own[1:], to_second)
+    parting = own[1:]
+    if relay:
+        ring, pair = seq_index // RING, lax.axis_index("dp") // 2
+        relays = ((ring == seq // RING - 1) & (pair == 1)) | ((ring == seq // RING // 2 - 1) & (pair == 0))
+        parting = jnp.where(relays, move(parting, relay), parting)
+    before = move(parting, to_second)
     packed, start, low = pack_queries(flip, range_index, teacher_query[0], student_query[0], segment_ids)
     queries = exchange(packed)
     dq, dk_own, dk_last, dk_before = attend(head, low, head_weight, start, queries, *layout(own, last, before))
 
     back_last = move(dk_last, reverse(to_next)).astype(F32)
-    back_before = move(dk_before, reverse(to_second)).astype(F32)
+    back_before = move(dk_before, reverse(to_second_straight)).astype(F32)
     dq_home = exchange(dq)
     total = dk_own + back_last + jnp.pad(back_before, ((1, 0), (0, 0), (0, 0)))
     query_grad, key_grad = unpack(flip, dq_home, exchange(total.astype(BF16)))

time: 103 us -> 108 us (1.049); the launches traced: 101 us -> 108 us
  waiting for transfers between devices: 28.9 us -> 34 us
  starting transfers between devices: 24.9 us -> 28 us
  local copies, waits for them, and re-layouts: 2.74 us -> 0.7 us
    all_to_all x2, waiting for transfers between devices: 3.57 us -> 8.09 us  [exchange(): return lax.all_to_all(x, 'seq', 0, 0, axis_index_groups=lines)]
    ppermute x4 -> x5, starting transfers between devices: 17.8 us -> 20.7 us  [move(): return lax.ppermute(x, AXES, route)]
    unnamed x12 -> x8, local copies, waits for them, and re-layouts: 2.71 us -> 0.67 us
    ppermute x4 -> x5, waiting for transfers between devices: 25.4 us -> 25.9 us  [move(): return lax.ppermute(x, AXES, route)]
  transfers between devices with their start and end apart: 6 -> 7, of which waited for: 5 -> 4; matrix products, arithmetic and copies ran while one was open for 0% -> 0% of each run, Pallas kernels for 3% -> 3%
where the time goes in v6:
time: 108 us
  waiting for transfers between devices  34 us (31%)
  blocking collectives  30.2 us (28%)
  starting transfers between devices  28 us (26%)
  Pallas kernels  13.7 us (13%)
    all_to_all x2, blocking collectives, exchange(): return lax.all_to_all(x, 'seq', 0, 0, axis_index_groups=lines)  30.2 us
    ppermute x5, waiting for transfers between devices, move(): return lax.ppermute(x, AXES, route)  25.9 us
    ppermute x5, starting transfers between devices, move(): return lax.ppermute(x, AXES, route)  20.7 us
    all_to_all x2, waiting for transfers between devices, exchange(): return lax.all_to_all(x, 'seq', 0, 0, axis_index_groups=lines)  8.09 us
    all_to_all x2, starting transfers between devices, exchange(): return lax.all_to_all(x, 'seq', 0, 0, axis_index_groups=lines)  7.31 us
    pallas_call x1, Pallas kernels, attend(): pl.pallas_call(main_kernel, out_shape=[jax.ShapeDtypeStruct((LINE, TOK, D...  6.93 us
    pallas_call x1, Pallas kernels, pack_queries(): pl.pallas_call(pack_queries_kernel, out_shape=[jax.ShapeDtypeStruct((HEAD...  2.61 us
  transfers between devices with their start and end apart: 7, of which 4 were waited for; matrix products, arithmetic and copies ran while one was open for 0% of the time, Pallas kernels for 3%

profile of v6, /device:TPU:6, one launch (start us, length us, event | category | flops | bytes accessed | tf_op | source)
XLA Modules:
  0.0 107.5 jit_solution(11570593238705517496)
XLA Ops:
  0.7 1.9 %shard_map.78 = bf16[4,2,256,128]{3,2,1,0:T(8,128)(2,1)} custom-call(s32[1]{0:T(128)} %bitcast.flip_ref, bf16[256,512]{1,0:T(8,128)(2,1)} %bitcast.11, bf16[256,512]{1,0:T(8,128)(2,1)} %bitcast.12), custom_call_target="tpu_custom_call" | custom-call | bytes 1048576 | tf_op jit(solution)/shard_map/pallas_call | solution.py:101
  2.6 19.4 %all_to_all.20.own_ref = bf16[4,2,256,128]{3,2,1,0:T(8,128)(2,1)S(1)} all-to-all(bf16[4,2,256,128]{3,2,1,0:T(8,128)(2,1)} %shard_map.78), channel_id=1, replica_groups={{0,4,8,12},{16,20,24,28},{32,36,40,44},{48,52,56,60},{64,68,72,76},{80,..., dimensions={0} | all-to-all | bytes 1048576 | tf_op jit(solution)/shard_map/all_to_all | solution.py:281
  22.0 0.7 collective-permute-start.1
  22.7 4.8 %collective-permute-start = (bf16[4,2,256,128]{3,2,1,0:T(8,128)(2,1)S(1)}, bf16[4,2,256,128]{3,2,1,0:T(8,128)(2,1)S(1)}, u32[]{:S(2)}, u32[]{:S(2)}) collective-permute-start(bf16[4,2,256,128]{3,2,1,0:T(8,128)(2,1)S(1)} %all_to_all.20.own_ref), channel_id=1, source_target_pairs={{0,28},{1,29},{2,30},{3,31},{4,24},{5,25},{6,26},{7,27},{8,20},{9,... | collective-permute-start | bytes 1572872 | tf_op jit(solution)/shard_map/ppermute | solution.py:278
  27.5 0.0 collective-permute-done.1
  27.5 4.3 %collective-permute-start.2 = (bf16[3,2,256,128]{3,2,1,0:T(8,128)(2,1)S(1)}, bf16[3,2,256,128]{3,2,1,0:T(8,128)(2,1)S(1)}, u32[]{:S(2)}, u32[]{:S(2)}) collective-permute-start(bf16[3,2,256,128]{3,2,1,0:T(8,128)(2,1)S(1)} %broadcast_select_fusion), channel_id=1, source_target_pairs={{0,32},{1,33},{2,34},{3,35},{4,36},{5,37},{6,38},{7,39},{8,40},{9,... | collective-permute-start | bytes 1179656 | tf_op jit(solution)/shard_map/ppermute | solution.py:278
  31.8 2.6 %shard_map.77 = (bf16[4,2,256,128]{3,2,1,0:T(8,128)(2,1)}, s32[4,256]{1,0:T(4,128)}, s32[4]{0:T(128)}) custom-call(s32[1]{0:T(128)} %bitcast.flip_ref, s32[1]{0:T(128)} %bitcast.2.range_ref, bf16[256,512]{1,0:T(8,128)(2,1)} %bitcast.9, bf16[256,512]{1,0:T(8,128)(2,1)} %bitcast.10, s32[1,32768]{1,0:T(1,128)} %seg_ref.1), custom_call_target="tpu_custom_call" | custom-call | bytes 1048576 | tf_op jit(solution)/shard_map/pallas_call | solution.py:111
  34.4 3.6 %all-to-all-start = ((bf16[4,2,256,128]{3,2,1,0:T(8,128)(2,1)}), bf16[4,2,256,128]{3,2,1,0:T(8,128)(2,1)S(1)}, u32[]{:S(2)}, u32[]{:S(2)}) async-start(bf16[4,2,256,128]{3,2,1,0:T(8,128)(2,1)} %get-tuple-element.15), calls=%async_computation | async-start | bytes 1048576 | tf_op jit(solution)/shard_map/all_to_all | solution.py:281
  38.1 23.6 %collective-permute-done.last_ref = bf16[4,2,256,128]{3,2,1,0:T(8,128)(2,1)S(1)} collective-permute-done((bf16[4,2,256,128]{3,2,1,0:T(8,128)(2,1)S(1)}, bf16[4,2,256,128]{3,2,1,0:T(8,128)(2,1)S(1)}, u32[]{:S(2)}, u32[]{:S(2)}) %collective-permute-start) | collective-permute-done | bytes 524320 | tf_op jit(solution)/shard_map/ppermute | solution.py:278
  61.6 1.3 %collective-permute-done.2.before_ref = bf16[3,2,256,128]{3,2,1,0:T(8,128)(2,1)S(1)} collective-permute-done((bf16[3,2,256,128]{3,2,1,0:T(8,128)(2,1)S(1)}, bf16[3,2,256,128]{3,2,1,0:T(8,128)(2,1)S(1)}, u32[]{:S(2)}, u32[]{:S(2)}) %collective-permute-start.2) | collective-permute-done | bytes 393248 | tf_op jit(solution)/shard_map/ppermute | solution.py:278
  63.0 0.1 shard_map.79
  63.1 0.0 all-to-all-done.query_ref
  63.1 0.0 copy-start
  63.1 0.0 copy-start.1
  63.1 0.0 copy-start.2
  63.1 0.7 copy-done
  63.8 0.0 copy-done.1
  63.8 0.0 copy-done.2
  63.8 6.9 %shard_map.80 = (bf16[4,256,128]{2,1,0:T(8,128)(2,1)}, f32[4,256,128]{2,1,0:T(8,128)S(1)}, bf16[4,256,128]{2,1,0:T(8,128)(2,1)S(1)}, bf16[3,256,128]{2,1,0:T(8,128)(2,1)S(1)}) custom-call(s32[1]{0:T(128)} %bitcast.1.head_ref, s32[4]{0:T(128)S(1)} %copy-done.2, f32[4]{0:T(128)S(1)} %copy-done.1, s32[4,256]{1,0:T(4,128)S(1)} %copy-done, ...), custom_call_target="tpu_custom_call" | custom-call | flops 1000000000 | bytes 6291456 | tf_op jit(solution)/shard_map/pallas_call | solution.py:243
  70.7 3.6 %collective-permute-start.3 = (bf16[4,256,128]{2,1,0:T(8,128)(2,1)S(1)}, bf16[4,256,128]{2,1,0:T(8,128)(2,1)S(1)}, u32[]{:S(2)}, u32[]{:S(2)}) collective-permute-start(bf16[4,256,128]{2,1,0:T(8,128)(2,1)S(1)} %get-tuple-element.20), channel_id=1, source_target_pairs={{28,0},{29,1},{30,2},{31,3},{24,4},{25,5},{26,6},{27,7},{20,8},{21... | collective-permute-start | bytes 786440 | tf_op jit(solution)/shard_map/ppermute | solution.py:278
  74.3 7.3 %collective-permute-start.4 = (bf16[3,256,128]{2,1,0:T(8,128)(2,1)S(1)}, bf16[3,256,128]{2,1,0:T(8,128)(2,1)S(1)}, u32[]{:S(2)}, u32[]{:S(2)}) collective-permute-start(bf16[3,256,128]{2,1,0:T(8,128)(2,1)S(1)} %get-tuple-element.21), channel_id=1, source_target_pairs={{32,0},{33,1},{34,2},{35,3},{36,4},{37,5},{38,6},{39,7},{40,8},{41... | collective-permute-start | bytes 589832 | tf_op jit(solution)/shard_map/ppermute | solution.py:278
  81.6 3.7 %all-to-all-start.2 = ((bf16[4,256,128]{2,1,0:T(8,128)(2,1)}), bf16[4,256,128]{2,1,0:T(8,128)(2,1)S(1)}, u32[]{:S(2)}, u32[]{:S(2)}) async-start(bf16[4,256,128]{2,1,0:T(8,128)(2,1)} %get-tuple-element.18), calls=%async_computation.2 | async-start | bytes 524288 | tf_op jit(solution)/shard_map/all_to_all | solution.py:281
  85.3 1.1 %collective-permute-done.4 = bf16[3,256,128]{2,1,0:T(8,128)(2,1)S(1)} collective-permute-done((bf16[3,256,128]{2,1,0:T(8,128)(2,1)S(1)}, bf16[3,256,128]{2,1,0:T(8,128)(2,1)S(1)}, u32[]{:S(2)}, u32[]{:S(2)}) %collective-permute-start.4) | collective-permute-done | bytes 196640 | tf_op jit(solution)/shard_map/ppermute | solution.py:278
  86.4 0.0 collective-permute-done.3
  86.4 0.1 add_convert_fusion
  86.5 8.1 %all-to-all-done.2.dq_ref = bf16[4,256,128]{2,1,0:T(8,128)(2,1)S(1)} async-done(((bf16[4,256,128]{2,1,0:T(8,128)(2,1)}), bf16[4,256,128]{2,1,0:T(8,128)(2,1)S(1)}, u32[]{:S(2)}, u32[]{:S(2)}) %all-to-all-start.2) | async-done | bytes 262176 | tf_op jit(solution)/shard_map/all_to_all | solution.py:281
  94.5 0.0 copy-start.3
  94.5 10.9 %all_to_all.21.dk_ref = bf16[4,256,128]{2,1,0:T(8,128)(2,1)} all-to-all(bf16[4,256,128]{2,1,0:T(8,128)(2,1)S(1)} %add_convert_fusion), channel_id=1, replica_groups={{0,4,8,12},{16,20,24,28},{32,36,40,44},{48,52,56,60},{64,68,72,76},{80,..., dimensions={0} | all-to-all | bytes 524288 | tf_op jit(solution)/shard_map/all_to_all | solution.py:281
  105.4 0.0 copy-done.3
  105.4 2.1 %shard_map.81 = (f32[256,512]{1,0:T(8,128)}, f32[256,512]{1,0:T(8,128)}) custom-call(s32[1]{0:T(128)} %bitcast.flip_ref, bf16[4,256,128]{2,1,0:T(8,128)(2,1)} %copy-done.3, bf16[4,256,128]{2,1,0:T(8,128)(2,1)} %all_to_all.21.dk_ref), custom_call_target="tpu_custom_call" | custom-call | bytes 1572864 | tf_op jit(solution)/shard_map/pallas_call | solution.py:132
  (2 shorter events, 0.1 us)
Async XLA Ops:
  22.0 5.5 %collective-permute-start.1 = (bf16[3,2,256,128]{3,2,1,0:T(8,128)(2,1)S(1)}, bf16[3,2,256,128]{3,2,1,0:T(8,128)(2,1)S(1)}, u32[]{:S(2)}, u32[]{:S(2)}) collective-permute-start(bf16[3,2,256,128]{3,2,1,0:T(8,128)(2,1)S(1)} %slice.4), channel_id=1, source_target_pairs={{224,482},{225,483},{226,224},{227,225},{228,486},{229,487},{230,2... | collective-permute-start | bytes 1179656 | tf_op jit(solution)/shard_map/ppermute | solution.py:278
  22.7 39.0 %collective-permute-start = (bf16[4,2,256,128]{3,2,1,0:T(8,128)(2,1)S(1)}, bf16[4,2,256,128]{3,2,1,0:T(8,128)(2,1)S(1)}, u32[]{:S(2)}, u32[]{:S(2)}) collective-permute-start(bf16[4,2,256,128]{3,2,1,0:T(8,128)(2,1)S(1)} %all_to_all.20.own_ref), channel_id=1, source_target_pairs={{0,28},{1,29},{2,30},{3,31},{4,24},{5,25},{6,26},{7,27},{8,20},{9,... | collective-permute-start | bytes 1572872 | tf_op jit(solution)/shard_map/ppermute | solution.py:278
  27.5 35.4 %collective-permute-start.2 = (bf16[3,2,256,128]{3,2,1,0:T(8,128)(2,1)S(1)}, bf16[3,2,256,128]{3,2,1,0:T(8,128)(2,1)S(1)}, u32[]{:S(2)}, u32[]{:S(2)}) collective-permute-start(bf16[3,2,256,128]{3,2,1,0:T(8,128)(2,1)S(1)} %broadcast_select_fusion), channel_id=1, source_target_pairs={{0,32},{1,33},{2,34},{3,35},{4,36},{5,37},{6,38},{7,39},{8,40},{9,... | collective-permute-start | bytes 1179656 | tf_op jit(solution)/shard_map/ppermute | solution.py:278
  34.4 28.6 %all-to-all-start = ((bf16[4,2,256,128]{3,2,1,0:T(8,128)(2,1)}), bf16[4,2,256,128]{3,2,1,0:T(8,128)(2,1)S(1)}, u32[]{:S(2)}, u32[]{:S(2)}) async-start(bf16[4,2,256,128]{3,2,1,0:T(8,128)(2,1)} %get-tuple-element.15), calls=%async_computation | async-start | bytes 1048576 | tf_op jit(solution)/shard_map/all_to_all | solution.py:281
  63.1 0.7 copy-start
  63.1 0.7 copy-start.1
  63.1 0.7 copy-start.2
  70.7 15.7 %collective-permute-start.3 = (bf16[4,256,128]{2,1,0:T(8,128)(2,1)S(1)}, bf16[4,256,128]{2,1,0:T(8,128)(2,1)S(1)}, u32[]{:S(2)}, u32[]{:S(2)}) collective-permute-start(bf16[4,256,128]{2,1,0:T(8,128)(2,1)S(1)} %get-tuple-element.20), channel_id=1, source_target_pairs={{28,0},{29,1},{30,2},{31,3},{24,4},{25,5},{26,6},{27,7},{20,8},{21... | collective-permute-start | bytes 786440 | tf_op jit(solution)/shard_map/ppermute | solution.py:278
  74.3 12.1 %collective-permute-start.4 = (bf16[3,256,128]{2,1,0:T(8,128)(2,1)S(1)}, bf16[3,256,128]{2,1,0:T(8,128)(2,1)S(1)}, u32[]{:S(2)}, u32[]{:S(2)}) collective-permute-start(bf16[3,256,128]{2,1,0:T(8,128)(2,1)S(1)} %get-tuple-element.21), channel_id=1, source_target_pairs={{32,0},{33,1},{34,2},{35,3},{36,4},{37,5},{38,6},{39,7},{40,8},{41... | collective-permute-start | bytes 589832 | tf_op jit(solution)/shard_map/ppermute | solution.py:278
  81.6 12.9 %all-to-all-start.2 = ((bf16[4,256,128]{2,1,0:T(8,128)(2,1)}), bf16[4,256,128]{2,1,0:T(8,128)(2,1)S(1)}, u32[]{:S(2)}, u32[]{:S(2)}) async-start(bf16[4,256,128]{2,1,0:T(8,128)(2,1)} %get-tuple-element.18), calls=%async_computation.2 | async-start | bytes 524288 | tf_op jit(solution)/shard_map/all_to_all | solution.py:281
  94.5 10.9 %copy-start.3 = (bf16[4,256,128]{2,1,0:T(8,128)(2,1)}, bf16[4,256,128]{2,1,0:T(8,128)(2,1)S(1)}, u32[]{:S(2)}) copy-start(bf16[4,256,128]{2,1,0:T(8,128)(2,1)S(1)} %all-to-all-done.2.dq_ref) | copy-start | bytes 786436

commit v7 on v6

--- a/solution.py
+++ b/solution.py
@@ -39,7 +39,7 @@
                 if ring + 1 < rings:
                     target = ((ring + 1) * RING + y) * dp + part
                     if ring == seam:
-                        over = ((rings - 1 if part < 2 else seam) * RING + y) * dp + (part + 2) % 4
+                        over = ((rings - 1) * RING + y) * dp + part
                         relay.append((me, over))
                         before_last.append((over, target))
                     else:
@@ -56,15 +56,26 @@
     return pl.ds(pl.multiple_of(head * DIM, DIM), DIM)
 
 
-def pack_keys_kernel(flip_ref, a_ref, b_ref, out_ref):
+def pack_kernel(flip_ref, a_ref, b_ref, c_ref, d_ref, keys_ref, queries_ref):
     for place in range(HEADS):
         columns = head_columns(flip_ref[0], place)
-        out_ref[place, 0] = a_ref[:, columns]
-        out_ref[place, 1] = b_ref[:, columns]
-
-
-def pack_queries_kernel(flip_ref, range_ref, a_ref, b_ref, seg_ref, out_ref, start_ref, low_ref):
-    pack_keys_kernel(flip_ref, a_ref, b_ref, out_ref)
+        keys_ref[place, 0] = a_ref[:, columns]
+        keys_ref[place, 1] = b_ref[:, columns]
+        queries_ref[place, 0] = c_ref[:, columns]
+        queries_ref[place, 1] = d_ref[:, columns]
+
+
+def pack(flip, *states):
+    return pl.pallas_call(
+        pack_kernel,
+        out_shape=[jax.ShapeDtypeStruct((HEADS, 2, TOK, DIM), BF16)] * 2,
+        in_specs=[SMEM] + [VMEM] * 4,
+        out_specs=[VMEM] * 2,
+        cost_estimate=pl.CostEstimate(flops=0, bytes_accessed=2**21, transcendentals=0),
+    )(flip, *states)
+
+
+def starts_kernel(range_ref, seg_ref, start_ref, low_ref):
     first_block = range_ref[0] * LINE
 
     def ids(block):
@@ -97,28 +108,14 @@
         low_ref[j] = jnp.min(start[j : j + 1, :])
 
 
-def pack_keys(flip, a, b):
-    return pl.pallas_call(
-        pack_keys_kernel,
-        out_shape=jax.ShapeDtypeStruct((HEADS, 2, TOK, DIM), BF16),
-        in_specs=[SMEM, VMEM, VMEM],
-        out_specs=VMEM,
+def starts(range_index, seg):
+    return pl.pallas_call(
+        starts_kernel,
+        out_shape=[jax.ShapeDtypeStruct((LINE, TOK), jnp.int32), jax.ShapeDtypeStruct((LINE,), jnp.int32)],
+        in_specs=[SMEM, VMEM],
+        out_specs=[VMEM, SMEM],
         cost_estimate=pl.CostEstimate(flops=0, bytes_accessed=2**20, transcendentals=0),
-    )(flip, a, b)
-
-
-def pack_queries(flip, range_index, a, b, seg):
-    return pl.pallas_call(
-        pack_queries_kernel,
-        out_shape=[
-            jax.ShapeDtypeStruct((HEADS, 2, TOK, DIM), BF16),
-            jax.ShapeDtypeStruct((LINE, TOK), jnp.int32),
-            jax.ShapeDtypeStruct((LINE,), jnp.int32),
-        ],
-        in_specs=[SMEM, SMEM, VMEM, VMEM, VMEM],
-        out_specs=[VMEM, VMEM, SMEM],
-        cost_estimate=pl.CostEstimate(flops=0, bytes_accessed=2**20, transcendentals=0),
-    )(flip, range_index, a, b, seg)
+    )(range_index, seg)
 
 
 def unpack_kernel(flip_ref, dq_ref, dk_ref, query_ref, key_ref):
@@ -281,16 +278,16 @@
         return lax.all_to_all(x, "seq", 0, 0, axis_index_groups=lines)
 
     flip, range_index, head = flip.reshape(1), range_index.reshape(1), head.reshape(1)
-    own = exchange(pack_keys(flip, teacher_key[0], student_key[0]))
+    keys, queries = pack(flip, teacher_key[0], student_key[0], teacher_query[0], student_query[0])
+    own = exchange(keys)
     last = move(own, to_next)
     parting = own[1:]
     if relay:
-        ring, pair = seq_index // RING, lax.axis_index("dp") // 2
-        relays = ((ring == seq // RING - 1) & (pair == 1)) | ((ring == seq // RING // 2 - 1) & (pair == 0))
+        relays = seq_index >= seq - RING
         parting = jnp.where(relays, move(parting, relay), parting)
     before = move(parting, to_second)
-    packed, start, low = pack_queries(flip, range_index, teacher_query[0], student_query[0], segment_ids)
-    queries = exchange(packed)
+    start, low = starts(range_index, segment_ids)
+    queries = exchange(queries)
     dq, dk_own, dk_last, dk_before = attend(head, low, head_weight, start, queries, *layout(own, last, before))
 
     back_last = move(dk_last, reverse(to_next)).astype(F32)

time: 108 us -> 105 us (0.972); the launches traced: 108 us -> 103 us
  starting transfers between devices: 28 us -> 23.5 us
  Pallas kernels: 13.7 us -> 17.5 us
  waiting for transfers between devices: 34 us -> 30.8 us
    ppermute x5, starting transfers between devices: 20.7 us -> 16.5 us  [move(): return lax.ppermute(x, AXES, route)]
    all_to_all x2, waiting for transfers between devices: 8.09 us -> 3.96 us  [exchange(): return lax.all_to_all(x, 'seq', 0, 0, axis_index_groups=lines)]
    pallas_call x1, Pallas kernels: 6.93 us -> 10.8 us  [attend(): pl.pallas_call(main_kernel, out_shape=[jax.ShapeDtypeStruct((LINE, TOK, D...]
  transfers between devices with their start and end apart: 7 -> 7, of which waited for: 4 -> 4; matrix products, arithmetic and copies ran while one was open for 0% -> 0% of each run, Pallas kernels for 3% -> 2%
where the time goes in v7:
time: 105 us; the launch traced here: 103 us
  waiting for transfers between devices  30.8 us (29%)
  blocking collectives  29.8 us (28%)
  starting transfers between devices  23.5 us (22%)
  Pallas kernels  17.5 us (17%)
    all_to_all x2, blocking collectives, exchange(): return lax.all_to_all(x, 'seq', 0, 0, axis_index_groups=lines)  29.8 us
    ppermute x5, waiting for transfers between devices, move(): return lax.ppermute(x, AXES, route)  26.9 us
    ppermute x5, starting transfers between devices, move(): return lax.ppermute(x, AXES, route)  16.5 us
    pallas_call x1, Pallas kernels, attend(): pl.pallas_call(main_kernel, out_shape=[jax.ShapeDtypeStruct((LINE, TOK, D...  10.8 us
    all_to_all x2, starting transfers between devices, exchange(): return lax.all_to_all(x, 'seq', 0, 0, axis_index_groups=lines)  7.07 us
    all_to_all x2, waiting for transfers between devices, exchange(): return lax.all_to_all(x, 'seq', 0, 0, axis_index_groups=lines)  3.96 us
    pallas_call x1, Pallas kernels, pack(): pl.pallas_call(pack_kernel, out_shape=[jax.ShapeDtypeStruct((HEADS, 2, TO...  2.34 us
    pallas_call x1, Pallas kernels, starts(): pl.pallas_call(starts_kernel, out_shape=[jax.ShapeDtypeStruct((LINE, TOK)...  2.19 us
  transfers between devices with their start and end apart: 7, of which 4 were waited for; matrix products, arithmetic and copies ran while one was open for 0% of the time, Pallas kernels for 2%

profile of v7, /device:TPU:6, one launch (start us, length us, event | category | flops | bytes accessed | tf_op | source)
XLA Modules:
  0.0 103.3 jit_solution(13038791736011816730)
XLA Ops:
  0.7 2.3 %shard_map.78 = (bf16[4,2,256,128]{3,2,1,0:T(8,128)(2,1)}, bf16[4,2,256,128]{3,2,1,0:T(8,128)(2,1)}) custom-call(s32[1]{0:T(128)} %bitcast.flip_ref, bf16[256,512]{1,0:T(8,128)(2,1)} %bitcast.9, bf16[256,512]{1,0:T(8,128)(2,1)} %bitcast.10, bf16[256,512]{1,0:T(8,128)(2,1)} %bitcast.11, bf16[256,512]{1,0:T(8,128)(2,1)} %bitcast.12), custom_call_target="tpu_custom_call" | custom-call | bytes 2097152 | tf_op jit(solution)/shard_map/pallas_call | solution.py:69
  3.0 19.4 %all_to_all.20.own_ref = bf16[4,2,256,128]{3,2,1,0:T(8,128)(2,1)S(1)} all-to-all(bf16[4,2,256,128]{3,2,1,0:T(8,128)(2,1)} %get-tuple-element.17), channel_id=1, replica_groups={{0,4,8,12},{16,20,24,28},{32,36,40,44},{48,52,56,60},{64,68,72,76},{80,..., dimensions={0} | all-to-all | bytes 1048576 | tf_op jit(solution)/shard_map/all_to_all | solution.py:278
  22.4 0.7 collective-permute-start.1
  23.1 4.8 %collective-permute-start = (bf16[4,2,256,128]{3,2,1,0:T(8,128)(2,1)S(1)}, bf16[4,2,256,128]{3,2,1,0:T(8,128)(2,1)S(1)}, u32[]{:S(2)}, u32[]{:S(2)}) collective-permute-start(bf16[4,2,256,128]{3,2,1,0:T(8,128)(2,1)S(1)} %all_to_all.20.own_ref), channel_id=1, source_target_pairs={{0,28},{1,29},{2,30},{3,31},{4,24},{5,25},{6,26},{7,27},{8,20},{9,... | collective-permute-start | bytes 1572872 | tf_op jit(solution)/shard_map/ppermute | solution.py:275
  27.9 0.0 collective-permute-done.1
  27.9 4.3 %collective-permute-start.2 = (bf16[3,2,256,128]{3,2,1,0:T(8,128)(2,1)S(1)}, bf16[3,2,256,128]{3,2,1,0:T(8,128)(2,1)S(1)}, u32[]{:S(2)}, u32[]{:S(2)}) collective-permute-start(bf16[3,2,256,128]{3,2,1,0:T(8,128)(2,1)S(1)} %broadcast_select_fusion), channel_id=1, source_target_pairs={{0,32},{1,33},{2,34},{3,35},{4,36},{5,37},{6,38},{7,39},{8,40},{9,... | collective-permute-start | bytes 1179656 | tf_op jit(solution)/shard_map/ppermute | solution.py:275
  32.2 3.6 %all-to-all-start = ((bf16[4,2,256,128]{3,2,1,0:T(8,128)(2,1)}), bf16[4,2,256,128]{3,2,1,0:T(8,128)(2,1)S(1)}, u32[]{:S(2)}, u32[]{:S(2)}) async-start(bf16[4,2,256,128]{3,2,1,0:T(8,128)(2,1)} %get-tuple-element.16), calls=%async_computation | async-start | bytes 1048576 | tf_op jit(solution)/shard_map/all_to_all | solution.py:278
  35.9 2.2 %shard_map.77 = (s32[4,256]{1,0:T(4,128)}, s32[4]{0:T(128)}) custom-call(s32[1]{0:T(128)} %bitcast.2.range_ref, s32[1,32768]{1,0:T(1,128)} %seg_ref.1), custom_call_target="tpu_custom_call" | custom-call | bytes 1048576 | tf_op jit(solution)/shard_map/pallas_call | solution.py:112
  38.1 24.2 %collective-permute-done.last_ref = bf16[4,2,256,128]{3,2,1,0:T(8,128)(2,1)S(1)} collective-permute-done((bf16[4,2,256,128]{3,2,1,0:T(8,128)(2,1)S(1)}, bf16[4,2,256,128]{3,2,1,0:T(8,128)(2,1)S(1)}, u32[]{:S(2)}, u32[]{:S(2)}) %collective-permute-start) | collective-permute-done | bytes 524320 | tf_op jit(solution)/shard_map/ppermute | solution.py:275
  62.2 0.0 collective-permute-done.2.before_ref
  62.3 0.1 shard_map.79
  62.4 0.0 all-to-all-done.query_ref
  62.4 0.0 copy-start
  62.4 0.0 copy-start.1
  62.4 0.0 copy-start.2
  62.4 0.7 copy-done
  63.1 0.0 copy-done.1
  63.1 0.0 copy-done.2
  63.1 10.8 %shard_map.80 = (bf16[4,256,128]{2,1,0:T(8,128)(2,1)}, f32[4,256,128]{2,1,0:T(8,128)S(1)}, bf16[4,256,128]{2,1,0:T(8,128)(2,1)S(1)}, bf16[3,256,128]{2,1,0:T(8,128)(2,1)S(1)}) custom-call(s32[1]{0:T(128)} %bitcast.1.head_ref, s32[4]{0:T(128)S(1)} %copy-done.2, f32[4]{0:T(128)S(1)} %copy-done.1, s32[4,256]{1,0:T(4,128)S(1)} %copy-done, ...), custom_call_target="tpu_custom_call" | custom-call | flops 1000000000 | bytes 6291456 | tf_op jit(solution)/shard_map/pallas_call | solution.py:240
  73.9 4.8 %collective-permute-start.3 = (bf16[4,256,128]{2,1,0:T(8,128)(2,1)S(1)}, bf16[4,256,128]{2,1,0:T(8,128)(2,1)S(1)}, u32[]{:S(2)}, u32[]{:S(2)}) collective-permute-start(bf16[4,256,128]{2,1,0:T(8,128)(2,1)S(1)} %get-tuple-element.22), channel_id=1, source_target_pairs={{28,0},{29,1},{30,2},{31,3},{24,4},{25,5},{26,6},{27,7},{20,8},{21... | collective-permute-start | bytes 786440 | tf_op jit(solution)/shard_map/ppermute | solution.py:275
  78.7 1.9 %collective-permute-start.4 = (bf16[3,256,128]{2,1,0:T(8,128)(2,1)S(1)}, bf16[3,256,128]{2,1,0:T(8,128)(2,1)S(1)}, u32[]{:S(2)}, u32[]{:S(2)}) collective-permute-start(bf16[3,256,128]{2,1,0:T(8,128)(2,1)S(1)} %get-tuple-element.23), channel_id=1, source_target_pairs={{32,0},{33,1},{34,2},{35,3},{36,4},{37,5},{38,6},{39,7},{40,8},{41... | collective-permute-start | bytes 589832 | tf_op jit(solution)/shard_map/ppermute | solution.py:275
  80.6 3.4 %all-to-all-start.2 = ((bf16[4,256,128]{2,1,0:T(8,128)(2,1)}), bf16[4,256,128]{2,1,0:T(8,128)(2,1)S(1)}, u32[]{:S(2)}, u32[]{:S(2)}) async-start(bf16[4,256,128]{2,1,0:T(8,128)(2,1)} %get-tuple-element.20), calls=%async_computation.2 | async-start | bytes 524288 | tf_op jit(solution)/shard_map/all_to_all | solution.py:278
  84.0 2.2 %collective-permute-done.4 = bf16[3,256,128]{2,1,0:T(8,128)(2,1)S(1)} collective-permute-done((bf16[3,256,128]{2,1,0:T(8,128)(2,1)S(1)}, bf16[3,256,128]{2,1,0:T(8,128)(2,1)S(1)}, u32[]{:S(2)}, u32[]{:S(2)}) %collective-permute-start.4) | collective-permute-done | bytes 196640 | tf_op jit(solution)/shard_map/ppermute | solution.py:275
  86.2 0.5 collective-permute-done.3
  86.7 0.1 add_convert_fusion
  86.8 4.0 %all-to-all-done.2.dq_ref = bf16[4,256,128]{2,1,0:T(8,128)(2,1)S(1)} async-done(((bf16[4,256,128]{2,1,0:T(8,128)(2,1)}), bf16[4,256,128]{2,1,0:T(8,128)(2,1)S(1)}, u32[]{:S(2)}, u32[]{:S(2)}) %all-to-all-start.2) | async-done | bytes 262176 | tf_op jit(solution)/shard_map/all_to_all | solution.py:278
  90.8 0.0 copy-start.3
  90.8 10.5 %all_to_all.21.dk_ref = bf16[4,256,128]{2,1,0:T(8,128)(2,1)} all-to-all(bf16[4,256,128]{2,1,0:T(8,128)(2,1)S(1)} %add_convert_fusion), channel_id=1, replica_groups={{0,4,8,12},{16,20,24,28},{32,36,40,44},{48,52,56,60},{64,68,72,76},{80,..., dimensions={0} | all-to-all | bytes 524288 | tf_op jit(solution)/shard_map/all_to_all | solution.py:278
  101.2 0.0 copy-done.3
  101.2 2.1 %shard_map.81 = (f32[256,512]{1,0:T(8,128)}, f32[256,512]{1,0:T(8,128)}) custom-call(s32[1]{0:T(128)} %bitcast.flip_ref, bf16[4,256,128]{2,1,0:T(8,128)(2,1)} %copy-done.3, bf16[4,256,128]{2,1,0:T(8,128)(2,1)} %all_to_all.21.dk_ref), custom_call_target="tpu_custom_call" | custom-call | bytes 1572864 | tf_op jit(solution)/shard_map/pallas_call | solution.py:129
  (2 shorter events, 0.1 us)
Async XLA Ops:
  22.4 5.5 %collective-permute-start.1 = (bf16[3,2,256,128]{3,2,1,0:T(8,128)(2,1)S(1)}, bf16[3,2,256,128]{3,2,1,0:T(8,128)(2,1)S(1)}, u32[]{:S(2)}, u32[]{:S(2)}) collective-permute-start(bf16[3,2,256,128]{3,2,1,0:T(8,128)(2,1)S(1)} %slice.4), channel_id=1, source_target_pairs={{224,480},{225,481},{226,482},{227,483},{228,484},{229,485},{230,4... | collective-permute-start | bytes 1179656 | tf_op jit(solution)/shard_map/ppermute | solution.py:275
  23.1 39.2 %collective-permute-start = (bf16[4,2,256,128]{3,2,1,0:T(8,128)(2,1)S(1)}, bf16[4,2,256,128]{3,2,1,0:T(8,128)(2,1)S(1)}, u32[]{:S(2)}, u32[]{:S(2)}) collective-permute-start(bf16[4,2,256,128]{3,2,1,0:T(8,128)(2,1)S(1)} %all_to_all.20.own_ref), channel_id=1, source_target_pairs={{0,28},{1,29},{2,30},{3,31},{4,24},{5,25},{6,26},{7,27},{8,20},{9,... | collective-permute-start | bytes 1572872 | tf_op jit(solution)/shard_map/ppermute | solution.py:275
  27.9 34.3 %collective-permute-start.2 = (bf16[3,2,256,128]{3,2,1,0:T(8,128)(2,1)S(1)}, bf16[3,2,256,128]{3,2,1,0:T(8,128)(2,1)S(1)}, u32[]{:S(2)}, u32[]{:S(2)}) collective-permute-start(bf16[3,2,256,128]{3,2,1,0:T(8,128)(2,1)S(1)} %broadcast_select_fusion), channel_id=1, source_target_pairs={{0,32},{1,33},{2,34},{3,35},{4,36},{5,37},{6,38},{7,39},{8,40},{9,... | collective-permute-start | bytes 1179656 | tf_op jit(solution)/shard_map/ppermute | solution.py:275
  32.2 30.2 %all-to-all-start = ((bf16[4,2,256,128]{3,2,1,0:T(8,128)(2,1)}), bf16[4,2,256,128]{3,2,1,0:T(8,128)(2,1)S(1)}, u32[]{:S(2)}, u32[]{:S(2)}) async-start(bf16[4,2,256,128]{3,2,1,0:T(8,128)(2,1)} %get-tuple-element.16), calls=%async_computation | async-start | bytes 1048576 | tf_op jit(solution)/shard_map/all_to_all | solution.py:278
  62.4 0.7 copy-start
  62.4 0.7 copy-start.1
  62.4 0.7 copy-start.2
  73.9 12.9 %collective-permute-start.3 = (bf16[4,256,128]{2,1,0:T(8,128)(2,1)S(1)}, bf16[4,256,128]{2,1,0:T(8,128)(2,1)S(1)}, u32[]{:S(2)}, u32[]{:S(2)}) collective-permute-start(bf16[4,256,128]{2,1,0:T(8,128)(2,1)S(1)} %get-tuple-element.22), channel_id=1, source_target_pairs={{28,0},{29,1},{30,2},{31,3},{24,4},{25,5},{26,6},{27,7},{20,8},{21... | collective-permute-start | bytes 786440 | tf_op jit(solution)/shard_map/ppermute | solution.py:275
  78.7 7.6 %collective-permute-start.4 = (bf16[3,256,128]{2,1,0:T(8,128)(2,1)S(1)}, bf16[3,256,128]{2,1,0:T(8,128)(2,1)S(1)}, u32[]{:S(2)}, u32[]{:S(2)}) collective-permute-start(bf16[3,256,128]{2,1,0:T(8,128)(2,1)S(1)} %get-tuple-element.23), channel_id=1, source_target_pairs={{32,0},{33,1},{34,2},{35,3},{36,4},{37,5},{38,6},{39,7},{40,8},{41... | collective-permute-start | bytes 589832 | tf_op jit(solution)/shard_map/ppermute | solution.py:275
  80.6 10.2 %all-to-all-start.2 = ((bf16[4,256,128]{2,1,0:T(8,128)(2,1)}), bf16[4,256,128]{2,1,0:T(8,128)(2,1)S(1)}, u32[]{:S(2)}, u32[]{:S(2)}) async-start(bf16[4,256,128]{2,1,0:T(8,128)(2,1)} %get-tuple-element.20), calls=%async_computation.2 | async-start | bytes 524288 | tf_op jit(solution)/shard_map/all_to_all | solution.py:278
  90.8 10.5 %copy-start.3 = (bf16[4,256,128]{2,1,0:T(8,128)(2,1)}, bf16[4,256,128]{2,1,0:T(8,128)(2,1)S(1)}, u32[]{:S(2)}) copy-start(bf16[4,256,128]{2,1,0:T(8,128)(2,1)S(1)} %all-to-all-done.2.dq_ref) | copy-start | bytes 786436

commit v8 on v7

--- a/solution.py
+++ b/solution.py
@@ -28,7 +28,7 @@
 def routes(seq, dp):
     rings = seq // RING
     seam = rings // 2 - 1 if dp == 4 else None
-    last, before_last, relay = [], [], []
+    last, before_last, relay, cross = [], [], [], []
     for ring in range(rings):
         for y in range(RING):
             for part in range(dp):
@@ -39,12 +39,11 @@
                 if ring + 1 < rings:
                     target = ((ring + 1) * RING + y) * dp + part
                     if ring == seam:
-                        over = ((rings - 1) * RING + y) * dp + part
-                        relay.append((me, over))
-                        before_last.append((over, target))
+                        relay.append((me, y * dp + part))
+                        cross.append((y * dp + part, target))
                     else:
                         before_last.append((me, target))
-    return last, before_last, relay
+    return last, before_last, relay, cross
 
 
 def reverse(route):
@@ -135,32 +134,42 @@
     )(flip, dq, dk)
 
 
-def layout_kernel(own_ref, last_ref, before_ref, kt, ks):
+def layout_kernel(crossed_ref, own_ref, last_ref, before_ref, cross_ref, kt, ks):
     def load(block, teacher, student):
         here = pl.ds(block * TOK, TOK)
         kt[here, :] = teacher
         ks[here, :] = student
 
     load(0, jnp.zeros((TOK, DIM), BF16), jnp.zeros((TOK, DIM), BF16))
-    for i in range(LINE - 1):
-        load(1 + i, before_ref[i, 0], before_ref[i, 1])
+    crossed = crossed_ref[0] == 1
+
+    @pl.when(crossed)
+    def _():
+        for i in range(LINE - 1):
+            load(1 + i, cross_ref[i, 0], cross_ref[i, 1])
+
+    @pl.when(jnp.logical_not(crossed))
+    def _():
+        for i in range(LINE - 1):
+            load(1 + i, before_ref[i, 0], before_ref[i, 1])
+
     for i in range(LINE):
         load(LINE + i, last_ref[i, 0], last_ref[i, 1])
         load(OWN + i, own_ref[i, 0], own_ref[i, 1])
 
 
-def layout(own, last, before):
+def layout(crossed, own, last, before, cross):
     return pl.pallas_call(
         layout_kernel,
         out_shape=[
             jax.ShapeDtypeStruct((BAND * TOK, DIM), BF16),
             jax.ShapeDtypeStruct((BAND * TOK, DIM), BF16),
         ],
-        in_specs=[VMEM] * 3,
+        in_specs=[SMEM] + [VMEM] * 4,
         out_specs=[VMEM] * 2,
         compiler_params=pltpu.CompilerParams(vmem_limit_bytes=6 * 1024 * 1024),
         cost_estimate=pl.CostEstimate(flops=10**10, bytes_accessed=16 * 2**20, transcendentals=0),
-    )(own, last, before)
+    )(crossed, own, last, before, cross)
 
 
 def main_kernel(
@@ -262,7 +271,7 @@
 
 
 def per_device(seq, dp, teacher_query, teacher_key, student_query, student_key, segment_ids, head_weight):
-    to_next, to_second, relay = routes(seq, dp)
+    to_next, to_second, relay, to_cross = routes(seq, dp)
     to_second_straight = [(i, i + RING * dp) for i in range((seq - RING) * dp)]
     lines = [list(range(i, i + LINE)) for i in range(0, seq, LINE)]
     seq_index = lax.axis_index("seq")
@@ -282,13 +291,14 @@
     own = exchange(keys)
     last = move(own, to_next)
     parting = own[1:]
+    before = cross = move(parting, to_second)
     if relay:
-        relays = seq_index >= seq - RING
-        parting = jnp.where(relays, move(parting, relay), parting)
-    before = move(parting, to_second)
+        cross = move(move(parting, relay), to_cross)
+    crossed = (seq_index // RING == seq // RING // 2) & (len(relay) > 0)
+    keys = layout(crossed.astype(jnp.int32).reshape(1), own, last, before, cross)
     start, low = starts(range_index, segment_ids)
     queries = exchange(queries)
-    dq, dk_own, dk_last, dk_before = attend(head, low, head_weight, start, queries, *layout(own, last, before))
+    dq, dk_own, dk_last, dk_before = attend(head, low, head_weight, start, queries, *keys)
 
     back_last = move(dk_last, reverse(to_next)).astype(F32)
     back_before = move(dk_before, reverse(to_second_straight)).astype(F32)

time: 105 us -> 109 us (1.038)
  blocking collectives: 29.8 us -> 33.2 us
  Pallas kernels: 17.5 us -> 15.2 us
  local copies, waits for them, and re-layouts: 0.72 us -> 2.73 us
  starting transfers between devices: 23.5 us -> 25.1 us
    all_to_all x2, blocking collectives: 29.8 us -> 33.2 us  [exchange(): return lax.all_to_all(x, 'seq', 0, 0, axis_index_groups=lines)]
    pallas_call x1, Pallas kernels: 10.8 us -> 8.49 us  [attend(): pl.pallas_call(main_kernel, out_shape=[jax.ShapeDtypeStruct((LINE, TOK, D...]
    all_to_all x2, waiting for transfers between devices: 3.96 us -> 6.11 us  [exchange(): return lax.all_to_all(x, 'seq', 0, 0, axis_index_groups=lines)]
    unnamed x8 -> x12, local copies, waits for them, and re-layouts: 0.69 us -> 2.7 us
    ppermute x5 -> x6, waiting for transfers between devices: 26.9 us -> 25 us  [move(): return lax.ppermute(x, AXES, route)]
    ppermute x5 -> x6, starting transfers between devices: 16.5 us -> 18.1 us  [move(): return lax.ppermute(x, AXES, route)]
  transfers between devices with their start and end apart: 7 -> 8, of which waited for: 4 -> 6; matrix products, arithmetic and copies ran while one was open for 0% -> 0% of each run, Pallas kernels for 2% -> 2%
where the time goes in v8:
time: 109 us; the launch traced here: 108 us
  blocking collectives  33.2 us (30%)
  waiting for transfers between devices  31.2 us (29%)
  starting transfers between devices  25.1 us (23%)
  Pallas kernels  15.2 us (14%)
  local copies, waits for them, and re-layouts  2.73 us (3%)
    all_to_all x2, blocking collectives, exchange(): return lax.all_to_all(x, 'seq', 0, 0, axis_index_groups=lines)  33.2 us
    ppermute x6, waiting for transfers between devices, move(): return lax.ppermute(x, AXES, route)  25 us
    ppermute x6, starting transfers between devices, move(): return lax.ppermute(x, AXES, route)  18.1 us
    pallas_call x1, Pallas kernels, attend(): pl.pallas_call(main_kernel, out_shape=[jax.ShapeDtypeStruct((LINE, TOK, D...  8.49 us
    all_to_all x2, starting transfers between devices, exchange(): return lax.all_to_all(x, 'seq', 0, 0, axis_index_groups=lines)  7.07 us
    all_to_all x2, waiting for transfers between devices, exchange(): return lax.all_to_all(x, 'seq', 0, 0, axis_index_groups=lines)  6.11 us
    unnamed x12, local copies, waits for them, and re-layouts  2.7 us
    pallas_call x1, Pallas kernels, pack(): pl.pallas_call(pack_kernel, out_shape=[jax.ShapeDtypeStruct((HEADS, 2, TO...  2.34 us
  transfers between devices with their start and end apart: 8, of which 6 were waited for; matrix products, arithmetic and copies ran while one was open for 0% of the time, Pallas kernels for 2%

profile of v8, /device:TPU:6, one launch (start us, length us, event | category | flops | bytes accessed | tf_op | source)
XLA Modules:
  0.0 108.3 jit_solution(14146841918035626354)
XLA Ops:
  0.7 2.3 %shard_map.78 = (bf16[4,2,256,128]{3,2,1,0:T(8,128)(2,1)}, bf16[4,2,256,128]{3,2,1,0:T(8,128)(2,1)}) custom-call(s32[1]{0:T(128)} %bitcast.flip_ref, bf16[256,512]{1,0:T(8,128)(2,1)} %bitcast.10, bf16[256,512]{1,0:T(8,128)(2,1)} %bitcast.11, bf16[256,512]{1,0:T(8,128)(2,1)} %bitcast.12, bf16[256,512]{1,0:T(8,128)(2,1)} %bitcast.13), custom_call_target="tpu_custom_call" | custom-call | bytes 2097152 | tf_op jit(solution)/shard_map/pallas_call | solution.py:68
  3.0 19.4 %all_to_all.20.own_ref = bf16[4,2,256,128]{3,2,1,0:T(8,128)(2,1)S(1)} all-to-all(bf16[4,2,256,128]{3,2,1,0:T(8,128)(2,1)} %get-tuple-element.17), channel_id=1, replica_groups={{0,4,8,12},{16,20,24,28},{32,36,40,44},{48,52,56,60},{64,68,72,76},{80,..., dimensions={0} | all-to-all | bytes 1048576 | tf_op jit(solution)/shard_map/all_to_all | solution.py:287
  22.4 0.7 collective-permute-start.2
  23.1 4.8 %collective-permute-start = (bf16[4,2,256,128]{3,2,1,0:T(8,128)(2,1)S(1)}, bf16[4,2,256,128]{3,2,1,0:T(8,128)(2,1)S(1)}, u32[]{:S(2)}, u32[]{:S(2)}) collective-permute-start(bf16[4,2,256,128]{3,2,1,0:T(8,128)(2,1)S(1)} %all_to_all.20.own_ref), channel_id=1, source_target_pairs={{0,28},{1,29},{2,30},{3,31},{4,24},{5,25},{6,26},{7,27},{8,20},{9,... | collective-permute-start | bytes 1572872 | tf_op jit(solution)/shard_map/ppermute | solution.py:284
  27.9 4.3 %collective-permute-start.1 = (bf16[3,2,256,128]{3,2,1,0:T(8,128)(2,1)S(1)}, bf16[3,2,256,128]{3,2,1,0:T(8,128)(2,1)S(1)}, u32[]{:S(2)}, u32[]{:S(2)}) collective-permute-start(bf16[3,2,256,128]{3,2,1,0:T(8,128)(2,1)S(1)} %slice.4), channel_id=1, source_target_pairs={{0,32},{1,33},{2,34},{3,35},{4,36},{5,37},{6,38},{7,39},{8,40},{9,... | collective-permute-start | bytes 1179656 | tf_op jit(solution)/shard_map/ppermute | solution.py:284
  32.2 0.0 collective-permute-done.2
  32.2 1.3 %collective-permute-start.3 = (bf16[3,2,256,128]{3,2,1,0:T(8,128)(2,1)S(1)}, bf16[3,2,256,128]{3,2,1,0:T(8,128)(2,1)S(1)}, u32[]{:S(2)}, u32[]{:S(2)}) collective-permute-start(bf16[3,2,256,128]{3,2,1,0:T(8,128)(2,1)S(1)} %collective-permute-done.2), channel_id=1, source_target_pairs={{0,256},{1,257},{2,258},{3,259},{4,260},{5,261},{6,262},{7,263},{8... | collective-permute-start | bytes 1179656 | tf_op jit(solution)/shard_map/ppermute | solution.py:284
  33.5 3.6 %all-to-all-start = ((bf16[4,2,256,128]{3,2,1,0:T(8,128)(2,1)}), bf16[4,2,256,128]{3,2,1,0:T(8,128)(2,1)S(1)}, u32[]{:S(2)}, u32[]{:S(2)}) async-start(bf16[4,2,256,128]{3,2,1,0:T(8,128)(2,1)} %get-tuple-element.16), calls=%async_computation | async-start | bytes 1048576 | tf_op jit(solution)/shard_map/all_to_all | solution.py:287
  37.1 2.2 %shard_map.77 = (s32[4,256]{1,0:T(4,128)}, s32[4]{0:T(128)}) custom-call(s32[1]{0:T(128)} %bitcast.2.range_ref, s32[1,32768]{1,0:T(1,128)} %seg_ref.1), custom_call_target="tpu_custom_call" | custom-call | bytes 1048576 | tf_op jit(solution)/shard_map/pallas_call | solution.py:111
  39.3 0.7 collective-permute-done.1.before_ref
  40.1 19.8 %collective-permute-done.last_ref = bf16[4,2,256,128]{3,2,1,0:T(8,128)(2,1)S(1)} collective-permute-done((bf16[4,2,256,128]{3,2,1,0:T(8,128)(2,1)S(1)}, bf16[4,2,256,128]{3,2,1,0:T(8,128)(2,1)S(1)}, u32[]{:S(2)}, u32[]{:S(2)}) %collective-permute-start) | collective-permute-done | bytes 524320 | tf_op jit(solution)/shard_map/ppermute | solution.py:284
  59.9 2.0 %collective-permute-done.3.cross_ref = bf16[3,2,256,128]{3,2,1,0:T(8,128)(2,1)S(1)} collective-permute-done((bf16[3,2,256,128]{3,2,1,0:T(8,128)(2,1)S(1)}, bf16[3,2,256,128]{3,2,1,0:T(8,128)(2,1)S(1)}, u32[]{:S(2)}, u32[]{:S(2)}) %collective-permute-start.3) | collective-permute-done | bytes 393248 | tf_op jit(solution)/shard_map/ppermute | solution.py:284
  61.9 0.1 shard_map.79
  62.0 0.0 copy-start.3
  62.0 0.9 copy-done.3
  62.9 0.0 all-to-all-done.query_ref
  62.9 0.0 copy-start
  62.9 0.0 copy-start.1
  62.9 0.0 copy-start.2
  62.9 0.7 copy-done
  63.6 0.0 copy-done.1
  63.6 0.0 copy-done.2
  63.6 0.0 copy-start.4
  63.6 1.1 %copy-done.4 = bf16[3072,128]{1,0:T(8,128)(2,1)S(1)} copy-done((bf16[3072,128]{1,0:T(8,128)(2,1)S(1)}, bf16[3072,128]{1,0:T(8,128)(2,1)}, u32[]{:S(2)}) %copy-start.4) | copy-done | bytes 786456
  64.8 8.5 %shard_map.80 = (bf16[4,256,128]{2,1,0:T(8,128)(2,1)}, f32[4,256,128]{2,1,0:T(8,128)S(1)}, bf16[4,256,128]{2,1,0:T(8,128)(2,1)S(1)}, bf16[3,256,128]{2,1,0:T(8,128)(2,1)S(1)}) custom-call(s32[1]{0:T(128)} %bitcast.1.head_ref, s32[4]{0:T(128)S(1)} %copy-done.2, f32[4]{0:T(128)S(1)} %copy-done.1, s32[4,256]{1,0:T(4,128)S(1)} %copy-done, ...), custom_call_target="tpu_custom_call" | custom-call | flops 1000000000 | bytes 6291456 | tf_op jit(solution)/shard_map/pallas_call | solution.py:249
  73.2 2.6 %collective-permute-start.4 = (bf16[4,256,128]{2,1,0:T(8,128)(2,1)S(1)}, bf16[4,256,128]{2,1,0:T(8,128)(2,1)S(1)}, u32[]{:S(2)}, u32[]{:S(2)}) collective-permute-start(bf16[4,256,128]{2,1,0:T(8,128)(2,1)S(1)} %get-tuple-element.22), channel_id=1, source_target_pairs={{28,0},{29,1},{30,2},{31,3},{24,4},{25,5},{26,6},{27,7},{20,8},{21... | collective-permute-start | bytes 786440 | tf_op jit(solution)/shard_map/ppermute | solution.py:284
  75.9 4.4 %collective-permute-start.5 = (bf16[3,256,128]{2,1,0:T(8,128)(2,1)S(1)}, bf16[3,256,128]{2,1,0:T(8,128)(2,1)S(1)}, u32[]{:S(2)}, u32[]{:S(2)}) collective-permute-start(bf16[3,256,128]{2,1,0:T(8,128)(2,1)S(1)} %get-tuple-element.23), channel_id=1, source_target_pairs={{32,0},{33,1},{34,2},{35,3},{36,4},{37,5},{38,6},{39,7},{40,8},{41... | collective-permute-start | bytes 589832 | tf_op jit(solution)/shard_map/ppermute | solution.py:284
  80.3 3.4 %all-to-all-start.2 = ((bf16[4,256,128]{2,1,0:T(8,128)(2,1)}), bf16[4,256,128]{2,1,0:T(8,128)(2,1)S(1)}, u32[]{:S(2)}, u32[]{:S(2)}) async-start(bf16[4,256,128]{2,1,0:T(8,128)(2,1)} %get-tuple-element.20), calls=%async_computation.2 | async-start | bytes 524288 | tf_op jit(solution)/shard_map/all_to_all | solution.py:287
  83.7 0.8 collective-permute-done.5
  84.5 1.6 %collective-permute-done.4 = bf16[4,256,128]{2,1,0:T(8,128)(2,1)S(1)} collective-permute-done((bf16[4,256,128]{2,1,0:T(8,128)(2,1)S(1)}, bf16[4,256,128]{2,1,0:T(8,128)(2,1)S(1)}, u32[]{:S(2)}, u32[]{:S(2)}) %collective-permute-start.4) | collective-permute-done | bytes 262176 | tf_op jit(solution)/shard_map/ppermute | solution.py:284
  86.1 0.1 add_convert_fusion
  86.2 6.1 %all-to-all-done.2.dq_ref = bf16[4,256,128]{2,1,0:T(8,128)(2,1)S(1)} async-done(((bf16[4,256,128]{2,1,0:T(8,128)(2,1)}), bf16[4,256,128]{2,1,0:T(8,128)(2,1)S(1)}, u32[]{:S(2)}, u32[]{:S(2)}) %all-to-all-start.2) | async-done | bytes 262176 | tf_op jit(solution)/shard_map/all_to_all | solution.py:287
  92.3 0.0 copy-start.5
  92.3 13.8 %all_to_all.21.dk_ref = bf16[4,256,128]{2,1,0:T(8,128)(2,1)} all-to-all(bf16[4,256,128]{2,1,0:T(8,128)(2,1)S(1)} %add_convert_fusion), channel_id=1, replica_groups={{0,4,8,12},{16,20,24,28},{32,36,40,44},{48,52,56,60},{64,68,72,76},{80,..., dimensions={0} | all-to-all | bytes 524288 | tf_op jit(solution)/shard_map/all_to_all | solution.py:287
  106.1 0.0 copy-done.5
  106.1 2.1 %shard_map.81 = (f32[256,512]{1,0:T(8,128)}, f32[256,512]{1,0:T(8,128)}) custom-call(s32[1]{0:T(128)} %bitcast.flip_ref, bf16[4,256,128]{2,1,0:T(8,128)(2,1)} %copy-done.5, bf16[4,256,128]{2,1,0:T(8,128)(2,1)} %all_to_all.21.dk_ref), custom_call_target="tpu_custom_call" | custom-call | bytes 1572864 | tf_op jit(solution)/shard_map/pallas_call | solution.py:128
  (1 shorter events, 0.0 us)
Async XLA Ops:
  22.4 9.8 %collective-permute-start.2 = (bf16[3,2,256,128]{3,2,1,0:T(8,128)(2,1)S(1)}, bf16[3,2,256,128]{3,2,1,0:T(8,128)(2,1)S(1)}, u32[]{:S(2)}, u32[]{:S(2)}) collective-permute-start(bf16[3,2,256,128]{3,2,1,0:T(8,128)(2,1)S(1)} %slice.4), channel_id=1, source_target_pairs={{224,0},{225,1},{226,2},{227,3},{228,4},{229,5},{230,6},{231,7},{2... | collective-permute-start | bytes 1179656 | tf_op jit(solution)/shard_map/ppermute | solution.py:284
  23.1 36.8 %collective-permute-start = (bf16[4,2,256,128]{3,2,1,0:T(8,128)(2,1)S(1)}, bf16[4,2,256,128]{3,2,1,0:T(8,128)(2,1)S(1)}, u32[]{:S(2)}, u32[]{:S(2)}) collective-permute-start(bf16[4,2,256,128]{3,2,1,0:T(8,128)(2,1)S(1)} %all_to_all.20.own_ref), channel_id=1, source_target_pairs={{0,28},{1,29},{2,30},{3,31},{4,24},{5,25},{6,26},{7,27},{8,20},{9,... | collective-permute-start | bytes 1572872 | tf_op jit(solution)/shard_map/ppermute | solution.py:284
  27.9 12.2 %collective-permute-start.1 = (bf16[3,2,256,128]{3,2,1,0:T(8,128)(2,1)S(1)}, bf16[3,2,256,128]{3,2,1,0:T(8,128)(2,1)S(1)}, u32[]{:S(2)}, u32[]{:S(2)}) collective-permute-start(bf16[3,2,256,128]{3,2,1,0:T(8,128)(2,1)S(1)} %slice.4), channel_id=1, source_target_pairs={{0,32},{1,33},{2,34},{3,35},{4,36},{5,37},{6,38},{7,39},{8,40},{9,... | collective-permute-start | bytes 1179656 | tf_op jit(solution)/shard_map/ppermute | solution.py:284
  32.2 29.7 %collective-permute-start.3 = (bf16[3,2,256,128]{3,2,1,0:T(8,128)(2,1)S(1)}, bf16[3,2,256,128]{3,2,1,0:T(8,128)(2,1)S(1)}, u32[]{:S(2)}, u32[]{:S(2)}) collective-permute-start(bf16[3,2,256,128]{3,2,1,0:T(8,128)(2,1)S(1)} %collective-permute-done.2), channel_id=1, source_target_pairs={{0,256},{1,257},{2,258},{3,259},{4,260},{5,261},{6,262},{7,263},{8... | collective-permute-start | bytes 1179656 | tf_op jit(solution)/shard_map/ppermute | solution.py:284
  33.5 29.4 %all-to-all-start = ((bf16[4,2,256,128]{3,2,1,0:T(8,128)(2,1)}), bf16[4,2,256,128]{3,2,1,0:T(8,128)(2,1)S(1)}, u32[]{:S(2)}, u32[]{:S(2)}) async-start(bf16[4,2,256,128]{3,2,1,0:T(8,128)(2,1)} %get-tuple-element.16), calls=%async_computation | async-start | bytes 1048576 | tf_op jit(solution)/shard_map/all_to_all | solution.py:287
  62.0 0.9 copy-start.3
  62.9 0.7 copy-start
  62.9 0.7 copy-start.1
  62.9 0.7 copy-start.2
  63.6 1.1 %copy-start.4 = (bf16[3072,128]{1,0:T(8,128)(2,1)S(1)}, bf16[3072,128]{1,0:T(8,128)(2,1)}, u32[]{:S(2)}) copy-start(bf16[3072,128]{1,0:T(8,128)(2,1)} %copy-done.3) | copy-start | bytes 2359300
  73.2 12.9 %collective-permute-start.4 = (bf16[4,256,128]{2,1,0:T(8,128)(2,1)S(1)}, bf16[4,256,128]{2,1,0:T(8,128)(2,1)S(1)}, u32[]{:S(2)}, u32[]{:S(2)}) collective-permute-start(bf16[4,256,128]{2,1,0:T(8,128)(2,1)S(1)} %get-tuple-element.22), channel_id=1, source_target_pairs={{28,0},{29,1},{30,2},{31,3},{24,4},{25,5},{26,6},{27,7},{20,8},{21... | collective-permute-start | bytes 786440 | tf_op jit(solution)/shard_map/ppermute | solution.py:284
  75.9 8.6 %collective-permute-start.5 = (bf16[3,256,128]{2,1,0:T(8,128)(2,1)S(1)}, bf16[3,256,128]{2,1,0:T(8,128)(2,1)S(1)}, u32[]{:S(2)}, u32[]{:S(2)}) collective-permute-start(bf16[3,256,128]{2,1,0:T(8,128)(2,1)S(1)} %get-tuple-element.23), channel_id=1, source_target_pairs={{32,0},{33,1},{34,2},{35,3},{36,4},{37,5},{38,6},{39,7},{40,8},{41... | collective-permute-start | bytes 589832 | tf_op jit(solution)/shard_map/ppermute | solution.py:284
  80.3 12.1 %all-to-all-start.2 = ((bf16[4,256,128]{2,1,0:T(8,128)(2,1)}), bf16[4,256,128]{2,1,0:T(8,128)(2,1)S(1)}, u32[]{:S(2)}, u32[]{:S(2)}) async-start(bf16[4,256,128]{2,1,0:T(8,128)(2,1)} %get-tuple-element.20), calls=%async_computation.2 | async-start | bytes 524288 | tf_op jit(solution)/shard_map/all_to_all | solution.py:287
  92.3 13.8 %copy-start.5 = (bf16[4,256,128]{2,1,0:T(8,128)(2,1)}, bf16[4,256,128]{2,1,0:T(8,128)(2,1)S(1)}, u32[]{:S(2)}) copy-start(bf16[4,256,128]{2,1,0:T(8,128)(2,1)S(1)} %all-to-all-done.2.dq_ref) | copy-start | bytes 786436

commit v9 on v4

--- a/solution.py
+++ b/solution.py
@@ -26,16 +26,17 @@
 
 
 def routes(seq, dp):
+    rings = seq // RING
     last, before_last = [], []
-    for ring in range(seq // RING):
+    for ring in range(rings):
         for y in range(RING):
             for part in range(dp):
                 me = (ring * RING + y) * dp + part
                 ahead = ring + (y >= LINE)
-                if ahead < seq // RING:
+                if ahead < rings:
                     last.append((me, (ahead * RING + RING - 1 - y) * dp + part))
-                if ring + 1 < seq // RING:
-                    before_last.append((me, ((ring + 1) * RING + y) * dp + part))
+                if ring + 1 < rings:
+                    before_last.append((me, me + RING * dp))
     return last, before_last
 
 
@@ -48,18 +49,31 @@
     return pl.ds(pl.multiple_of(head * DIM, DIM), DIM)
 
 
-def pack_keys_kernel(flip_ref, a_ref, b_ref, a_out_ref, b_out_ref):
+def pack_kernel(flip_ref, a_ref, b_ref, c_ref, d_ref, halo_ref, all_ref):
+    for place in range(HEADS):
+        columns = head_columns(1 - flip_ref[0], place)
+        halo_ref[place, 0] = a_ref[:, columns]
+        halo_ref[place, 1] = b_ref[:, columns]
     for place in range(HEADS):
         columns = head_columns(flip_ref[0], place)
-        a_out_ref[place] = a_ref[:, columns]
-        b_out_ref[place] = b_ref[:, columns]
-
-
-def pack_queries_kernel(flip_ref, range_ref, a_ref, b_ref, seg_ref, out_ref, start_ref, low_ref):
-    for place in range(HEADS):
-        columns = head_columns(flip_ref[0], place)
-        out_ref[place, 0] = a_ref[:, columns]
-        out_ref[place, 1] = b_ref[:, columns]
+        for i, ref in enumerate((a_ref, b_ref, c_ref, d_ref)):
+            all_ref[place, i] = ref[:, columns]
+
+
+def pack(flip, *states):
+    return pl.pallas_call(
+        pack_kernel,
+        out_shape=[
+            jax.ShapeDtypeStruct((HEADS, 2, TOK, DIM), BF16),
+            jax.ShapeDtypeStruct((HEADS, 4, TOK, DIM), BF16),
+        ],
+        in_specs=[SMEM] + [VMEM] * 4,
+        out_specs=[VMEM] * 2,
+        cost_estimate=pl.CostEstimate(flops=0, bytes_accessed=2**21, transcendentals=0),
+    )(flip, *states)
+
+
+def starts_kernel(range_ref, seg_ref, start_ref, low_ref):
     first_block = range_ref[0] * LINE
 
     def ids(block):
@@ -92,28 +106,14 @@
         low_ref[j] = jnp.min(start[j : j + 1, :])
 
 
-def pack_keys(flip, a, b):
+def starts(range_index, seg):
     return pl.pallas_call(
-        pack_keys_kernel,
-        out_shape=[jax.ShapeDtypeStruct((HEADS, TOK, DIM), BF16)] * 2,
-        in_specs=[SMEM, VMEM, VMEM],
-        out_specs=[VMEM] * 2,
+        starts_kernel,
+        out_shape=[jax.ShapeDtypeStruct((LINE, TOK), jnp.int32), jax.ShapeDtypeStruct((LINE,), jnp.int32)],
+        in_specs=[SMEM, VMEM],
+        out_specs=[VMEM, SMEM],
         cost_estimate=pl.CostEstimate(flops=0, bytes_accessed=2**20, transcendentals=0),
-    )(flip, a, b)
-
-
-def pack_queries(flip, range_index, a, b, seg):
-    return pl.pallas_call(
-        pack_queries_kernel,
-        out_shape=[
-            jax.ShapeDtypeStruct((HEADS, 2, TOK, DIM), BF16),
-            jax.ShapeDtypeStruct((LINE, TOK), jnp.int32),
-            jax.ShapeDtypeStruct((LINE,), jnp.int32),
-        ],
-        in_specs=[SMEM, SMEM, VMEM, VMEM, VMEM],
-        out_specs=[VMEM, VMEM, SMEM],
-        cost_estimate=pl.CostEstimate(flops=0, bytes_accessed=2**20, transcendentals=0),
-    )(flip, range_index, a, b, seg)
+    )(range_index, seg)
 
 
 def unpack_kernel(flip_ref, dq_ref, dk_ref, query_ref, key_ref):
@@ -134,7 +134,7 @@
 
 
 def main_kernel(
-    head_ref, low_ref, weight_ref, start_ref, query_ref, own_t_ref, own_s_ref, last_t_ref, last_s_ref, before_ref,
+    head_ref, low_ref, weight_ref, start_ref, all_ref, last_ref, before_ref,
     dq_ref, dk_own_ref, dk_last_ref, dk_before_ref,
     kt, ks, ks_turned, dk, et, es, top_t, top_s, dq_acc,
 ):
@@ -142,10 +142,11 @@
     scale = 1.0 / math.sqrt(DIM)
     pace = scale * math.log2(math.e)
     along_depth = (((1,), (1,)), ((), ()))
-    lowest = low_ref[0] // TOK
 
     def rows(block):
         return pl.ds(block * TOK, TOK)
+
+    lowest = low_ref[0] // TOK
 
     def load(block, teacher, student):
         kt[rows(block), :] = teacher
@@ -154,18 +155,15 @@
         dk[rows(block), :] = jnp.zeros((TOK, DIM), F32)
 
     def clear(block):
-        kt[rows(block), :] = jnp.zeros((TOK, DIM), BF16)
-        ks[rows(block), :] = jnp.zeros((TOK, DIM), BF16)
-        ks_turned[:, rows(block)] = jnp.zeros((DIM, TOK), BF16)
-        dk[rows(block), :] = jnp.zeros((TOK, DIM), F32)
+        load(block, jnp.zeros((TOK, DIM), BF16), jnp.zeros((TOK, DIM), BF16))
 
     for i in range(LINE):
-        load(OWN + i, own_t_ref[i], own_s_ref[i])
+        load(OWN + i, all_ref[i, 0], all_ref[i, 1])
 
     @pl.when(lowest <= OWN)
     def _():
         for i in range(LINE):
-            load(LINE + i, last_t_ref[i], last_s_ref[i])
+            load(LINE + i, last_ref[LINE - 1 - i, 0], last_ref[LINE - 1 - i, 1])
 
     @pl.when(lowest > OWN)
     def _():
@@ -175,7 +173,7 @@
     @pl.when(lowest <= LINE)
     def _():
         for i in range(LINE - 1):
-            load(1 + i, before_ref[0, i], before_ref[1, i])
+            load(1 + i, before_ref[i, 0], before_ref[i, 1])
 
     @pl.when(lowest > LINE)
     def _():
@@ -188,7 +186,7 @@
     for j in range(LINE):
         block = OWN + j
         pairs = (block + 2 - low_ref[j] // TOK) // 2
-        q_t, q_s = query_ref[j, 0], query_ref[j, 1]
+        q_t, q_s = all_ref[j, 2], all_ref[j, 3]
         start = start_ref[j : j + 1, :]
 
         def at(t):
@@ -239,7 +237,7 @@
         dk_before_ref[i] = (dk[rows(1 + i), :] * scale).astype(BF16)
 
 
-def attend(head, low, weight, start, queries, *keys):
+def attend(head, low, weight, start, *states):
     return pl.pallas_call(
         main_kernel,
         out_shape=[
@@ -248,7 +246,7 @@
             jax.ShapeDtypeStruct((LINE, TOK, DIM), BF16),
             jax.ShapeDtypeStruct((LINE - 1, TOK, DIM), BF16),
         ],
-        in_specs=[SMEM] * 3 + [VMEM] * 7,
+        in_specs=[SMEM] * 3 + [VMEM] * 4,
         out_specs=[VMEM] * 4,
         scratch_shapes=[
             pltpu.VMEM((BAND * TOK, DIM), BF16),
@@ -261,9 +259,9 @@
             pltpu.VMEM((LINE, 1, TOK), F32),
             pltpu.VMEM((DIM, TOK), F32),
         ],
-        compiler_params=pltpu.CompilerParams(vmem_limit_bytes=32 * 1024 * 1024),
+        compiler_params=pltpu.CompilerParams(vmem_limit_bytes=14 * 1024 * 1024),
         cost_estimate=pl.CostEstimate(flops=10**9, bytes_accessed=6 * 2**20, transcendentals=4 * 10**6),
-    )(head, low, weight, start, queries, *keys)
+    )(head, low, weight, start, *states)
 
 
 def per_device(seq, dp, teacher_query, teacher_key, student_query, student_key, segment_ids, head_weight):
@@ -282,15 +280,13 @@
         return lax.all_to_all(x, "seq", 0, 0, axis_index_groups=lines)
 
     flip, range_index, head = flip.reshape(1), range_index.reshape(1), head.reshape(1)
-    own_t, own_s = [exchange(x) for x in pack_keys(flip, teacher_key[0], student_key[0])]
-    last_t, last_s = move(own_t, to_next), move(own_s, to_next)
-    before = move(jnp.stack([own_t[1:], own_s[1:]]), to_second)
-    teacher_query, own_s = lax.optimization_barrier((teacher_query, own_s))
-    packed, start, low = pack_queries(flip, range_index, teacher_query[0], student_query[0], segment_ids)
-    queries = exchange(packed)
-    dq, dk_own, dk_last, dk_before = attend(
-        head, low, head_weight, start, queries, own_t, own_s, last_t, last_s, before
-    )
+    halo, states = pack(flip, teacher_key[0], student_key[0], teacher_query[0], student_query[0])
+    halo = move(halo, to_next)
+    states = exchange(states)
+    before = move(states[1:, :2], to_second)
+    last = exchange(halo)
+    start, low = starts(range_index, segment_ids)
+    dq, dk_own, dk_last, dk_before = attend(head, low, head_weight, start, states, last, before)
 
     back_last = move(dk_last, reverse(to_next)).astype(F32)
     back_before = move(dk_before, reverse(to_second)).astype(F32)

time: 114 us -> 110 us (0.965)
  the two profiles are of different devices: /device:TPU:4 before, /device:TPU:6 now
where the time goes in v9:
time: 110 us; the launch traced here: 109 us
  waiting for transfers between devices  41.7 us (38%)
  starting transfers between devices  38.9 us (35%)
  Pallas kernels  15 us (14%)
  blocking collectives  12.2 us (11%)
    ppermute x4, waiting for transfers between devices, move(): return lax.ppermute(x, AXES, route)  30.5 us
    all_to_all x3, starting transfers between devices, exchange(): return lax.all_to_all(x, 'seq', 0, 0, axis_index_groups=lines)  25.9 us
    ppermute x4, starting transfers between devices, move(): return lax.ppermute(x, AXES, route)  13 us
    all_to_all x1, blocking collectives, exchange(): return lax.all_to_all(x, 'seq', 0, 0, axis_index_groups=lines)  12.2 us
    all_to_all x3, waiting for transfers between devices, exchange(): return lax.all_to_all(x, 'seq', 0, 0, axis_index_groups=lines)  11.3 us
    pallas_call x1, Pallas kernels, attend(): pl.pallas_call(main_kernel, out_shape=[jax.ShapeDtypeStruct((LINE, TOK, D...  8.06 us
    pallas_call x1, Pallas kernels, pack(): pl.pallas_call(pack_kernel, out_shape=[jax.ShapeDtypeStruct((HEADS, 2, TO...  2.62 us
  transfers between devices with their start and end apart: 7, of which 6 were waited for; matrix products, arithmetic and copies ran while one was open for 0% of the time, Pallas kernels for 2%

profile of v9, /device:TPU:6, one launch (start us, length us, event | category | flops | bytes accessed | tf_op | source)
XLA Modules:
  0.0 109.4 jit_solution(6442383006172597458)
XLA Ops:
  0.7 2.6 %shard_map.78 = (bf16[4,2,256,128]{3,2,1,0:T(8,128)(2,1)}, bf16[4,4,256,128]{3,2,1,0:T(8,128)(2,1)}) custom-call(s32[1]{0:T(128)} %bitcast.flip_ref, bf16[256,512]{1,0:T(8,128)(2,1)} %bitcast.9, bf16[256,512]{1,0:T(8,128)(2,1)} %bitcast.10, bf16[256,512]{1,0:T(8,128)(2,1)} %bitcast.11, bf16[256,512]{1,0:T(8,128)(2,1)} %bitcast.12), custom_call_target="tpu_custom_call" | custom-call | bytes 2097152 | tf_op jit(solution)/shard_map/pallas_call | solution.py:64
  3.3 0.0 copy-start.4
  3.3 5.0 %all-to-all-start = ((bf16[4,4,256,128]{3,2,1,0:T(8,128)(2,1)}), bf16[4,4,256,128]{3,2,1,0:T(8,128)(2,1)S(1)}, u32[]{:S(2)}, u32[]{:S(2)}) async-start(bf16[4,4,256,128]{3,2,1,0:T(8,128)(2,1)} %get-tuple-element.14), calls=%async_computation | async-start | bytes 2097152 | tf_op jit(solution)/shard_map/all_to_all | solution.py:280
  8.3 0.0 copy-done.4
  8.3 6.9 %collective-permute-start = (bf16[4,2,256,128]{3,2,1,0:T(8,128)(2,1)S(1)}, bf16[4,2,256,128]{3,2,1,0:T(8,128)(2,1)}, u32[]{:S(2)}, u32[]{:S(2)}) collective-permute-start(bf16[4,2,256,128]{3,2,1,0:T(8,128)(2,1)S(1)} %copy-done.4), channel_id=1, source_target_pairs={{0,28},{1,29},{2,30},{3,31},{4,24},{5,25},{6,26},{7,27},{8,20},{9,... | collective-permute-start | bytes 1572872 | tf_op jit(solution)/shard_map/ppermute | solution.py:277
  15.2 22.8 %collective-permute-done = bf16[4,2,256,128]{3,2,1,0:T(8,128)(2,1)} collective-permute-done((bf16[4,2,256,128]{3,2,1,0:T(8,128)(2,1)S(1)}, bf16[4,2,256,128]{3,2,1,0:T(8,128)(2,1)}, u32[]{:S(2)}, u32[]{:S(2)}) %collective-permute-start) | collective-permute-done | bytes 524320 | tf_op jit(solution)/shard_map/ppermute | solution.py:277
  38.0 0.0 all-to-all-done.all_ref
  38.0 16.1 %all-to-all-start.1 = ((bf16[4,2,256,128]{3,2,1,0:T(8,128)(2,1)}), bf16[4,2,256,128]{3,2,1,0:T(8,128)(2,1)S(1)}, u32[]{:S(2)}, u32[]{:S(2)}) async-start(bf16[4,2,256,128]{3,2,1,0:T(8,128)(2,1)} %collective-permute-done), calls=%async_computation.1 | async-start | bytes 1048576 | tf_op jit(solution)/shard_map/all_to_all | solution.py:280
  54.2 1.9 %collective-permute-start.1 = (bf16[3,2,256,128]{3,2,1,0:T(8,128)(2,1)S(1)}, bf16[3,2,256,128]{3,2,1,0:T(8,128)(2,1)S(1)}, u32[]{:S(2)}, u32[]{:S(2)}) collective-permute-start(bf16[3,2,256,128]{3,2,1,0:T(8,128)(2,1)S(1)} %slice.4), channel_id=1, source_target_pairs={{0,32},{1,33},{2,34},{3,35},{4,36},{5,37},{6,38},{7,39},{8,40},{9,... | collective-permute-start | bytes 1179656 | tf_op jit(solution)/shard_map/ppermute | solution.py:277
  56.1 2.2 %shard_map.77 = (s32[4,256]{1,0:T(4,128)}, s32[4]{0:T(128)}) custom-call(s32[1]{0:T(128)} %bitcast.2.range_ref, s32[1,32768]{1,0:T(1,128)} %seg_ref.1), custom_call_target="tpu_custom_call" | custom-call | bytes 1048576 | tf_op jit(solution)/shard_map/pallas_call | solution.py:110
  58.3 0.0 copy-start
  58.3 9.4 %all-to-all-done.1.last_ref = bf16[4,2,256,128]{3,2,1,0:T(8,128)(2,1)S(1)} async-done(((bf16[4,2,256,128]{3,2,1,0:T(8,128)(2,1)}), bf16[4,2,256,128]{3,2,1,0:T(8,128)(2,1)S(1)}, u32[]{:S(2)}, u32[]{:S(2)}) %all-to-all-start.1) | async-done | bytes 524320 | tf_op jit(solution)/shard_map/all_to_all | solution.py:280
  67.8 1.6 %collective-permute-done.1.before_ref = bf16[3,2,256,128]{3,2,1,0:T(8,128)(2,1)S(1)} collective-permute-done((bf16[3,2,256,128]{3,2,1,0:T(8,128)(2,1)S(1)}, bf16[3,2,256,128]{3,2,1,0:T(8,128)(2,1)S(1)}, u32[]{:S(2)}, u32[]{:S(2)}) %collective-permute-start.1) | collective-permute-done | bytes 393248 | tf_op jit(solution)/shard_map/ppermute | solution.py:277
  69.4 0.0 copy-start.1
  69.4 0.0 copy-start.2
  69.4 0.0 copy-done
  69.4 0.6 copy-done.1
  70.0 0.0 copy-done.2
  70.1 8.1 %shard_map.79 = (bf16[4,256,128]{2,1,0:T(8,128)(2,1)}, f32[4,256,128]{2,1,0:T(8,128)S(1)}, bf16[4,256,128]{2,1,0:T(8,128)(2,1)S(1)}, bf16[3,256,128]{2,1,0:T(8,128)(2,1)S(1)}) custom-call(s32[1]{0:T(128)} %bitcast.1.head_ref, s32[4]{0:T(128)S(1)} %copy-done.2, f32[4]{0:T(128)S(1)} %copy-done.1, s32[4,256]{1,0:T(4,128)S(1)} %copy-done, ...), custom_call_target="tpu_custom_call" | custom-call | flops 1000000000 | bytes 6291456 | tf_op jit(solution)/shard_map/pallas_call | solution.py:241
  78.1 1.9 %collective-permute-start.2 = (bf16[4,256,128]{2,1,0:T(8,128)(2,1)S(1)}, bf16[4,256,128]{2,1,0:T(8,128)(2,1)S(1)}, u32[]{:S(2)}, u32[]{:S(2)}) collective-permute-start(bf16[4,256,128]{2,1,0:T(8,128)(2,1)S(1)} %get-tuple-element.18), channel_id=1, source_target_pairs={{28,0},{29,1},{30,2},{31,3},{24,4},{25,5},{26,6},{27,7},{20,8},{21... | collective-permute-start | bytes 786440 | tf_op jit(solution)/shard_map/ppermute | solution.py:277
  80.0 2.2 %collective-permute-start.3 = (bf16[3,256,128]{2,1,0:T(8,128)(2,1)S(1)}, bf16[3,256,128]{2,1,0:T(8,128)(2,1)S(1)}, u32[]{:S(2)}, u32[]{:S(2)}) collective-permute-start(bf16[3,256,128]{2,1,0:T(8,128)(2,1)S(1)} %get-tuple-element.19), channel_id=1, source_target_pairs={{32,0},{33,1},{34,2},{35,3},{36,4},{37,5},{38,6},{39,7},{40,8},{41... | collective-permute-start | bytes 589832 | tf_op jit(solution)/shard_map/ppermute | solution.py:277
  82.3 4.8 %all-to-all-start.2 = ((bf16[4,256,128]{2,1,0:T(8,128)(2,1)}), bf16[4,256,128]{2,1,0:T(8,128)(2,1)S(1)}, u32[]{:S(2)}, u32[]{:S(2)}) async-start(bf16[4,256,128]{2,1,0:T(8,128)(2,1)} %get-tuple-element.16), calls=%async_computation.2 | async-start | bytes 524288 | tf_op jit(solution)/shard_map/all_to_all | solution.py:280
  87.1 0.5 collective-permute-done.3
  87.6 5.5 %collective-permute-done.2 = bf16[4,256,128]{2,1,0:T(8,128)(2,1)S(1)} collective-permute-done((bf16[4,256,128]{2,1,0:T(8,128)(2,1)S(1)}, bf16[4,256,128]{2,1,0:T(8,128)(2,1)S(1)}, u32[]{:S(2)}, u32[]{:S(2)}) %collective-permute-start.2) | collective-permute-done | bytes 262176 | tf_op jit(solution)/shard_map/ppermute | solution.py:277
  93.1 0.1 add_convert_fusion
  93.2 1.8 %all-to-all-done.2.dq_ref = bf16[4,256,128]{2,1,0:T(8,128)(2,1)S(1)} async-done(((bf16[4,256,128]{2,1,0:T(8,128)(2,1)}), bf16[4,256,128]{2,1,0:T(8,128)(2,1)S(1)}, u32[]{:S(2)}, u32[]{:S(2)}) %all-to-all-start.2) | async-done | bytes 262176 | tf_op jit(solution)/shard_map/all_to_all | solution.py:280
  95.0 0.0 copy-start.3
  95.0 12.2 %all_to_all.20.dk_ref = bf16[4,256,128]{2,1,0:T(8,128)(2,1)} all-to-all(bf16[4,256,128]{2,1,0:T(8,128)(2,1)S(1)} %add_convert_fusion), channel_id=1, replica_groups={{0,4,8,12},{16,20,24,28},{32,36,40,44},{48,52,56,60},{64,68,72,76},{80,..., dimensions={0} | all-to-all | bytes 524288 | tf_op jit(solution)/shard_map/all_to_all | solution.py:280
  107.2 0.0 copy-done.3
  107.2 2.1 %shard_map.80 = (f32[256,512]{1,0:T(8,128)}, f32[256,512]{1,0:T(8,128)}) custom-call(s32[1]{0:T(128)} %bitcast.flip_ref, bf16[4,256,128]{2,1,0:T(8,128)(2,1)} %copy-done.3, bf16[4,256,128]{2,1,0:T(8,128)(2,1)} %all_to_all.20.dk_ref), custom_call_target="tpu_custom_call" | custom-call | bytes 1572864 | tf_op jit(solution)/shard_map/pallas_call | solution.py:127
  (1 shorter events, 0.0 us)
Async XLA Ops:
  3.3 5.0 %copy-start.4 = (bf16[4,2,256,128]{3,2,1,0:T(8,128)(2,1)S(1)}, bf16[4,2,256,128]{3,2,1,0:T(8,128)(2,1)}, u32[]{:S(2)}) copy-start(bf16[4,2,256,128]{3,2,1,0:T(8,128)(2,1)} %get-tuple-element.15) | copy-start | bytes 1572868
  3.3 34.7 %all-to-all-start = ((bf16[4,4,256,128]{3,2,1,0:T(8,128)(2,1)}), bf16[4,4,256,128]{3,2,1,0:T(8,128)(2,1)S(1)}, u32[]{:S(2)}, u32[]{:S(2)}) async-start(bf16[4,4,256,128]{3,2,1,0:T(8,128)(2,1)} %get-tuple-element.14), calls=%async_computation | async-start | bytes 2097152 | tf_op jit(solution)/shard_map/all_to_all | solution.py:280
  8.3 29.7 %collective-permute-start = (bf16[4,2,256,128]{3,2,1,0:T(8,128)(2,1)S(1)}, bf16[4,2,256,128]{3,2,1,0:T(8,128)(2,1)}, u32[]{:S(2)}, u32[]{:S(2)}) collective-permute-start(bf16[4,2,256,128]{3,2,1,0:T(8,128)(2,1)S(1)} %copy-done.4), channel_id=1, source_target_pairs={{0,28},{1,29},{2,30},{3,31},{4,24},{5,25},{6,26},{7,27},{8,20},{9,... | collective-permute-start | bytes 1572872 | tf_op jit(solution)/shard_map/ppermute | solution.py:277
  38.0 29.7 %all-to-all-start.1 = ((bf16[4,2,256,128]{3,2,1,0:T(8,128)(2,1)}), bf16[4,2,256,128]{3,2,1,0:T(8,128)(2,1)S(1)}, u32[]{:S(2)}, u32[]{:S(2)}) async-start(bf16[4,2,256,128]{3,2,1,0:T(8,128)(2,1)} %collective-permute-done), calls=%async_computation.1 | async-start | bytes 1048576 | tf_op jit(solution)/shard_map/all_to_all | solution.py:280
  54.2 15.2 %collective-permute-start.1 = (bf16[3,2,256,128]{3,2,1,0:T(8,128)(2,1)S(1)}, bf16[3,2,256,128]{3,2,1,0:T(8,128)(2,1)S(1)}, u32[]{:S(2)}, u32[]{:S(2)}) collective-permute-start(bf16[3,2,256,128]{3,2,1,0:T(8,128)(2,1)S(1)} %slice.4), channel_id=1, source_target_pairs={{0,32},{1,33},{2,34},{3,35},{4,36},{5,37},{6,38},{7,39},{8,40},{9,... | collective-permute-start | bytes 1179656 | tf_op jit(solution)/shard_map/ppermute | solution.py:277
  58.3 11.1 %copy-start = (s32[4,256]{1,0:T(4,128)S(1)}, s32[4,256]{1,0:T(4,128)}, u32[]{:S(2)}) copy-start(s32[4,256]{1,0:T(4,128)} %get-tuple-element.13.start_ref) | copy-start | bytes 12292
  69.4 0.7 copy-start.1
  69.4 0.7 copy-start.2
  78.1 15.0 %collective-permute-start.2 = (bf16[4,256,128]{2,1,0:T(8,128)(2,1)S(1)}, bf16[4,256,128]{2,1,0:T(8,128)(2,1)S(1)}, u32[]{:S(2)}, u32[]{:S(2)}) collective-permute-start(bf16[4,256,128]{2,1,0:T(8,128)(2,1)S(1)} %get-tuple-element.18), channel_id=1, source_target_pairs={{28,0},{29,1},{30,2},{31,3},{24,4},{25,5},{26,6},{27,7},{20,8},{21... | collective-permute-start | bytes 786440 | tf_op jit(solution)/shard_map/ppermute | solution.py:277
  80.0 7.6 %collective-permute-start.3 = (bf16[3,256,128]{2,1,0:T(8,128)(2,1)S(1)}, bf16[3,256,128]{2,1,0:T(8,128)(2,1)S(1)}, u32[]{:S(2)}, u32[]{:S(2)}) collective-permute-start(bf16[3,256,128]{2,1,0:T(8,128)(2,1)S(1)} %get-tuple-element.19), channel_id=1, source_target_pairs={{32,0},{33,1},{34,2},{35,3},{36,4},{37,5},{38,6},{39,7},{40,8},{41... | collective-permute-start | bytes 589832 | tf_op jit(solution)/shard_map/ppermute | solution.py:277
  82.3 12.7 %all-to-all-start.2 = ((bf16[4,256,128]{2,1,0:T(8,128)(2,1)}), bf16[4,256,128]{2,1,0:T(8,128)(2,1)S(1)}, u32[]{:S(2)}, u32[]{:S(2)}) async-start(bf16[4,256,128]{2,1,0:T(8,128)(2,1)} %get-tuple-element.16), calls=%async_computation.2 | async-start | bytes 524288 | tf_op jit(solution)/shard_map/all_to_all | solution.py:280
  95.0 12.2 %copy-start.3 = (bf16[4,256,128]{2,1,0:T(8,128)(2,1)}, bf16[4,256,128]{2,1,0:T(8,128)(2,1)S(1)}, u32[]{:S(2)}) copy-start(bf16[4,256,128]{2,1,0:T(8,128)(2,1)S(1)} %all-to-all-done.2.dq_ref) | copy-start | bytes 786436

commit v10 on v7

--- a/solution.py
+++ b/solution.py
@@ -16,7 +16,6 @@
 BEHIND = 7
 BAND = 12
 OWN = 8
-PAIR = 2 * TOK
 MASKED = -1e30
 F32 = jnp.float32
 BF16 = jnp.bfloat16
@@ -27,8 +26,7 @@
 
 def routes(seq, dp):
     rings = seq // RING
-    seam = rings // 2 - 1 if dp == 4 else None
-    last, before_last, relay = [], [], []
+    last, before_last = [], []
     for ring in range(rings):
         for y in range(RING):
             for part in range(dp):
@@ -37,14 +35,8 @@
                 if ahead < rings:
                     last.append((me, (ahead * RING + RING - 1 - y) * dp + part))
                 if ring + 1 < rings:
-                    target = ((ring + 1) * RING + y) * dp + part
-                    if ring == seam:
-                        over = ((rings - 1) * RING + y) * dp + part
-                        relay.append((me, over))
-                        before_last.append((over, target))
-                    else:
-                        before_last.append((me, target))
-    return last, before_last, relay
+                    before_last.append((me, me + RING * dp))
+    return last, before_last
 
 
 def reverse(route):
@@ -166,68 +158,75 @@
 def main_kernel(
     head_ref, low_ref, weight_ref, start_ref, query_ref, kt, ks,
     dq_ref, dk_own_ref, dk_last_ref, dk_before_ref,
-    ks_turned, dk, et, es, top_t, top_s, dq_acc,
+    ks_turned, dk, et, es, grad,
 ):
     weight = weight_ref[head_ref[0]]
     scale = 1.0 / math.sqrt(DIM)
     pace = scale * math.log2(math.e)
     along_depth = (((1,), (1,)), ((), ()))
+    lowest = low_ref[0] // TOK
 
     def rows(block):
         return pl.ds(block * TOK, TOK)
 
     dk[...] = jnp.zeros((BAND * TOK, DIM), F32)
     for block in range(BAND):
-        ks_turned[:, rows(block)] = ks[rows(block), :].T
-    key_row = lax.broadcasted_iota(jnp.int32, (PAIR, TOK), 0)
-    query_column = lax.broadcasted_iota(jnp.int32, (PAIR, TOK), 1)
-
-    for j in range(LINE):
-        block = OWN + j
-        pairs = (block + 2 - low_ref[j] // TOK) // 2
+        @pl.when(block >= lowest - 1)
+        def _():
+            ks_turned[:, rows(block)] = ks[rows(block), :].T
+
+    def work(j, blocks):
+        base = pl.multiple_of((OWN + j + 1 - blocks) * TOK, TOK)
         q_t, q_s = query_ref[j, 0], query_ref[j, 1]
-        start = start_ref[j : j + 1, :]
-
-        def at(t):
-            return pl.multiple_of((block - 1 - 2 * t) * TOK, TOK)
-
-        def one(keys, queries, visible, t, top, total, top_out, out):
-            s = lax.dot_general(keys, queries, along_depth, preferred_element_type=F32)
-            s = jnp.where(visible, s, MASKED)
-            new_top = jnp.maximum(top, jnp.max(s, axis=0, keepdims=True))
-            e = jnp.exp2((s - new_top) * pace)
-            out[t] = e
-            top_out[t] = new_top
-            return new_top, total * jnp.exp2((top - new_top) * pace) + jnp.sum(e, axis=0, keepdims=True)
-
-        def score(t, visible, carry):
-            m_t, l_t, m_s, l_s = carry
-            here = pl.ds(at(t), PAIR)
-            m_t, l_t = one(kt[here, :], q_t, visible, t, m_t, l_t, top_t, et)
-            m_s, l_s = one(ks[here, :], q_s, visible, t, m_s, l_s, top_s, es)
-            return m_t, l_t, m_s, l_s
-
-        def score_before(t, carry):
-            return score(t, key_row >= start - at(t), carry)
-
-        none, zero = jnp.full((1, TOK), MASKED, F32), jnp.zeros((1, TOK), F32)
-        own_visible = (key_row <= query_column + TOK) & (key_row >= start - at(0))
-        carry = score(0, own_visible, (none, zero, none, zero))
-        m_t, l_t, m_s, l_s = lax.fori_loop(1, pairs, score_before, carry)
+        start = start_ref[pl.ds(j, 1), :] - base
+        key_row = lax.broadcasted_iota(jnp.int32, (TOK, TOK), 0)
+        causal = key_row <= lax.broadcasted_iota(jnp.int32, (TOK, TOK), 1)
+
+        def keys(i):
+            return pl.ds(pl.multiple_of(base + i * TOK, TOK), TOK)
+
+        m_t = m_s = None
+        for i in range(blocks):
+            visible = key_row >= start - i * TOK
+            if i == blocks - 1:
+                visible = visible & causal
+            s_t = lax.dot_general(kt[keys(i), :], q_t, along_depth, preferred_element_type=F32)
+            s_s = lax.dot_general(ks[keys(i), :], q_s, along_depth, preferred_element_type=F32)
+            s_t = jnp.where(visible, s_t, MASKED)
+            s_s = jnp.where(visible, s_s, MASKED)
+            et[i] = s_t
+            es[i] = s_s
+            h_t, h_s = jnp.max(s_t, axis=0, keepdims=True), jnp.max(s_s, axis=0, keepdims=True)
+            m_t = h_t if m_t is None else jnp.maximum(m_t, h_t)
+            m_s = h_s if m_s is None else jnp.maximum(m_s, h_s)
+        l_t = l_s = jnp.zeros((1, TOK), F32)
+        for i in range(blocks):
+            e_t = jnp.exp2((et[i] - m_t) * pace)
+            e_s = jnp.exp2((es[i] - m_s) * pace)
+            et[i] = e_t
+            es[i] = e_s
+            l_t += jnp.sum(e_t, axis=0, keepdims=True)
+            l_s += jnp.sum(e_s, axis=0, keepdims=True)
         r_t, r_s = weight / l_t, weight / l_s
-        dq_acc[...] = jnp.zeros((DIM, TOK), F32)
-
-        def grads(t, _):
-            here = pl.ds(at(t), PAIR)
-            f_t = jnp.exp2((top_t[t] - m_t) * pace) * r_t
-            f_s = jnp.exp2((top_s[t] - m_s) * pace) * r_s
-            grad = (es[t] * f_s - et[t] * f_t).astype(BF16)
-            dk[here, :] += jnp.dot(grad, q_s, preferred_element_type=F32)
-            dq_acc[...] += jnp.dot(ks_turned[:, here], grad, preferred_element_type=F32)
-            return 0
-
-        lax.fori_loop(0, pairs, grads, 0)
-        dq_ref[j] = (dq_acc[...] * scale).T.astype(BF16)
+        for i in range(blocks):
+            g = (es[i] * r_s - et[i] * r_t).astype(BF16)
+            grad[rows(i), :] = g
+            dk[keys(i), :] += jnp.dot(g, q_s, preferred_element_type=F32)
+        dq = jnp.dot(
+            ks_turned[:, pl.ds(base, blocks * TOK)], grad[: blocks * TOK, :], preferred_element_type=F32
+        )
+        dq_ref[j] = (dq * scale).T.astype(BF16)
+
+    def query_block(j, _):
+        pairs = (OWN + j + 2 - low_ref[j] // TOK) // 2
+        for p in range(1, LINE + 1):
+            @pl.when(pairs == p)
+            def _():
+                work(j, 2 * p)
+
+        return 0
+
+    lax.fori_loop(0, LINE, query_block, 0)
 
     for i in range(LINE):
         dk_own_ref[i] = dk[rows(OWN + i), :] * scale
@@ -250,11 +249,9 @@
         scratch_shapes=[
             pltpu.VMEM((DIM, BAND * TOK), BF16),
             pltpu.VMEM((BAND * TOK, DIM), F32),
-            pltpu.VMEM((LINE, PAIR, TOK), F32),
-            pltpu.VMEM((LINE, PAIR, TOK), F32),
-            pltpu.VMEM((LINE, 1, TOK), F32),
-            pltpu.VMEM((LINE, 1, TOK), F32),
-            pltpu.VMEM((DIM, TOK), F32),
+            pltpu.VMEM((OWN, TOK, TOK), F32),
+            pltpu.VMEM((OWN, TOK, TOK), F32),
+            pltpu.VMEM((OWN * TOK, TOK), BF16),
         ],
         compiler_params=pltpu.CompilerParams(vmem_limit_bytes=12 * 1024 * 1024),
         cost_estimate=pl.CostEstimate(flops=10**9, bytes_accessed=6 * 2**20, transcendentals=4 * 10**6),
@@ -262,8 +259,7 @@
 
 
 def per_device(seq, dp, teacher_query, teacher_key, student_query, student_key, segment_ids, head_weight):
-    to_next, to_second, relay = routes(seq, dp)
-    to_second_straight = [(i, i + RING * dp) for i in range((seq - RING) * dp)]
+    to_next, to_second = routes(seq, dp)
     lines = [list(range(i, i + LINE)) for i in range(0, seq, LINE)]
     seq_index = lax.axis_index("seq")
     range_index = seq_index // LINE
@@ -281,17 +277,13 @@
     keys, queries = pack(flip, teacher_key[0], student_key[0], teacher_query[0], student_query[0])
     own = exchange(keys)
     last = move(own, to_next)
-    parting = own[1:]
-    if relay:
-        relays = seq_index >= seq - RING
-        parting = jnp.where(relays, move(parting, relay), parting)
-    before = move(parting, to_second)
+    before = move(own[1:], to_second)
     start, low = starts(range_index, segment_ids)
     queries = exchange(queries)
     dq, dk_own, dk_last, dk_before = attend(head, low, head_weight, start, queries, *layout(own, last, before))
 
     back_last = move(dk_last, reverse(to_next)).astype(F32)
-    back_before = move(dk_before, reverse(to_second_straight)).astype(F32)
+    back_before = move(dk_before, reverse(to_second)).astype(F32)
     dq_home = exchange(dq)
     total = dk_own + back_last + jnp.pad(back_before, ((1, 0), (0, 0), (0, 0)))
     query_grad, key_grad = unpack(flip, dq_home, exchange(total.astype(BF16)))

time: 105 us -> 101 us (0.962)
  waiting for transfers between devices: 30.8 us -> 27.8 us
  Pallas kernels: 17.5 us -> 15.6 us
  starting transfers between devices: 23.5 us -> 24.9 us
    pallas_call x1, Pallas kernels: 10.8 us -> 8.85 us  [attend(): pl.pallas_call(main_kernel, out_shape=[jax.ShapeDtypeStruct((LINE, TOK, D...]
    ppermute x5 -> x4, waiting for transfers between devices: 26.9 us -> 25.3 us  [move(): return lax.ppermute(x, AXES, route)]
    ppermute x5 -> x4, starting transfers between devices: 16.5 us -> 17.9 us  [move(): return lax.ppermute(x, AXES, route)]
    all_to_all x2, waiting for transfers between devices: 3.96 us -> 2.56 us  [exchange(): return lax.all_to_all(x, 'seq', 0, 0, axis_index_groups=lines)]
  transfers between devices with their start and end apart: 7 -> 6, of which waited for: 4 -> 4; matrix products, arithmetic and copies ran while one was open for 0% -> 0% of each run, Pallas kernels for 2% -> 2%
where the time goes in v10:
time: 101 us; the launch traced here: 99.7 us
  blocking collectives  29.8 us (30%)
  waiting for transfers between devices  27.8 us (28%)
  starting transfers between devices  24.9 us (25%)
  Pallas kernels  15.6 us (15%)
    all_to_all x2, blocking collectives, exchange(): return lax.all_to_all(x, 'seq', 0, 0, axis_index_groups=lines)  29.8 us
    ppermute x4, waiting for transfers between devices, move(): return lax.ppermute(x, AXES, route)  25.3 us
    ppermute x4, starting transfers between devices, move(): return lax.ppermute(x, AXES, route)  17.9 us
    pallas_call x1, Pallas kernels, attend(): pl.pallas_call(main_kernel, out_shape=[jax.ShapeDtypeStruct((LINE, TOK, D...  8.85 us
    all_to_all x2, starting transfers between devices, exchange(): return lax.all_to_all(x, 'seq', 0, 0, axis_index_groups=lines)  7.07 us
    all_to_all x2, waiting for transfers between devices, exchange(): return lax.all_to_all(x, 'seq', 0, 0, axis_index_groups=lines)  2.56 us
    pallas_call x1, Pallas kernels, pack(): pl.pallas_call(pack_kernel, out_shape=[jax.ShapeDtypeStruct((HEADS, 2, TO...  2.34 us
    pallas_call x1, Pallas kernels, starts(): pl.pallas_call(starts_kernel, out_shape=[jax.ShapeDtypeStruct((LINE, TOK)...  2.19 us
  transfers between devices with their start and end apart: 6, of which 4 were waited for; matrix products, arithmetic and copies ran while one was open for 0% of the time, Pallas kernels for 2%

profile of v10, /device:TPU:6, one launch (start us, length us, event | category | flops | bytes accessed | tf_op | source)
XLA Modules:
  0.0 99.7 jit_solution(10383898842541327254)
XLA Ops:
  0.7 2.3 %shard_map.78 = (bf16[4,2,256,128]{3,2,1,0:T(8,128)(2,1)}, bf16[4,2,256,128]{3,2,1,0:T(8,128)(2,1)}) custom-call(s32[1]{0:T(128)} %bitcast.flip_ref, bf16[256,512]{1,0:T(8,128)(2,1)} %bitcast.9, bf16[256,512]{1,0:T(8,128)(2,1)} %bitcast.10, bf16[256,512]{1,0:T(8,128)(2,1)} %bitcast.11, bf16[256,512]{1,0:T(8,128)(2,1)} %bitcast.12), custom_call_target="tpu_custom_call" | custom-call | bytes 2097152 | tf_op jit(solution)/shard_map/pallas_call | solution.py:61
  3.0 19.4 %all_to_all.20.own_ref = bf16[4,2,256,128]{3,2,1,0:T(8,128)(2,1)S(1)} all-to-all(bf16[4,2,256,128]{3,2,1,0:T(8,128)(2,1)} %get-tuple-element.17), channel_id=1, replica_groups={{0,4,8,12},{16,20,24,28},{32,36,40,44},{48,52,56,60},{64,68,72,76},{80,..., dimensions={0} | all-to-all | bytes 1048576 | tf_op jit(solution)/shard_map/all_to_all | solution.py:274
  22.4 4.8 %collective-permute-start = (bf16[4,2,256,128]{3,2,1,0:T(8,128)(2,1)S(1)}, bf16[4,2,256,128]{3,2,1,0:T(8,128)(2,1)S(1)}, u32[]{:S(2)}, u32[]{:S(2)}) collective-permute-start(bf16[4,2,256,128]{3,2,1,0:T(8,128)(2,1)S(1)} %all_to_all.20.own_ref), channel_id=1, source_target_pairs={{0,28},{1,29},{2,30},{3,31},{4,24},{5,25},{6,26},{7,27},{8,20},{9,... | collective-permute-start | bytes 1572872 | tf_op jit(solution)/shard_map/ppermute | solution.py:271
  27.2 4.3 %collective-permute-start.1 = (bf16[3,2,256,128]{3,2,1,0:T(8,128)(2,1)S(1)}, bf16[3,2,256,128]{3,2,1,0:T(8,128)(2,1)S(1)}, u32[]{:S(2)}, u32[]{:S(2)}) collective-permute-start(bf16[3,2,256,128]{3,2,1,0:T(8,128)(2,1)S(1)} %slice.4), channel_id=1, source_target_pairs={{0,32},{1,33},{2,34},{3,35},{4,36},{5,37},{6,38},{7,39},{8,40},{9,... | collective-permute-start | bytes 1179656 | tf_op jit(solution)/shard_map/ppermute | solution.py:271
  31.4 3.6 %all-to-all-start = ((bf16[4,2,256,128]{3,2,1,0:T(8,128)(2,1)}), bf16[4,2,256,128]{3,2,1,0:T(8,128)(2,1)S(1)}, u32[]{:S(2)}, u32[]{:S(2)}) async-start(bf16[4,2,256,128]{3,2,1,0:T(8,128)(2,1)} %get-tuple-element.16), calls=%async_computation | async-start | bytes 1048576 | tf_op jit(solution)/shard_map/all_to_all | solution.py:274
  35.1 2.2 %shard_map.77 = (s32[4,256]{1,0:T(4,128)}, s32[4]{0:T(128)}) custom-call(s32[1]{0:T(128)} %bitcast.2.range_ref, s32[1,32768]{1,0:T(1,128)} %seg_ref.1), custom_call_target="tpu_custom_call" | custom-call | bytes 1048576 | tf_op jit(solution)/shard_map/pallas_call | solution.py:104
  37.3 21.2 %collective-permute-done.1.before_ref = bf16[3,2,256,128]{3,2,1,0:T(8,128)(2,1)S(1)} collective-permute-done((bf16[3,2,256,128]{3,2,1,0:T(8,128)(2,1)S(1)}, bf16[3,2,256,128]{3,2,1,0:T(8,128)(2,1)S(1)}, u32[]{:S(2)}, u32[]{:S(2)}) %collective-permute-start.1) | collective-permute-done | bytes 393248 | tf_op jit(solution)/shard_map/ppermute | solution.py:271
  58.5 0.0 collective-permute-done.last_ref
  58.5 0.1 shard_map.79
  58.6 0.0 all-to-all-done.query_ref
  58.6 0.0 copy-start
  58.6 0.0 copy-start.1
  58.6 0.0 copy-start.2
  58.6 0.7 copy-done
  59.3 0.0 copy-done.1
  59.3 0.0 copy-done.2
  59.3 8.9 %shard_map.80 = (bf16[4,256,128]{2,1,0:T(8,128)(2,1)}, f32[4,256,128]{2,1,0:T(8,128)S(1)}, bf16[4,256,128]{2,1,0:T(8,128)(2,1)S(1)}, bf16[3,256,128]{2,1,0:T(8,128)(2,1)S(1)}) custom-call(s32[1]{0:T(128)} %bitcast.1.head_ref, s32[4]{0:T(128)S(1)} %copy-done.2, f32[4]{0:T(128)S(1)} %copy-done.1, s32[4,256]{1,0:T(4,128)S(1)} %copy-done, ...), custom_call_target="tpu_custom_call" | custom-call | flops 1000000000 | bytes 6291456 | tf_op jit(solution)/shard_map/pallas_call | solution.py:239
  68.1 6.9 %collective-permute-start.2 = (bf16[4,256,128]{2,1,0:T(8,128)(2,1)S(1)}, bf16[4,256,128]{2,1,0:T(8,128)(2,1)S(1)}, u32[]{:S(2)}, u32[]{:S(2)}) collective-permute-start(bf16[4,256,128]{2,1,0:T(8,128)(2,1)S(1)} %get-tuple-element.22), channel_id=1, source_target_pairs={{28,0},{29,1},{30,2},{31,3},{24,4},{25,5},{26,6},{27,7},{20,8},{21... | collective-permute-start | bytes 786440 | tf_op jit(solution)/shard_map/ppermute | solution.py:271
  75.0 1.9 %collective-permute-start.3 = (bf16[3,256,128]{2,1,0:T(8,128)(2,1)S(1)}, bf16[3,256,128]{2,1,0:T(8,128)(2,1)S(1)}, u32[]{:S(2)}, u32[]{:S(2)}) collective-permute-start(bf16[3,256,128]{2,1,0:T(8,128)(2,1)S(1)} %get-tuple-element.23), channel_id=1, source_target_pairs={{32,0},{33,1},{34,2},{35,3},{36,4},{37,5},{38,6},{39,7},{40,8},{41... | collective-permute-start | bytes 589832 | tf_op jit(solution)/shard_map/ppermute | solution.py:271
  77.0 3.4 %all-to-all-start.2 = ((bf16[4,256,128]{2,1,0:T(8,128)(2,1)}), bf16[4,256,128]{2,1,0:T(8,128)(2,1)S(1)}, u32[]{:S(2)}, u32[]{:S(2)}) async-start(bf16[4,256,128]{2,1,0:T(8,128)(2,1)} %get-tuple-element.20), calls=%async_computation.2 | async-start | bytes 524288 | tf_op jit(solution)/shard_map/all_to_all | solution.py:274
  80.4 2.2 %collective-permute-done.3 = bf16[3,256,128]{2,1,0:T(8,128)(2,1)S(1)} collective-permute-done((bf16[3,256,128]{2,1,0:T(8,128)(2,1)S(1)}, bf16[3,256,128]{2,1,0:T(8,128)(2,1)S(1)}, u32[]{:S(2)}, u32[]{:S(2)}) %collective-permute-start.3) | collective-permute-done | bytes 196640 | tf_op jit(solution)/shard_map/ppermute | solution.py:271
  82.6 1.9 %collective-permute-done.2 = bf16[4,256,128]{2,1,0:T(8,128)(2,1)S(1)} collective-permute-done((bf16[4,256,128]{2,1,0:T(8,128)(2,1)S(1)}, bf16[4,256,128]{2,1,0:T(8,128)(2,1)S(1)}, u32[]{:S(2)}, u32[]{:S(2)}) %collective-permute-start.2) | collective-permute-done | bytes 262176 | tf_op jit(solution)/shard_map/ppermute | solution.py:271
  84.5 0.1 add_convert_fusion
  84.6 2.6 %all-to-all-done.2.dq_ref = bf16[4,256,128]{2,1,0:T(8,128)(2,1)S(1)} async-done(((bf16[4,256,128]{2,1,0:T(8,128)(2,1)}), bf16[4,256,128]{2,1,0:T(8,128)(2,1)S(1)}, u32[]{:S(2)}, u32[]{:S(2)}) %all-to-all-start.2) | async-done | bytes 262176 | tf_op jit(solution)/shard_map/all_to_all | solution.py:274
  87.1 0.0 copy-start.3
  87.1 10.5 %all_to_all.21.dk_ref = bf16[4,256,128]{2,1,0:T(8,128)(2,1)} all-to-all(bf16[4,256,128]{2,1,0:T(8,128)(2,1)S(1)} %add_convert_fusion), channel_id=1, replica_groups={{0,4,8,12},{16,20,24,28},{32,36,40,44},{48,52,56,60},{64,68,72,76},{80,..., dimensions={0} | all-to-all | bytes 524288 | tf_op jit(solution)/shard_map/all_to_all | solution.py:274
  97.6 0.0 copy-done.3
  97.6 2.1 %shard_map.81 = (f32[256,512]{1,0:T(8,128)}, f32[256,512]{1,0:T(8,128)}) custom-call(s32[1]{0:T(128)} %bitcast.flip_ref, bf16[4,256,128]{2,1,0:T(8,128)(2,1)} %copy-done.3, bf16[4,256,128]{2,1,0:T(8,128)(2,1)} %all_to_all.21.dk_ref), custom_call_target="tpu_custom_call" | custom-call | bytes 1572864 | tf_op jit(solution)/shard_map/pallas_call | solution.py:121
  (1 shorter events, 0.0 us)
Async XLA Ops:
  22.4 36.1 %collective-permute-start = (bf16[4,2,256,128]{3,2,1,0:T(8,128)(2,1)S(1)}, bf16[4,2,256,128]{3,2,1,0:T(8,128)(2,1)S(1)}, u32[]{:S(2)}, u32[]{:S(2)}) collective-permute-start(bf16[4,2,256,128]{3,2,1,0:T(8,128)(2,1)S(1)} %all_to_all.20.own_ref), channel_id=1, source_target_pairs={{0,28},{1,29},{2,30},{3,31},{4,24},{5,25},{6,26},{7,27},{8,20},{9,... | collective-permute-start | bytes 1572872 | tf_op jit(solution)/shard_map/ppermute | solution.py:271
  27.2 31.3 %collective-permute-start.1 = (bf16[3,2,256,128]{3,2,1,0:T(8,128)(2,1)S(1)}, bf16[3,2,256,128]{3,2,1,0:T(8,128)(2,1)S(1)}, u32[]{:S(2)}, u32[]{:S(2)}) collective-permute-start(bf16[3,2,256,128]{3,2,1,0:T(8,128)(2,1)S(1)} %slice.4), channel_id=1, source_target_pairs={{0,32},{1,33},{2,34},{3,35},{4,36},{5,37},{6,38},{7,39},{8,40},{9,... | collective-permute-start | bytes 1179656 | tf_op jit(solution)/shard_map/ppermute | solution.py:271
  31.4 27.1 %all-to-all-start = ((bf16[4,2,256,128]{3,2,1,0:T(8,128)(2,1)}), bf16[4,2,256,128]{3,2,1,0:T(8,128)(2,1)S(1)}, u32[]{:S(2)}, u32[]{:S(2)}) async-start(bf16[4,2,256,128]{3,2,1,0:T(8,128)(2,1)} %get-tuple-element.16), calls=%async_computation | async-start | bytes 1048576 | tf_op jit(solution)/shard_map/all_to_all | solution.py:274
  58.6 0.7 copy-start
  58.6 0.7 copy-start.1
  58.6 0.7 copy-start.2
  68.1 16.4 %collective-permute-start.2 = (bf16[4,256,128]{2,1,0:T(8,128)(2,1)S(1)}, bf16[4,256,128]{2,1,0:T(8,128)(2,1)S(1)}, u32[]{:S(2)}, u32[]{:S(2)}) collective-permute-start(bf16[4,256,128]{2,1,0:T(8,128)(2,1)S(1)} %get-tuple-element.22), channel_id=1, source_target_pairs={{28,0},{29,1},{30,2},{31,3},{24,4},{25,5},{26,6},{27,7},{20,8},{21... | collective-permute-start | bytes 786440 | tf_op jit(solution)/shard_map/ppermute | solution.py:271
  75.0 7.6 %collective-permute-start.3 = (bf16[3,256,128]{2,1,0:T(8,128)(2,1)S(1)}, bf16[3,256,128]{2,1,0:T(8,128)(2,1)S(1)}, u32[]{:S(2)}, u32[]{:S(2)}) collective-permute-start(bf16[3,256,128]{2,1,0:T(8,128)(2,1)S(1)} %get-tuple-element.23), channel_id=1, source_target_pairs={{32,0},{33,1},{34,2},{35,3},{36,4},{37,5},{38,6},{39,7},{40,8},{41... | collective-permute-start | bytes 589832 | tf_op jit(solution)/shard_map/ppermute | solution.py:271
  77.0 10.2 %all-to-all-start.2 = ((bf16[4,256,128]{2,1,0:T(8,128)(2,1)}), bf16[4,256,128]{2,1,0:T(8,128)(2,1)S(1)}, u32[]{:S(2)}, u32[]{:S(2)}) async-start(bf16[4,256,128]{2,1,0:T(8,128)(2,1)} %get-tuple-element.20), calls=%async_computation.2 | async-start | bytes 524288 | tf_op jit(solution)/shard_map/all_to_all | solution.py:274
  87.1 10.5 %copy-start.3 = (bf16[4,256,128]{2,1,0:T(8,128)(2,1)}, bf16[4,256,128]{2,1,0:T(8,128)(2,1)S(1)}, u32[]{:S(2)}) copy-start(bf16[4,256,128]{2,1,0:T(8,128)(2,1)S(1)} %all-to-all-done.2.dq_ref) | copy-start | bytes 786436

commit v11 on v10

--- a/solution.py
+++ b/solution.py
@@ -16,6 +16,7 @@
 BEHIND = 7
 BAND = 12
 OWN = 8
+PART = 64
 MASKED = -1e30
 F32 = jnp.float32
 BF16 = jnp.bfloat16
@@ -158,12 +159,11 @@
 def main_kernel(
     head_ref, low_ref, weight_ref, start_ref, query_ref, kt, ks,
     dq_ref, dk_own_ref, dk_last_ref, dk_before_ref,
-    ks_turned, dk, et, es, grad,
+    ks_turned, dk, et, es, grad, top_t, top_s, sum_t, sum_s, factor_t, factor_s,
 ):
     weight = weight_ref[head_ref[0]]
     scale = 1.0 / math.sqrt(DIM)
     pace = scale * math.log2(math.e)
-    along_depth = (((1,), (1,)), ((), ()))
     lowest = low_ref[0] // TOK
 
     def rows(block):
@@ -178,40 +178,43 @@
     def work(j, blocks):
         base = pl.multiple_of((OWN + j + 1 - blocks) * TOK, TOK)
         q_t, q_s = query_ref[j, 0], query_ref[j, 1]
+        sides = (
+            (kt, q_t.T, et, top_t, sum_t, factor_t),
+            (ks, q_s.T, es, top_s, sum_s, factor_s),
+        )
         start = start_ref[pl.ds(j, 1), :] - base
-        key_row = lax.broadcasted_iota(jnp.int32, (TOK, TOK), 0)
-        causal = key_row <= lax.broadcasted_iota(jnp.int32, (TOK, TOK), 1)
+        key_row = lax.broadcasted_iota(jnp.int32, (PART, TOK), 0)
+        query_column = lax.broadcasted_iota(jnp.int32, (PART, TOK), 1)
+        parts = [(i, c) for i in range(blocks) for c in range(TOK // PART)]
+        held = pl.ds(0, len(parts))
 
         def keys(i):
             return pl.ds(pl.multiple_of(base + i * TOK, TOK), TOK)
 
-        m_t = m_s = None
         for i in range(blocks):
-            visible = key_row >= start - i * TOK
-            if i == blocks - 1:
-                visible = visible & causal
-            s_t = lax.dot_general(kt[keys(i), :], q_t, along_depth, preferred_element_type=F32)
-            s_s = lax.dot_general(ks[keys(i), :], q_s, along_depth, preferred_element_type=F32)
-            s_t = jnp.where(visible, s_t, MASKED)
-            s_s = jnp.where(visible, s_s, MASKED)
-            et[i] = s_t
-            es[i] = s_s
-            h_t, h_s = jnp.max(s_t, axis=0, keepdims=True), jnp.max(s_s, axis=0, keepdims=True)
-            m_t = h_t if m_t is None else jnp.maximum(m_t, h_t)
-            m_s = h_s if m_s is None else jnp.maximum(m_s, h_s)
-        l_t = l_s = jnp.zeros((1, TOK), F32)
+            scores = [jnp.dot(k[keys(i), :], q, preferred_element_type=F32) for k, q, *_ in sides]
+            for c in range(TOK // PART):
+                here, at = pl.ds(c * PART, PART), i * (TOK // PART) + c
+                visible = key_row >= start - (i * TOK + c * PART)
+                if i == blocks - 1:
+                    visible = visible & (key_row <= query_column - c * PART)
+                for s, (_, _, e, top, total, _) in zip(scores, sides):
+                    x = jnp.where(visible, s[c * PART : (c + 1) * PART], MASKED)
+                    h = jnp.max(x, axis=0, keepdims=True)
+                    x = jnp.exp2((x - h) * pace)
+                    e[i, here, :] = x
+                    top[pl.ds(at, 1), :] = h
+                    total[pl.ds(at, 1), :] = jnp.sum(x, axis=0, keepdims=True)
+        for _, _, _, top, total, factor in sides:
+            tops = top[held, :]
+            f = jnp.exp2((tops - jnp.max(tops, axis=0, keepdims=True)) * pace)
+            factor[held, :] = f * (weight / jnp.sum(total[held, :] * f, axis=0, keepdims=True))
         for i in range(blocks):
-            e_t = jnp.exp2((et[i] - m_t) * pace)
-            e_s = jnp.exp2((es[i] - m_s) * pace)
-            et[i] = e_t
-            es[i] = e_s
-            l_t += jnp.sum(e_t, axis=0, keepdims=True)
-            l_s += jnp.sum(e_s, axis=0, keepdims=True)
-        r_t, r_s = weight / l_t, weight / l_s
-        for i in range(blocks):
-            g = (es[i] * r_s - et[i] * r_t).astype(BF16)
-            grad[rows(i), :] = g
-            dk[keys(i), :] += jnp.dot(g, q_s, preferred_element_type=F32)
+            for c in range(TOK // PART):
+                here, at = pl.ds(c * PART, PART), pl.ds(i * (TOK // PART) + c, 1)
+                g = es[i, here, :] * factor_s[at, :] - et[i, here, :] * factor_t[at, :]
+                grad[pl.ds(i * TOK + c * PART, PART), :] = g.astype(BF16)
+            dk[keys(i), :] += jnp.dot(grad[rows(i), :], q_s, preferred_element_type=F32)
         dq = jnp.dot(
             ks_turned[:, pl.ds(base, blocks * TOK)], grad[: blocks * TOK, :], preferred_element_type=F32
         )
@@ -252,7 +255,8 @@
             pltpu.VMEM((OWN, TOK, TOK), F32),
             pltpu.VMEM((OWN, TOK, TOK), F32),
             pltpu.VMEM((OWN * TOK, TOK), BF16),
-        ],
+        ]
+        + [pltpu.VMEM((OWN * TOK // PART, TOK), F32)] * 6,
         compiler_params=pltpu.CompilerParams(vmem_limit_bytes=12 * 1024 * 1024),
         cost_estimate=pl.CostEstimate(flops=10**9, bytes_accessed=6 * 2**20, transcendentals=4 * 10**6),
     )(head, low, weight, start, queries, *keys)

time: 101 us -> 101 us (level); the launches traced: 99.7 us -> 101 us
  starting transfers between devices: 24.9 us -> 26.1 us
    ppermute x4, starting transfers between devices: 17.9 us -> 19 us  [move(): return lax.ppermute(x, AXES, route)]
  transfers between devices with their start and end apart: 6 -> 6, of which waited for: 4 -> 3; matrix products, arithmetic and copies ran while one was open for 0% -> 0% of each run, Pallas kernels for 2% -> 2%
where the time goes in v11:
time: 101 us
  blocking collectives  29.8 us (30%)
  waiting for transfers between devices  27.8 us (28%)
  starting transfers between devices  26.1 us (26%)
  Pallas kernels  15.7 us (16%)
    all_to_all x2, blocking collectives, exchange(): return lax.all_to_all(x, 'seq', 0, 0, axis_index_groups=lines)  29.8 us
    ppermute x4, waiting for transfers between devices, move(): return lax.ppermute(x, AXES, route)  24.6 us
    ppermute x4, starting transfers between devices, move(): return lax.ppermute(x, AXES, route)  19 us
    pallas_call x1, Pallas kernels, attend(): pl.pallas_call(main_kernel, out_shape=[jax.ShapeDtypeStruct((LINE, TOK, D...  8.93 us
    all_to_all x2, starting transfers between devices, exchange(): return lax.all_to_all(x, 'seq', 0, 0, axis_index_groups=lines)  7.07 us
    all_to_all x2, waiting for transfers between devices, exchange(): return lax.all_to_all(x, 'seq', 0, 0, axis_index_groups=lines)  3.21 us
    pallas_call x1, Pallas kernels, pack(): pl.pallas_call(pack_kernel, out_shape=[jax.ShapeDtypeStruct((HEADS, 2, TO...  2.34 us
    pallas_call x1, Pallas kernels, starts(): pl.pallas_call(starts_kernel, out_shape=[jax.ShapeDtypeStruct((LINE, TOK)...  2.19 us
  transfers between devices with their start and end apart: 6, of which 3 were waited for; matrix products, arithmetic and copies ran while one was open for 0% of the time, Pallas kernels for 2%

profile of v11, /device:TPU:6, one launch (start us, length us, event | category | flops | bytes accessed | tf_op | source)
XLA Modules:
  0.0 101.0 jit_solution(9305539261866115203)
XLA Ops:
  0.7 2.3 %shard_map.78 = (bf16[4,2,256,128]{3,2,1,0:T(8,128)(2,1)}, bf16[4,2,256,128]{3,2,1,0:T(8,128)(2,1)}) custom-call(s32[1]{0:T(128)} %bitcast.flip_ref, bf16[256,512]{1,0:T(8,128)(2,1)} %bitcast.9, bf16[256,512]{1,0:T(8,128)(2,1)} %bitcast.10, bf16[256,512]{1,0:T(8,128)(2,1)} %bitcast.11, bf16[256,512]{1,0:T(8,128)(2,1)} %bitcast.12), custom_call_target="tpu_custom_call" | custom-call | bytes 2097152 | tf_op jit(solution)/shard_map/pallas_call | solution.py:62
  3.0 19.4 %all_to_all.20.own_ref = bf16[4,2,256,128]{3,2,1,0:T(8,128)(2,1)S(1)} all-to-all(bf16[4,2,256,128]{3,2,1,0:T(8,128)(2,1)} %get-tuple-element.17), channel_id=1, replica_groups={{0,4,8,12},{16,20,24,28},{32,36,40,44},{48,52,56,60},{64,68,72,76},{80,..., dimensions={0} | all-to-all | bytes 1048576 | tf_op jit(solution)/shard_map/all_to_all | solution.py:278
  22.4 4.8 %collective-permute-start = (bf16[4,2,256,128]{3,2,1,0:T(8,128)(2,1)S(1)}, bf16[4,2,256,128]{3,2,1,0:T(8,128)(2,1)S(1)}, u32[]{:S(2)}, u32[]{:S(2)}) collective-permute-start(bf16[4,2,256,128]{3,2,1,0:T(8,128)(2,1)S(1)} %all_to_all.20.own_ref), channel_id=1, source_target_pairs={{0,28},{1,29},{2,30},{3,31},{4,24},{5,25},{6,26},{7,27},{8,20},{9,... | collective-permute-start | bytes 1572872 | tf_op jit(solution)/shard_map/ppermute | solution.py:275
  27.2 4.3 %collective-permute-start.1 = (bf16[3,2,256,128]{3,2,1,0:T(8,128)(2,1)S(1)}, bf16[3,2,256,128]{3,2,1,0:T(8,128)(2,1)S(1)}, u32[]{:S(2)}, u32[]{:S(2)}) collective-permute-start(bf16[3,2,256,128]{3,2,1,0:T(8,128)(2,1)S(1)} %slice.4), channel_id=1, source_target_pairs={{0,32},{1,33},{2,34},{3,35},{4,36},{5,37},{6,38},{7,39},{8,40},{9,... | collective-permute-start | bytes 1179656 | tf_op jit(solution)/shard_map/ppermute | solution.py:275
  31.4 3.6 %all-to-all-start = ((bf16[4,2,256,128]{3,2,1,0:T(8,128)(2,1)}), bf16[4,2,256,128]{3,2,1,0:T(8,128)(2,1)S(1)}, u32[]{:S(2)}, u32[]{:S(2)}) async-start(bf16[4,2,256,128]{3,2,1,0:T(8,128)(2,1)} %get-tuple-element.16), calls=%async_computation | async-start | bytes 1048576 | tf_op jit(solution)/shard_map/all_to_all | solution.py:278
  35.1 2.2 %shard_map.77 = (s32[4,256]{1,0:T(4,128)}, s32[4]{0:T(128)}) custom-call(s32[1]{0:T(128)} %bitcast.2.range_ref, s32[1,32768]{1,0:T(1,128)} %seg_ref.1), custom_call_target="tpu_custom_call" | custom-call | bytes 1048576 | tf_op jit(solution)/shard_map/pallas_call | solution.py:105
  37.3 21.2 %collective-permute-done.1.before_ref = bf16[3,2,256,128]{3,2,1,0:T(8,128)(2,1)S(1)} collective-permute-done((bf16[3,2,256,128]{3,2,1,0:T(8,128)(2,1)S(1)}, bf16[3,2,256,128]{3,2,1,0:T(8,128)(2,1)S(1)}, u32[]{:S(2)}, u32[]{:S(2)}) %collective-permute-start.1) | collective-permute-done | bytes 393248 | tf_op jit(solution)/shard_map/ppermute | solution.py:275
  58.5 0.0 collective-permute-done.last_ref
  58.5 0.1 shard_map.79
  58.6 0.0 all-to-all-done.query_ref
  58.6 0.0 copy-start
  58.6 0.0 copy-start.1
  58.6 0.0 copy-start.2
  58.6 0.7 copy-done
  59.3 0.0 copy-done.1
  59.3 0.0 copy-done.2
  59.3 8.9 %shard_map.80 = (bf16[4,256,128]{2,1,0:T(8,128)(2,1)}, f32[4,256,128]{2,1,0:T(8,128)S(1)}, bf16[4,256,128]{2,1,0:T(8,128)(2,1)S(1)}, bf16[3,256,128]{2,1,0:T(8,128)(2,1)S(1)}) custom-call(s32[1]{0:T(128)} %bitcast.1.head_ref, s32[4]{0:T(128)S(1)} %copy-done.2, f32[4]{0:T(128)S(1)} %copy-done.1, s32[4,256]{1,0:T(4,128)S(1)} %copy-done, ...), custom_call_target="tpu_custom_call" | custom-call | flops 1000000000 | bytes 6291456 | tf_op jit(solution)/shard_map/pallas_call | solution.py:242
  68.2 4.2 %collective-permute-start.2 = (bf16[4,256,128]{2,1,0:T(8,128)(2,1)S(1)}, bf16[4,256,128]{2,1,0:T(8,128)(2,1)S(1)}, u32[]{:S(2)}, u32[]{:S(2)}) collective-permute-start(bf16[4,256,128]{2,1,0:T(8,128)(2,1)S(1)} %get-tuple-element.22), channel_id=1, source_target_pairs={{28,0},{29,1},{30,2},{31,3},{24,4},{25,5},{26,6},{27,7},{20,8},{21... | collective-permute-start | bytes 786440 | tf_op jit(solution)/shard_map/ppermute | solution.py:275
  72.4 5.8 %collective-permute-start.3 = (bf16[3,256,128]{2,1,0:T(8,128)(2,1)S(1)}, bf16[3,256,128]{2,1,0:T(8,128)(2,1)S(1)}, u32[]{:S(2)}, u32[]{:S(2)}) collective-permute-start(bf16[3,256,128]{2,1,0:T(8,128)(2,1)S(1)} %get-tuple-element.23), channel_id=1, source_target_pairs={{32,0},{33,1},{34,2},{35,3},{36,4},{37,5},{38,6},{39,7},{40,8},{41... | collective-permute-start | bytes 589832 | tf_op jit(solution)/shard_map/ppermute | solution.py:275
  78.2 3.4 %all-to-all-start.2 = ((bf16[4,256,128]{2,1,0:T(8,128)(2,1)}), bf16[4,256,128]{2,1,0:T(8,128)(2,1)S(1)}, u32[]{:S(2)}, u32[]{:S(2)}) async-start(bf16[4,256,128]{2,1,0:T(8,128)(2,1)} %get-tuple-element.20), calls=%async_computation.2 | async-start | bytes 524288 | tf_op jit(solution)/shard_map/all_to_all | solution.py:278
  81.6 0.0 collective-permute-done.3
  81.7 3.4 %collective-permute-done.2 = bf16[4,256,128]{2,1,0:T(8,128)(2,1)S(1)} collective-permute-done((bf16[4,256,128]{2,1,0:T(8,128)(2,1)S(1)}, bf16[4,256,128]{2,1,0:T(8,128)(2,1)S(1)}, u32[]{:S(2)}, u32[]{:S(2)}) %collective-permute-start.2) | collective-permute-done | bytes 262176 | tf_op jit(solution)/shard_map/ppermute | solution.py:275
  85.1 0.1 add_convert_fusion
  85.2 3.2 %all-to-all-done.2.dq_ref = bf16[4,256,128]{2,1,0:T(8,128)(2,1)S(1)} async-done(((bf16[4,256,128]{2,1,0:T(8,128)(2,1)}), bf16[4,256,128]{2,1,0:T(8,128)(2,1)S(1)}, u32[]{:S(2)}, u32[]{:S(2)}) %all-to-all-start.2) | async-done | bytes 262176 | tf_op jit(solution)/shard_map/all_to_all | solution.py:278
  88.4 0.0 copy-start.3
  88.4 10.5 %all_to_all.21.dk_ref = bf16[4,256,128]{2,1,0:T(8,128)(2,1)} all-to-all(bf16[4,256,128]{2,1,0:T(8,128)(2,1)S(1)} %add_convert_fusion), channel_id=1, replica_groups={{0,4,8,12},{16,20,24,28},{32,36,40,44},{48,52,56,60},{64,68,72,76},{80,..., dimensions={0} | all-to-all | bytes 524288 | tf_op jit(solution)/shard_map/all_to_all | solution.py:278
  98.8 0.0 copy-done.3
  98.8 2.1 %shard_map.81 = (f32[256,512]{1,0:T(8,128)}, f32[256,512]{1,0:T(8,128)}) custom-call(s32[1]{0:T(128)} %bitcast.flip_ref, bf16[4,256,128]{2,1,0:T(8,128)(2,1)} %copy-done.3, bf16[4,256,128]{2,1,0:T(8,128)(2,1)} %all_to_all.21.dk_ref), custom_call_target="tpu_custom_call" | custom-call | bytes 1572864 | tf_op jit(solution)/shard_map/pallas_call | solution.py:122
  (1 shorter events, 0.0 us)
Async XLA Ops:
  22.4 36.1 %collective-permute-start = (bf16[4,2,256,128]{3,2,1,0:T(8,128)(2,1)S(1)}, bf16[4,2,256,128]{3,2,1,0:T(8,128)(2,1)S(1)}, u32[]{:S(2)}, u32[]{:S(2)}) collective-permute-start(bf16[4,2,256,128]{3,2,1,0:T(8,128)(2,1)S(1)} %all_to_all.20.own_ref), channel_id=1, source_target_pairs={{0,28},{1,29},{2,30},{3,31},{4,24},{5,25},{6,26},{7,27},{8,20},{9,... | collective-permute-start | bytes 1572872 | tf_op jit(solution)/shard_map/ppermute | solution.py:275
  27.2 31.3 %collective-permute-start.1 = (bf16[3,2,256,128]{3,2,1,0:T(8,128)(2,1)S(1)}, bf16[3,2,256,128]{3,2,1,0:T(8,128)(2,1)S(1)}, u32[]{:S(2)}, u32[]{:S(2)}) collective-permute-start(bf16[3,2,256,128]{3,2,1,0:T(8,128)(2,1)S(1)} %slice.4), channel_id=1, source_target_pairs={{0,32},{1,33},{2,34},{3,35},{4,36},{5,37},{6,38},{7,39},{8,40},{9,... | collective-permute-start | bytes 1179656 | tf_op jit(solution)/shard_map/ppermute | solution.py:275
  31.4 27.1 %all-to-all-start = ((bf16[4,2,256,128]{3,2,1,0:T(8,128)(2,1)}), bf16[4,2,256,128]{3,2,1,0:T(8,128)(2,1)S(1)}, u32[]{:S(2)}, u32[]{:S(2)}) async-start(bf16[4,2,256,128]{3,2,1,0:T(8,128)(2,1)} %get-tuple-element.16), calls=%async_computation | async-start | bytes 1048576 | tf_op jit(solution)/shard_map/all_to_all | solution.py:278
  58.6 0.7 copy-start
  58.6 0.7 copy-start.1
  58.6 0.7 copy-start.2
  68.2 16.9 %collective-permute-start.2 = (bf16[4,256,128]{2,1,0:T(8,128)(2,1)S(1)}, bf16[4,256,128]{2,1,0:T(8,128)(2,1)S(1)}, u32[]{:S(2)}, u32[]{:S(2)}) collective-permute-start(bf16[4,256,128]{2,1,0:T(8,128)(2,1)S(1)} %get-tuple-element.22), channel_id=1, source_target_pairs={{28,0},{29,1},{30,2},{31,3},{24,4},{25,5},{26,6},{27,7},{20,8},{21... | collective-permute-start | bytes 786440 | tf_op jit(solution)/shard_map/ppermute | solution.py:275
  72.4 9.3 %collective-permute-start.3 = (bf16[3,256,128]{2,1,0:T(8,128)(2,1)S(1)}, bf16[3,256,128]{2,1,0:T(8,128)(2,1)S(1)}, u32[]{:S(2)}, u32[]{:S(2)}) collective-permute-start(bf16[3,256,128]{2,1,0:T(8,128)(2,1)S(1)} %get-tuple-element.23), channel_id=1, source_target_pairs={{32,0},{33,1},{34,2},{35,3},{36,4},{37,5},{38,6},{39,7},{40,8},{41... | collective-permute-start | bytes 589832 | tf_op jit(solution)/shard_map/ppermute | solution.py:275
  78.2 10.2 %all-to-all-start.2 = ((bf16[4,256,128]{2,1,0:T(8,128)(2,1)}), bf16[4,256,128]{2,1,0:T(8,128)(2,1)S(1)}, u32[]{:S(2)}, u32[]{:S(2)}) async-start(bf16[4,256,128]{2,1,0:T(8,128)(2,1)} %get-tuple-element.20), calls=%async_computation.2 | async-start | bytes 524288 | tf_op jit(solution)/shard_map/all_to_all | solution.py:278
  88.4 10.5 %copy-start.3 = (bf16[4,256,128]{2,1,0:T(8,128)(2,1)}, bf16[4,256,128]{2,1,0:T(8,128)(2,1)S(1)}, u32[]{:S(2)}) copy-start(bf16[4,256,128]{2,1,0:T(8,128)(2,1)S(1)} %all-to-all-done.2.dq_ref) | copy-start | bytes 786436

commit v12 on v11

--- a/solution.py
+++ b/solution.py
@@ -17,6 +17,8 @@
 BAND = 12
 OWN = 8
 PART = 64
+WIDE = 2 * TOK
+SPAN = 10
 MASKED = -1e30
 F32 = jnp.float32
 BF16 = jnp.bfloat16
@@ -169,6 +171,9 @@
     def rows(block):
         return pl.ds(block * TOK, TOK)
 
+    def turned(j, kind):
+        return jnp.concatenate([query_ref[j, kind].T, query_ref[j + 1, kind].T], axis=1)
+
     dk[...] = jnp.zeros((BAND * TOK, DIM), F32)
     for block in range(BAND):
         @pl.when(block >= lowest - 1)
@@ -176,15 +181,15 @@
             ks_turned[:, rows(block)] = ks[rows(block), :].T
 
     def work(j, blocks):
-        base = pl.multiple_of((OWN + j + 1 - blocks) * TOK, TOK)
-        q_t, q_s = query_ref[j, 0], query_ref[j, 1]
+        base = pl.multiple_of((OWN + j + 2 - blocks) * TOK, TOK)
         sides = (
-            (kt, q_t.T, et, top_t, sum_t, factor_t),
-            (ks, q_s.T, es, top_s, sum_s, factor_s),
+            (kt, turned(j, 0), et, top_t, sum_t, factor_t),
+            (ks, turned(j, 1), es, top_s, sum_s, factor_s),
         )
-        start = start_ref[pl.ds(j, 1), :] - base
-        key_row = lax.broadcasted_iota(jnp.int32, (PART, TOK), 0)
-        query_column = lax.broadcasted_iota(jnp.int32, (PART, TOK), 1)
+        q_s = jnp.concatenate([query_ref[j, 1], query_ref[j + 1, 1]], axis=0)
+        start = jnp.concatenate([start_ref[pl.ds(j, 1), :], start_ref[pl.ds(j + 1, 1), :]], axis=1) - base
+        key_row = lax.broadcasted_iota(jnp.int32, (PART, WIDE), 0)
+        query_column = lax.broadcasted_iota(jnp.int32, (PART, WIDE), 1)
         parts = [(i, c) for i in range(blocks) for c in range(TOK // PART)]
         held = pl.ds(0, len(parts))
 
@@ -196,8 +201,8 @@
             for c in range(TOK // PART):
                 here, at = pl.ds(c * PART, PART), i * (TOK // PART) + c
                 visible = key_row >= start - (i * TOK + c * PART)
-                if i == blocks - 1:
-                    visible = visible & (key_row <= query_column - c * PART)
+                if i >= blocks - 2:
+                    visible = visible & (key_row <= query_column - ((i - blocks + 2) * TOK + c * PART))
                 for s, (_, _, e, top, total, _) in zip(scores, sides):
                     x = jnp.where(visible, s[c * PART : (c + 1) * PART], MASKED)
                     h = jnp.max(x, axis=0, keepdims=True)
@@ -218,18 +223,20 @@
         dq = jnp.dot(
             ks_turned[:, pl.ds(base, blocks * TOK)], grad[: blocks * TOK, :], preferred_element_type=F32
         )
-        dq_ref[j] = (dq * scale).T.astype(BF16)
-
-    def query_block(j, _):
-        pairs = (OWN + j + 2 - low_ref[j] // TOK) // 2
-        for p in range(1, LINE + 1):
+        dq_ref[j] = (dq[:, :TOK] * scale).T.astype(BF16)
+        dq_ref[j + 1] = (dq[:, TOK:] * scale).T.astype(BF16)
+
+    def query_blocks(step, _):
+        j = 2 * step
+        pairs = (OWN + j + 3 - low_ref[j] // TOK) // 2
+        for p in range(1, SPAN // 2 + 1):
             @pl.when(pairs == p)
             def _():
                 work(j, 2 * p)
 
         return 0
 
-    lax.fori_loop(0, LINE, query_block, 0)
+    lax.fori_loop(0, LINE // 2, query_blocks, 0)
 
     for i in range(LINE):
         dk_own_ref[i] = dk[rows(OWN + i), :] * scale
@@ -252,12 +259,12 @@
         scratch_shapes=[
             pltpu.VMEM((DIM, BAND * TOK), BF16),
             pltpu.VMEM((BAND * TOK, DIM), F32),
-            pltpu.VMEM((OWN, TOK, TOK), F32),
-            pltpu.VMEM((OWN, TOK, TOK), F32),
-            pltpu.VMEM((OWN * TOK, TOK), BF16),
+            pltpu.VMEM((SPAN, TOK, WIDE), F32),
+            pltpu.VMEM((SPAN, TOK, WIDE), F32),
+            pltpu.VMEM((SPAN * TOK, WIDE), BF16),
         ]
-        + [pltpu.VMEM((OWN * TOK // PART, TOK), F32)] * 6,
-        compiler_params=pltpu.CompilerParams(vmem_limit_bytes=12 * 1024 * 1024),
+        + [pltpu.VMEM((SPAN * TOK // PART, WIDE), F32)] * 6,
+        compiler_params=pltpu.CompilerParams(vmem_limit_bytes=24 * 1024 * 1024),
         cost_estimate=pl.CostEstimate(flops=10**9, bytes_accessed=6 * 2**20, transcendentals=4 * 10**6),
     )(head, low, weight, start, queries, *keys)
 

time: 101 us -> 102 us (level)
  the two profiles are of different devices: /device:TPU:6 before, /device:TPU:4 now
where the time goes in v12:
time: 102 us
  blocking collectives  29.8 us (29%)
  starting transfers between devices  28.8 us (28%)
  waiting for transfers between devices  26.9 us (26%)
  Pallas kernels  14.5 us (14%)
    all_to_all x2, blocking collectives, exchange(): return lax.all_to_all(x, 'seq', 0, 0, axis_index_groups=lines)  29.8 us
    ppermute x4, starting transfers between devices, move(): return lax.ppermute(x, AXES, route)  21.7 us
    ppermute x4, waiting for transfers between devices, move(): return lax.ppermute(x, AXES, route)  21.6 us
    pallas_call x1, Pallas kernels, attend(): pl.pallas_call(main_kernel, out_shape=[jax.ShapeDtypeStruct((LINE, TOK, D...  7.75 us
    all_to_all x2, starting transfers between devices, exchange(): return lax.all_to_all(x, 'seq', 0, 0, axis_index_groups=lines)  7.07 us
    all_to_all x2, waiting for transfers between devices, exchange(): return lax.all_to_all(x, 'seq', 0, 0, axis_index_groups=lines)  5.29 us
    pallas_call x1, Pallas kernels, pack(): pl.pallas_call(pack_kernel, out_shape=[jax.ShapeDtypeStruct((HEADS, 2, TO...  2.34 us
    pallas_call x1, Pallas kernels, starts(): pl.pallas_call(starts_kernel, out_shape=[jax.ShapeDtypeStruct((LINE, TOK)...  2.19 us
  transfers between devices with their start and end apart: 6, of which 3 were waited for; matrix products, arithmetic and copies ran while one was open for 0% of the time, Pallas kernels for 2%

profile of v12, /device:TPU:4, one launch (start us, length us, event | category | flops | bytes accessed | tf_op | source)
XLA Modules:
  0.0 101.6 jit_solution(1475378624499332662)
XLA Ops:
  0.7 2.3 %shard_map.78 = (bf16[4,2,256,128]{3,2,1,0:T(8,128)(2,1)}, bf16[4,2,256,128]{3,2,1,0:T(8,128)(2,1)}) custom-call(s32[1]{0:T(128)} %bitcast.flip_ref, bf16[256,512]{1,0:T(8,128)(2,1)} %bitcast.9, bf16[256,512]{1,0:T(8,128)(2,1)} %bitcast.10, bf16[256,512]{1,0:T(8,128)(2,1)} %bitcast.11, bf16[256,512]{1,0:T(8,128)(2,1)} %bitcast.12), custom_call_target="tpu_custom_call" | custom-call | bytes 2097152 | tf_op jit(solution)/shard_map/pallas_call | solution.py:64
  3.0 19.4 %all_to_all.20.own_ref = bf16[4,2,256,128]{3,2,1,0:T(8,128)(2,1)S(1)} all-to-all(bf16[4,2,256,128]{3,2,1,0:T(8,128)(2,1)} %get-tuple-element.17), channel_id=1, replica_groups={{0,4,8,12},{16,20,24,28},{32,36,40,44},{48,52,56,60},{64,68,72,76},{80,..., dimensions={0} | all-to-all | bytes 1048576 | tf_op jit(solution)/shard_map/all_to_all | solution.py:285
  22.4 4.8 %collective-permute-start = (bf16[4,2,256,128]{3,2,1,0:T(8,128)(2,1)S(1)}, bf16[4,2,256,128]{3,2,1,0:T(8,128)(2,1)S(1)}, u32[]{:S(2)}, u32[]{:S(2)}) collective-permute-start(bf16[4,2,256,128]{3,2,1,0:T(8,128)(2,1)S(1)} %all_to_all.20.own_ref), channel_id=1, source_target_pairs={{0,28},{1,29},{2,30},{3,31},{4,24},{5,25},{6,26},{7,27},{8,20},{9,... | collective-permute-start | bytes 1572872 | tf_op jit(solution)/shard_map/ppermute | solution.py:282
  27.2 4.3 %collective-permute-start.1 = (bf16[3,2,256,128]{3,2,1,0:T(8,128)(2,1)S(1)}, bf16[3,2,256,128]{3,2,1,0:T(8,128)(2,1)S(1)}, u32[]{:S(2)}, u32[]{:S(2)}) collective-permute-start(bf16[3,2,256,128]{3,2,1,0:T(8,128)(2,1)S(1)} %slice.4), channel_id=1, source_target_pairs={{0,32},{1,33},{2,34},{3,35},{4,36},{5,37},{6,38},{7,39},{8,40},{9,... | collective-permute-start | bytes 1179656 | tf_op jit(solution)/shard_map/ppermute | solution.py:282
  31.4 3.6 %all-to-all-start = ((bf16[4,2,256,128]{3,2,1,0:T(8,128)(2,1)}), bf16[4,2,256,128]{3,2,1,0:T(8,128)(2,1)S(1)}, u32[]{:S(2)}, u32[]{:S(2)}) async-start(bf16[4,2,256,128]{3,2,1,0:T(8,128)(2,1)} %get-tuple-element.16), calls=%async_computation | async-start | bytes 1048576 | tf_op jit(solution)/shard_map/all_to_all | solution.py:285
  35.1 2.2 %shard_map.77 = (s32[4,256]{1,0:T(4,128)}, s32[4]{0:T(128)}) custom-call(s32[1]{0:T(128)} %bitcast.2.range_ref, s32[1,32768]{1,0:T(1,128)} %seg_ref.1), custom_call_target="tpu_custom_call" | custom-call | bytes 1048576 | tf_op jit(solution)/shard_map/pallas_call | solution.py:107
  37.3 20.3 %collective-permute-done.1.before_ref = bf16[3,2,256,128]{3,2,1,0:T(8,128)(2,1)S(1)} collective-permute-done((bf16[3,2,256,128]{3,2,1,0:T(8,128)(2,1)S(1)}, bf16[3,2,256,128]{3,2,1,0:T(8,128)(2,1)S(1)}, u32[]{:S(2)}, u32[]{:S(2)}) %collective-permute-start.1) | collective-permute-done | bytes 393248 | tf_op jit(solution)/shard_map/ppermute | solution.py:282
  57.6 0.0 collective-permute-done.last_ref
  57.6 0.1 shard_map.79
  57.7 0.0 all-to-all-done.query_ref
  57.7 0.0 copy-start
  57.7 0.0 copy-start.1
  57.7 0.0 copy-start.2
  57.7 0.7 copy-done
  58.4 0.0 copy-done.1
  58.4 0.0 copy-done.2
  58.4 7.7 %shard_map.80 = (bf16[4,256,128]{2,1,0:T(8,128)(2,1)}, f32[4,256,128]{2,1,0:T(8,128)S(1)}, bf16[4,256,128]{2,1,0:T(8,128)(2,1)S(1)}, bf16[3,256,128]{2,1,0:T(8,128)(2,1)S(1)}) custom-call(s32[1]{0:T(128)} %bitcast.1.head_ref, s32[4]{0:T(128)S(1)} %copy-done.2, f32[4]{0:T(128)S(1)} %copy-done.1, s32[4,256]{1,0:T(4,128)S(1)} %copy-done, ...), custom_call_target="tpu_custom_call" | custom-call | flops 1000000000 | bytes 6291456 | tf_op jit(solution)/shard_map/pallas_call | solution.py:249
  66.1 5.5 %collective-permute-start.2 = (bf16[4,256,128]{2,1,0:T(8,128)(2,1)S(1)}, bf16[4,256,128]{2,1,0:T(8,128)(2,1)S(1)}, u32[]{:S(2)}, u32[]{:S(2)}) collective-permute-start(bf16[4,256,128]{2,1,0:T(8,128)(2,1)S(1)} %get-tuple-element.22), channel_id=1, source_target_pairs={{28,0},{29,1},{30,2},{31,3},{24,4},{25,5},{26,6},{27,7},{20,8},{21... | collective-permute-start | bytes 786440 | tf_op jit(solution)/shard_map/ppermute | solution.py:282
  71.6 7.2 %collective-permute-start.3 = (bf16[3,256,128]{2,1,0:T(8,128)(2,1)S(1)}, bf16[3,256,128]{2,1,0:T(8,128)(2,1)S(1)}, u32[]{:S(2)}, u32[]{:S(2)}) collective-permute-start(bf16[3,256,128]{2,1,0:T(8,128)(2,1)S(1)} %get-tuple-element.23), channel_id=1, source_target_pairs={{32,0},{33,1},{34,2},{35,3},{36,4},{37,5},{38,6},{39,7},{40,8},{41... | collective-permute-start | bytes 589832 | tf_op jit(solution)/shard_map/ppermute | solution.py:282
  78.8 3.4 %all-to-all-start.2 = ((bf16[4,256,128]{2,1,0:T(8,128)(2,1)}), bf16[4,256,128]{2,1,0:T(8,128)(2,1)S(1)}, u32[]{:S(2)}, u32[]{:S(2)}) async-start(bf16[4,256,128]{2,1,0:T(8,128)(2,1)} %get-tuple-element.20), calls=%async_computation.2 | async-start | bytes 524288 | tf_op jit(solution)/shard_map/all_to_all | solution.py:285
  82.3 0.0 collective-permute-done.3
  82.3 1.4 %collective-permute-done.2 = bf16[4,256,128]{2,1,0:T(8,128)(2,1)S(1)} collective-permute-done((bf16[4,256,128]{2,1,0:T(8,128)(2,1)S(1)}, bf16[4,256,128]{2,1,0:T(8,128)(2,1)S(1)}, u32[]{:S(2)}, u32[]{:S(2)}) %collective-permute-start.2) | collective-permute-done | bytes 262176 | tf_op jit(solution)/shard_map/ppermute | solution.py:282
  83.6 0.1 add_convert_fusion
  83.7 5.3 %all-to-all-done.2.dq_ref = bf16[4,256,128]{2,1,0:T(8,128)(2,1)S(1)} async-done(((bf16[4,256,128]{2,1,0:T(8,128)(2,1)}), bf16[4,256,128]{2,1,0:T(8,128)(2,1)S(1)}, u32[]{:S(2)}, u32[]{:S(2)}) %all-to-all-start.2) | async-done | bytes 262176 | tf_op jit(solution)/shard_map/all_to_all | solution.py:285
  89.0 0.0 copy-start.3
  89.0 10.5 %all_to_all.21.dk_ref = bf16[4,256,128]{2,1,0:T(8,128)(2,1)} all-to-all(bf16[4,256,128]{2,1,0:T(8,128)(2,1)S(1)} %add_convert_fusion), channel_id=1, replica_groups={{0,4,8,12},{16,20,24,28},{32,36,40,44},{48,52,56,60},{64,68,72,76},{80,..., dimensions={0} | all-to-all | bytes 524288 | tf_op jit(solution)/shard_map/all_to_all | solution.py:285
  99.4 0.0 copy-done.3
  99.5 2.1 %shard_map.81 = (f32[256,512]{1,0:T(8,128)}, f32[256,512]{1,0:T(8,128)}) custom-call(s32[1]{0:T(128)} %bitcast.flip_ref, bf16[4,256,128]{2,1,0:T(8,128)(2,1)} %copy-done.3, bf16[4,256,128]{2,1,0:T(8,128)(2,1)} %all_to_all.21.dk_ref), custom_call_target="tpu_custom_call" | custom-call | bytes 1572864 | tf_op jit(solution)/shard_map/pallas_call | solution.py:124
  (1 shorter events, 0.0 us)
Async XLA Ops:
  22.4 35.2 %collective-permute-start = (bf16[4,2,256,128]{3,2,1,0:T(8,128)(2,1)S(1)}, bf16[4,2,256,128]{3,2,1,0:T(8,128)(2,1)S(1)}, u32[]{:S(2)}, u32[]{:S(2)}) collective-permute-start(bf16[4,2,256,128]{3,2,1,0:T(8,128)(2,1)S(1)} %all_to_all.20.own_ref), channel_id=1, source_target_pairs={{0,28},{1,29},{2,30},{3,31},{4,24},{5,25},{6,26},{7,27},{8,20},{9,... | collective-permute-start | bytes 1572872 | tf_op jit(solution)/shard_map/ppermute | solution.py:282
  27.2 30.4 %collective-permute-start.1 = (bf16[3,2,256,128]{3,2,1,0:T(8,128)(2,1)S(1)}, bf16[3,2,256,128]{3,2,1,0:T(8,128)(2,1)S(1)}, u32[]{:S(2)}, u32[]{:S(2)}) collective-permute-start(bf16[3,2,256,128]{3,2,1,0:T(8,128)(2,1)S(1)} %slice.4), channel_id=1, source_target_pairs={{0,32},{1,33},{2,34},{3,35},{4,36},{5,37},{6,38},{7,39},{8,40},{9,... | collective-permute-start | bytes 1179656 | tf_op jit(solution)/shard_map/ppermute | solution.py:282
  31.4 26.2 %all-to-all-start = ((bf16[4,2,256,128]{3,2,1,0:T(8,128)(2,1)}), bf16[4,2,256,128]{3,2,1,0:T(8,128)(2,1)S(1)}, u32[]{:S(2)}, u32[]{:S(2)}) async-start(bf16[4,2,256,128]{3,2,1,0:T(8,128)(2,1)} %get-tuple-element.16), calls=%async_computation | async-start | bytes 1048576 | tf_op jit(solution)/shard_map/all_to_all | solution.py:285
  57.7 0.7 copy-start
  57.7 0.7 copy-start.1
  57.7 0.7 copy-start.2
  66.1 17.5 %collective-permute-start.2 = (bf16[4,256,128]{2,1,0:T(8,128)(2,1)S(1)}, bf16[4,256,128]{2,1,0:T(8,128)(2,1)S(1)}, u32[]{:S(2)}, u32[]{:S(2)}) collective-permute-start(bf16[4,256,128]{2,1,0:T(8,128)(2,1)S(1)} %get-tuple-element.22), channel_id=1, source_target_pairs={{28,0},{29,1},{30,2},{31,3},{24,4},{25,5},{26,6},{27,7},{20,8},{21... | collective-permute-start | bytes 786440 | tf_op jit(solution)/shard_map/ppermute | solution.py:282
  71.6 10.6 %collective-permute-start.3 = (bf16[3,256,128]{2,1,0:T(8,128)(2,1)S(1)}, bf16[3,256,128]{2,1,0:T(8,128)(2,1)S(1)}, u32[]{:S(2)}, u32[]{:S(2)}) collective-permute-start(bf16[3,256,128]{2,1,0:T(8,128)(2,1)S(1)} %get-tuple-element.23), channel_id=1, source_target_pairs={{32,0},{33,1},{34,2},{35,3},{36,4},{37,5},{38,6},{39,7},{40,8},{41... | collective-permute-start | bytes 589832 | tf_op jit(solution)/shard_map/ppermute | solution.py:282
  78.8 10.2 %all-to-all-start.2 = ((bf16[4,256,128]{2,1,0:T(8,128)(2,1)}), bf16[4,256,128]{2,1,0:T(8,128)(2,1)S(1)}, u32[]{:S(2)}, u32[]{:S(2)}) async-start(bf16[4,256,128]{2,1,0:T(8,128)(2,1)} %get-tuple-element.20), calls=%async_computation.2 | async-start | bytes 524288 | tf_op jit(solution)/shard_map/all_to_all | solution.py:285
  89.0 10.5 %copy-start.3 = (bf16[4,256,128]{2,1,0:T(8,128)(2,1)}, bf16[4,256,128]{2,1,0:T(8,128)(2,1)S(1)}, u32[]{:S(2)}) copy-start(bf16[4,256,128]{2,1,0:T(8,128)(2,1)S(1)} %all-to-all-done.2.dq_ref) | copy-start | bytes 786436

commit v13 on v11

--- a/solution.py
+++ b/solution.py
@@ -188,18 +188,17 @@
         parts = [(i, c) for i in range(blocks) for c in range(TOK // PART)]
         held = pl.ds(0, len(parts))
 
-        def keys(i):
-            return pl.ds(pl.multiple_of(base + i * TOK, TOK), TOK)
-
+        span = pl.ds(base, blocks * TOK)
+
+        scores = [jnp.dot(k[span, :], q, preferred_element_type=F32) for k, q, *_ in sides]
         for i in range(blocks):
-            scores = [jnp.dot(k[keys(i), :], q, preferred_element_type=F32) for k, q, *_ in sides]
             for c in range(TOK // PART):
                 here, at = pl.ds(c * PART, PART), i * (TOK // PART) + c
                 visible = key_row >= start - (i * TOK + c * PART)
                 if i == blocks - 1:
                     visible = visible & (key_row <= query_column - c * PART)
                 for s, (_, _, e, top, total, _) in zip(scores, sides):
-                    x = jnp.where(visible, s[c * PART : (c + 1) * PART], MASKED)
+                    x = jnp.where(visible, s[at * PART : (at + 1) * PART], MASKED)
                     h = jnp.max(x, axis=0, keepdims=True)
                     x = jnp.exp2((x - h) * pace)
                     e[i, here, :] = x
@@ -214,10 +213,9 @@
                 here, at = pl.ds(c * PART, PART), pl.ds(i * (TOK // PART) + c, 1)
                 g = es[i, here, :] * factor_s[at, :] - et[i, here, :] * factor_t[at, :]
                 grad[pl.ds(i * TOK + c * PART, PART), :] = g.astype(BF16)
-            dk[keys(i), :] += jnp.dot(grad[rows(i), :], q_s, preferred_element_type=F32)
-        dq = jnp.dot(
-            ks_turned[:, pl.ds(base, blocks * TOK)], grad[: blocks * TOK, :], preferred_element_type=F32
-        )
+        grads = grad[: blocks * TOK, :]
+        dk[span, :] += jnp.dot(grads, q_s, preferred_element_type=F32)
+        dq = jnp.dot(ks_turned[:, span], grads, preferred_element_type=F32)
         dq_ref[j] = (dq * scale).T.astype(BF16)
 
     def query_block(j, _):
@@ -257,7 +255,7 @@
             pltpu.VMEM((OWN * TOK, TOK), BF16),
         ]
         + [pltpu.VMEM((OWN * TOK // PART, TOK), F32)] * 6,
-        compiler_params=pltpu.CompilerParams(vmem_limit_bytes=12 * 1024 * 1024),
+        compiler_params=pltpu.CompilerParams(vmem_limit_bytes=20 * 1024 * 1024),
         cost_estimate=pl.CostEstimate(flops=10**9, bytes_accessed=6 * 2**20, transcendentals=4 * 10**6),
     )(head, low, weight, start, queries, *keys)
 

time: 101 us -> 99.4 us (0.984)
  Pallas kernels: 15.7 us -> 14.4 us
    pallas_call x1, Pallas kernels: 8.93 us -> 7.63 us  [attend(): pl.pallas_call(main_kernel, out_shape=[jax.ShapeDtypeStruct((LINE, TOK, D...]
  transfers between devices with their start and end apart: 6 -> 6, of which waited for: 3 -> 4; matrix products, arithmetic and copies ran while one was open for 0% -> 0% of each run, Pallas kernels for 2% -> 2%
where the time goes in v13:
time: 99.4 us; the launch traced here: 98.9 us
  blocking collectives  29.8 us (30%)
  waiting for transfers between devices  27.8 us (28%)
  starting transfers between devices  25.3 us (25%)
  Pallas kernels  14.4 us (14%)
    all_to_all x2, blocking collectives, exchange(): return lax.all_to_all(x, 'seq', 0, 0, axis_index_groups=lines)  29.8 us
    ppermute x4, waiting for transfers between devices, move(): return lax.ppermute(x, AXES, route)  24.8 us
    ppermute x4, starting transfers between devices, move(): return lax.ppermute(x, AXES, route)  18.2 us
    pallas_call x1, Pallas kernels, attend(): pl.pallas_call(main_kernel, out_shape=[jax.ShapeDtypeStruct((LINE, TOK, D...  7.63 us
    all_to_all x2, starting transfers between devices, exchange(): return lax.all_to_all(x, 'seq', 0, 0, axis_index_groups=lines)  7.07 us
    all_to_all x2, waiting for transfers between devices, exchange(): return lax.all_to_all(x, 'seq', 0, 0, axis_index_groups=lines)  2.97 us
    pallas_call x1, Pallas kernels, pack(): pl.pallas_call(pack_kernel, out_shape=[jax.ShapeDtypeStruct((HEADS, 2, TO...  2.34 us
    pallas_call x1, Pallas kernels, starts(): pl.pallas_call(starts_kernel, out_shape=[jax.ShapeDtypeStruct((LINE, TOK)...  2.19 us
  transfers between devices with their start and end apart: 6, of which 4 were waited for; matrix products, arithmetic and copies ran while one was open for 0% of the time, Pallas kernels for 2%

profile of v13, /device:TPU:6, one launch (start us, length us, event | category | flops | bytes accessed | tf_op | source)
XLA Modules:
  0.0 98.9 jit_solution(8826070087913516756)
XLA Ops:
  0.7 2.3 %shard_map.78 = (bf16[4,2,256,128]{3,2,1,0:T(8,128)(2,1)}, bf16[4,2,256,128]{3,2,1,0:T(8,128)(2,1)}) custom-call(s32[1]{0:T(128)} %bitcast.flip_ref, bf16[256,512]{1,0:T(8,128)(2,1)} %bitcast.9, bf16[256,512]{1,0:T(8,128)(2,1)} %bitcast.10, bf16[256,512]{1,0:T(8,128)(2,1)} %bitcast.11, bf16[256,512]{1,0:T(8,128)(2,1)} %bitcast.12), custom_call_target="tpu_custom_call" | custom-call | bytes 2097152 | tf_op jit(solution)/shard_map/pallas_call | solution.py:62
  3.0 19.4 %all_to_all.20.own_ref = bf16[4,2,256,128]{3,2,1,0:T(8,128)(2,1)S(1)} all-to-all(bf16[4,2,256,128]{3,2,1,0:T(8,128)(2,1)} %get-tuple-element.17), channel_id=1, replica_groups={{0,4,8,12},{16,20,24,28},{32,36,40,44},{48,52,56,60},{64,68,72,76},{80,..., dimensions={0} | all-to-all | bytes 1048576 | tf_op jit(solution)/shard_map/all_to_all | solution.py:276
  22.4 4.8 %collective-permute-start = (bf16[4,2,256,128]{3,2,1,0:T(8,128)(2,1)S(1)}, bf16[4,2,256,128]{3,2,1,0:T(8,128)(2,1)S(1)}, u32[]{:S(2)}, u32[]{:S(2)}) collective-permute-start(bf16[4,2,256,128]{3,2,1,0:T(8,128)(2,1)S(1)} %all_to_all.20.own_ref), channel_id=1, source_target_pairs={{0,28},{1,29},{2,30},{3,31},{4,24},{5,25},{6,26},{7,27},{8,20},{9,... | collective-permute-start | bytes 1572872 | tf_op jit(solution)/shard_map/ppermute | solution.py:273
  27.2 4.3 %collective-permute-start.1 = (bf16[3,2,256,128]{3,2,1,0:T(8,128)(2,1)S(1)}, bf16[3,2,256,128]{3,2,1,0:T(8,128)(2,1)S(1)}, u32[]{:S(2)}, u32[]{:S(2)}) collective-permute-start(bf16[3,2,256,128]{3,2,1,0:T(8,128)(2,1)S(1)} %slice.4), channel_id=1, source_target_pairs={{0,32},{1,33},{2,34},{3,35},{4,36},{5,37},{6,38},{7,39},{8,40},{9,... | collective-permute-start | bytes 1179656 | tf_op jit(solution)/shard_map/ppermute | solution.py:273
  31.4 3.6 %all-to-all-start = ((bf16[4,2,256,128]{3,2,1,0:T(8,128)(2,1)}), bf16[4,2,256,128]{3,2,1,0:T(8,128)(2,1)S(1)}, u32[]{:S(2)}, u32[]{:S(2)}) async-start(bf16[4,2,256,128]{3,2,1,0:T(8,128)(2,1)} %get-tuple-element.16), calls=%async_computation | async-start | bytes 1048576 | tf_op jit(solution)/shard_map/all_to_all | solution.py:276
  35.1 2.2 %shard_map.77 = (s32[4,256]{1,0:T(4,128)}, s32[4]{0:T(128)}) custom-call(s32[1]{0:T(128)} %bitcast.2.range_ref, s32[1,32768]{1,0:T(1,128)} %seg_ref.1), custom_call_target="tpu_custom_call" | custom-call | bytes 1048576 | tf_op jit(solution)/shard_map/pallas_call | solution.py:105
  37.3 21.2 %collective-permute-done.1.before_ref = bf16[3,2,256,128]{3,2,1,0:T(8,128)(2,1)S(1)} collective-permute-done((bf16[3,2,256,128]{3,2,1,0:T(8,128)(2,1)S(1)}, bf16[3,2,256,128]{3,2,1,0:T(8,128)(2,1)S(1)}, u32[]{:S(2)}, u32[]{:S(2)}) %collective-permute-start.1) | collective-permute-done | bytes 393248 | tf_op jit(solution)/shard_map/ppermute | solution.py:273
  58.5 0.0 collective-permute-done.last_ref
  58.5 0.1 shard_map.79
  58.6 0.0 all-to-all-done.query_ref
  58.6 0.0 copy-start
  58.6 0.0 copy-start.1
  58.6 0.0 copy-start.2
  58.6 0.7 copy-done
  59.3 0.0 copy-done.1
  59.3 0.0 copy-done.2
  59.3 7.6 %shard_map.80 = (bf16[4,256,128]{2,1,0:T(8,128)(2,1)}, f32[4,256,128]{2,1,0:T(8,128)S(1)}, bf16[4,256,128]{2,1,0:T(8,128)(2,1)S(1)}, bf16[3,256,128]{2,1,0:T(8,128)(2,1)S(1)}) custom-call(s32[1]{0:T(128)} %bitcast.1.head_ref, s32[4]{0:T(128)S(1)} %copy-done.2, f32[4]{0:T(128)S(1)} %copy-done.1, s32[4,256]{1,0:T(4,128)S(1)} %copy-done, ...), custom_call_target="tpu_custom_call" | custom-call | flops 1000000000 | bytes 6291456 | tf_op jit(solution)/shard_map/pallas_call | solution.py:240
  66.9 7.3 %collective-permute-start.2 = (bf16[4,256,128]{2,1,0:T(8,128)(2,1)S(1)}, bf16[4,256,128]{2,1,0:T(8,128)(2,1)S(1)}, u32[]{:S(2)}, u32[]{:S(2)}) collective-permute-start(bf16[4,256,128]{2,1,0:T(8,128)(2,1)S(1)} %get-tuple-element.22), channel_id=1, source_target_pairs={{28,0},{29,1},{30,2},{31,3},{24,4},{25,5},{26,6},{27,7},{20,8},{21... | collective-permute-start | bytes 786440 | tf_op jit(solution)/shard_map/ppermute | solution.py:273
  74.2 1.9 %collective-permute-start.3 = (bf16[3,256,128]{2,1,0:T(8,128)(2,1)S(1)}, bf16[3,256,128]{2,1,0:T(8,128)(2,1)S(1)}, u32[]{:S(2)}, u32[]{:S(2)}) collective-permute-start(bf16[3,256,128]{2,1,0:T(8,128)(2,1)S(1)} %get-tuple-element.23), channel_id=1, source_target_pairs={{32,0},{33,1},{34,2},{35,3},{36,4},{37,5},{38,6},{39,7},{40,8},{41... | collective-permute-start | bytes 589832 | tf_op jit(solution)/shard_map/ppermute | solution.py:273
  76.1 3.4 %all-to-all-start.2 = ((bf16[4,256,128]{2,1,0:T(8,128)(2,1)}), bf16[4,256,128]{2,1,0:T(8,128)(2,1)S(1)}, u32[]{:S(2)}, u32[]{:S(2)}) async-start(bf16[4,256,128]{2,1,0:T(8,128)(2,1)} %get-tuple-element.20), calls=%async_computation.2 | async-start | bytes 524288 | tf_op jit(solution)/shard_map/all_to_all | solution.py:276
  79.5 2.2 %collective-permute-done.3 = bf16[3,256,128]{2,1,0:T(8,128)(2,1)S(1)} collective-permute-done((bf16[3,256,128]{2,1,0:T(8,128)(2,1)S(1)}, bf16[3,256,128]{2,1,0:T(8,128)(2,1)S(1)}, u32[]{:S(2)}, u32[]{:S(2)}) %collective-permute-start.3) | collective-permute-done | bytes 196640 | tf_op jit(solution)/shard_map/ppermute | solution.py:273
  81.8 1.5 %collective-permute-done.2 = bf16[4,256,128]{2,1,0:T(8,128)(2,1)S(1)} collective-permute-done((bf16[4,256,128]{2,1,0:T(8,128)(2,1)S(1)}, bf16[4,256,128]{2,1,0:T(8,128)(2,1)S(1)}, u32[]{:S(2)}, u32[]{:S(2)}) %collective-permute-start.2) | collective-permute-done | bytes 262176 | tf_op jit(solution)/shard_map/ppermute | solution.py:273
  83.2 0.1 add_convert_fusion
  83.3 3.0 %all-to-all-done.2.dq_ref = bf16[4,256,128]{2,1,0:T(8,128)(2,1)S(1)} async-done(((bf16[4,256,128]{2,1,0:T(8,128)(2,1)}), bf16[4,256,128]{2,1,0:T(8,128)(2,1)S(1)}, u32[]{:S(2)}, u32[]{:S(2)}) %all-to-all-start.2) | async-done | bytes 262176 | tf_op jit(solution)/shard_map/all_to_all | solution.py:276
  86.3 0.0 copy-start.3
  86.3 10.5 %all_to_all.21.dk_ref = bf16[4,256,128]{2,1,0:T(8,128)(2,1)} all-to-all(bf16[4,256,128]{2,1,0:T(8,128)(2,1)S(1)} %add_convert_fusion), channel_id=1, replica_groups={{0,4,8,12},{16,20,24,28},{32,36,40,44},{48,52,56,60},{64,68,72,76},{80,..., dimensions={0} | all-to-all | bytes 524288 | tf_op jit(solution)/shard_map/all_to_all | solution.py:276
  96.7 0.0 copy-done.3
  96.7 2.1 %shard_map.81 = (f32[256,512]{1,0:T(8,128)}, f32[256,512]{1,0:T(8,128)}) custom-call(s32[1]{0:T(128)} %bitcast.flip_ref, bf16[4,256,128]{2,1,0:T(8,128)(2,1)} %copy-done.3, bf16[4,256,128]{2,1,0:T(8,128)(2,1)} %all_to_all.21.dk_ref), custom_call_target="tpu_custom_call" | custom-call | bytes 1572864 | tf_op jit(solution)/shard_map/pallas_call | solution.py:122
  (1 shorter events, 0.0 us)
Async XLA Ops:
  22.4 36.1 %collective-permute-start = (bf16[4,2,256,128]{3,2,1,0:T(8,128)(2,1)S(1)}, bf16[4,2,256,128]{3,2,1,0:T(8,128)(2,1)S(1)}, u32[]{:S(2)}, u32[]{:S(2)}) collective-permute-start(bf16[4,2,256,128]{3,2,1,0:T(8,128)(2,1)S(1)} %all_to_all.20.own_ref), channel_id=1, source_target_pairs={{0,28},{1,29},{2,30},{3,31},{4,24},{5,25},{6,26},{7,27},{8,20},{9,... | collective-permute-start | bytes 1572872 | tf_op jit(solution)/shard_map/ppermute | solution.py:273
  27.2 31.3 %collective-permute-start.1 = (bf16[3,2,256,128]{3,2,1,0:T(8,128)(2,1)S(1)}, bf16[3,2,256,128]{3,2,1,0:T(8,128)(2,1)S(1)}, u32[]{:S(2)}, u32[]{:S(2)}) collective-permute-start(bf16[3,2,256,128]{3,2,1,0:T(8,128)(2,1)S(1)} %slice.4), channel_id=1, source_target_pairs={{0,32},{1,33},{2,34},{3,35},{4,36},{5,37},{6,38},{7,39},{8,40},{9,... | collective-permute-start | bytes 1179656 | tf_op jit(solution)/shard_map/ppermute | solution.py:273
  31.4 27.1 %all-to-all-start = ((bf16[4,2,256,128]{3,2,1,0:T(8,128)(2,1)}), bf16[4,2,256,128]{3,2,1,0:T(8,128)(2,1)S(1)}, u32[]{:S(2)}, u32[]{:S(2)}) async-start(bf16[4,2,256,128]{3,2,1,0:T(8,128)(2,1)} %get-tuple-element.16), calls=%async_computation | async-start | bytes 1048576 | tf_op jit(solution)/shard_map/all_to_all | solution.py:276
  58.6 0.7 copy-start
  58.6 0.7 copy-start.1
  58.6 0.7 copy-start.2
  66.9 16.3 %collective-permute-start.2 = (bf16[4,256,128]{2,1,0:T(8,128)(2,1)S(1)}, bf16[4,256,128]{2,1,0:T(8,128)(2,1)S(1)}, u32[]{:S(2)}, u32[]{:S(2)}) collective-permute-start(bf16[4,256,128]{2,1,0:T(8,128)(2,1)S(1)} %get-tuple-element.22), channel_id=1, source_target_pairs={{28,0},{29,1},{30,2},{31,3},{24,4},{25,5},{26,6},{27,7},{20,8},{21... | collective-permute-start | bytes 786440 | tf_op jit(solution)/shard_map/ppermute | solution.py:273
  74.2 7.6 %collective-permute-start.3 = (bf16[3,256,128]{2,1,0:T(8,128)(2,1)S(1)}, bf16[3,256,128]{2,1,0:T(8,128)(2,1)S(1)}, u32[]{:S(2)}, u32[]{:S(2)}) collective-permute-start(bf16[3,256,128]{2,1,0:T(8,128)(2,1)S(1)} %get-tuple-element.23), channel_id=1, source_target_pairs={{32,0},{33,1},{34,2},{35,3},{36,4},{37,5},{38,6},{39,7},{40,8},{41... | collective-permute-start | bytes 589832 | tf_op jit(solution)/shard_map/ppermute | solution.py:273
  76.1 10.2 %all-to-all-start.2 = ((bf16[4,256,128]{2,1,0:T(8,128)(2,1)}), bf16[4,256,128]{2,1,0:T(8,128)(2,1)S(1)}, u32[]{:S(2)}, u32[]{:S(2)}) async-start(bf16[4,256,128]{2,1,0:T(8,128)(2,1)} %get-tuple-element.20), calls=%async_computation.2 | async-start | bytes 524288 | tf_op jit(solution)/shard_map/all_to_all | solution.py:276
  86.3 10.5 %copy-start.3 = (bf16[4,256,128]{2,1,0:T(8,128)(2,1)}, bf16[4,256,128]{2,1,0:T(8,128)(2,1)S(1)}, u32[]{:S(2)}) copy-start(bf16[4,256,128]{2,1,0:T(8,128)(2,1)S(1)} %all-to-all-done.2.dq_ref) | copy-start | bytes 786436

commit v14 on v13

--- a/solution.py
+++ b/solution.py
@@ -111,21 +111,21 @@
     )(range_index, seg)
 
 
-def unpack_kernel(flip_ref, dq_ref, dk_ref, query_ref, key_ref):
+def unpack_kernel(flip_ref, grads_ref, query_ref, key_ref):
     for place in range(HEADS):
         columns = head_columns(flip_ref[0], place)
-        query_ref[:, columns] = dq_ref[place].astype(F32)
-        key_ref[:, columns] = dk_ref[place].astype(F32)
-
-
-def unpack(flip, dq, dk):
+        query_ref[:, columns] = grads_ref[place, 0].astype(F32)
+        key_ref[:, columns] = grads_ref[place, 1].astype(F32)
+
+
+def unpack(flip, grads):
     return pl.pallas_call(
         unpack_kernel,
         out_shape=[jax.ShapeDtypeStruct((TOK, HEADS * DIM), F32)] * 2,
-        in_specs=[SMEM, VMEM, VMEM],
+        in_specs=[SMEM, VMEM],
         out_specs=[VMEM] * 2,
         cost_estimate=pl.CostEstimate(flops=0, bytes_accessed=12 * TOK * 512, transcendentals=0),
-    )(flip, dq, dk)
+    )(flip, grads)
 
 
 def layout_kernel(own_ref, last_ref, before_ref, kt, ks):
@@ -286,9 +286,8 @@
 
     back_last = move(dk_last, reverse(to_next)).astype(F32)
     back_before = move(dk_before, reverse(to_second)).astype(F32)
-    dq_home = exchange(dq)
     total = dk_own + back_last + jnp.pad(back_before, ((1, 0), (0, 0), (0, 0)))
-    query_grad, key_grad = unpack(flip, dq_home, exchange(total.astype(BF16)))
+    query_grad, key_grad = unpack(flip, exchange(jnp.stack([dq, total.astype(BF16)], axis=1)))
     return query_grad[None], key_grad[None]
 
 

time: 99.4 us -> 104 us (1.046)
  blocking collectives: 29.8 us -> 37.4 us
  starting transfers between devices: 25.3 us -> 21.7 us
  Pallas kernels: 14.4 us -> 13.3 us
  waiting for transfers between devices: 27.8 us -> 28.9 us
    all_to_all x2, blocking collectives: 29.8 us -> 37.4 us  [exchange(): return lax.all_to_all(x, 'seq', 0, 0, axis_index_groups=lines)]
    ppermute x4, waiting for transfers between devices: 24.8 us -> 28.9 us  [move(): return lax.ppermute(x, AXES, route)]
    all_to_all x2 -> x1, starting transfers between devices: 7.07 us -> 3.65 us  [exchange(): return lax.all_to_all(x, 'seq', 0, 0, axis_index_groups=lines)]
    all_to_all x2 -> x1, waiting for transfers between devices: 2.97 us -> 0.01 us  [exchange(): return lax.all_to_all(x, 'seq', 0, 0, axis_index_groups=lines)]
    pallas_call x1, Pallas kernels: 7.63 us -> 6.56 us  [attend(): pl.pallas_call(main_kernel, out_shape=[jax.ShapeDtypeStruct((LINE, TOK, D...]
  transfers between devices with their start and end apart: 6 -> 5, of which waited for: 4 -> 3; matrix products, arithmetic and copies ran while one was open for 0% -> 0% of each run, Pallas kernels for 2% -> 2%
where the time goes in v14:
time: 104 us; the launch traced here: 103 us
  blocking collectives  37.4 us (36%)
  waiting for transfers between devices  28.9 us (28%)
  starting transfers between devices  21.7 us (21%)
  Pallas kernels  13.3 us (13%)
    all_to_all x2, blocking collectives, exchange(): return lax.all_to_all(x, 'seq', 0, 0, axis_index_groups=lines)  37.4 us
    ppermute x4, waiting for transfers between devices, move(): return lax.ppermute(x, AXES, route)  28.9 us
    ppermute x4, starting transfers between devices, move(): return lax.ppermute(x, AXES, route)  18.1 us
    pallas_call x1, Pallas kernels, attend(): pl.pallas_call(main_kernel, out_shape=[jax.ShapeDtypeStruct((LINE, TOK, D...  6.56 us
    all_to_all x1, starting transfers between devices, exchange(): return lax.all_to_all(x, 'seq', 0, 0, axis_index_groups=lines)  3.65 us
    pallas_call x1, Pallas kernels, pack(): pl.pallas_call(pack_kernel, out_shape=[jax.ShapeDtypeStruct((HEADS, 2, TO...  2.34 us
    pallas_call x1, Pallas kernels, starts(): pl.pallas_call(starts_kernel, out_shape=[jax.ShapeDtypeStruct((LINE, TOK)...  2.19 us
    pallas_call x1, Pallas kernels, unpack(): pl.pallas_call(unpack_kernel, out_shape=[jax.ShapeDtypeStruct((TOK, HEADS...  2.13 us
  transfers between devices with their start and end apart: 5, of which 3 were waited for; matrix products, arithmetic and copies ran while one was open for 0% of the time, Pallas kernels for 2%

profile of v14, /device:TPU:6, one launch (start us, length us, event | category | flops | bytes accessed | tf_op | source)
XLA Modules:
  0.0 103.0 jit_solution(14625801356480531414)
XLA Ops:
  0.7 2.3 %shard_map.78 = (bf16[4,2,256,128]{3,2,1,0:T(8,128)(2,1)}, bf16[4,2,256,128]{3,2,1,0:T(8,128)(2,1)}) custom-call(s32[1]{0:T(128)} %bitcast.flip_ref, bf16[256,512]{1,0:T(8,128)(2,1)} %bitcast.13, bf16[256,512]{1,0:T(8,128)(2,1)} %bitcast.14, bf16[256,512]{1,0:T(8,128)(2,1)} %bitcast.15, bf16[256,512]{1,0:T(8,128)(2,1)} %bitcast.16), custom_call_target="tpu_custom_call" | custom-call | bytes 2097152 | tf_op jit(solution)/shard_map/pallas_call | solution.py:62
  3.0 19.4 %all_to_all.15.own_ref = bf16[4,2,256,128]{3,2,1,0:T(8,128)(2,1)S(1)} all-to-all(bf16[4,2,256,128]{3,2,1,0:T(8,128)(2,1)} %get-tuple-element.17), channel_id=1, replica_groups={{0,4,8,12},{16,20,24,28},{32,36,40,44},{48,52,56,60},{64,68,72,76},{80,..., dimensions={0} | all-to-all | bytes 1048576 | tf_op jit(solution)/shard_map/all_to_all | solution.py:276
  22.4 4.8 %collective-permute-start = (bf16[4,2,256,128]{3,2,1,0:T(8,128)(2,1)S(1)}, bf16[4,2,256,128]{3,2,1,0:T(8,128)(2,1)S(1)}, u32[]{:S(2)}, u32[]{:S(2)}) collective-permute-start(bf16[4,2,256,128]{3,2,1,0:T(8,128)(2,1)S(1)} %all_to_all.15.own_ref), channel_id=1, source_target_pairs={{0,28},{1,29},{2,30},{3,31},{4,24},{5,25},{6,26},{7,27},{8,20},{9,... | collective-permute-start | bytes 1572872 | tf_op jit(solution)/shard_map/ppermute | solution.py:273
  27.2 4.3 %collective-permute-start.1 = (bf16[3,2,256,128]{3,2,1,0:T(8,128)(2,1)S(1)}, bf16[3,2,256,128]{3,2,1,0:T(8,128)(2,1)S(1)}, u32[]{:S(2)}, u32[]{:S(2)}) collective-permute-start(bf16[3,2,256,128]{3,2,1,0:T(8,128)(2,1)S(1)} %slice.4), channel_id=1, source_target_pairs={{0,32},{1,33},{2,34},{3,35},{4,36},{5,37},{6,38},{7,39},{8,40},{9,... | collective-permute-start | bytes 1179656 | tf_op jit(solution)/shard_map/ppermute | solution.py:273
  31.4 3.6 %all-to-all-start = ((bf16[4,2,256,128]{3,2,1,0:T(8,128)(2,1)}), bf16[4,2,256,128]{3,2,1,0:T(8,128)(2,1)S(1)}, u32[]{:S(2)}, u32[]{:S(2)}) async-start(bf16[4,2,256,128]{3,2,1,0:T(8,128)(2,1)} %get-tuple-element.16), calls=%async_computation | async-start | bytes 1048576 | tf_op jit(solution)/shard_map/all_to_all | solution.py:276
  35.1 2.2 %shard_map.77 = (s32[4,256]{1,0:T(4,128)}, s32[4]{0:T(128)}) custom-call(s32[1]{0:T(128)} %bitcast.2.range_ref, s32[1,32768]{1,0:T(1,128)} %seg_ref.1), custom_call_target="tpu_custom_call" | custom-call | bytes 1048576 | tf_op jit(solution)/shard_map/pallas_call | solution.py:105
  37.3 21.2 %collective-permute-done.1.before_ref = bf16[3,2,256,128]{3,2,1,0:T(8,128)(2,1)S(1)} collective-permute-done((bf16[3,2,256,128]{3,2,1,0:T(8,128)(2,1)S(1)}, bf16[3,2,256,128]{3,2,1,0:T(8,128)(2,1)S(1)}, u32[]{:S(2)}, u32[]{:S(2)}) %collective-permute-start.1) | collective-permute-done | bytes 393248 | tf_op jit(solution)/shard_map/ppermute | solution.py:273
  58.5 0.0 collective-permute-done.last_ref
  58.5 0.1 shard_map.79
  58.6 0.0 all-to-all-done.query_ref
  58.6 0.0 copy-start
  58.6 0.0 copy-start.1
  58.6 0.0 copy-start.2
  58.6 0.7 copy-done
  59.3 0.0 copy-done.1
  59.3 0.0 copy-done.2
  59.3 6.6 %shard_map.80 = (bf16[4,256,128]{2,1,0:T(8,128)(2,1)S(1)}, f32[4,256,128]{2,1,0:T(8,128)S(1)}, bf16[4,256,128]{2,1,0:T(8,128)(2,1)S(1)}, bf16[3,256,128]{2,1,0:T(8,128)(2,1)S(1)}) custom-call(s32[1]{0:T(128)} %bitcast.1.head_ref, s32[4]{0:T(128)S(1)} %copy-done.2, f32[4]{0:T(128)S(1)} %copy-done.1, s32[4,256]{1,0:T(4,128)S(1)} %copy-done, ...), custom_call_target="tpu_custom_call" | custom-call | flops 1000000000 | bytes 6291456 | tf_op jit(solution)/shard_map/pallas_call | solution.py:240
  65.8 6.9 %collective-permute-start.2 = (bf16[4,256,128]{2,1,0:T(8,128)(2,1)S(1)}, bf16[4,256,128]{2,1,0:T(8,128)(2,1)S(1)}, u32[]{:S(2)}, u32[]{:S(2)}) collective-permute-start(bf16[4,256,128]{2,1,0:T(8,128)(2,1)S(1)} %get-tuple-element.22), channel_id=1, source_target_pairs={{28,0},{29,1},{30,2},{31,3},{24,4},{25,5},{26,6},{27,7},{20,8},{21... | collective-permute-start | bytes 786440 | tf_op jit(solution)/shard_map/ppermute | solution.py:273
  72.7 2.2 %collective-permute-start.3 = (bf16[3,256,128]{2,1,0:T(8,128)(2,1)S(1)}, bf16[3,256,128]{2,1,0:T(8,128)(2,1)S(1)}, u32[]{:S(2)}, u32[]{:S(2)}) collective-permute-start(bf16[3,256,128]{2,1,0:T(8,128)(2,1)S(1)} %get-tuple-element.23), channel_id=1, source_target_pairs={{32,0},{33,1},{34,2},{35,3},{36,4},{37,5},{38,6},{39,7},{40,8},{41... | collective-permute-start | bytes 589832 | tf_op jit(solution)/shard_map/ppermute | solution.py:273
  74.9 5.4 %collective-permute-done.3 = bf16[3,256,128]{2,1,0:T(8,128)(2,1)S(1)} collective-permute-done((bf16[3,256,128]{2,1,0:T(8,128)(2,1)S(1)}, bf16[3,256,128]{2,1,0:T(8,128)(2,1)S(1)}, u32[]{:S(2)}, u32[]{:S(2)}) %collective-permute-start.3) | collective-permute-done | bytes 196640 | tf_op jit(solution)/shard_map/ppermute | solution.py:273
  80.3 2.3 %collective-permute-done.2 = bf16[4,256,128]{2,1,0:T(8,128)(2,1)S(1)} collective-permute-done((bf16[4,256,128]{2,1,0:T(8,128)(2,1)S(1)}, bf16[4,256,128]{2,1,0:T(8,128)(2,1)S(1)}, u32[]{:S(2)}, u32[]{:S(2)}) %collective-permute-start.2) | collective-permute-done | bytes 262176 | tf_op jit(solution)/shard_map/ppermute | solution.py:273
  82.6 0.1 fusion
  82.7 0.1 pad_maximum_fusion
  82.8 18.0 %all_to_all.16.grads_ref = bf16[4,2,256,128]{3,2,1,0:T(8,128)(2,1)} all-to-all(bf16[4,2,256,128]{3,2,1,0:T(8,128)(2,1)S(1)} %pad_maximum_fusion), channel_id=1, replica_groups={{0,4,8,12},{16,20,24,28},{32,36,40,44},{48,52,56,60},{64,68,72,76},{80,..., dimensions={0} | all-to-all | bytes 1048576 | tf_op jit(solution)/shard_map/all_to_all | solution.py:276
  100.8 2.1 %shard_map.81 = (f32[256,512]{1,0:T(8,128)}, f32[256,512]{1,0:T(8,128)}) custom-call(s32[1]{0:T(128)} %bitcast.flip_ref, bf16[4,2,256,128]{3,2,1,0:T(8,128)(2,1)} %all_to_all.16.grads_ref), custom_call_target="tpu_custom_call" | custom-call | bytes 1572864 | tf_op jit(solution)/shard_map/pallas_call | solution.py:122
  (1 shorter events, 0.0 us)
Async XLA Ops:
  22.4 36.1 %collective-permute-start = (bf16[4,2,256,128]{3,2,1,0:T(8,128)(2,1)S(1)}, bf16[4,2,256,128]{3,2,1,0:T(8,128)(2,1)S(1)}, u32[]{:S(2)}, u32[]{:S(2)}) collective-permute-start(bf16[4,2,256,128]{3,2,1,0:T(8,128)(2,1)S(1)} %all_to_all.15.own_ref), channel_id=1, source_target_pairs={{0,28},{1,29},{2,30},{3,31},{4,24},{5,25},{6,26},{7,27},{8,20},{9,... | collective-permute-start | bytes 1572872 | tf_op jit(solution)/shard_map/ppermute | solution.py:273
  27.2 31.3 %collective-permute-start.1 = (bf16[3,2,256,128]{3,2,1,0:T(8,128)(2,1)S(1)}, bf16[3,2,256,128]{3,2,1,0:T(8,128)(2,1)S(1)}, u32[]{:S(2)}, u32[]{:S(2)}) collective-permute-start(bf16[3,2,256,128]{3,2,1,0:T(8,128)(2,1)S(1)} %slice.4), channel_id=1, source_target_pairs={{0,32},{1,33},{2,34},{3,35},{4,36},{5,37},{6,38},{7,39},{8,40},{9,... | collective-permute-start | bytes 1179656 | tf_op jit(solution)/shard_map/ppermute | solution.py:273
  31.4 27.1 %all-to-all-start = ((bf16[4,2,256,128]{3,2,1,0:T(8,128)(2,1)}), bf16[4,2,256,128]{3,2,1,0:T(8,128)(2,1)S(1)}, u32[]{:S(2)}, u32[]{:S(2)}) async-start(bf16[4,2,256,128]{3,2,1,0:T(8,128)(2,1)} %get-tuple-element.16), calls=%async_computation | async-start | bytes 1048576 | tf_op jit(solution)/shard_map/all_to_all | solution.py:276
  58.6 0.7 copy-start
  58.6 0.7 copy-start.1
  58.6 0.7 copy-start.2
  65.8 16.8 %collective-permute-start.2 = (bf16[4,256,128]{2,1,0:T(8,128)(2,1)S(1)}, bf16[4,256,128]{2,1,0:T(8,128)(2,1)S(1)}, u32[]{:S(2)}, u32[]{:S(2)}) collective-permute-start(bf16[4,256,128]{2,1,0:T(8,128)(2,1)S(1)} %get-tuple-element.22), channel_id=1, source_target_pairs={{28,0},{29,1},{30,2},{31,3},{24,4},{25,5},{26,6},{27,7},{20,8},{21... | collective-permute-start | bytes 786440 | tf_op jit(solution)/shard_map/ppermute | solution.py:273
  72.7 7.6 %collective-permute-start.3 = (bf16[3,256,128]{2,1,0:T(8,128)(2,1)S(1)}, bf16[3,256,128]{2,1,0:T(8,128)(2,1)S(1)}, u32[]{:S(2)}, u32[]{:S(2)}) collective-permute-start(bf16[3,256,128]{2,1,0:T(8,128)(2,1)S(1)} %get-tuple-element.23), channel_id=1, source_target_pairs={{32,0},{33,1},{34,2},{35,3},{36,4},{37,5},{38,6},{39,7},{40,8},{41... | collective-permute-start | bytes 589832 | tf_op jit(solution)/shard_map/ppermute | solution.py:273
